TPU v7x, 32 devices: a whole 2x2x4 slice. The times are simulated.
32 devices in a mesh: rep: 4 (over x, core), shard: 8 (over z, y).
Axes of the slice: x: 2, y: 2, z: 4, core: 2. Of those that a mesh axis runs over, the one named last changes fastest.
Arguments:
- hidden_acts: bfloat16 [24576, 128], P(('rep', 'shard')), may hold values from -6 to 6
- out_cotangent: bfloat16 [24576, 4096], P(('rep', 'shard')), may hold values from -0.0390625 to 0.0390625
- weight: bfloat16 [128, 4096], P('shard'), may hold values from -6 to 6
- first_moment: float32 [128, 4096], P('shard'), may hold values from -6 to 6
- second_moment: float32 [128, 4096], P('shard'), may hold values from 0.05 to 2
Outputs:
- new_weight: bfloat16 [128, 4096], replicated
- new_first: float32 [128, 4096], P('shard')
- new_second: float32 [128, 4096], P('shard')
All inputs are finite; a program needn't handle non-finite values.
Results may differ from a plain program's by a relative error of at most 0.0014.
Values may be sent and summed in bfloat16 or wider, within the bound.
No kernel may reach another device: no remote copies, remote signals or barrier semaphores. Data moves between devices by JAX's collectives and lax.ppermute only.
A program may use at most 128 MiB of HBM per device.

v0:
```python
import functools

import jax
import jax.numpy as jnp
from jax import lax
from jax.experimental import pallas as pl
from jax.experimental.pallas import tpu as pltpu
from jax.sharding import PartitionSpec as P

F32 = jnp.float32
BF16 = jnp.bfloat16
CHUNK = 512
LOAD_LIMIT = 45 * 1024 * 1024


def adamw_moments(first_moment, second_moment, grad):
    new_first = 0.9 * first_moment + 0.1 * grad
    new_second = 0.999 * second_moment + 0.001 * grad * grad
    return new_first, new_second


def adamw_weight(weight, new_first, new_second):
    corr_one = 0.9999734386011124
    corr_two = 0.0952078528
    wfloat = weight.astype(F32)
    update = new_first / corr_one / (jnp.sqrt(new_second / corr_two) + 1e-08)
    return (wfloat - 0.05 * (update + 0.1 * wfloat)).astype(BF16)


def shape(dims, kind):
    return jax.ShapeDtypeStruct(dims, kind)


def call(kernel, outs, *args, far_in=(), far_out=0, scratch=(), aliases=None, limit=48 * 1024 * 1024):
    near, far = pl.BlockSpec(memory_space=pltpu.VMEM), pl.BlockSpec(memory_space=pltpu.HBM)
    return pl.pallas_call(
        kernel,
        out_shape=outs,
        in_specs=[far if i in tuple(far_in) else near for i in range(len(args))],
        out_specs=[far if i < far_out else near for i in range(len(outs))],
        scratch_shapes=scratch,
        input_output_aliases=aliases or {},
        compiler_params=pltpu.CompilerParams(vmem_limit_bytes=limit),
    )(*args)


def exchange(value, other):
    reps, shards = lax.axis_size("rep"), lax.axis_size("shard")
    pairs = []
    for rep in range(reps):
        for shard in range(shards):
            to_rep, to_shard = other(rep, shard)
            pairs.append((rep * shards + shard, to_rep * shards + to_shard))
    return lax.ppermute(value, ("rep", "shard"), pairs)


def to_sibling(value):
    return exchange(value, lambda rep, shard: (rep ^ 1, shard))


SQUARE = ((1, 1), (1, 0), (0, 1))
LINE = (3, 2, 1)
STEPS = tuple(zip(SQUARE, LINE))
STAY = ((0, 0), 0)


def stage(value, step, square_core):
    (dy, dx), k = step
    return exchange(
        value,
        lambda rep, shard: (rep ^ (2 * dx), shard ^ dy) if rep & 1 == square_core else (rep, shard ^ (2 * k)),
    )


def wide_stage(value, step):
    return stage(value, step, 0)


def narrow_stage(value, step):
    return stage(value, step, 1)


def along_rest(value, k):
    return exchange(value, lambda rep, shard: (rep, shard ^ (8 * k)))


def place():
    rep, shard = lax.axis_index("rep"), lax.axis_index("shard")
    return rep & 1, rep >> 1, shard & 1, (shard >> 1) & 3, shard >> 3


def in_half(step, group):
    core, x, y, z, _ = place()
    (dy, dx), k = step
    first = core == 0
    return (
        jnp.where(first, y ^ dy, group >> 1), jnp.where(first, x ^ dx, group & 1), jnp.where(first, group, z ^ k),
    )


def group_of(step):
    core, x, y, z, _ = place()
    (dy, dx), k = step
    return jnp.where(core == 0, z ^ k, 2 * (y ^ dy) + (x ^ dx))


def block(index, size):
    return pl.ds(pl.multiple_of(index * size, size), size)


def load_kernel(cots_ref, away, kept, sems):
    core = place()[0]
    copies = []
    for out, side in ((away, 1 - core), (kept, core)):
        source = cots_ref.at[:, block(side, out.shape[1])]
        copies.append(pltpu.make_async_copy(source, out, sems.at[len(copies)]))
        copies[-1].start()
    for copy in copies:
        copy.wait()


def turn_kernel(acts, cots, out, turned):
    turned[...] = acts[...].T
    for i in range(out.shape[1] // CHUNK):
        at = slice(i * CHUNK, (i + 1) * CHUNK)
        out[:, at] = jnp.dot(turned[...], cots[:, at], preferred_element_type=F32).astype(BF16)


def product_kernel(turned, cots, out):
    skip = cots.shape[1] - out.shape[1]
    for i in range(out.shape[1] // CHUNK):
        at = slice(i * CHUNK, (i + 1) * CHUNK)
        term = jnp.dot(turned[...], cots[:, skip + i * CHUNK:skip + (i + 1) * CHUNK], preferred_element_type=F32)
        out[:, at] = term.astype(out.dtype)


def wide_kernel(rows, kept, came_low, came_high, own, *pieces):
    quarter = own.shape[1]
    count = own.shape[0] // (4 * rows)
    for step, out in zip((STAY,) + STEPS, (own,) + pieces):
        for group in range(4):
            y, x, z = in_half(step, group)
            cols = block(x, quarter)
            for w in range(count):
                at = block(8 * w + 2 * z + y, rows)
                came = jnp.where(x == 0, came_low[at, :], came_high[at, :])
                total = kept[at, cols] + came.astype(F32)
                to = (group * count + w) * rows
                out[to:to + rows, :] = total.astype(out.dtype)


def narrow_kernel(kept, *refs):
    came, (own, *pieces) = refs[:len(STEPS)], refs[len(STEPS):]
    for step, out in zip((STAY,) + STEPS, [own] + pieces):
        at = block(group_of(step), out.shape[0])
        total = kept[at, :]
        for ref in came:
            total += ref[at, :].astype(F32)
        out[...] = total.astype(out.dtype)


def rest_kernel(kept, *refs):
    came, outs = refs[:len(STEPS)], refs[len(STEPS):]
    w = place()[4]
    for k, out in enumerate(outs):
        at = block(w ^ k, out.shape[0])
        total = kept[at, :]
        for ref in came:
            total += ref[at, :].astype(F32)
        out[...] = total.astype(out.dtype)


def update_kernel(w, m, v, own, *refs):
    pieces, (new_w, grad) = refs[:-2], refs[-2:]
    core, x, _, _, _ = place()
    total = own[...]
    for ref in pieces:
        total += ref[...].astype(F32)
    grad[...] = total.astype(BF16)
    at = block(core * 2 + x, total.shape[1])
    new_m, new_v = adamw_moments(m[:, at], v[:, at], total)
    new_w[...] = adamw_weight(w[:, at], new_m, new_v)


def put(outs, at, value):
    for out in outs:
        out[at, :] = value


def put(outs, at, value):
    for out in outs:
        out[at, :] = value


def rest_back_kernel(*refs):
    pieces, outs = refs[:1 - len(STEPS)], refs[1 - len(STEPS):]
    w = place()[4]
    rows = pieces[0].shape[0]
    for k, ref in enumerate(pieces):
        put(outs, block(w ^ k, rows), ref[...])


def with_gradients_kernel(part, grad, sibling_grad, out):
    core = place()[0]
    size, rows = part.shape[0], grad.shape[0]
    out[:size, :] = part[...]
    out[block(size // rows + core, rows), :] = grad[...]
    out[block(size // rows + 1 - core, rows), :] = sibling_grad[...]


def narrow_back_kernel(own, *refs):
    parts, (*outs, far) = (own,) + refs[:-1 - len(STEPS)], refs[-1 - len(STEPS):]
    size = own.shape[0]
    for step, ref in zip((STAY,) + STEPS, parts):
        put(outs, block(group_of(step), size), ref[:size, :])
    far[...] = parts[-1][size:, :]


def half_blocks(rows, sibling, parts, out):
    core, x, y, z, _ = place()
    first = (core == 0) != sibling
    size, quarter = parts[0].shape
    count = size // (4 * rows)
    for ((dy, dx), k), ref in zip((STAY,) + STEPS, parts):
        for group in range(4):
            to_y = jnp.where(first, y ^ dy, group >> 1)
            to_x = jnp.where(first, x ^ dx, group & 1)
            to_z = jnp.where(first, group, z ^ k)
            for w in range(count):
                at = (group * count + w) * rows
                out[block(8 * w + 2 * to_z + to_y, rows), block(to_x, quarter)] = ref[at:at + rows, :]


def moments_kernel(m, v, grad, sibling_grad, far, sibling_far, new_m, new_v):
    core, x, _, _, _ = place()
    rows, quarter = grad.shape

    def fill(side, to_x, ref, at):
        cols = block(2 * side + to_x, quarter)
        new_m[:, cols], new_v[:, cols] = adamw_moments(m[:, cols], v[:, cols], ref[at, :].astype(F32))

    def fill_far(ref):
        for side in range(2):
            fill(side, 1 - x, ref, pl.ds(side * rows, rows))

    fill(core, x, grad, slice(None))
    fill(1 - core, x, sibling_grad, slice(None))

    @pl.when(core == 1)
    def _():
        fill_far(far)

    @pl.when(core != 1)
    def _():
        fill_far(sibling_far)


def write_kernel(sibling, *refs):
    parts, (out, half, sem) = refs[:1 + len(STEPS)], refs[-3:]
    rows = out.shape[0] // lax.axis_size("shard")
    half_blocks(rows, sibling, parts, half)
    copy = pltpu.make_async_copy(half, out.at[:, block(place()[0] ^ sibling, half.shape[1])], sem)
    copy.start()
    copy.wait()


def body(hidden_acts, out_cotangent, weight, first_moment, second_moment):
    rows, width = weight.shape
    tokens, all_rows = hidden_acts.shape
    half, quarter = width // 2, width // 4
    rest = lax.axis_size("shard") // 8
    wide_rows, narrow_rows = all_rows // 2, all_rows // 8

    away_cots, kept_cots = call(
        load_kernel, [shape((tokens, half), BF16)] * 2, out_cotangent,
        far_in=(0,), scratch=[pltpu.SemaphoreType.DMA((2,))], limit=LOAD_LIMIT,
    )
    low, turned = call(
        turn_kernel, [shape((all_rows, quarter), BF16), shape((all_rows, tokens), BF16)], hidden_acts, away_cots,
    )
    came_low = to_sibling(low)
    came_high = to_sibling(call(product_kernel, [shape((all_rows, quarter), BF16)], turned, away_cots)[0])
    kept = call(product_kernel, [shape((all_rows, half), F32)], turned, kept_cots)[0]

    def split(kernel, size, parts, *args):
        kept, sent = shape((size, quarter), F32), shape((size, quarter), BF16)
        return call(kernel, [kept] + [sent] * (parts - 1), *args)

    own, *pieces = split(functools.partial(wide_kernel, rows), wide_rows, 4, kept, came_low, came_high)
    came = [wide_stage(piece, step) for step, piece in zip(STEPS, pieces)]
    own, *pieces = split(narrow_kernel, narrow_rows, 4, own, *came)
    came = [narrow_stage(piece, step) for step, piece in zip(STEPS, pieces)]
    if rest > 1:
        own, *pieces = split(rest_kernel, rows, rest, own, *came)
        came = [along_rest(piece, k + 1) for k, piece in enumerate(pieces)]
    new_w, grad = call(
        update_kernel, [shape((rows, quarter), BF16)] * 2, weight, first_moment, second_moment, own, *came,
    )

    sibling_grad = to_sibling(grad)
    pieces = [along_rest(new_w, k) for k in range(1, rest)]
    parts = call(rest_back_kernel, [shape((narrow_rows, quarter), BF16)] * (len(STEPS) - 1), new_w, *pieces)
    parts += call(
        with_gradients_kernel, [shape((narrow_rows + 2 * rows, quarter), BF16)], parts[-1], grad, sibling_grad,
    )
    came = [narrow_stage(part, step) for step, part in zip(STEPS, parts)]
    *parts, far = call(
        narrow_back_kernel,
        [shape((wide_rows, quarter), BF16)] * len(STEPS) + [shape((2 * rows, quarter), BF16)], parts[-2], *came,
    )
    came = [wide_stage(part, step) for step, part in zip(STEPS, parts)]
    new_m, new_v = call(
        moments_kernel, [shape((rows, width), F32)] * 2,
        first_moment, second_moment, grad, sibling_grad, far, to_sibling(far),
    )
    came[0], new_m, new_v = lax.optimization_barrier((came[0], new_m, new_v))

    mine = [parts[-1]] + came
    others = [to_sibling(part) for part in mine]
    out = [shape((all_rows, width), BF16)]
    scratch = [pltpu.VMEM((all_rows, half), BF16), pltpu.SemaphoreType.DMA]
    new_w = call(functools.partial(write_kernel, 0), out, *mine, far_out=1, scratch=scratch)[0]
    new_w = call(
        functools.partial(write_kernel, 1), out, *others, new_w,
        far_in=(len(others),), far_out=1, scratch=scratch, aliases={len(others): 0},
    )[0]
    return new_w, new_m, new_v


def solution(mesh):
    return jax.shard_map(
        body,
        mesh=mesh,
        in_specs=(
            P(("rep", "shard"), None),
            P(("rep", "shard"), None),
            P("shard", None),
            P("shard", None),
            P("shard", None),
        ),
        out_specs=(P(), P("shard", None), P("shard", None)),
        check_vma=False,
    )
```

profile of v0, /device:TPU:0, one launch (start us, length us, event | category | flops | bytes accessed | tf_op | source)
XLA Modules:
  0.0 44.2 jit_solution(10743171657308121311)
XLA Ops:
  0.6 2.9 %shard_map.76 = (bf16[768,2048]{1,0:T(8,128)(2,1)S(1)}, bf16[768,2048]{1,0:T(8,128)(2,1)S(1)}) custom-call(bf16[768,4096]{1,0:T(8,128)(2,1)} %cots_ref.1), custom_call_target="tpu_custom_call" | custom-call | tf_op jit(solution)/shard_map/pallas_call | solution.py:36
  5.0 0.6 %shard_map.78.kept = f32[128,2048]{1,0:T(8,128)S(1)} custom-call(bf16[128,768]{1,0:T(8,128)(2,1)S(1)} %get-tuple-element.29.turned, bf16[768,2048]{1,0:T(8,128)(2,1)S(1)} %get-tuple-element.30.cots), custom_call_target="tpu_custom_call" | custom-call | tf_op jit(solution)/shard_map/pallas_call | solution.py:36
  5.6 0.8 %collective-permute-done.1.came_high = bf16[128,1024]{1,0:T(8,128)(2,1)S(1)} collective-permute-done((bf16[128,1024]{1,0:T(8,128)(2,1)S(1)}, bf16[128,1024]{1,0:T(8,128)(2,1)S(1)}, u32[]{:S(2)}, u32[]{:S(2)}) %collective-permute-start.1) | collective-permute-done | bytes 262176 | tf_op jit(solution)/shard_map/ppermute | solution.py:54
  6.6 3.6 %collective-permute-start.2 = (bf16[64,1024]{1,0:T(8,128)(2,1)S(1)}, bf16[64,1024]{1,0:T(8,128)(2,1)S(1)}, u32[]{:S(2)}, u32[]{:S(2)}) collective-permute-start(bf16[64,1024]{1,0:T(8,128)(2,1)S(1)} %get-tuple-element.33), channel_id=1, source_target_pairs={{0,17},{1,16},{2,19},{3,18},{4,21},{5,20},{6,23},{7,22},{8,14},{9,... | collective-permute-start | bytes 393224 | tf_op jit(solution)/shard_map/ppermute | solution.py:54
  10.2 0.5 %collective-permute-start.3 = (bf16[64,1024]{1,0:T(8,128)(2,1)S(1)}, bf16[64,1024]{1,0:T(8,128)(2,1)S(1)}, u32[]{:S(2)}, u32[]{:S(2)}) collective-permute-start(bf16[64,1024]{1,0:T(8,128)(2,1)S(1)} %get-tuple-element.34), channel_id=1, source_target_pairs={{0,1},{1,0},{2,3},{3,2},{4,5},{5,4},{6,7},{7,6},{8,12},{9,13},{10,... | collective-permute-start | bytes 393224 | tf_op jit(solution)/shard_map/ppermute | solution.py:54
  10.9 2.3 %collective-permute-done.2.refs_0_ = bf16[64,1024]{1,0:T(8,128)(2,1)S(1)} collective-permute-done((bf16[64,1024]{1,0:T(8,128)(2,1)S(1)}, bf16[64,1024]{1,0:T(8,128)(2,1)S(1)}, u32[]{:S(2)}, u32[]{:S(2)}) %collective-permute-start.2) | collective-permute-done | bytes 131104 | tf_op jit(solution)/shard_map/ppermute | solution.py:54
  13.2 2.0 %collective-permute-done.3.refs_1_ = bf16[64,1024]{1,0:T(8,128)(2,1)S(1)} collective-permute-done((bf16[64,1024]{1,0:T(8,128)(2,1)S(1)}, bf16[64,1024]{1,0:T(8,128)(2,1)S(1)}, u32[]{:S(2)}, u32[]{:S(2)}) %collective-permute-start.3) | collective-permute-done | bytes 131104 | tf_op jit(solution)/shard_map/ppermute | solution.py:54
  15.2 0.5 %collective-permute-done.4.refs_2_ = bf16[64,1024]{1,0:T(8,128)(2,1)S(1)} collective-permute-done((bf16[64,1024]{1,0:T(8,128)(2,1)S(1)}, bf16[64,1024]{1,0:T(8,128)(2,1)S(1)}, u32[]{:S(2)}, u32[]{:S(2)}) %collective-permute-start.4) | collective-permute-done | bytes 131104 | tf_op jit(solution)/shard_map/ppermute | solution.py:54
  15.8 3.7 %collective-permute-start.5 = (bf16[16,1024]{1,0:T(8,128)(2,1)S(1)}, bf16[16,1024]{1,0:T(8,128)(2,1)S(1)}, u32[]{:S(2)}, u32[]{:S(2)}) collective-permute-start(bf16[16,1024]{1,0:T(8,128)(2,1)S(1)} %get-tuple-element.37), channel_id=1, source_target_pairs={{0,6},{1,7},{2,4},{3,5},{4,2},{5,3},{6,0},{7,1},{8,25},{9,24},{10,... | collective-permute-start | bytes 98312 | tf_op jit(solution)/shard_map/ppermute | solution.py:54
  19.4 0.8 %collective-permute-start.7 = (bf16[16,1024]{1,0:T(8,128)(2,1)S(1)}, bf16[16,1024]{1,0:T(8,128)(2,1)S(1)}, u32[]{:S(2)}, u32[]{:S(2)}) collective-permute-start(bf16[16,1024]{1,0:T(8,128)(2,1)S(1)} %get-tuple-element.39), channel_id=1, source_target_pairs={{0,2},{1,3},{2,0},{3,1},{4,6},{5,7},{6,4},{7,5},{8,24},{9,25},{10,... | collective-permute-start | bytes 98312 | tf_op jit(solution)/shard_map/ppermute | solution.py:54
  20.2 1.3 %collective-permute-done.5.refs_0_ = bf16[16,1024]{1,0:T(8,128)(2,1)S(1)} collective-permute-done((bf16[16,1024]{1,0:T(8,128)(2,1)S(1)}, bf16[16,1024]{1,0:T(8,128)(2,1)S(1)}, u32[]{:S(2)}, u32[]{:S(2)}) %collective-permute-start.5) | collective-permute-done | bytes 32800 | tf_op jit(solution)/shard_map/ppermute | solution.py:54
  21.5 2.7 %collective-permute-done.6.refs_1_ = bf16[16,1024]{1,0:T(8,128)(2,1)S(1)} collective-permute-done((bf16[16,1024]{1,0:T(8,128)(2,1)S(1)}, bf16[16,1024]{1,0:T(8,128)(2,1)S(1)}, u32[]{:S(2)}, u32[]{:S(2)}) %collective-permute-start.6) | collective-permute-done | bytes 32800 | tf_op jit(solution)/shard_map/ppermute | solution.py:54
  24.5 1.2 %collective-permute-done.10.sibling_grad = bf16[16,1024]{1,0:T(8,128)(2,1)S(1)} collective-permute-done((bf16[16,1024]{1,0:T(8,128)(2,1)S(1)}, bf16[16,1024]{1,0:T(8,128)(2,1)S(1)}, u32[]{:S(2)}, u32[]{:S(2)}) %collective-permute-start.10) | collective-permute-done | bytes 32800 | tf_op jit(solution)/shard_map/ppermute | solution.py:54
  25.7 3.5 %collective-permute-start.8 = (bf16[16,1024]{1,0:T(8,128)(2,1)S(1)}, bf16[16,1024]{1,0:T(8,128)(2,1)S(1)}, u32[]{:S(2)}, u32[]{:S(2)}) collective-permute-start(bf16[16,1024]{1,0:T(8,128)(2,1)S(1)} %get-tuple-element.42), channel_id=1, source_target_pairs={{0,6},{1,7},{2,4},{3,5},{4,2},{5,3},{6,0},{7,1},{8,25},{9,24},{10,... | collective-permute-start | bytes 98312 | tf_op jit(solution)/shard_map/ppermute | solution.py:54
  29.2 2.9 %collective-permute-done.8.refs_0_ = bf16[16,1024]{1,0:T(8,128)(2,1)S(1)} collective-permute-done((bf16[16,1024]{1,0:T(8,128)(2,1)S(1)}, bf16[16,1024]{1,0:T(8,128)(2,1)S(1)}, u32[]{:S(2)}, u32[]{:S(2)}) %collective-permute-start.8) | collective-permute-done | bytes 32800 | tf_op jit(solution)/shard_map/ppermute | solution.py:54
  32.1 1.9 %collective-permute-done.9.refs_1_ = bf16[16,1024]{1,0:T(8,128)(2,1)S(1)} collective-permute-done((bf16[16,1024]{1,0:T(8,128)(2,1)S(1)}, bf16[16,1024]{1,0:T(8,128)(2,1)S(1)}, u32[]{:S(2)}, u32[]{:S(2)}) %collective-permute-start.9) | collective-permute-done | bytes 32800 | tf_op jit(solution)/shard_map/ppermute | solution.py:54
  34.1 1.7 %collective-permute-start.13 = (bf16[64,1024]{1,0:T(8,128)(2,1)S(1)}, bf16[64,1024]{1,0:T(8,128)(2,1)S(1)}, u32[]{:S(2)}, u32[]{:S(2)}) collective-permute-start(bf16[64,1024]{1,0:T(8,128)(2,1)S(1)} %get-tuple-element.45), channel_id=1, source_target_pairs={{0,17},{1,16},{2,19},{3,18},{4,21},{5,20},{6,23},{7,22},{8,14},{9,... | collective-permute-start | bytes 393224 | tf_op jit(solution)/shard_map/ppermute | solution.py:54
  35.8 1.1 %collective-permute-start.16 = (bf16[64,1024]{1,0:T(8,128)(2,1)S(1)}, bf16[64,1024]{1,0:T(8,128)(2,1)S(1)}, u32[]{:S(2)}, u32[]{:S(2)}) collective-permute-start(bf16[64,1024]{1,0:T(8,128)(2,1)S(1)} %get-tuple-element.50), channel_id=1, source_target_pairs={{0,1},{1,0},{2,3},{3,2},{4,5},{5,4},{6,7},{7,6},{8,12},{9,13},{10,... | collective-permute-start | bytes 393224 | tf_op jit(solution)/shard_map/ppermute | solution.py:54
  36.9 0.8 %collective-permute-start.18 = (bf16[64,1024]{1,0:T(8,128)(2,1)S(1)}, bf16[64,1024]{1,0:T(8,128)(2,1)S(1)}, u32[]{:S(2)}, u32[]{:S(2)}) collective-permute-start(bf16[64,1024]{1,0:T(8,128)(2,1)S(1)} %get-tuple-element.44.refs_0_), channel_id=1, source_target_pairs={{0,16},{1,17},{2,18},{3,19},{4,20},{5,21},{6,22},{7,23},{8,10},{9,... | collective-permute-start | bytes 393224 | tf_op jit(solution)/shard_map/ppermute | solution.py:54
  38.1 0.7 %collective-permute-done.14.sibling_far = bf16[32,1024]{1,0:T(8,128)(2,1)S(1)} collective-permute-done((bf16[32,1024]{1,0:T(8,128)(2,1)S(1)}, bf16[32,1024]{1,0:T(8,128)(2,1)S(1)}, u32[]{:S(2)}, u32[]{:S(2)}) %collective-permute-start.14) | collective-permute-done | bytes 65568 | tf_op jit(solution)/shard_map/ppermute | solution.py:54
  38.9 0.9 %shard_map.86 = (f32[16,4096]{1,0:T(8,128)}, f32[16,4096]{1,0:T(8,128)}) custom-call(f32[16,4096]{1,0:T(8,128)S(1)} %copy-done, f32[16,4096]{1,0:T(8,128)S(1)} %copy-done.1, bf16[16,1024]{1,0:T(8,128)(2,1)S(1)} %get-tuple-element.43.grad, bf16[16,1024]{1,0:T(8,128)(2,1)S(1)} %collective-permute-done.10.sibling_grad, ...), custom_call_target="tpu_custom_call" | custom-call | tf_op jit(solution)/shard_map/pallas_call | solution.py:36
  40.1 1.3 %collective-permute-done.16.refs_2_ = bf16[64,1024]{1,0:T(8,128)(2,1)S(1)} collective-permute-done((bf16[64,1024]{1,0:T(8,128)(2,1)S(1)}, bf16[64,1024]{1,0:T(8,128)(2,1)S(1)}, u32[]{:S(2)}, u32[]{:S(2)}) %collective-permute-start.16) | collective-permute-done | bytes 131104 | tf_op jit(solution)/shard_map/ppermute | solution.py:54
  42.4 0.8 %shard_map.87.refs_4_ = bf16[128,4096]{1,0:T(8,128)(2,1)} custom-call(bf16[64,1024]{1,0:T(8,128)(2,1)S(1)} %get-tuple-element.44.refs_0_, bf16[64,1024]{1,0:T(8,128)(2,1)S(1)} %collective-permute-done.13.refs_1_, bf16[64,1024]{1,0:T(8,128)(2,1)S(1)} %collective-permute-done.16.refs_2_, bf16[64,1024]{1,0:T(8,128)(2,1)S(1)} %collective-permute-done.18.refs_3_), custom_call_target="tpu_custom_call" | custom-call | tf_op jit(solution)/shard_map/pallas_call | solution.py:36
  43.4 0.8 %shard_map.88 = bf16[128,4096]{1,0:T(8,128)(2,1)} custom-call(bf16[64,1024]{1,0:T(8,128)(2,1)S(1)} %collective-permute-done.12.refs_0_, bf16[64,1024]{1,0:T(8,128)(2,1)S(1)} %collective-permute-done.15.refs_1_, bf16[64,1024]{1,0:T(8,128)(2,1)S(1)} %collective-permute-done.17.refs_2_, ...), custom_call_target="tpu_custom_call", output_to_operand_aliasing={{}: (4, {})} | custom-call | tf_op jit(solution)/shard_map/pallas_call | solution.py:36
  (37 shorter events, 4.0 us)
Async XLA Ops:
  0.6 2.9 %copy-start.2 = (bf16[768,128]{1,0:T(8,128)(2,1)S(1)}, bf16[768,128]{1,0:T(8,128)(2,1)}, u32[]{:S(2)}) copy-start(bf16[768,128]{1,0:T(8,128)(2,1)} %acts.1) | copy-start | bytes 589828
  4.0 1.7 %collective-permute-start = (bf16[128,1024]{1,0:T(8,128)(2,1)S(1)}, bf16[128,1024]{1,0:T(8,128)(2,1)S(1)}, u32[]{:S(2)}, u32[]{:S(2)}) collective-permute-start(bf16[128,1024]{1,0:T(8,128)(2,1)S(1)} %get-tuple-element.31), channel_id=1, source_target_pairs={{0,8},{1,9},{2,10},{3,11},{4,12},{5,13},{6,14},{7,15},{8,0},{9,1},... | collective-permute-start | bytes 786440 | tf_op jit(solution)/shard_map/ppermute | solution.py:54
  4.9 1.6 %collective-permute-start.1 = (bf16[128,1024]{1,0:T(8,128)(2,1)S(1)}, bf16[128,1024]{1,0:T(8,128)(2,1)S(1)}, u32[]{:S(2)}, u32[]{:S(2)}) collective-permute-start(bf16[128,1024]{1,0:T(8,128)(2,1)S(1)} %shard_map.79), channel_id=1, source_target_pairs={{0,8},{1,9},{2,10},{3,11},{4,12},{5,13},{6,14},{7,15},{8,0},{9,1},... | collective-permute-start | bytes 786440 | tf_op jit(solution)/shard_map/ppermute | solution.py:54
  5.0 19.2 %copy-start = (f32[16,4096]{1,0:T(8,128)S(1)}, f32[16,4096]{1,0:T(8,128)}, u32[]{:S(2)}) copy-start(f32[16,4096]{1,0:T(8,128)} %m.3) | copy-start | bytes 786436
  5.0 19.2 %copy-start.1 = (f32[16,4096]{1,0:T(8,128)S(1)}, f32[16,4096]{1,0:T(8,128)}, u32[]{:S(2)}) copy-start(f32[16,4096]{1,0:T(8,128)} %v.3) | copy-start | bytes 786436
  5.0 19.2 %copy-start.3 = (bf16[16,4096]{1,0:T(8,128)(2,1)S(1)}, bf16[16,4096]{1,0:T(8,128)(2,1)}, u32[]{:S(2)}) copy-start(bf16[16,4096]{1,0:T(8,128)(2,1)} %w.1) | copy-start | bytes 393220
  6.6 6.6 %collective-permute-start.2 = (bf16[64,1024]{1,0:T(8,128)(2,1)S(1)}, bf16[64,1024]{1,0:T(8,128)(2,1)S(1)}, u32[]{:S(2)}, u32[]{:S(2)}) collective-permute-start(bf16[64,1024]{1,0:T(8,128)(2,1)S(1)} %get-tuple-element.33), channel_id=1, source_target_pairs={{0,17},{1,16},{2,19},{3,18},{4,21},{5,20},{6,23},{7,22},{8,14},{9,... | collective-permute-start | bytes 393224 | tf_op jit(solution)/shard_map/ppermute | solution.py:54
  10.2 5.0 %collective-permute-start.3 = (bf16[64,1024]{1,0:T(8,128)(2,1)S(1)}, bf16[64,1024]{1,0:T(8,128)(2,1)S(1)}, u32[]{:S(2)}, u32[]{:S(2)}) collective-permute-start(bf16[64,1024]{1,0:T(8,128)(2,1)S(1)} %get-tuple-element.34), channel_id=1, source_target_pairs={{0,1},{1,0},{2,3},{3,2},{4,5},{5,4},{6,7},{7,6},{8,12},{9,13},{10,... | collective-permute-start | bytes 393224 | tf_op jit(solution)/shard_map/ppermute | solution.py:54
  10.7 5.0 %collective-permute-start.4 = (bf16[64,1024]{1,0:T(8,128)(2,1)S(1)}, bf16[64,1024]{1,0:T(8,128)(2,1)S(1)}, u32[]{:S(2)}, u32[]{:S(2)}) collective-permute-start(bf16[64,1024]{1,0:T(8,128)(2,1)S(1)} %get-tuple-element.35), channel_id=1, source_target_pairs={{0,16},{1,17},{2,18},{3,19},{4,20},{5,21},{6,22},{7,23},{8,10},{9,... | collective-permute-start | bytes 393224 | tf_op jit(solution)/shard_map/ppermute | solution.py:54
  15.8 5.8 %collective-permute-start.5 = (bf16[16,1024]{1,0:T(8,128)(2,1)S(1)}, bf16[16,1024]{1,0:T(8,128)(2,1)S(1)}, u32[]{:S(2)}, u32[]{:S(2)}) collective-permute-start(bf16[16,1024]{1,0:T(8,128)(2,1)S(1)} %get-tuple-element.37), channel_id=1, source_target_pairs={{0,6},{1,7},{2,4},{3,5},{4,2},{5,3},{6,0},{7,1},{8,25},{9,24},{10,... | collective-permute-start | bytes 98312 | tf_op jit(solution)/shard_map/ppermute | solution.py:54
  19.4 4.8 %collective-permute-start.6 = (bf16[16,1024]{1,0:T(8,128)(2,1)S(1)}, bf16[16,1024]{1,0:T(8,128)(2,1)S(1)}, u32[]{:S(2)}, u32[]{:S(2)}) collective-permute-start(bf16[16,1024]{1,0:T(8,128)(2,1)S(1)} %get-tuple-element.38), channel_id=1, source_target_pairs={{0,4},{1,5},{2,6},{3,7},{4,0},{5,1},{6,2},{7,3},{8,9},{9,8},{10,11... | collective-permute-start | bytes 98312 | tf_op jit(solution)/shard_map/ppermute | solution.py:54
  19.4 4.8 %collective-permute-start.7 = (bf16[16,1024]{1,0:T(8,128)(2,1)S(1)}, bf16[16,1024]{1,0:T(8,128)(2,1)S(1)}, u32[]{:S(2)}, u32[]{:S(2)}) collective-permute-start(bf16[16,1024]{1,0:T(8,128)(2,1)S(1)} %get-tuple-element.39), channel_id=1, source_target_pairs={{0,2},{1,3},{2,0},{3,1},{4,6},{5,7},{6,4},{7,5},{8,24},{9,25},{10,... | collective-permute-start | bytes 98312 | tf_op jit(solution)/shard_map/ppermute | solution.py:54
  24.4 1.3 %collective-permute-start.10 = (bf16[16,1024]{1,0:T(8,128)(2,1)S(1)}, bf16[16,1024]{1,0:T(8,128)(2,1)S(1)}, u32[]{:S(2)}, u32[]{:S(2)}) collective-permute-start(bf16[16,1024]{1,0:T(8,128)(2,1)S(1)} %get-tuple-element.43.grad), channel_id=1, source_target_pairs={{0,8},{1,9},{2,10},{3,11},{4,12},{5,13},{6,14},{7,15},{8,0},{9,1},... | collective-permute-start | bytes 98312 | tf_op jit(solution)/shard_map/ppermute | solution.py:54
  25.6 8.4 %collective-permute-start.11 = (bf16[48,1024]{1,0:T(8,128)(2,1)S(1)}, bf16[48,1024]{1,0:T(8,128)(2,1)S(1)}, u32[]{:S(2)}, u32[]{:S(2)}) collective-permute-start(bf16[48,1024]{1,0:T(8,128)(2,1)S(1)} %shard_map.84), channel_id=1, source_target_pairs={{0,2},{1,3},{2,0},{3,1},{4,6},{5,7},{6,4},{7,5},{8,24},{9,25},{10,... | collective-permute-start | bytes 294920 | tf_op jit(solution)/shard_map/ppermute | solution.py:54
  25.7 6.4 %collective-permute-start.8 = (bf16[16,1024]{1,0:T(8,128)(2,1)S(1)}, bf16[16,1024]{1,0:T(8,128)(2,1)S(1)}, u32[]{:S(2)}, u32[]{:S(2)}) collective-permute-start(bf16[16,1024]{1,0:T(8,128)(2,1)S(1)} %get-tuple-element.42), channel_id=1, source_target_pairs={{0,6},{1,7},{2,4},{3,5},{4,2},{5,3},{6,0},{7,1},{8,25},{9,24},{10,... | collective-permute-start | bytes 98312 | tf_op jit(solution)/shard_map/ppermute | solution.py:54
  29.2 4.8 %collective-permute-start.9 = (bf16[16,1024]{1,0:T(8,128)(2,1)S(1)}, bf16[16,1024]{1,0:T(8,128)(2,1)S(1)}, u32[]{:S(2)}, u32[]{:S(2)}) collective-permute-start(bf16[16,1024]{1,0:T(8,128)(2,1)S(1)} %get-tuple-element.41.part.own), channel_id=1, source_target_pairs={{0,4},{1,5},{2,6},{3,7},{4,0},{5,1},{6,2},{7,3},{8,9},{9,8},{10,11... | collective-permute-start | bytes 98312 | tf_op jit(solution)/shard_map/ppermute | solution.py:54
  34.1 6.0 %collective-permute-start.13 = (bf16[64,1024]{1,0:T(8,128)(2,1)S(1)}, bf16[64,1024]{1,0:T(8,128)(2,1)S(1)}, u32[]{:S(2)}, u32[]{:S(2)}) collective-permute-start(bf16[64,1024]{1,0:T(8,128)(2,1)S(1)} %get-tuple-element.45), channel_id=1, source_target_pairs={{0,17},{1,16},{2,19},{3,18},{4,21},{5,20},{6,23},{7,22},{8,14},{9,... | collective-permute-start | bytes 393224 | tf_op jit(solution)/shard_map/ppermute | solution.py:54
  35.8 5.6 %collective-permute-start.16 = (bf16[64,1024]{1,0:T(8,128)(2,1)S(1)}, bf16[64,1024]{1,0:T(8,128)(2,1)S(1)}, u32[]{:S(2)}, u32[]{:S(2)}) collective-permute-start(bf16[64,1024]{1,0:T(8,128)(2,1)S(1)} %get-tuple-element.50), channel_id=1, source_target_pairs={{0,1},{1,0},{2,3},{3,2},{4,5},{5,4},{6,7},{7,6},{8,12},{9,13},{10,... | collective-permute-start | bytes 393224 | tf_op jit(solution)/shard_map/ppermute | solution.py:54
  36.9 5.0 %collective-permute-start.18 = (bf16[64,1024]{1,0:T(8,128)(2,1)S(1)}, bf16[64,1024]{1,0:T(8,128)(2,1)S(1)}, u32[]{:S(2)}, u32[]{:S(2)}) collective-permute-start(bf16[64,1024]{1,0:T(8,128)(2,1)S(1)} %get-tuple-element.44.refs_0_), channel_id=1, source_target_pairs={{0,16},{1,17},{2,18},{3,19},{4,20},{5,21},{6,22},{7,23},{8,10},{9,... | collective-permute-start | bytes 393224 | tf_op jit(solution)/shard_map/ppermute | solution.py:54
  37.6 1.3 %collective-permute-start.14 = (bf16[32,1024]{1,0:T(8,128)(2,1)S(1)}, bf16[32,1024]{1,0:T(8,128)(2,1)S(1)}, u32[]{:S(2)}, u32[]{:S(2)}) collective-permute-start(bf16[32,1024]{1,0:T(8,128)(2,1)S(1)} %get-tuple-element.46.far), channel_id=1, source_target_pairs={{0,8},{1,9},{2,10},{3,11},{4,12},{5,13},{6,14},{7,15},{8,0},{9,1},... | collective-permute-start | bytes 196616 | tf_op jit(solution)/shard_map/ppermute | solution.py:54
  37.6 5.6 %collective-permute-start.12 = (bf16[64,1024]{1,0:T(8,128)(2,1)S(1)}, bf16[64,1024]{1,0:T(8,128)(2,1)S(1)}, u32[]{:S(2)}, u32[]{:S(2)}) collective-permute-start(bf16[64,1024]{1,0:T(8,128)(2,1)S(1)} %get-tuple-element.44.refs_0_), channel_id=1, source_target_pairs={{0,8},{1,9},{2,10},{3,11},{4,12},{5,13},{6,14},{7,15},{8,0},{9,1},... | collective-permute-start | bytes 393224 | tf_op jit(solution)/shard_map/ppermute | solution.py:54
  41.4 1.8 %collective-permute-start.17 = (bf16[64,1024]{1,0:T(8,128)(2,1)S(1)}, bf16[64,1024]{1,0:T(8,128)(2,1)S(1)}, u32[]{:S(2)}, u32[]{:S(2)}) collective-permute-start(bf16[64,1024]{1,0:T(8,128)(2,1)S(1)} %collective-permute-done.16.refs_2_), channel_id=1, source_target_pairs={{0,8},{1,9},{2,10},{3,11},{4,12},{5,13},{6,14},{7,15},{8,0},{9,1},... | collective-permute-start | bytes 393224 | tf_op jit(solution)/shard_map/ppermute | solution.py:54
  41.8 1.4 %collective-permute-start.19 = (bf16[64,1024]{1,0:T(8,128)(2,1)S(1)}, bf16[64,1024]{1,0:T(8,128)(2,1)S(1)}, u32[]{:S(2)}, u32[]{:S(2)}) collective-permute-start(bf16[64,1024]{1,0:T(8,128)(2,1)S(1)} %collective-permute-done.18.refs_3_), channel_id=1, source_target_pairs={{0,8},{1,9},{2,10},{3,11},{4,12},{5,13},{6,14},{7,15},{8,0},{9,1},... | collective-permute-start | bytes 393224 | tf_op jit(solution)/shard_map/ppermute | solution.py:54
  41.9 1.5 %collective-permute-start.15 = (bf16[64,1024]{1,0:T(8,128)(2,1)S(1)}, bf16[64,1024]{1,0:T(8,128)(2,1)S(1)}, u32[]{:S(2)}, u32[]{:S(2)}) collective-permute-start(bf16[64,1024]{1,0:T(8,128)(2,1)S(1)} %collective-permute-done.13.refs_1_), channel_id=1, source_target_pairs={{0,8},{1,9},{2,10},{3,11},{4,12},{5,13},{6,14},{7,15},{8,0},{9,1},... | collective-permute-start | bytes 393224 | tf_op jit(solution)/shard_map/ppermute | solution.py:54
where the time goes:
time: 44.4 us; the launch traced here: 44.2 us
  waiting for transfers between devices  18.7 us (42%)
  starting transfers between devices  17.6 us (40%)
  Pallas kernels  7.14 us (16%)
  between operations  0.78 us (2%)
    ppermute x20, waiting for transfers between devices, exchange(): return lax.ppermute(value, ('rep', 'shard'), pairs)  18.7 us
    ppermute x20, starting transfers between devices, exchange(): return lax.ppermute(value, ('rep', 'shard'), pairs)  17.6 us
    pallas_call x13, Pallas kernels, call(): pl.pallas_call(kernel, out_shape=outs, in_specs=[far if i in tuple(far_in...  7.14 us
  transfers between devices with their start and end apart: 20, of which 14 were waited for; matrix products, arithmetic and copies ran while one was open for 0% of the time, Pallas kernels for 6%

commit v1 on v0

--- a/solution.py
+++ b/solution.py
@@ -10,7 +10,8 @@
 F32 = jnp.float32
 BF16 = jnp.bfloat16
 CHUNK = 512
-LOAD_LIMIT = 45 * 1024 * 1024
+LOAD_LIMIT = 48 * 1024 * 1024
+KEPT_LIMIT = 50 * 1024 * 1024
 
 
 def adamw_moments(first_moment, second_moment, grad):
@@ -80,6 +81,10 @@
     return stage(value, step, 1)
 
 
+def along_x(value):
+    return exchange(value, lambda rep, shard: (rep ^ 2, shard))
+
+
 def along_rest(value, k):
     return exchange(value, lambda rep, shard: (rep, shard ^ (8 * k)))
 
@@ -108,33 +113,41 @@
     return pl.ds(pl.multiple_of(index * size, size), size)
 
 
-def load_kernel(cots_ref, away, kept, sems):
+def load_kernel(cots_ref, away, first, sems):
     core = place()[0]
     copies = []
-    for out, side in ((away, 1 - core), (kept, core)):
-        source = cots_ref.at[:, block(side, out.shape[1])]
-        copies.append(pltpu.make_async_copy(source, out, sems.at[len(copies)]))
+    for out, side in ((away, 1 - core), (first, core)):
+        at = pl.ds(pl.multiple_of(side * away.shape[1], CHUNK), out.shape[1])
+        copies.append(pltpu.make_async_copy(cots_ref.at[:, at], out, sems.at[len(copies)]))
         copies[-1].start()
     for copy in copies:
         copy.wait()
 
 
-def turn_kernel(acts, cots, out, turned):
+def away_kernel(acts, cots, out, turned):
     turned[...] = acts[...].T
     for i in range(out.shape[1] // CHUNK):
         at = slice(i * CHUNK, (i + 1) * CHUNK)
         out[:, at] = jnp.dot(turned[...], cots[:, at], preferred_element_type=F32).astype(BF16)
 
 
-def product_kernel(turned, cots, out):
-    skip = cots.shape[1] - out.shape[1]
-    for i in range(out.shape[1] // CHUNK):
+def kept_kernel(turned, first, cots_ref, out, cots, sems):
+    core = place()[0]
+    ready, count = first.shape[1] // CHUNK, out.shape[1] // CHUNK
+    copies = []
+    for i in range(ready, count):
+        source = cots_ref.at[:, block(core * count + i, CHUNK)]
+        copies.append(pltpu.make_async_copy(source, cots.at[i - ready], sems.at[i - ready]))
+        copies[-1].start()
+    for i in range(count):
         at = slice(i * CHUNK, (i + 1) * CHUNK)
-        term = jnp.dot(turned[...], cots[:, skip + i * CHUNK:skip + (i + 1) * CHUNK], preferred_element_type=F32)
-        out[:, at] = term.astype(out.dtype)
-
-
-def wide_kernel(rows, kept, came_low, came_high, own, *pieces):
+        if i >= ready:
+            copies[i - ready].wait()
+        chunk = cots[i - ready] if i >= ready else first[:, at]
+        out[:, at] = jnp.dot(turned[...], chunk, preferred_element_type=F32)
+
+
+def wide_kernel(rows, kept, came, own, *pieces):
     quarter = own.shape[1]
     count = own.shape[0] // (4 * rows)
     for step, out in zip((STAY,) + STEPS, (own,) + pieces):
@@ -143,8 +156,7 @@
             cols = block(x, quarter)
             for w in range(count):
                 at = block(8 * w + 2 * z + y, rows)
-                came = jnp.where(x == 0, came_low[at, :], came_high[at, :])
-                total = kept[at, cols] + came.astype(F32)
+                total = kept[at, cols] + came[at, cols].astype(F32)
                 to = (group * count + w) * rows
                 out[to:to + rows, :] = total.astype(out.dtype)
 
@@ -193,27 +205,21 @@
 
 
 def rest_back_kernel(*refs):
-    pieces, outs = refs[:1 - len(STEPS)], refs[1 - len(STEPS):]
+    pieces, outs = refs[:-len(STEPS)], refs[-len(STEPS):]
     w = place()[4]
     rows = pieces[0].shape[0]
     for k, ref in enumerate(pieces):
         put(outs, block(w ^ k, rows), ref[...])
 
 
-def with_gradients_kernel(part, grad, sibling_grad, out):
+def narrow_back_kernel(grad, sibling_grad, own, *refs):
+    parts, (*outs, grads) = (own,) + refs[:-1 - len(STEPS)], refs[-1 - len(STEPS):]
+    size, rows = own.shape[0], grad.shape[0]
+    for step, ref in zip((STAY,) + STEPS, parts):
+        put(outs, block(group_of(step), size), ref[...])
     core = place()[0]
-    size, rows = part.shape[0], grad.shape[0]
-    out[:size, :] = part[...]
-    out[block(size // rows + core, rows), :] = grad[...]
-    out[block(size // rows + 1 - core, rows), :] = sibling_grad[...]
-
-
-def narrow_back_kernel(own, *refs):
-    parts, (*outs, far) = (own,) + refs[:-1 - len(STEPS)], refs[-1 - len(STEPS):]
-    size = own.shape[0]
-    for step, ref in zip((STAY,) + STEPS, parts):
-        put(outs, block(group_of(step), size), ref[:size, :])
-    far[...] = parts[-1][size:, :]
+    grads[block(core, rows), :] = grad[...]
+    grads[block(1 - core, rows), :] = sibling_grad[...]
 
 
 def half_blocks(rows, sibling, parts, out):
@@ -231,37 +237,43 @@
                 out[block(8 * w + 2 * to_z + to_y, rows), block(to_x, quarter)] = ref[at:at + rows, :]
 
 
-def moments_kernel(m, v, grad, sibling_grad, far, sibling_far, new_m, new_v):
-    core, x, _, _, _ = place()
-    rows, quarter = grad.shape
-
-    def fill(side, to_x, ref, at):
-        cols = block(2 * side + to_x, quarter)
-        new_m[:, cols], new_v[:, cols] = adamw_moments(m[:, cols], v[:, cols], ref[at, :].astype(F32))
-
-    def fill_far(ref):
-        for side in range(2):
-            fill(side, 1 - x, ref, pl.ds(side * rows, rows))
-
-    fill(core, x, grad, slice(None))
-    fill(1 - core, x, sibling_grad, slice(None))
-
-    @pl.when(core == 1)
-    def _():
-        fill_far(far)
-
-    @pl.when(core != 1)
-    def _():
-        fill_far(sibling_far)
-
-
-def write_kernel(sibling, *refs):
-    parts, (out, half, sem) = refs[:1 + len(STEPS)], refs[-3:]
-    rows = out.shape[0] // lax.axis_size("shard")
-    half_blocks(rows, sibling, parts, half)
+def write_moments(far, grads, m, v, m_out, v_out, new_m, new_v, sems):
+    x = place()[1]
+    rows, quarter = new_m.shape[1:]
+    copies = []
+    for side in range(2):
+        at = block(2 * side + (x ^ far), quarter)
+        grad = grads[side * rows:(side + 1) * rows, :].astype(F32)
+        new_m[side], new_v[side] = adamw_moments(m[:, at], v[:, at], grad)
+        for source, out in ((new_m, m_out), (new_v, v_out)):
+            copies.append(pltpu.make_async_copy(source.at[side], out.at[:, at], sems.at[len(copies)]))
+            copies[-1].start()
+    return copies
+
+
+def moments_kernel(m, v, grads, m_out, v_out, *scratch):
+    for copy in write_moments(0, grads, m, v, m_out, v_out, *scratch):
+        copy.wait()
+
+
+def write_half(sibling, parts, out, half, sem):
+    half_blocks(out.shape[0] // lax.axis_size("shard"), sibling, parts, half)
     copy = pltpu.make_async_copy(half, out.at[:, block(place()[0] ^ sibling, half.shape[1])], sem)
     copy.start()
-    copy.wait()
+    return copy
+
+
+def write_own_kernel(m, v, grads, _m, _v, *refs):
+    parts, (m_out, v_out, out, half, sem, *scratch) = refs[:1 + len(STEPS)], refs[1 + len(STEPS):]
+    rows = write_half(0, parts, out, half, sem)
+    for copy in write_moments(1, grads, m, v, m_out, v_out, *scratch):
+        copy.wait()
+    rows.wait()
+
+
+def write_other_kernel(_, *refs):
+    parts, (out, half, sem) = refs[:1 + len(STEPS)], refs[1 + len(STEPS):]
+    write_half(1, parts, out, half, sem).wait()
 
 
 def body(hidden_acts, out_cotangent, weight, first_moment, second_moment):
@@ -271,22 +283,26 @@
     rest = lax.axis_size("shard") // 8
     wide_rows, narrow_rows = all_rows // 2, all_rows // 8
 
-    away_cots, kept_cots = call(
-        load_kernel, [shape((tokens, half), BF16)] * 2, out_cotangent,
+    away_cots, first = call(
+        load_kernel, [shape((tokens, half), BF16), shape((tokens, quarter), BF16)], out_cotangent,
         far_in=(0,), scratch=[pltpu.SemaphoreType.DMA((2,))], limit=LOAD_LIMIT,
     )
-    low, turned = call(
-        turn_kernel, [shape((all_rows, quarter), BF16), shape((all_rows, tokens), BF16)], hidden_acts, away_cots,
-    )
-    came_low = to_sibling(low)
-    came_high = to_sibling(call(product_kernel, [shape((all_rows, quarter), BF16)], turned, away_cots)[0])
-    kept = call(product_kernel, [shape((all_rows, half), F32)], turned, kept_cots)[0]
+    away, turned = call(
+        away_kernel, [shape((all_rows, half), BF16), shape((all_rows, tokens), BF16)], hidden_acts, away_cots,
+    )
+    came = to_sibling(away)
+    later = (half - quarter) // CHUNK
+    kept = call(
+        kept_kernel, [shape((all_rows, half), F32)], turned, first, out_cotangent,
+        far_in=(2,), limit=KEPT_LIMIT,
+        scratch=[pltpu.VMEM((later, tokens, CHUNK), BF16), pltpu.SemaphoreType.DMA((later,))],
+    )[0]
 
     def split(kernel, size, parts, *args):
         kept, sent = shape((size, quarter), F32), shape((size, quarter), BF16)
         return call(kernel, [kept] + [sent] * (parts - 1), *args)
 
-    own, *pieces = split(functools.partial(wide_kernel, rows), wide_rows, 4, kept, came_low, came_high)
+    own, *pieces = split(functools.partial(wide_kernel, rows), wide_rows, 4, kept, came)
     came = [wide_stage(piece, step) for step, piece in zip(STEPS, pieces)]
     own, *pieces = split(narrow_kernel, narrow_rows, 4, own, *came)
     came = [narrow_stage(piece, step) for step, piece in zip(STEPS, pieces)]
@@ -299,30 +315,32 @@
 
     sibling_grad = to_sibling(grad)
     pieces = [along_rest(new_w, k) for k in range(1, rest)]
-    parts = call(rest_back_kernel, [shape((narrow_rows, quarter), BF16)] * (len(STEPS) - 1), new_w, *pieces)
-    parts += call(
-        with_gradients_kernel, [shape((narrow_rows + 2 * rows, quarter), BF16)], parts[-1], grad, sibling_grad,
-    )
+    parts = call(rest_back_kernel, [shape((narrow_rows, quarter), BF16)] * len(STEPS), new_w, *pieces)
     came = [narrow_stage(part, step) for step, part in zip(STEPS, parts)]
-    *parts, far = call(
+    *parts, grads = call(
         narrow_back_kernel,
-        [shape((wide_rows, quarter), BF16)] * len(STEPS) + [shape((2 * rows, quarter), BF16)], parts[-2], *came,
+        [shape((wide_rows, quarter), BF16)] * len(STEPS) + [shape((2 * rows, quarter), BF16)],
+        grad, sibling_grad, parts[-1], *came,
     )
     came = [wide_stage(part, step) for step, part in zip(STEPS, parts)]
+    far_grads = along_x(grads)
+    moments = [shape((rows, width), F32)] * 2
+    moments_scratch = [pltpu.VMEM((2, rows, quarter), F32)] * 2 + [pltpu.SemaphoreType.DMA((4,))]
     new_m, new_v = call(
-        moments_kernel, [shape((rows, width), F32)] * 2,
-        first_moment, second_moment, grad, sibling_grad, far, to_sibling(far),
-    )
-    came[0], new_m, new_v = lax.optimization_barrier((came[0], new_m, new_v))
+        moments_kernel, moments, first_moment, second_moment, grads, far_out=2, scratch=moments_scratch,
+    )
+    came[0], far_grads, new_m, new_v = lax.optimization_barrier((came[0], far_grads, new_m, new_v))
 
     mine = [parts[-1]] + came
     others = [to_sibling(part) for part in mine]
     out = [shape((all_rows, width), BF16)]
     scratch = [pltpu.VMEM((all_rows, half), BF16), pltpu.SemaphoreType.DMA]
-    new_w = call(functools.partial(write_kernel, 0), out, *mine, far_out=1, scratch=scratch)[0]
+    new_m, new_v, new_w = call(
+        write_own_kernel, moments + out, first_moment, second_moment, far_grads, new_m, new_v, *mine,
+        far_in=(3, 4), far_out=3, scratch=scratch + moments_scratch, aliases={3: 0, 4: 1},
+    )
     new_w = call(
-        functools.partial(write_kernel, 1), out, *others, new_w,
-        far_in=(len(others),), far_out=1, scratch=scratch, aliases={len(others): 0},
+        write_other_kernel, out, new_w, *others, far_in=(0,), far_out=1, scratch=scratch, aliases={0: 0},
     )[0]
     return new_w, new_m, new_v
 

time: 44.4 us -> 42.4 us (0.955)
  waiting for transfers between devices: 18.7 us -> 14.9 us
  starting transfers between devices: 17.6 us -> 18.8 us
  Pallas kernels: 7.14 us -> 7.82 us
    ppermute x20 -> x19, waiting for transfers between devices: 18.7 us -> 14.9 us  [exchange(): return lax.ppermute(value, ('rep', 'shard'), pairs)]
    ppermute x20 -> x19, starting transfers between devices: 17.6 us -> 18.8 us  [exchange(): return lax.ppermute(value, ('rep', 'shard'), pairs)]
    pallas_call x13 -> x11, Pallas kernels: 7.14 us -> 7.82 us  [call(): pl.pallas_call(kernel, out_shape=outs, in_specs=[far if i in tuple(far_in...]
  transfers between devices with their start and end apart: 20 -> 19, of which waited for: 14 -> 10; matrix products, arithmetic and copies ran while one was open for 0% -> 0% of each run, Pallas kernels for 6% -> 9%
where the time goes in v1:
time: 42.4 us; the launch traced here: 42.3 us
  starting transfers between devices  18.8 us (44%)
  waiting for transfers between devices  14.9 us (35%)
  Pallas kernels  7.82 us (18%)
  between operations  0.8 us (2%)
    ppermute x19, starting transfers between devices, exchange(): return lax.ppermute(value, ('rep', 'shard'), pairs)  18.8 us
    ppermute x19, waiting for transfers between devices, exchange(): return lax.ppermute(value, ('rep', 'shard'), pairs)  14.9 us
    pallas_call x11, Pallas kernels, call(): pl.pallas_call(kernel, out_shape=outs, in_specs=[far if i in tuple(far_in...  7.82 us
  transfers between devices with their start and end apart: 19, of which 10 were waited for; matrix products, arithmetic and copies ran while one was open for 0% of the time, Pallas kernels for 9%

profile of v1, /device:TPU:0, one launch (start us, length us, event | category | flops | bytes accessed | tf_op | source)
XLA Modules:
  0.0 42.3 jit_solution(8785618496929610695)
XLA Ops:
  0.6 2.4 %shard_map.76 = (bf16[768,2048]{1,0:T(8,128)(2,1)S(1)}, bf16[768,1024]{1,0:T(8,128)(2,1)S(1)}) custom-call(bf16[768,4096]{1,0:T(8,128)(2,1)} %cots_ref.3), custom_call_target="tpu_custom_call" | custom-call | tf_op jit(solution)/shard_map/pallas_call | solution.py:37
  3.1 0.6 %shard_map.77 = (bf16[128,2048]{1,0:T(8,128)(2,1)S(1)}, bf16[128,768]{1,0:T(8,128)(2,1)S(1)}) custom-call(bf16[768,128]{1,0:T(8,128)(2,1)S(1)} %copy-done.2, bf16[768,2048]{1,0:T(8,128)(2,1)S(1)} %get-tuple-element.33.cots), custom_call_target="tpu_custom_call" | custom-call | tf_op jit(solution)/shard_map/pallas_call | solution.py:37
  3.7 0.5 %collective-permute-start = (bf16[128,2048]{1,0:T(8,128)(2,1)S(1)}, bf16[128,2048]{1,0:T(8,128)(2,1)S(1)}, u32[]{:S(2)}, u32[]{:S(2)}) collective-permute-start(bf16[128,2048]{1,0:T(8,128)(2,1)S(1)} %get-tuple-element.36), channel_id=1, source_target_pairs={{0,8},{1,9},{2,10},{3,11},{4,12},{5,13},{6,14},{7,15},{8,0},{9,1},... | collective-permute-start | bytes 1572872 | tf_op jit(solution)/shard_map/ppermute | solution.py:55
  4.2 1.9 %shard_map.78.kept = f32[128,2048]{1,0:T(8,128)S(1)} custom-call(bf16[128,768]{1,0:T(8,128)(2,1)S(1)} %get-tuple-element.34.turned, bf16[768,1024]{1,0:T(8,128)(2,1)S(1)} %get-tuple-element.35.first, bf16[768,4096]{1,0:T(8,128)(2,1)} %cots_ref.3), custom_call_target="tpu_custom_call" | custom-call | tf_op jit(solution)/shard_map/pallas_call | solution.py:37
  6.3 3.6 %collective-permute-start.1 = (bf16[64,1024]{1,0:T(8,128)(2,1)S(1)}, bf16[64,1024]{1,0:T(8,128)(2,1)S(1)}, u32[]{:S(2)}, u32[]{:S(2)}) collective-permute-start(bf16[64,1024]{1,0:T(8,128)(2,1)S(1)} %get-tuple-element.38), channel_id=1, source_target_pairs={{0,17},{1,16},{2,19},{3,18},{4,21},{5,20},{6,23},{7,22},{8,14},{9,... | collective-permute-start | bytes 393224 | tf_op jit(solution)/shard_map/ppermute | solution.py:55
  10.5 2.3 %collective-permute-done.1.refs_0_ = bf16[64,1024]{1,0:T(8,128)(2,1)S(1)} collective-permute-done((bf16[64,1024]{1,0:T(8,128)(2,1)S(1)}, bf16[64,1024]{1,0:T(8,128)(2,1)S(1)}, u32[]{:S(2)}, u32[]{:S(2)}) %collective-permute-start.1) | collective-permute-done | bytes 131104 | tf_op jit(solution)/shard_map/ppermute | solution.py:55
  12.8 2.0 %collective-permute-done.2.refs_1_ = bf16[64,1024]{1,0:T(8,128)(2,1)S(1)} collective-permute-done((bf16[64,1024]{1,0:T(8,128)(2,1)S(1)}, bf16[64,1024]{1,0:T(8,128)(2,1)S(1)}, u32[]{:S(2)}, u32[]{:S(2)}) %collective-permute-start.2) | collective-permute-done | bytes 131104 | tf_op jit(solution)/shard_map/ppermute | solution.py:55
  15.4 3.7 %collective-permute-start.4 = (bf16[16,1024]{1,0:T(8,128)(2,1)S(1)}, bf16[16,1024]{1,0:T(8,128)(2,1)S(1)}, u32[]{:S(2)}, u32[]{:S(2)}) collective-permute-start(bf16[16,1024]{1,0:T(8,128)(2,1)S(1)} %get-tuple-element.42), channel_id=1, source_target_pairs={{0,6},{1,7},{2,4},{3,5},{4,2},{5,3},{6,0},{7,1},{8,25},{9,24},{10,... | collective-permute-start | bytes 98312 | tf_op jit(solution)/shard_map/ppermute | solution.py:55
  19.0 0.8 %collective-permute-start.6 = (bf16[16,1024]{1,0:T(8,128)(2,1)S(1)}, bf16[16,1024]{1,0:T(8,128)(2,1)S(1)}, u32[]{:S(2)}, u32[]{:S(2)}) collective-permute-start(bf16[16,1024]{1,0:T(8,128)(2,1)S(1)} %get-tuple-element.44), channel_id=1, source_target_pairs={{0,2},{1,3},{2,0},{3,1},{4,6},{5,7},{6,4},{7,5},{8,24},{9,25},{10,... | collective-permute-start | bytes 98312 | tf_op jit(solution)/shard_map/ppermute | solution.py:55
  19.8 1.3 %collective-permute-done.4.refs_0_ = bf16[16,1024]{1,0:T(8,128)(2,1)S(1)} collective-permute-done((bf16[16,1024]{1,0:T(8,128)(2,1)S(1)}, bf16[16,1024]{1,0:T(8,128)(2,1)S(1)}, u32[]{:S(2)}, u32[]{:S(2)}) %collective-permute-start.4) | collective-permute-done | bytes 32800 | tf_op jit(solution)/shard_map/ppermute | solution.py:55
  21.1 2.7 %collective-permute-done.5.refs_1_ = bf16[16,1024]{1,0:T(8,128)(2,1)S(1)} collective-permute-done((bf16[16,1024]{1,0:T(8,128)(2,1)S(1)}, bf16[16,1024]{1,0:T(8,128)(2,1)S(1)}, u32[]{:S(2)}, u32[]{:S(2)}) %collective-permute-start.5) | collective-permute-done | bytes 32800 | tf_op jit(solution)/shard_map/ppermute | solution.py:55
  24.1 1.5 %collective-permute-start.8 = (bf16[16,1024]{1,0:T(8,128)(2,1)S(1)}, bf16[16,1024]{1,0:T(8,128)(2,1)S(1)}, u32[]{:S(2)}, u32[]{:S(2)}) collective-permute-start(bf16[16,1024]{1,0:T(8,128)(2,1)S(1)} %get-tuple-element.48), channel_id=1, source_target_pairs={{0,6},{1,7},{2,4},{3,5},{4,2},{5,3},{6,0},{7,1},{8,25},{9,24},{10,... | collective-permute-start | bytes 98312 | tf_op jit(solution)/shard_map/ppermute | solution.py:55
  25.6 0.6 %collective-permute-start.9 = (bf16[16,1024]{1,0:T(8,128)(2,1)S(1)}, bf16[16,1024]{1,0:T(8,128)(2,1)S(1)}, u32[]{:S(2)}, u32[]{:S(2)}) collective-permute-start(bf16[16,1024]{1,0:T(8,128)(2,1)S(1)} %get-tuple-element.49), channel_id=1, source_target_pairs={{0,4},{1,5},{2,6},{3,7},{4,0},{5,1},{6,2},{7,3},{8,9},{9,8},{10,11... | collective-permute-start | bytes 98312 | tf_op jit(solution)/shard_map/ppermute | solution.py:55
  26.2 2.3 %collective-permute-start.10 = (bf16[16,1024]{1,0:T(8,128)(2,1)S(1)}, bf16[16,1024]{1,0:T(8,128)(2,1)S(1)}, u32[]{:S(2)}, u32[]{:S(2)}) collective-permute-start(bf16[16,1024]{1,0:T(8,128)(2,1)S(1)} %get-tuple-element.47.own), channel_id=1, source_target_pairs={{0,2},{1,3},{2,0},{3,1},{4,6},{5,7},{6,4},{7,5},{8,24},{9,25},{10,... | collective-permute-start | bytes 98312 | tf_op jit(solution)/shard_map/ppermute | solution.py:55
  28.5 1.3 %collective-permute-done.8.refs_0_ = bf16[16,1024]{1,0:T(8,128)(2,1)S(1)} collective-permute-done((bf16[16,1024]{1,0:T(8,128)(2,1)S(1)}, bf16[16,1024]{1,0:T(8,128)(2,1)S(1)}, u32[]{:S(2)}, u32[]{:S(2)}) %collective-permute-start.8) | collective-permute-done | bytes 32800 | tf_op jit(solution)/shard_map/ppermute | solution.py:55
  29.8 0.6 %collective-permute-done.9.refs_1_ = bf16[16,1024]{1,0:T(8,128)(2,1)S(1)} collective-permute-done((bf16[16,1024]{1,0:T(8,128)(2,1)S(1)}, bf16[16,1024]{1,0:T(8,128)(2,1)S(1)}, u32[]{:S(2)}, u32[]{:S(2)}) %collective-permute-start.9) | collective-permute-done | bytes 32800 | tf_op jit(solution)/shard_map/ppermute | solution.py:55
  30.8 1.6 %collective-permute-start.11 = (bf16[64,1024]{1,0:T(8,128)(2,1)S(1)}, bf16[64,1024]{1,0:T(8,128)(2,1)S(1)}, u32[]{:S(2)}, u32[]{:S(2)}) collective-permute-start(bf16[64,1024]{1,0:T(8,128)(2,1)S(1)} %get-tuple-element.50), channel_id=1, source_target_pairs={{0,17},{1,16},{2,19},{3,18},{4,21},{5,20},{6,23},{7,22},{8,14},{9,... | collective-permute-start | bytes 393224 | tf_op jit(solution)/shard_map/ppermute | solution.py:55
  32.3 0.9 %collective-permute-start.13 = (bf16[64,1024]{1,0:T(8,128)(2,1)S(1)}, bf16[64,1024]{1,0:T(8,128)(2,1)S(1)}, u32[]{:S(2)}, u32[]{:S(2)}) collective-permute-start(bf16[64,1024]{1,0:T(8,128)(2,1)S(1)} %get-tuple-element.59), channel_id=1, source_target_pairs={{0,1},{1,0},{2,3},{3,2},{4,5},{5,4},{6,7},{7,6},{8,12},{9,13},{10,... | collective-permute-start | bytes 393224 | tf_op jit(solution)/shard_map/ppermute | solution.py:55
  33.3 1.1 %collective-permute-start.14 = (bf16[64,1024]{1,0:T(8,128)(2,1)S(1)}, bf16[64,1024]{1,0:T(8,128)(2,1)S(1)}, u32[]{:S(2)}, u32[]{:S(2)}) collective-permute-start(bf16[64,1024]{1,0:T(8,128)(2,1)S(1)} %get-tuple-element.57.refs_0_), channel_id=1, source_target_pairs={{0,16},{1,17},{2,18},{3,19},{4,20},{5,21},{6,22},{7,23},{8,10},{9,... | collective-permute-start | bytes 393224 | tf_op jit(solution)/shard_map/ppermute | solution.py:55
  34.3 0.9 %collective-permute-start.12 = (bf16[32,1024]{1,0:T(8,128)(2,1)S(1)}, bf16[32,1024]{1,0:T(8,128)(2,1)S(1)}, u32[]{:S(2)}, u32[]{:S(2)}) collective-permute-start(bf16[32,1024]{1,0:T(8,128)(2,1)S(1)} %get-tuple-element.51.grads), channel_id=1, source_target_pairs={{0,16},{1,17},{2,18},{3,19},{4,20},{5,21},{6,22},{7,23},{8,24},{9,... | collective-permute-start | bytes 196616 | tf_op jit(solution)/shard_map/ppermute | solution.py:55
  35.3 0.7 %shard_map.84 = (f32[16,4096]{1,0:T(8,128)}, f32[16,4096]{1,0:T(8,128)}) custom-call(f32[16,4096]{1,0:T(8,128)S(1)} %copy-done, f32[16,4096]{1,0:T(8,128)S(1)} %copy-done.1, bf16[32,1024]{1,0:T(8,128)(2,1)S(1)} %get-tuple-element.51.grads), custom_call_target="tpu_custom_call" | custom-call | tf_op jit(solution)/shard_map/pallas_call | solution.py:37
  36.0 3.5 %collective-permute-done.12.grads = bf16[32,1024]{1,0:T(8,128)(2,1)S(1)} collective-permute-done((bf16[32,1024]{1,0:T(8,128)(2,1)S(1)}, bf16[32,1024]{1,0:T(8,128)(2,1)S(1)}, u32[]{:S(2)}, u32[]{:S(2)}) %collective-permute-start.12) | collective-permute-done | bytes 65568 | tf_op jit(solution)/shard_map/ppermute | solution.py:55
  40.2 1.0 %shard_map.85 = (f32[16,4096]{1,0:T(8,128)}, f32[16,4096]{1,0:T(8,128)}, bf16[128,4096]{1,0:T(8,128)(2,1)}) custom-call(f32[16,4096]{1,0:T(8,128)S(1)} %copy-done, f32[16,4096]{1,0:T(8,128)S(1)} %copy-done.1, bf16[32,1024]{1,0:T(8,128)(2,1)S(1)} %collective-permute-done.12.grads, ...), custom_call_target="tpu_custom_call", output_to_operand_aliasing={{0}: (3, {}), {1}: (4, {})} | custom-call | tf_op jit(solution)/shard_map/pallas_call | solution.py:37
  41.5 0.8 %shard_map.86 = bf16[128,4096]{1,0:T(8,128)(2,1)} custom-call(bf16[128,4096]{1,0:T(8,128)(2,1)} %get-tuple-element.60._, bf16[64,1024]{1,0:T(8,128)(2,1)S(1)} %collective-permute-done.15.refs_0_, bf16[64,1024]{1,0:T(8,128)(2,1)S(1)} %collective-permute-done.16.refs_1_, ...), custom_call_target="tpu_custom_call", output_to_operand_aliasing={{}: (0, {})} | custom-call | tf_op jit(solution)/shard_map/pallas_call | solution.py:37
  (33 shorter events, 2.7 us)
Async XLA Ops:
  0.6 2.4 %copy-start.2 = (bf16[768,128]{1,0:T(8,128)(2,1)S(1)}, bf16[768,128]{1,0:T(8,128)(2,1)}, u32[]{:S(2)}) copy-start(bf16[768,128]{1,0:T(8,128)(2,1)} %acts.1) | copy-start | bytes 589828
  3.7 2.5 %collective-permute-start = (bf16[128,2048]{1,0:T(8,128)(2,1)S(1)}, bf16[128,2048]{1,0:T(8,128)(2,1)S(1)}, u32[]{:S(2)}, u32[]{:S(2)}) collective-permute-start(bf16[128,2048]{1,0:T(8,128)(2,1)S(1)} %get-tuple-element.36), channel_id=1, source_target_pairs={{0,8},{1,9},{2,10},{3,11},{4,12},{5,13},{6,14},{7,15},{8,0},{9,1},... | collective-permute-start | bytes 1572872 | tf_op jit(solution)/shard_map/ppermute | solution.py:55
  4.2 19.6 %copy-start = (f32[16,4096]{1,0:T(8,128)S(1)}, f32[16,4096]{1,0:T(8,128)}, u32[]{:S(2)}) copy-start(f32[16,4096]{1,0:T(8,128)} %m.5) | copy-start | bytes 786436
  4.2 19.6 %copy-start.1 = (f32[16,4096]{1,0:T(8,128)S(1)}, f32[16,4096]{1,0:T(8,128)}, u32[]{:S(2)}) copy-start(f32[16,4096]{1,0:T(8,128)} %v.5) | copy-start | bytes 786436
  4.2 19.6 %copy-start.3 = (bf16[16,4096]{1,0:T(8,128)(2,1)S(1)}, bf16[16,4096]{1,0:T(8,128)(2,1)}, u32[]{:S(2)}) copy-start(bf16[16,4096]{1,0:T(8,128)(2,1)} %w.1) | copy-start | bytes 393220
  6.3 6.5 %collective-permute-start.1 = (bf16[64,1024]{1,0:T(8,128)(2,1)S(1)}, bf16[64,1024]{1,0:T(8,128)(2,1)S(1)}, u32[]{:S(2)}, u32[]{:S(2)}) collective-permute-start(bf16[64,1024]{1,0:T(8,128)(2,1)S(1)} %get-tuple-element.38), channel_id=1, source_target_pairs={{0,17},{1,16},{2,19},{3,18},{4,21},{5,20},{6,23},{7,22},{8,14},{9,... | collective-permute-start | bytes 393224 | tf_op jit(solution)/shard_map/ppermute | solution.py:55
  9.8 5.0 %collective-permute-start.2 = (bf16[64,1024]{1,0:T(8,128)(2,1)S(1)}, bf16[64,1024]{1,0:T(8,128)(2,1)S(1)}, u32[]{:S(2)}, u32[]{:S(2)}) collective-permute-start(bf16[64,1024]{1,0:T(8,128)(2,1)S(1)} %get-tuple-element.39), channel_id=1, source_target_pairs={{0,1},{1,0},{2,3},{3,2},{4,5},{5,4},{6,7},{7,6},{8,12},{9,13},{10,... | collective-permute-start | bytes 393224 | tf_op jit(solution)/shard_map/ppermute | solution.py:55
  10.3 5.0 %collective-permute-start.3 = (bf16[64,1024]{1,0:T(8,128)(2,1)S(1)}, bf16[64,1024]{1,0:T(8,128)(2,1)S(1)}, u32[]{:S(2)}, u32[]{:S(2)}) collective-permute-start(bf16[64,1024]{1,0:T(8,128)(2,1)S(1)} %get-tuple-element.40), channel_id=1, source_target_pairs={{0,16},{1,17},{2,18},{3,19},{4,20},{5,21},{6,22},{7,23},{8,10},{9,... | collective-permute-start | bytes 393224 | tf_op jit(solution)/shard_map/ppermute | solution.py:55
  15.4 5.8 %collective-permute-start.4 = (bf16[16,1024]{1,0:T(8,128)(2,1)S(1)}, bf16[16,1024]{1,0:T(8,128)(2,1)S(1)}, u32[]{:S(2)}, u32[]{:S(2)}) collective-permute-start(bf16[16,1024]{1,0:T(8,128)(2,1)S(1)} %get-tuple-element.42), channel_id=1, source_target_pairs={{0,6},{1,7},{2,4},{3,5},{4,2},{5,3},{6,0},{7,1},{8,25},{9,24},{10,... | collective-permute-start | bytes 98312 | tf_op jit(solution)/shard_map/ppermute | solution.py:55
  19.0 4.8 %collective-permute-start.5 = (bf16[16,1024]{1,0:T(8,128)(2,1)S(1)}, bf16[16,1024]{1,0:T(8,128)(2,1)S(1)}, u32[]{:S(2)}, u32[]{:S(2)}) collective-permute-start(bf16[16,1024]{1,0:T(8,128)(2,1)S(1)} %get-tuple-element.43), channel_id=1, source_target_pairs={{0,4},{1,5},{2,6},{3,7},{4,0},{5,1},{6,2},{7,3},{8,9},{9,8},{10,11... | collective-permute-start | bytes 98312 | tf_op jit(solution)/shard_map/ppermute | solution.py:55
  19.0 4.8 %collective-permute-start.6 = (bf16[16,1024]{1,0:T(8,128)(2,1)S(1)}, bf16[16,1024]{1,0:T(8,128)(2,1)S(1)}, u32[]{:S(2)}, u32[]{:S(2)}) collective-permute-start(bf16[16,1024]{1,0:T(8,128)(2,1)S(1)} %get-tuple-element.44), channel_id=1, source_target_pairs={{0,2},{1,3},{2,0},{3,1},{4,6},{5,7},{6,4},{7,5},{8,24},{9,25},{10,... | collective-permute-start | bytes 98312 | tf_op jit(solution)/shard_map/ppermute | solution.py:55
  24.0 4.6 %collective-permute-start.7 = (bf16[16,1024]{1,0:T(8,128)(2,1)S(1)}, bf16[16,1024]{1,0:T(8,128)(2,1)S(1)}, u32[]{:S(2)}, u32[]{:S(2)}) collective-permute-start(bf16[16,1024]{1,0:T(8,128)(2,1)S(1)} %get-tuple-element.45.grad), channel_id=1, source_target_pairs={{0,8},{1,9},{2,10},{3,11},{4,12},{5,13},{6,14},{7,15},{8,0},{9,1},... | collective-permute-start | bytes 98312 | tf_op jit(solution)/shard_map/ppermute | solution.py:55
  24.1 5.8 %collective-permute-start.8 = (bf16[16,1024]{1,0:T(8,128)(2,1)S(1)}, bf16[16,1024]{1,0:T(8,128)(2,1)S(1)}, u32[]{:S(2)}, u32[]{:S(2)}) collective-permute-start(bf16[16,1024]{1,0:T(8,128)(2,1)S(1)} %get-tuple-element.48), channel_id=1, source_target_pairs={{0,6},{1,7},{2,4},{3,5},{4,2},{5,3},{6,0},{7,1},{8,25},{9,24},{10,... | collective-permute-start | bytes 98312 | tf_op jit(solution)/shard_map/ppermute | solution.py:55
  25.6 4.8 %collective-permute-start.9 = (bf16[16,1024]{1,0:T(8,128)(2,1)S(1)}, bf16[16,1024]{1,0:T(8,128)(2,1)S(1)}, u32[]{:S(2)}, u32[]{:S(2)}) collective-permute-start(bf16[16,1024]{1,0:T(8,128)(2,1)S(1)} %get-tuple-element.49), channel_id=1, source_target_pairs={{0,4},{1,5},{2,6},{3,7},{4,0},{5,1},{6,2},{7,3},{8,9},{9,8},{10,11... | collective-permute-start | bytes 98312 | tf_op jit(solution)/shard_map/ppermute | solution.py:55
  26.2 4.5 %collective-permute-start.10 = (bf16[16,1024]{1,0:T(8,128)(2,1)S(1)}, bf16[16,1024]{1,0:T(8,128)(2,1)S(1)}, u32[]{:S(2)}, u32[]{:S(2)}) collective-permute-start(bf16[16,1024]{1,0:T(8,128)(2,1)S(1)} %get-tuple-element.47.own), channel_id=1, source_target_pairs={{0,2},{1,3},{2,0},{3,1},{4,6},{5,7},{6,4},{7,5},{8,24},{9,25},{10,... | collective-permute-start | bytes 98312 | tf_op jit(solution)/shard_map/ppermute | solution.py:55
  30.8 8.8 %collective-permute-start.11 = (bf16[64,1024]{1,0:T(8,128)(2,1)S(1)}, bf16[64,1024]{1,0:T(8,128)(2,1)S(1)}, u32[]{:S(2)}, u32[]{:S(2)}) collective-permute-start(bf16[64,1024]{1,0:T(8,128)(2,1)S(1)} %get-tuple-element.50), channel_id=1, source_target_pairs={{0,17},{1,16},{2,19},{3,18},{4,21},{5,20},{6,23},{7,22},{8,14},{9,... | collective-permute-start | bytes 393224 | tf_op jit(solution)/shard_map/ppermute | solution.py:55
  32.3 7.2 %collective-permute-start.13 = (bf16[64,1024]{1,0:T(8,128)(2,1)S(1)}, bf16[64,1024]{1,0:T(8,128)(2,1)S(1)}, u32[]{:S(2)}, u32[]{:S(2)}) collective-permute-start(bf16[64,1024]{1,0:T(8,128)(2,1)S(1)} %get-tuple-element.59), channel_id=1, source_target_pairs={{0,1},{1,0},{2,3},{3,2},{4,5},{5,4},{6,7},{7,6},{8,12},{9,13},{10,... | collective-permute-start | bytes 393224 | tf_op jit(solution)/shard_map/ppermute | solution.py:55
  33.3 6.3 %collective-permute-start.14 = (bf16[64,1024]{1,0:T(8,128)(2,1)S(1)}, bf16[64,1024]{1,0:T(8,128)(2,1)S(1)}, u32[]{:S(2)}, u32[]{:S(2)}) collective-permute-start(bf16[64,1024]{1,0:T(8,128)(2,1)S(1)} %get-tuple-element.57.refs_0_), channel_id=1, source_target_pairs={{0,16},{1,17},{2,18},{3,19},{4,20},{5,21},{6,22},{7,23},{8,10},{9,... | collective-permute-start | bytes 393224 | tf_op jit(solution)/shard_map/ppermute | solution.py:55
  34.3 5.2 %collective-permute-start.12 = (bf16[32,1024]{1,0:T(8,128)(2,1)S(1)}, bf16[32,1024]{1,0:T(8,128)(2,1)S(1)}, u32[]{:S(2)}, u32[]{:S(2)}) collective-permute-start(bf16[32,1024]{1,0:T(8,128)(2,1)S(1)} %get-tuple-element.51.grads), channel_id=1, source_target_pairs={{0,16},{1,17},{2,18},{3,19},{4,20},{5,21},{6,22},{7,23},{8,24},{9,... | collective-permute-start | bytes 196616 | tf_op jit(solution)/shard_map/ppermute | solution.py:55
  35.3 5.9 %collective-permute-start.15 = (bf16[64,1024]{1,0:T(8,128)(2,1)S(1)}, bf16[64,1024]{1,0:T(8,128)(2,1)S(1)}, u32[]{:S(2)}, u32[]{:S(2)}) collective-permute-start(bf16[64,1024]{1,0:T(8,128)(2,1)S(1)} %get-tuple-element.57.refs_0_), channel_id=1, source_target_pairs={{0,8},{1,9},{2,10},{3,11},{4,12},{5,13},{6,14},{7,15},{8,0},{9,1},... | collective-permute-start | bytes 393224 | tf_op jit(solution)/shard_map/ppermute | solution.py:55
  39.6 1.6 %collective-permute-start.17 = (bf16[64,1024]{1,0:T(8,128)(2,1)S(1)}, bf16[64,1024]{1,0:T(8,128)(2,1)S(1)}, u32[]{:S(2)}, u32[]{:S(2)}) collective-permute-start(bf16[64,1024]{1,0:T(8,128)(2,1)S(1)} %collective-permute-done.13.refs_2_), channel_id=1, source_target_pairs={{0,8},{1,9},{2,10},{3,11},{4,12},{5,13},{6,14},{7,15},{8,0},{9,1},... | collective-permute-start | bytes 393224 | tf_op jit(solution)/shard_map/ppermute | solution.py:55
  39.6 1.6 %collective-permute-start.18 = (bf16[64,1024]{1,0:T(8,128)(2,1)S(1)}, bf16[64,1024]{1,0:T(8,128)(2,1)S(1)}, u32[]{:S(2)}, u32[]{:S(2)}) collective-permute-start(bf16[64,1024]{1,0:T(8,128)(2,1)S(1)} %collective-permute-done.14.refs_3_), channel_id=1, source_target_pairs={{0,8},{1,9},{2,10},{3,11},{4,12},{5,13},{6,14},{7,15},{8,0},{9,1},... | collective-permute-start | bytes 393224 | tf_op jit(solution)/shard_map/ppermute | solution.py:55
  40.1 1.3 %collective-permute-start.16 = (bf16[64,1024]{1,0:T(8,128)(2,1)S(1)}, bf16[64,1024]{1,0:T(8,128)(2,1)S(1)}, u32[]{:S(2)}, u32[]{:S(2)}) collective-permute-start(bf16[64,1024]{1,0:T(8,128)(2,1)S(1)} %collective-permute-done.11.refs_1_), channel_id=1, source_target_pairs={{0,8},{1,9},{2,10},{3,11},{4,12},{5,13},{6,14},{7,15},{8,0},{9,1},... | collective-permute-start | bytes 393224 | tf_op jit(solution)/shard_map/ppermute | solution.py:55

commit v2 on v1

--- a/solution.py
+++ b/solution.py
@@ -60,16 +60,25 @@
 
 
 SQUARE = ((1, 1), (1, 0), (0, 1))
-LINE = (3, 2, 1)
+LINE = (2, 3, 1)
 STEPS = tuple(zip(SQUARE, LINE))
 STAY = ((0, 0), 0)
 
 
-def stage(value, step, square_core):
+def role_of(rep, shard):
+    return (rep ^ (rep >> 1) ^ shard ^ (shard >> 1)) & 1
+
+
+def partner(rep, shard, dy, dx, k):
+    return rep ^ (2 * dx) ^ ((dy ^ dx ^ k) & 1), shard ^ dy ^ (2 * k)
+
+
+def stage(value, step, square_role):
     (dy, dx), k = step
     return exchange(
         value,
-        lambda rep, shard: (rep ^ (2 * dx), shard ^ dy) if rep & 1 == square_core else (rep, shard ^ (2 * k)),
+        lambda rep, shard: partner(rep, shard, dy, dx, 0) if role_of(rep, shard) == square_role
+        else partner(rep, shard, 0, 0, k),
     )
 
 
@@ -82,7 +91,7 @@
 
 
 def along_x(value):
-    return exchange(value, lambda rep, shard: (rep ^ 2, shard))
+    return exchange(value, lambda rep, shard: partner(rep, shard, 0, 1, 0))
 
 
 def along_rest(value, k):
@@ -91,22 +100,22 @@
 
 def place():
     rep, shard = lax.axis_index("rep"), lax.axis_index("shard")
-    return rep & 1, rep >> 1, shard & 1, (shard >> 1) & 3, shard >> 3
+    return role_of(rep, shard), rep >> 1, shard & 1, (shard >> 1) & 3, shard >> 3
 
 
 def in_half(step, group):
-    core, x, y, z, _ = place()
+    role, x, y, z, _ = place()
     (dy, dx), k = step
-    first = core == 0
+    first = role == 0
     return (
         jnp.where(first, y ^ dy, group >> 1), jnp.where(first, x ^ dx, group & 1), jnp.where(first, group, z ^ k),
     )
 
 
 def group_of(step):
-    core, x, y, z, _ = place()
+    role, x, y, z, _ = place()
     (dy, dx), k = step
-    return jnp.where(core == 0, z ^ k, 2 * (y ^ dy) + (x ^ dx))
+    return jnp.where(role == 0, z ^ k, 2 * (y ^ dy) + (x ^ dx))
 
 
 def block(index, size):
@@ -114,9 +123,9 @@
 
 
 def load_kernel(cots_ref, away, first, sems):
-    core = place()[0]
+    role = place()[0]
     copies = []
-    for out, side in ((away, 1 - core), (first, core)):
+    for out, side in ((away, 1 - role), (first, role)):
         at = pl.ds(pl.multiple_of(side * away.shape[1], CHUNK), out.shape[1])
         copies.append(pltpu.make_async_copy(cots_ref.at[:, at], out, sems.at[len(copies)]))
         copies[-1].start()
@@ -132,11 +141,11 @@
 
 
 def kept_kernel(turned, first, cots_ref, out, cots, sems):
-    core = place()[0]
+    role = place()[0]
     ready, count = first.shape[1] // CHUNK, out.shape[1] // CHUNK
     copies = []
     for i in range(ready, count):
-        source = cots_ref.at[:, block(core * count + i, CHUNK)]
+        source = cots_ref.at[:, block(role * count + i, CHUNK)]
         copies.append(pltpu.make_async_copy(source, cots.at[i - ready], sems.at[i - ready]))
         copies[-1].start()
     for i in range(count):
@@ -184,12 +193,12 @@
 
 def update_kernel(w, m, v, own, *refs):
     pieces, (new_w, grad) = refs[:-2], refs[-2:]
-    core, x, _, _, _ = place()
+    role, x, _, _, _ = place()
     total = own[...]
     for ref in pieces:
         total += ref[...].astype(F32)
     grad[...] = total.astype(BF16)
-    at = block(core * 2 + x, total.shape[1])
+    at = block(role * 2 + x, total.shape[1])
     new_m, new_v = adamw_moments(m[:, at], v[:, at], total)
     new_w[...] = adamw_weight(w[:, at], new_m, new_v)
 
@@ -217,14 +226,14 @@
     size, rows = own.shape[0], grad.shape[0]
     for step, ref in zip((STAY,) + STEPS, parts):
         put(outs, block(group_of(step), size), ref[...])
-    core = place()[0]
-    grads[block(core, rows), :] = grad[...]
-    grads[block(1 - core, rows), :] = sibling_grad[...]
+    role = place()[0]
+    grads[block(role, rows), :] = grad[...]
+    grads[block(1 - role, rows), :] = sibling_grad[...]
 
 
 def half_blocks(rows, sibling, parts, out):
-    core, x, y, z, _ = place()
-    first = (core == 0) != sibling
+    role, x, y, z, _ = place()
+    first = (role == 0) != sibling
     size, quarter = parts[0].shape
     count = size // (4 * rows)
     for ((dy, dx), k), ref in zip((STAY,) + STEPS, parts):
@@ -271,8 +280,16 @@
     rows.wait()
 
 
-def write_other_kernel(_, *refs):
-    parts, (out, half, sem) = refs[:1 + len(STEPS)], refs[1 + len(STEPS):]
+def pack_kernel(*refs):
+    *parts, out = refs
+    size = parts[0].shape[0]
+    for i, ref in enumerate(parts):
+        out[i * size:(i + 1) * size, :] = ref[...]
+
+
+def write_other_kernel(_, own, others, out, half, sem):
+    size = own.shape[0]
+    parts = [own] + [others.at[pl.ds(i * size, size), :] for i in range(len(STEPS))]
     write_half(1, parts, out, half, sem).wait()
 
 
@@ -332,7 +349,8 @@
     came[0], far_grads, new_m, new_v = lax.optimization_barrier((came[0], far_grads, new_m, new_v))
 
     mine = [parts[-1]] + came
-    others = [to_sibling(part) for part in mine]
+    landed = call(pack_kernel, [shape((len(STEPS) * wide_rows, quarter), BF16)], *came)[0]
+    others = [to_sibling(parts[-1]), to_sibling(landed)]
     out = [shape((all_rows, width), BF16)]
     scratch = [pltpu.VMEM((all_rows, half), BF16), pltpu.SemaphoreType.DMA]
     new_m, new_v, new_w = call(

time: 42.4 us -> 42 us (level)
  starting transfers between devices: 18.8 us -> 17.3 us
  waiting for transfers between devices: 14.9 us -> 15.9 us
    ppermute x19 -> x17, starting transfers between devices: 18.8 us -> 17.3 us  [exchange(): return lax.ppermute(value, ('rep', 'shard'), pairs)]
    ppermute x19 -> x17, waiting for transfers between devices: 14.9 us -> 15.9 us  [exchange(): return lax.ppermute(value, ('rep', 'shard'), pairs)]
    pallas_call x11 -> x12, Pallas kernels: 7.82 us -> 7.86 us  [call(): pl.pallas_call(kernel, out_shape=outs, in_specs=[far if i in tuple(far_in...]
  transfers between devices with their start and end apart: 19 -> 17, of which waited for: 10 -> 9; matrix products, arithmetic and copies ran while one was open for 0% -> 0% of each run, Pallas kernels for 9% -> 9%
where the time goes in v2:
time: 42 us; the launch traced here: 41.9 us
  starting transfers between devices  17.3 us (41%)
  waiting for transfers between devices  15.9 us (38%)
  Pallas kernels  7.86 us (19%)
  between operations  0.76 us (2%)
    ppermute x17, starting transfers between devices, exchange(): return lax.ppermute(value, ('rep', 'shard'), pairs)  17.3 us
    ppermute x17, waiting for transfers between devices, exchange(): return lax.ppermute(value, ('rep', 'shard'), pairs)  15.9 us
    pallas_call x12, Pallas kernels, call(): pl.pallas_call(kernel, out_shape=outs, in_specs=[far if i in tuple(far_in...  7.86 us
  transfers between devices with their start and end apart: 17, of which 9 were waited for; matrix products, arithmetic and copies ran while one was open for 0% of the time, Pallas kernels for 9%

profile of v2, /device:TPU:0, one launch (start us, length us, event | category | flops | bytes accessed | tf_op | source)
XLA Modules:
  0.0 41.9 jit_solution(3636725590376177737)
XLA Ops:
  0.6 2.4 %shard_map.76 = (bf16[768,2048]{1,0:T(8,128)(2,1)S(1)}, bf16[768,1024]{1,0:T(8,128)(2,1)S(1)}) custom-call(bf16[768,4096]{1,0:T(8,128)(2,1)} %cots_ref.3), custom_call_target="tpu_custom_call" | custom-call | tf_op jit(solution)/shard_map/pallas_call | solution.py:37
  3.1 0.6 %shard_map.77 = (bf16[128,2048]{1,0:T(8,128)(2,1)S(1)}, bf16[128,768]{1,0:T(8,128)(2,1)S(1)}) custom-call(bf16[768,128]{1,0:T(8,128)(2,1)S(1)} %copy-done.2, bf16[768,2048]{1,0:T(8,128)(2,1)S(1)} %get-tuple-element.33.cots), custom_call_target="tpu_custom_call" | custom-call | tf_op jit(solution)/shard_map/pallas_call | solution.py:37
  3.7 0.5 %collective-permute-start = (bf16[128,2048]{1,0:T(8,128)(2,1)S(1)}, bf16[128,2048]{1,0:T(8,128)(2,1)S(1)}, u32[]{:S(2)}, u32[]{:S(2)}) collective-permute-start(bf16[128,2048]{1,0:T(8,128)(2,1)S(1)} %get-tuple-element.36), channel_id=1, source_target_pairs={{0,8},{1,9},{2,10},{3,11},{4,12},{5,13},{6,14},{7,15},{8,0},{9,1},... | collective-permute-start | bytes 1572872 | tf_op jit(solution)/shard_map/ppermute | solution.py:55
  4.2 1.9 %shard_map.78.kept = f32[128,2048]{1,0:T(8,128)S(1)} custom-call(bf16[128,768]{1,0:T(8,128)(2,1)S(1)} %get-tuple-element.34.turned, bf16[768,1024]{1,0:T(8,128)(2,1)S(1)} %get-tuple-element.35.first, bf16[768,4096]{1,0:T(8,128)(2,1)} %cots_ref.3), custom_call_target="tpu_custom_call" | custom-call | tf_op jit(solution)/shard_map/pallas_call | solution.py:37
  6.3 3.6 %collective-permute-start.1 = (bf16[64,1024]{1,0:T(8,128)(2,1)S(1)}, bf16[64,1024]{1,0:T(8,128)(2,1)S(1)}, u32[]{:S(2)}, u32[]{:S(2)}) collective-permute-start(bf16[64,1024]{1,0:T(8,128)(2,1)S(1)} %get-tuple-element.38), channel_id=1, source_target_pairs={{0,17},{1,5},{2,6},{3,18},{4,21},{5,1},{6,2},{7,22},{8,12},{9,24},... | collective-permute-start | bytes 393224 | tf_op jit(solution)/shard_map/ppermute | solution.py:55
  10.2 2.6 %collective-permute-done.1.refs_0_ = bf16[64,1024]{1,0:T(8,128)(2,1)S(1)} collective-permute-done((bf16[64,1024]{1,0:T(8,128)(2,1)S(1)}, bf16[64,1024]{1,0:T(8,128)(2,1)S(1)}, u32[]{:S(2)}, u32[]{:S(2)}) %collective-permute-start.1) | collective-permute-done | bytes 131104 | tf_op jit(solution)/shard_map/ppermute | solution.py:55
  12.8 1.4 %collective-permute-done.2.refs_1_ = bf16[64,1024]{1,0:T(8,128)(2,1)S(1)} collective-permute-done((bf16[64,1024]{1,0:T(8,128)(2,1)S(1)}, bf16[64,1024]{1,0:T(8,128)(2,1)S(1)}, u32[]{:S(2)}, u32[]{:S(2)}) %collective-permute-start.2) | collective-permute-done | bytes 131104 | tf_op jit(solution)/shard_map/ppermute | solution.py:55
  14.6 2.8 %collective-permute-start.4 = (bf16[16,1024]{1,0:T(8,128)(2,1)S(1)}, bf16[16,1024]{1,0:T(8,128)(2,1)S(1)}, u32[]{:S(2)}, u32[]{:S(2)}) collective-permute-start(bf16[16,1024]{1,0:T(8,128)(2,1)S(1)} %get-tuple-element.42), channel_id=1, source_target_pairs={{0,4},{1,16},{2,19},{3,7},{4,0},{5,20},{6,23},{7,3},{8,25},{9,13},... | collective-permute-start | bytes 98312 | tf_op jit(solution)/shard_map/ppermute | solution.py:55
  17.4 1.2 %collective-permute-start.5 = (bf16[16,1024]{1,0:T(8,128)(2,1)S(1)}, bf16[16,1024]{1,0:T(8,128)(2,1)S(1)}, u32[]{:S(2)}, u32[]{:S(2)}) collective-permute-start(bf16[16,1024]{1,0:T(8,128)(2,1)S(1)} %get-tuple-element.43), channel_id=1, source_target_pairs={{0,14},{1,8},{2,11},{3,13},{4,10},{5,12},{6,15},{7,9},{8,1},{9,7},... | collective-permute-start | bytes 98312 | tf_op jit(solution)/shard_map/ppermute | solution.py:55
  18.8 0.7 %collective-permute-done.4.refs_0_ = bf16[16,1024]{1,0:T(8,128)(2,1)S(1)} collective-permute-done((bf16[16,1024]{1,0:T(8,128)(2,1)S(1)}, bf16[16,1024]{1,0:T(8,128)(2,1)S(1)}, u32[]{:S(2)}, u32[]{:S(2)}) %collective-permute-start.4) | collective-permute-done | bytes 32800 | tf_op jit(solution)/shard_map/ppermute | solution.py:55
  19.5 3.0 %collective-permute-done.5.refs_1_ = bf16[16,1024]{1,0:T(8,128)(2,1)S(1)} collective-permute-done((bf16[16,1024]{1,0:T(8,128)(2,1)S(1)}, bf16[16,1024]{1,0:T(8,128)(2,1)S(1)}, u32[]{:S(2)}, u32[]{:S(2)}) %collective-permute-start.5) | collective-permute-done | bytes 32800 | tf_op jit(solution)/shard_map/ppermute | solution.py:55
  22.6 1.5 %collective-permute-start.7 = (bf16[16,1024]{1,0:T(8,128)(2,1)S(1)}, bf16[16,1024]{1,0:T(8,128)(2,1)S(1)}, u32[]{:S(2)}, u32[]{:S(2)}) collective-permute-start(bf16[16,1024]{1,0:T(8,128)(2,1)S(1)} %get-tuple-element.45.grad), channel_id=1, source_target_pairs={{0,8},{1,9},{2,10},{3,11},{4,12},{5,13},{6,14},{7,15},{8,0},{9,1},... | collective-permute-start | bytes 98312 | tf_op jit(solution)/shard_map/ppermute | solution.py:55
  24.2 2.3 %collective-permute-start.8 = (bf16[16,1024]{1,0:T(8,128)(2,1)S(1)}, bf16[16,1024]{1,0:T(8,128)(2,1)S(1)}, u32[]{:S(2)}, u32[]{:S(2)}) collective-permute-start(bf16[16,1024]{1,0:T(8,128)(2,1)S(1)} %get-tuple-element.48), channel_id=1, source_target_pairs={{0,4},{1,16},{2,19},{3,7},{4,0},{5,20},{6,23},{7,3},{8,25},{9,13},... | collective-permute-start | bytes 98312 | tf_op jit(solution)/shard_map/ppermute | solution.py:55
  26.8 0.6 %collective-permute-start.10 = (bf16[16,1024]{1,0:T(8,128)(2,1)S(1)}, bf16[16,1024]{1,0:T(8,128)(2,1)S(1)}, u32[]{:S(2)}, u32[]{:S(2)}) collective-permute-start(bf16[16,1024]{1,0:T(8,128)(2,1)S(1)} %get-tuple-element.47.own), channel_id=1, source_target_pairs={{0,10},{1,25},{2,26},{3,9},{4,14},{5,29},{6,30},{7,13},{8,16},{9,3... | collective-permute-start | bytes 98312 | tf_op jit(solution)/shard_map/ppermute | solution.py:55
  27.4 1.6 %collective-permute-done.8.refs_0_ = bf16[16,1024]{1,0:T(8,128)(2,1)S(1)} collective-permute-done((bf16[16,1024]{1,0:T(8,128)(2,1)S(1)}, bf16[16,1024]{1,0:T(8,128)(2,1)S(1)}, u32[]{:S(2)}, u32[]{:S(2)}) %collective-permute-start.8) | collective-permute-done | bytes 32800 | tf_op jit(solution)/shard_map/ppermute | solution.py:55
  29.1 2.6 %collective-permute-done.9.refs_1_ = bf16[16,1024]{1,0:T(8,128)(2,1)S(1)} collective-permute-done((bf16[16,1024]{1,0:T(8,128)(2,1)S(1)}, bf16[16,1024]{1,0:T(8,128)(2,1)S(1)}, u32[]{:S(2)}, u32[]{:S(2)}) %collective-permute-start.9) | collective-permute-done | bytes 32800 | tf_op jit(solution)/shard_map/ppermute | solution.py:55
  31.7 1.6 %collective-permute-start.11 = (bf16[64,1024]{1,0:T(8,128)(2,1)S(1)}, bf16[64,1024]{1,0:T(8,128)(2,1)S(1)}, u32[]{:S(2)}, u32[]{:S(2)}) collective-permute-start(bf16[64,1024]{1,0:T(8,128)(2,1)S(1)} %get-tuple-element.50), channel_id=1, source_target_pairs={{0,17},{1,5},{2,6},{3,18},{4,21},{5,1},{6,2},{7,22},{8,12},{9,24},... | collective-permute-start | bytes 393224 | tf_op jit(solution)/shard_map/ppermute | solution.py:55
  33.2 1.7 %collective-permute-start.14 = (bf16[64,1024]{1,0:T(8,128)(2,1)S(1)}, bf16[64,1024]{1,0:T(8,128)(2,1)S(1)}, u32[]{:S(2)}, u32[]{:S(2)}) collective-permute-start(bf16[64,1024]{1,0:T(8,128)(2,1)S(1)} %get-tuple-element.57.refs_0_), channel_id=1, source_target_pairs={{0,24},{1,11},{2,8},{3,27},{4,28},{5,15},{6,12},{7,31},{8,2},{9,17... | collective-permute-start | bytes 393224 | tf_op jit(solution)/shard_map/ppermute | solution.py:55
  35.0 0.7 %shard_map.84 = (f32[16,4096]{1,0:T(8,128)}, f32[16,4096]{1,0:T(8,128)}) custom-call(f32[16,4096]{1,0:T(8,128)S(1)} %copy-done, f32[16,4096]{1,0:T(8,128)S(1)} %copy-done.1, bf16[32,1024]{1,0:T(8,128)(2,1)S(1)} %get-tuple-element.51.grads), custom_call_target="tpu_custom_call" | custom-call | tf_op jit(solution)/shard_map/pallas_call | solution.py:37
  35.7 3.2 %collective-permute-done.12.grads = bf16[32,1024]{1,0:T(8,128)(2,1)S(1)} collective-permute-done((bf16[32,1024]{1,0:T(8,128)(2,1)S(1)}, bf16[32,1024]{1,0:T(8,128)(2,1)S(1)}, u32[]{:S(2)}, u32[]{:S(2)}) %collective-permute-start.12) | collective-permute-done | bytes 65568 | tf_op jit(solution)/shard_map/ppermute | solution.py:55
  39.1 0.5 %collective-permute-start.15 = (bf16[64,1024]{1,0:T(8,128)(2,1)S(1)}, bf16[64,1024]{1,0:T(8,128)(2,1)S(1)}, u32[]{:S(2)}, u32[]{:S(2)}) collective-permute-start(bf16[64,1024]{1,0:T(8,128)(2,1)S(1)} %get-tuple-element.57.refs_0_), channel_id=1, source_target_pairs={{0,8},{1,9},{2,10},{3,11},{4,12},{5,13},{6,14},{7,15},{8,0},{9,1},... | collective-permute-start | bytes 393224 | tf_op jit(solution)/shard_map/ppermute | solution.py:55
  39.6 1.0 %shard_map.85 = (f32[16,4096]{1,0:T(8,128)}, f32[16,4096]{1,0:T(8,128)}, bf16[128,4096]{1,0:T(8,128)(2,1)}) custom-call(f32[16,4096]{1,0:T(8,128)S(1)} %copy-done, f32[16,4096]{1,0:T(8,128)S(1)} %copy-done.1, bf16[32,1024]{1,0:T(8,128)(2,1)S(1)} %collective-permute-done.12.grads, ...), custom_call_target="tpu_custom_call", output_to_operand_aliasing={{0}: (3, {}), {1}: (4, {})} | custom-call | tf_op jit(solution)/shard_map/pallas_call | solution.py:37
  40.6 0.4 collective-permute-done.15.own
  41.0 0.8 %shard_map.87 = bf16[128,4096]{1,0:T(8,128)(2,1)} custom-call(bf16[128,4096]{1,0:T(8,128)(2,1)} %get-tuple-element.60._, bf16[64,1024]{1,0:T(8,128)(2,1)S(1)} %collective-permute-done.15.own, bf16[192,1024]{1,0:T(8,128)(2,1)S(1)} %collective-permute-done.16.others), custom_call_target="tpu_custom_call", output_to_operand_aliasing={{}: (0, {})} | custom-call | tf_op jit(solution)/shard_map/pallas_call | solution.py:37
  (30 shorter events, 1.7 us)
Async XLA Ops:
  0.6 2.4 %copy-start.2 = (bf16[768,128]{1,0:T(8,128)(2,1)S(1)}, bf16[768,128]{1,0:T(8,128)(2,1)}, u32[]{:S(2)}) copy-start(bf16[768,128]{1,0:T(8,128)(2,1)} %acts.1) | copy-start | bytes 589828
  3.7 2.4 %collective-permute-start = (bf16[128,2048]{1,0:T(8,128)(2,1)S(1)}, bf16[128,2048]{1,0:T(8,128)(2,1)S(1)}, u32[]{:S(2)}, u32[]{:S(2)}) collective-permute-start(bf16[128,2048]{1,0:T(8,128)(2,1)S(1)} %get-tuple-element.36), channel_id=1, source_target_pairs={{0,8},{1,9},{2,10},{3,11},{4,12},{5,13},{6,14},{7,15},{8,0},{9,1},... | collective-permute-start | bytes 1572872 | tf_op jit(solution)/shard_map/ppermute | solution.py:55
  4.2 18.3 %copy-start = (f32[16,4096]{1,0:T(8,128)S(1)}, f32[16,4096]{1,0:T(8,128)}, u32[]{:S(2)}) copy-start(f32[16,4096]{1,0:T(8,128)} %m.5) | copy-start | bytes 786436
  4.2 18.3 %copy-start.1 = (f32[16,4096]{1,0:T(8,128)S(1)}, f32[16,4096]{1,0:T(8,128)}, u32[]{:S(2)}) copy-start(f32[16,4096]{1,0:T(8,128)} %v.5) | copy-start | bytes 786436
  4.2 18.3 %copy-start.3 = (bf16[16,4096]{1,0:T(8,128)(2,1)S(1)}, bf16[16,4096]{1,0:T(8,128)(2,1)}, u32[]{:S(2)}) copy-start(bf16[16,4096]{1,0:T(8,128)(2,1)} %w.1) | copy-start | bytes 393220
  6.3 6.5 %collective-permute-start.1 = (bf16[64,1024]{1,0:T(8,128)(2,1)S(1)}, bf16[64,1024]{1,0:T(8,128)(2,1)S(1)}, u32[]{:S(2)}, u32[]{:S(2)}) collective-permute-start(bf16[64,1024]{1,0:T(8,128)(2,1)S(1)} %get-tuple-element.38), channel_id=1, source_target_pairs={{0,17},{1,5},{2,6},{3,18},{4,21},{5,1},{6,2},{7,22},{8,12},{9,24},... | collective-permute-start | bytes 393224 | tf_op jit(solution)/shard_map/ppermute | solution.py:55
  9.8 4.4 %collective-permute-start.2 = (bf16[64,1024]{1,0:T(8,128)(2,1)S(1)}, bf16[64,1024]{1,0:T(8,128)(2,1)S(1)}, u32[]{:S(2)}, u32[]{:S(2)}) collective-permute-start(bf16[64,1024]{1,0:T(8,128)(2,1)S(1)} %get-tuple-element.39), channel_id=1, source_target_pairs={{0,9},{1,15},{2,12},{3,10},{4,13},{5,11},{6,8},{7,14},{8,6},{9,0},... | collective-permute-start | bytes 393224 | tf_op jit(solution)/shard_map/ppermute | solution.py:55
  10.1 4.4 %collective-permute-start.3 = (bf16[64,1024]{1,0:T(8,128)(2,1)S(1)}, bf16[64,1024]{1,0:T(8,128)(2,1)S(1)}, u32[]{:S(2)}, u32[]{:S(2)}) collective-permute-start(bf16[64,1024]{1,0:T(8,128)(2,1)S(1)} %get-tuple-element.40), channel_id=1, source_target_pairs={{0,24},{1,11},{2,8},{3,27},{4,28},{5,15},{6,12},{7,31},{8,2},{9,17... | collective-permute-start | bytes 393224 | tf_op jit(solution)/shard_map/ppermute | solution.py:55
  14.6 4.9 %collective-permute-start.4 = (bf16[16,1024]{1,0:T(8,128)(2,1)S(1)}, bf16[16,1024]{1,0:T(8,128)(2,1)S(1)}, u32[]{:S(2)}, u32[]{:S(2)}) collective-permute-start(bf16[16,1024]{1,0:T(8,128)(2,1)S(1)} %get-tuple-element.42), channel_id=1, source_target_pairs={{0,4},{1,16},{2,19},{3,7},{4,0},{5,20},{6,23},{7,3},{8,25},{9,13},... | collective-permute-start | bytes 98312 | tf_op jit(solution)/shard_map/ppermute | solution.py:55
  17.4 5.1 %collective-permute-start.5 = (bf16[16,1024]{1,0:T(8,128)(2,1)S(1)}, bf16[16,1024]{1,0:T(8,128)(2,1)S(1)}, u32[]{:S(2)}, u32[]{:S(2)}) collective-permute-start(bf16[16,1024]{1,0:T(8,128)(2,1)S(1)} %get-tuple-element.43), channel_id=1, source_target_pairs={{0,14},{1,8},{2,11},{3,13},{4,10},{5,12},{6,15},{7,9},{8,1},{9,7},... | collective-permute-start | bytes 98312 | tf_op jit(solution)/shard_map/ppermute | solution.py:55
  18.5 4.0 %collective-permute-start.6 = (bf16[16,1024]{1,0:T(8,128)(2,1)S(1)}, bf16[16,1024]{1,0:T(8,128)(2,1)S(1)}, u32[]{:S(2)}, u32[]{:S(2)}) collective-permute-start(bf16[16,1024]{1,0:T(8,128)(2,1)S(1)} %get-tuple-element.44), channel_id=1, source_target_pairs={{0,10},{1,25},{2,26},{3,9},{4,14},{5,29},{6,30},{7,13},{8,16},{9,3... | collective-permute-start | bytes 98312 | tf_op jit(solution)/shard_map/ppermute | solution.py:55
  22.6 4.8 %collective-permute-start.7 = (bf16[16,1024]{1,0:T(8,128)(2,1)S(1)}, bf16[16,1024]{1,0:T(8,128)(2,1)S(1)}, u32[]{:S(2)}, u32[]{:S(2)}) collective-permute-start(bf16[16,1024]{1,0:T(8,128)(2,1)S(1)} %get-tuple-element.45.grad), channel_id=1, source_target_pairs={{0,8},{1,9},{2,10},{3,11},{4,12},{5,13},{6,14},{7,15},{8,0},{9,1},... | collective-permute-start | bytes 98312 | tf_op jit(solution)/shard_map/ppermute | solution.py:55
  24.2 4.9 %collective-permute-start.8 = (bf16[16,1024]{1,0:T(8,128)(2,1)S(1)}, bf16[16,1024]{1,0:T(8,128)(2,1)S(1)}, u32[]{:S(2)}, u32[]{:S(2)}) collective-permute-start(bf16[16,1024]{1,0:T(8,128)(2,1)S(1)} %get-tuple-element.48), channel_id=1, source_target_pairs={{0,4},{1,16},{2,19},{3,7},{4,0},{5,20},{6,23},{7,3},{8,25},{9,13},... | collective-permute-start | bytes 98312 | tf_op jit(solution)/shard_map/ppermute | solution.py:55
  26.5 5.1 %collective-permute-start.9 = (bf16[16,1024]{1,0:T(8,128)(2,1)S(1)}, bf16[16,1024]{1,0:T(8,128)(2,1)S(1)}, u32[]{:S(2)}, u32[]{:S(2)}) collective-permute-start(bf16[16,1024]{1,0:T(8,128)(2,1)S(1)} %get-tuple-element.49), channel_id=1, source_target_pairs={{0,14},{1,8},{2,11},{3,13},{4,10},{5,12},{6,15},{7,9},{8,1},{9,7},... | collective-permute-start | bytes 98312 | tf_op jit(solution)/shard_map/ppermute | solution.py:55
  26.8 4.8 %collective-permute-start.10 = (bf16[16,1024]{1,0:T(8,128)(2,1)S(1)}, bf16[16,1024]{1,0:T(8,128)(2,1)S(1)}, u32[]{:S(2)}, u32[]{:S(2)}) collective-permute-start(bf16[16,1024]{1,0:T(8,128)(2,1)S(1)} %get-tuple-element.47.own), channel_id=1, source_target_pairs={{0,10},{1,25},{2,26},{3,9},{4,14},{5,29},{6,30},{7,13},{8,16},{9,3... | collective-permute-start | bytes 98312 | tf_op jit(solution)/shard_map/ppermute | solution.py:55
  31.7 7.3 %collective-permute-start.11 = (bf16[64,1024]{1,0:T(8,128)(2,1)S(1)}, bf16[64,1024]{1,0:T(8,128)(2,1)S(1)}, u32[]{:S(2)}, u32[]{:S(2)}) collective-permute-start(bf16[64,1024]{1,0:T(8,128)(2,1)S(1)} %get-tuple-element.50), channel_id=1, source_target_pairs={{0,17},{1,5},{2,6},{3,18},{4,21},{5,1},{6,2},{7,22},{8,12},{9,24},... | collective-permute-start | bytes 393224 | tf_op jit(solution)/shard_map/ppermute | solution.py:55
  33.2 5.8 %collective-permute-start.13 = (bf16[64,1024]{1,0:T(8,128)(2,1)S(1)}, bf16[64,1024]{1,0:T(8,128)(2,1)S(1)}, u32[]{:S(2)}, u32[]{:S(2)}) collective-permute-start(bf16[64,1024]{1,0:T(8,128)(2,1)S(1)} %get-tuple-element.59), channel_id=1, source_target_pairs={{0,9},{1,15},{2,12},{3,10},{4,13},{5,11},{6,8},{7,14},{8,6},{9,0},... | collective-permute-start | bytes 393224 | tf_op jit(solution)/shard_map/ppermute | solution.py:55
  33.2 5.8 %collective-permute-start.14 = (bf16[64,1024]{1,0:T(8,128)(2,1)S(1)}, bf16[64,1024]{1,0:T(8,128)(2,1)S(1)}, u32[]{:S(2)}, u32[]{:S(2)}) collective-permute-start(bf16[64,1024]{1,0:T(8,128)(2,1)S(1)} %get-tuple-element.57.refs_0_), channel_id=1, source_target_pairs={{0,24},{1,11},{2,8},{3,27},{4,28},{5,15},{6,12},{7,31},{8,2},{9,17... | collective-permute-start | bytes 393224 | tf_op jit(solution)/shard_map/ppermute | solution.py:55
  34.9 4.0 %collective-permute-start.12 = (bf16[32,1024]{1,0:T(8,128)(2,1)S(1)}, bf16[32,1024]{1,0:T(8,128)(2,1)S(1)}, u32[]{:S(2)}, u32[]{:S(2)}) collective-permute-start(bf16[32,1024]{1,0:T(8,128)(2,1)S(1)} %get-tuple-element.51.grads), channel_id=1, source_target_pairs={{0,24},{1,25},{2,26},{3,27},{4,28},{5,29},{6,30},{7,31},{8,16},{9,... | collective-permute-start | bytes 196616 | tf_op jit(solution)/shard_map/ppermute | solution.py:55
  39.0 2.0 %collective-permute-start.16 = (bf16[192,1024]{1,0:T(8,128)(2,1)S(1)}, bf16[192,1024]{1,0:T(8,128)(2,1)S(1)}, u32[]{:S(2)}, u32[]{:S(2)}) collective-permute-start(bf16[192,1024]{1,0:T(8,128)(2,1)S(1)} %shard_map.86), channel_id=1, source_target_pairs={{0,8},{1,9},{2,10},{3,11},{4,12},{5,13},{6,14},{7,15},{8,0},{9,1},... | collective-permute-start | bytes 1179656 | tf_op jit(solution)/shard_map/ppermute | solution.py:55
  39.1 1.9 %collective-permute-start.15 = (bf16[64,1024]{1,0:T(8,128)(2,1)S(1)}, bf16[64,1024]{1,0:T(8,128)(2,1)S(1)}, u32[]{:S(2)}, u32[]{:S(2)}) collective-permute-start(bf16[64,1024]{1,0:T(8,128)(2,1)S(1)} %get-tuple-element.57.refs_0_), channel_id=1, source_target_pairs={{0,8},{1,9},{2,10},{3,11},{4,12},{5,13},{6,14},{7,15},{8,0},{9,1},... | collective-permute-start | bytes 393224 | tf_op jit(solution)/shard_map/ppermute | solution.py:55

commit v3 on v2

--- a/solution.py
+++ b/solution.py
@@ -82,14 +82,6 @@
     )
 
 
-def wide_stage(value, step):
-    return stage(value, step, 0)
-
-
-def narrow_stage(value, step):
-    return stage(value, step, 1)
-
-
 def along_x(value):
     return exchange(value, lambda rep, shard: partner(rep, shard, 0, 1, 0))
 
@@ -112,10 +104,10 @@
     )
 
 
-def group_of(step):
+def group_of(step, line_role):
     role, x, y, z, _ = place()
     (dy, dx), k = step
-    return jnp.where(role == 0, z ^ k, 2 * (y ^ dy) + (x ^ dx))
+    return jnp.where(role == line_role, z ^ k, 2 * (y ^ dy) + (x ^ dx))
 
 
 def block(index, size):
@@ -173,7 +165,7 @@
 def narrow_kernel(kept, *refs):
     came, (own, *pieces) = refs[:len(STEPS)], refs[len(STEPS):]
     for step, out in zip((STAY,) + STEPS, [own] + pieces):
-        at = block(group_of(step), out.shape[0])
+        at = block(group_of(step, 0), out.shape[0])
         total = kept[at, :]
         for ref in came:
             total += ref[at, :].astype(F32)
@@ -221,76 +213,65 @@
         put(outs, block(w ^ k, rows), ref[...])
 
 
-def narrow_back_kernel(grad, sibling_grad, own, *refs):
-    parts, (*outs, grads) = (own,) + refs[:-1 - len(STEPS)], refs[-1 - len(STEPS):]
-    size, rows = own.shape[0], grad.shape[0]
+def narrow_back_kernel(own, *refs):
+    parts, outs = (own,) + refs[:-len(STEPS)], refs[-len(STEPS):]
     for step, ref in zip((STAY,) + STEPS, parts):
-        put(outs, block(group_of(step), size), ref[...])
-    role = place()[0]
-    grads[block(role, rows), :] = grad[...]
-    grads[block(1 - role, rows), :] = sibling_grad[...]
-
-
-def half_blocks(rows, sibling, parts, out):
+        put(outs, block(group_of(step, 1), own.shape[0]), ref[...])
+
+
+def half_blocks(sibling, parts, out):
     role, x, y, z, _ = place()
-    first = (role == 0) != sibling
+    square = (role == 1) != sibling
     size, quarter = parts[0].shape
+    rows = out.shape[0] // lax.axis_size("shard")
     count = size // (4 * rows)
     for ((dy, dx), k), ref in zip((STAY,) + STEPS, parts):
         for group in range(4):
-            to_y = jnp.where(first, y ^ dy, group >> 1)
-            to_x = jnp.where(first, x ^ dx, group & 1)
-            to_z = jnp.where(first, group, z ^ k)
+            to_y = jnp.where(square, y ^ dy, group >> 1)
+            to_x = jnp.where(square, x ^ dx, group & 1)
+            to_z = jnp.where(square, group, z ^ k)
             for w in range(count):
                 at = (group * count + w) * rows
                 out[block(8 * w + 2 * to_z + to_y, rows), block(to_x, quarter)] = ref[at:at + rows, :]
 
 
-def write_moments(far, grads, m, v, m_out, v_out, new_m, new_v, sems):
-    x = place()[1]
-    rows, quarter = new_m.shape[1:]
-    copies = []
-    for side in range(2):
-        at = block(2 * side + (x ^ far), quarter)
-        grad = grads[side * rows:(side + 1) * rows, :].astype(F32)
-        new_m[side], new_v[side] = adamw_moments(m[:, at], v[:, at], grad)
+def write(sibling, parts, grads, m, v, w_out, m_out, v_out, half, new_m, new_v, sems):
+    role, x, _, _, _ = place()
+    side = role ^ sibling
+    half_blocks(sibling, parts, half)
+    copies = [pltpu.make_async_copy(half, w_out.at[:, block(side, half.shape[1])], sems.at[0])]
+    copies[0].start()
+    for far, grad in enumerate(grads):
+        at = block(2 * side + (x ^ far), grad.shape[1])
+        new_m[far], new_v[far] = adamw_moments(m[:, at], v[:, at], grad[...].astype(F32))
         for source, out in ((new_m, m_out), (new_v, v_out)):
-            copies.append(pltpu.make_async_copy(source.at[side], out.at[:, at], sems.at[len(copies)]))
+            copies.append(pltpu.make_async_copy(source.at[far], out.at[:, at], sems.at[len(copies)]))
             copies[-1].start()
-    return copies
-
-
-def moments_kernel(m, v, grads, m_out, v_out, *scratch):
-    for copy in write_moments(0, grads, m, v, m_out, v_out, *scratch):
+    for copy in copies:
         copy.wait()
 
 
-def write_half(sibling, parts, out, half, sem):
-    half_blocks(out.shape[0] // lax.axis_size("shard"), sibling, parts, half)
-    copy = pltpu.make_async_copy(half, out.at[:, block(place()[0] ^ sibling, half.shape[1])], sem)
-    copy.start()
-    return copy
-
-
-def write_own_kernel(m, v, grads, _m, _v, *refs):
-    parts, (m_out, v_out, out, half, sem, *scratch) = refs[:1 + len(STEPS)], refs[1 + len(STEPS):]
-    rows = write_half(0, parts, out, half, sem)
-    for copy in write_moments(1, grads, m, v, m_out, v_out, *scratch):
-        copy.wait()
-    rows.wait()
-
-
 def pack_kernel(*refs):
-    *parts, out = refs
-    size = parts[0].shape[0]
-    for i, ref in enumerate(parts):
-        out[i * size:(i + 1) * size, :] = ref[...]
-
-
-def write_other_kernel(_, own, others, out, half, sem):
-    size = own.shape[0]
-    parts = [own] + [others.at[pl.ds(i * size, size), :] for i in range(len(STEPS))]
-    write_half(1, parts, out, half, sem).wait()
+    *parts, _, out = refs
+    at = 0
+    for ref in parts:
+        out[at:at + ref.shape[0], :] = ref[...]
+        at += ref.shape[0]
+
+
+def write_own_kernel(m, v, grad, far_grad, *refs):
+    parts, refs = refs[:1 + len(STEPS)], refs[1 + len(STEPS):]
+    write(0, parts, (grad, far_grad), m, v, *refs)
+
+
+def write_other_kernel(m, v, own, landed, _w, _m, _v, *refs):
+    size, rows = own.shape[0], m.shape[0]
+    sizes = [size] * len(STEPS) + [rows] * 2
+    parts, at = [], 0
+    for count in sizes:
+        parts.append(landed.at[pl.ds(at, count), :])
+        at += count
+    write(1, [own] + parts[:len(STEPS)], parts[len(STEPS):], m, v, *refs)
 
 
 def body(hidden_acts, out_cotangent, weight, first_moment, second_moment):
@@ -320,9 +301,9 @@
         return call(kernel, [kept] + [sent] * (parts - 1), *args)
 
     own, *pieces = split(functools.partial(wide_kernel, rows), wide_rows, 4, kept, came)
-    came = [wide_stage(piece, step) for step, piece in zip(STEPS, pieces)]
+    came = [stage(piece, step, 0) for step, piece in zip(STEPS, pieces)]
     own, *pieces = split(narrow_kernel, narrow_rows, 4, own, *came)
-    came = [narrow_stage(piece, step) for step, piece in zip(STEPS, pieces)]
+    came = [stage(piece, step, 1) for step, piece in zip(STEPS, pieces)]
     if rest > 1:
         own, *pieces = split(rest_kernel, rows, rest, own, *came)
         came = [along_rest(piece, k + 1) for k, piece in enumerate(pieces)]
@@ -330,37 +311,28 @@
         update_kernel, [shape((rows, quarter), BF16)] * 2, weight, first_moment, second_moment, own, *came,
     )
 
-    sibling_grad = to_sibling(grad)
     pieces = [along_rest(new_w, k) for k in range(1, rest)]
     parts = call(rest_back_kernel, [shape((narrow_rows, quarter), BF16)] * len(STEPS), new_w, *pieces)
-    came = [narrow_stage(part, step) for step, part in zip(STEPS, parts)]
-    *parts, grads = call(
-        narrow_back_kernel,
-        [shape((wide_rows, quarter), BF16)] * len(STEPS) + [shape((2 * rows, quarter), BF16)],
-        grad, sibling_grad, parts[-1], *came,
-    )
-    came = [wide_stage(part, step) for step, part in zip(STEPS, parts)]
-    far_grads = along_x(grads)
-    moments = [shape((rows, width), F32)] * 2
-    moments_scratch = [pltpu.VMEM((2, rows, quarter), F32)] * 2 + [pltpu.SemaphoreType.DMA((4,))]
-    new_m, new_v = call(
-        moments_kernel, moments, first_moment, second_moment, grads, far_out=2, scratch=moments_scratch,
-    )
-    came[0], far_grads, new_m, new_v = lax.optimization_barrier((came[0], far_grads, new_m, new_v))
-
-    mine = [parts[-1]] + came
-    landed = call(pack_kernel, [shape((len(STEPS) * wide_rows, quarter), BF16)], *came)[0]
-    others = [to_sibling(parts[-1]), to_sibling(landed)]
-    out = [shape((all_rows, width), BF16)]
-    scratch = [pltpu.VMEM((all_rows, half), BF16), pltpu.SemaphoreType.DMA]
-    new_m, new_v, new_w = call(
-        write_own_kernel, moments + out, first_moment, second_moment, far_grads, new_m, new_v, *mine,
-        far_in=(3, 4), far_out=3, scratch=scratch + moments_scratch, aliases={3: 0, 4: 1},
-    )
-    new_w = call(
-        write_other_kernel, out, new_w, *others, far_in=(0,), far_out=1, scratch=scratch, aliases={0: 0},
-    )[0]
-    return new_w, new_m, new_v
+    came = [stage(part, step, 0) for step, part in zip(STEPS, parts)]
+    parts = call(narrow_back_kernel, [shape((wide_rows, quarter), BF16)] * len(STEPS), parts[-1], *came)
+    came = [stage(part, step, 1) for step, part in zip(STEPS, parts)]
+    far_grad, own = along_x(grad), to_sibling(parts[-1])
+    came[0], far_grad = lax.optimization_barrier((came[0], far_grad))
+
+    landed = to_sibling(call(
+        pack_kernel, [shape((len(STEPS) * wide_rows + 2 * rows, quarter), BF16)], *came, grad, far_grad, own,
+    )[0])
+    outs = [shape((all_rows, width), BF16), shape((rows, width), F32), shape((rows, width), F32)]
+    scratch = [pltpu.VMEM((all_rows, half), BF16)] + [pltpu.VMEM((2, rows, quarter), F32)] * 2
+    scratch += [pltpu.SemaphoreType.DMA((5,))]
+    written = call(
+        write_own_kernel, outs, first_moment, second_moment, grad, far_grad, parts[-1], *came,
+        far_out=3, scratch=scratch,
+    )
+    return tuple(call(
+        write_other_kernel, outs, first_moment, second_moment, own, landed, *written,
+        far_in=(4, 5, 6), far_out=3, scratch=scratch, aliases={4: 0, 5: 1, 6: 2},
+    ))
 
 
 def solution(mesh):

time: 42 us -> 41.3 us (0.983)
  waiting for transfers between devices: 15.9 us -> 13.8 us
  starting transfers between devices: 17.3 us -> 19.3 us
  Pallas kernels: 7.86 us -> 7.28 us
    ppermute x17 -> x16, waiting for transfers between devices: 15.9 us -> 13.8 us  [exchange(): return lax.ppermute(value, ('rep', 'shard'), pairs)]
    ppermute x17 -> x16, starting transfers between devices: 17.3 us -> 19.3 us  [exchange(): return lax.ppermute(value, ('rep', 'shard'), pairs)]
    pallas_call x12 -> x11, Pallas kernels: 7.86 us -> 7.28 us  [call(): pl.pallas_call(kernel, out_shape=outs, in_specs=[far if i in tuple(far_in...]
  transfers between devices with their start and end apart: 17 -> 16, of which waited for: 9 -> 10; matrix products, arithmetic and copies ran while one was open for 0% -> 0% of each run, Pallas kernels for 9% -> 7%
where the time goes in v3:
time: 41.3 us; the launch traced here: 41.2 us
  starting transfers between devices  19.3 us (47%)
  waiting for transfers between devices  13.8 us (33%)
  Pallas kernels  7.28 us (18%)
  between operations  0.76 us (2%)
    ppermute x16, starting transfers between devices, exchange(): return lax.ppermute(value, ('rep', 'shard'), pairs)  19.3 us
    ppermute x16, waiting for transfers between devices, exchange(): return lax.ppermute(value, ('rep', 'shard'), pairs)  13.8 us
    pallas_call x11, Pallas kernels, call(): pl.pallas_call(kernel, out_shape=outs, in_specs=[far if i in tuple(far_in...  7.28 us
  transfers between devices with their start and end apart: 16, of which 10 were waited for; matrix products, arithmetic and copies ran while one was open for 0% of the time, Pallas kernels for 7%

profile of v3, /device:TPU:0, one launch (start us, length us, event | category | flops | bytes accessed | tf_op | source)
XLA Modules:
  0.0 41.2 jit_solution(16611545665217112038)
XLA Ops:
  0.6 2.4 %shard_map.76 = (bf16[768,2048]{1,0:T(8,128)(2,1)S(1)}, bf16[768,1024]{1,0:T(8,128)(2,1)S(1)}) custom-call(bf16[768,4096]{1,0:T(8,128)(2,1)} %cots_ref.3), custom_call_target="tpu_custom_call" | custom-call | tf_op jit(solution)/shard_map/pallas_call | solution.py:37
  3.1 0.6 %shard_map.77 = (bf16[128,2048]{1,0:T(8,128)(2,1)S(1)}, bf16[128,768]{1,0:T(8,128)(2,1)S(1)}) custom-call(bf16[768,128]{1,0:T(8,128)(2,1)S(1)} %copy-done.2, bf16[768,2048]{1,0:T(8,128)(2,1)S(1)} %get-tuple-element.28.cots), custom_call_target="tpu_custom_call" | custom-call | tf_op jit(solution)/shard_map/pallas_call | solution.py:37
  3.7 0.5 %collective-permute-start = (bf16[128,2048]{1,0:T(8,128)(2,1)S(1)}, bf16[128,2048]{1,0:T(8,128)(2,1)S(1)}, u32[]{:S(2)}, u32[]{:S(2)}) collective-permute-start(bf16[128,2048]{1,0:T(8,128)(2,1)S(1)} %get-tuple-element.31), channel_id=1, source_target_pairs={{0,8},{1,9},{2,10},{3,11},{4,12},{5,13},{6,14},{7,15},{8,0},{9,1},... | collective-permute-start | bytes 1572872 | tf_op jit(solution)/shard_map/ppermute | solution.py:55
  4.2 1.9 %shard_map.78.kept = f32[128,2048]{1,0:T(8,128)S(1)} custom-call(bf16[128,768]{1,0:T(8,128)(2,1)S(1)} %get-tuple-element.29.turned, bf16[768,1024]{1,0:T(8,128)(2,1)S(1)} %get-tuple-element.30.first, bf16[768,4096]{1,0:T(8,128)(2,1)} %cots_ref.3), custom_call_target="tpu_custom_call" | custom-call | tf_op jit(solution)/shard_map/pallas_call | solution.py:37
  6.3 3.6 %collective-permute-start.1 = (bf16[64,1024]{1,0:T(8,128)(2,1)S(1)}, bf16[64,1024]{1,0:T(8,128)(2,1)S(1)}, u32[]{:S(2)}, u32[]{:S(2)}) collective-permute-start(bf16[64,1024]{1,0:T(8,128)(2,1)S(1)} %get-tuple-element.33), channel_id=1, source_target_pairs={{0,17},{1,5},{2,6},{3,18},{4,21},{5,1},{6,2},{7,22},{8,12},{9,24},... | collective-permute-start | bytes 393224 | tf_op jit(solution)/shard_map/ppermute | solution.py:55
  10.2 2.6 %collective-permute-done.1.refs_0_ = bf16[64,1024]{1,0:T(8,128)(2,1)S(1)} collective-permute-done((bf16[64,1024]{1,0:T(8,128)(2,1)S(1)}, bf16[64,1024]{1,0:T(8,128)(2,1)S(1)}, u32[]{:S(2)}, u32[]{:S(2)}) %collective-permute-start.1) | collective-permute-done | bytes 131104 | tf_op jit(solution)/shard_map/ppermute | solution.py:55
  12.8 1.4 %collective-permute-done.2.refs_1_ = bf16[64,1024]{1,0:T(8,128)(2,1)S(1)} collective-permute-done((bf16[64,1024]{1,0:T(8,128)(2,1)S(1)}, bf16[64,1024]{1,0:T(8,128)(2,1)S(1)}, u32[]{:S(2)}, u32[]{:S(2)}) %collective-permute-start.2) | collective-permute-done | bytes 131104 | tf_op jit(solution)/shard_map/ppermute | solution.py:55
  14.6 2.8 %collective-permute-start.4 = (bf16[16,1024]{1,0:T(8,128)(2,1)S(1)}, bf16[16,1024]{1,0:T(8,128)(2,1)S(1)}, u32[]{:S(2)}, u32[]{:S(2)}) collective-permute-start(bf16[16,1024]{1,0:T(8,128)(2,1)S(1)} %get-tuple-element.37), channel_id=1, source_target_pairs={{0,4},{1,16},{2,19},{3,7},{4,0},{5,20},{6,23},{7,3},{8,25},{9,13},... | collective-permute-start | bytes 98312 | tf_op jit(solution)/shard_map/ppermute | solution.py:55
  17.4 1.2 %collective-permute-start.5 = (bf16[16,1024]{1,0:T(8,128)(2,1)S(1)}, bf16[16,1024]{1,0:T(8,128)(2,1)S(1)}, u32[]{:S(2)}, u32[]{:S(2)}) collective-permute-start(bf16[16,1024]{1,0:T(8,128)(2,1)S(1)} %get-tuple-element.38), channel_id=1, source_target_pairs={{0,14},{1,8},{2,11},{3,13},{4,10},{5,12},{6,15},{7,9},{8,1},{9,7},... | collective-permute-start | bytes 98312 | tf_op jit(solution)/shard_map/ppermute | solution.py:55
  18.8 0.7 %collective-permute-done.4.refs_0_ = bf16[16,1024]{1,0:T(8,128)(2,1)S(1)} collective-permute-done((bf16[16,1024]{1,0:T(8,128)(2,1)S(1)}, bf16[16,1024]{1,0:T(8,128)(2,1)S(1)}, u32[]{:S(2)}, u32[]{:S(2)}) %collective-permute-start.4) | collective-permute-done | bytes 32800 | tf_op jit(solution)/shard_map/ppermute | solution.py:55
  19.5 3.0 %collective-permute-done.5.refs_1_ = bf16[16,1024]{1,0:T(8,128)(2,1)S(1)} collective-permute-done((bf16[16,1024]{1,0:T(8,128)(2,1)S(1)}, bf16[16,1024]{1,0:T(8,128)(2,1)S(1)}, u32[]{:S(2)}, u32[]{:S(2)}) %collective-permute-start.5) | collective-permute-done | bytes 32800 | tf_op jit(solution)/shard_map/ppermute | solution.py:55
  22.6 1.5 %collective-permute-start.7 = (bf16[16,1024]{1,0:T(8,128)(2,1)S(1)}, bf16[16,1024]{1,0:T(8,128)(2,1)S(1)}, u32[]{:S(2)}, u32[]{:S(2)}) collective-permute-start(bf16[16,1024]{1,0:T(8,128)(2,1)S(1)} %get-tuple-element.42), channel_id=1, source_target_pairs={{0,17},{1,5},{2,6},{3,18},{4,21},{5,1},{6,2},{7,22},{8,12},{9,24},... | collective-permute-start | bytes 98312 | tf_op jit(solution)/shard_map/ppermute | solution.py:55
  24.2 0.8 %collective-permute-start.8 = (bf16[16,1024]{1,0:T(8,128)(2,1)S(1)}, bf16[16,1024]{1,0:T(8,128)(2,1)S(1)}, u32[]{:S(2)}, u32[]{:S(2)}) collective-permute-start(bf16[16,1024]{1,0:T(8,128)(2,1)S(1)} %get-tuple-element.43), channel_id=1, source_target_pairs={{0,9},{1,15},{2,12},{3,10},{4,13},{5,11},{6,8},{7,14},{8,6},{9,0},... | collective-permute-start | bytes 98312 | tf_op jit(solution)/shard_map/ppermute | solution.py:55
  25.0 0.9 %collective-permute-start.9 = (bf16[16,1024]{1,0:T(8,128)(2,1)S(1)}, bf16[16,1024]{1,0:T(8,128)(2,1)S(1)}, u32[]{:S(2)}, u32[]{:S(2)}) collective-permute-start(bf16[16,1024]{1,0:T(8,128)(2,1)S(1)} %get-tuple-element.41.own), channel_id=1, source_target_pairs={{0,24},{1,11},{2,8},{3,27},{4,28},{5,15},{6,12},{7,31},{8,2},{9,17... | collective-permute-start | bytes 98312 | tf_op jit(solution)/shard_map/ppermute | solution.py:55
  25.9 1.7 %collective-permute-done.7.refs_0_ = bf16[16,1024]{1,0:T(8,128)(2,1)S(1)} collective-permute-done((bf16[16,1024]{1,0:T(8,128)(2,1)S(1)}, bf16[16,1024]{1,0:T(8,128)(2,1)S(1)}, u32[]{:S(2)}, u32[]{:S(2)}) %collective-permute-start.7) | collective-permute-done | bytes 32800 | tf_op jit(solution)/shard_map/ppermute | solution.py:55
  28.4 1.4 %collective-permute-start.11 = (bf16[64,1024]{1,0:T(8,128)(2,1)S(1)}, bf16[64,1024]{1,0:T(8,128)(2,1)S(1)}, u32[]{:S(2)}, u32[]{:S(2)}) collective-permute-start(bf16[64,1024]{1,0:T(8,128)(2,1)S(1)} %get-tuple-element.45), channel_id=1, source_target_pairs={{0,4},{1,16},{2,19},{3,7},{4,0},{5,20},{6,23},{7,3},{8,25},{9,13},... | collective-permute-start | bytes 393224 | tf_op jit(solution)/shard_map/ppermute | solution.py:55
  29.8 1.2 %collective-permute-start.13 = (bf16[64,1024]{1,0:T(8,128)(2,1)S(1)}, bf16[64,1024]{1,0:T(8,128)(2,1)S(1)}, u32[]{:S(2)}, u32[]{:S(2)}) collective-permute-start(bf16[64,1024]{1,0:T(8,128)(2,1)S(1)} %get-tuple-element.48), channel_id=1, source_target_pairs={{0,14},{1,8},{2,11},{3,13},{4,10},{5,12},{6,15},{7,9},{8,1},{9,7},... | collective-permute-start | bytes 393224 | tf_op jit(solution)/shard_map/ppermute | solution.py:55
  30.9 0.7 %collective-permute-start.14 = (bf16[64,1024]{1,0:T(8,128)(2,1)S(1)}, bf16[64,1024]{1,0:T(8,128)(2,1)S(1)}, u32[]{:S(2)}, u32[]{:S(2)}) collective-permute-start(bf16[64,1024]{1,0:T(8,128)(2,1)S(1)} %get-tuple-element.44.refs_0_), channel_id=1, source_target_pairs={{0,10},{1,25},{2,26},{3,9},{4,14},{5,29},{6,30},{7,13},{8,16},{9,3... | collective-permute-start | bytes 393224 | tf_op jit(solution)/shard_map/ppermute | solution.py:55
  31.7 2.7 %collective-permute-start.10 = (bf16[64,1024]{1,0:T(8,128)(2,1)S(1)}, bf16[64,1024]{1,0:T(8,128)(2,1)S(1)}, u32[]{:S(2)}, u32[]{:S(2)}) collective-permute-start(bf16[64,1024]{1,0:T(8,128)(2,1)S(1)} %get-tuple-element.44.refs_0_), channel_id=1, source_target_pairs={{0,8},{1,9},{2,10},{3,11},{4,12},{5,13},{6,14},{7,15},{8,0},{9,1},... | collective-permute-start | bytes 393224 | tf_op jit(solution)/shard_map/ppermute | solution.py:55
  34.3 0.9 %collective-permute-start.12 = (bf16[16,1024]{1,0:T(8,128)(2,1)S(1)}, bf16[16,1024]{1,0:T(8,128)(2,1)S(1)}, u32[]{:S(2)}, u32[]{:S(2)}) collective-permute-start(bf16[16,1024]{1,0:T(8,128)(2,1)S(1)} %get-tuple-element.46.refs_3_.grad), channel_id=1, source_target_pairs={{0,24},{1,25},{2,26},{3,27},{4,28},{5,29},{6,30},{7,31},{8,16},{9,... | collective-permute-start | bytes 98312 | tf_op jit(solution)/shard_map/ppermute | solution.py:55
  35.3 2.8 %collective-permute-done.12.refs_4_.far_grad = bf16[16,1024]{1,0:T(8,128)(2,1)S(1)} collective-permute-done((bf16[16,1024]{1,0:T(8,128)(2,1)S(1)}, bf16[16,1024]{1,0:T(8,128)(2,1)S(1)}, u32[]{:S(2)}, u32[]{:S(2)}) %collective-permute-start.12) | collective-permute-done | bytes 32800 | tf_op jit(solution)/shard_map/ppermute | solution.py:55
  38.1 0.6 %collective-permute-start.15 = (bf16[224,1024]{1,0:T(8,128)(2,1)S(1)}, bf16[224,1024]{1,0:T(8,128)(2,1)S(1)}, u32[]{:S(2)}, u32[]{:S(2)}) collective-permute-start(bf16[224,1024]{1,0:T(8,128)(2,1)S(1)} %shard_map.84), channel_id=1, source_target_pairs={{0,8},{1,9},{2,10},{3,11},{4,12},{5,13},{6,14},{7,15},{8,0},{9,1},... | collective-permute-start | bytes 1376264 | tf_op jit(solution)/shard_map/ppermute | solution.py:55
  38.7 1.0 %shard_map.85 = (bf16[128,4096]{1,0:T(8,128)(2,1)}, f32[16,4096]{1,0:T(8,128)}, f32[16,4096]{1,0:T(8,128)}) custom-call(f32[16,4096]{1,0:T(8,128)S(1)} %copy-done, f32[16,4096]{1,0:T(8,128)S(1)} %copy-done.1, bf16[16,1024]{1,0:T(8,128)(2,1)S(1)} %get-tuple-element.46.refs_3_.grad, bf16[16,1024]{1,0:T(8,128)(2,1)S(1)} %collective-permute-done.12.refs_4_.far_grad, ...), custom_call_target="tpu_custom_call" | custom-call | tf_op jit(solution)/shard_map/pallas_call | solution.py:37
  40.2 1.0 %shard_map.86 = (bf16[128,4096]{1,0:T(8,128)(2,1)}, f32[16,4096]{1,0:T(8,128)}, f32[16,4096]{1,0:T(8,128)}) custom-call(f32[16,4096]{1,0:T(8,128)S(1)} %copy-done, f32[16,4096]{1,0:T(8,128)S(1)} %copy-done.1, bf16[64,1024]{1,0:T(8,128)(2,1)S(1)} %collective-permute-done.10.refs_5_.own, ...), custom_call_target="tpu_custom_call", output_to_operand_aliasing={{0}: (4, {}), {1}: (5, {}), {2}: (6, {})} | custom-call | tf_op jit(solution)/shard_map/pallas_call | solution.py:37
  (27 shorter events, 2.4 us)
Async XLA Ops:
  0.6 2.4 %copy-start.2 = (bf16[768,128]{1,0:T(8,128)(2,1)S(1)}, bf16[768,128]{1,0:T(8,128)(2,1)}, u32[]{:S(2)}) copy-start(bf16[768,128]{1,0:T(8,128)(2,1)} %acts.1) | copy-start | bytes 589828
  3.7 2.4 %collective-permute-start = (bf16[128,2048]{1,0:T(8,128)(2,1)S(1)}, bf16[128,2048]{1,0:T(8,128)(2,1)S(1)}, u32[]{:S(2)}, u32[]{:S(2)}) collective-permute-start(bf16[128,2048]{1,0:T(8,128)(2,1)S(1)} %get-tuple-element.31), channel_id=1, source_target_pairs={{0,8},{1,9},{2,10},{3,11},{4,12},{5,13},{6,14},{7,15},{8,0},{9,1},... | collective-permute-start | bytes 1572872 | tf_op jit(solution)/shard_map/ppermute | solution.py:55
  4.2 18.3 %copy-start = (f32[16,4096]{1,0:T(8,128)S(1)}, f32[16,4096]{1,0:T(8,128)}, u32[]{:S(2)}) copy-start(f32[16,4096]{1,0:T(8,128)} %m.5) | copy-start | bytes 786436
  4.2 18.3 %copy-start.1 = (f32[16,4096]{1,0:T(8,128)S(1)}, f32[16,4096]{1,0:T(8,128)}, u32[]{:S(2)}) copy-start(f32[16,4096]{1,0:T(8,128)} %v.5) | copy-start | bytes 786436
  4.2 18.3 %copy-start.3 = (bf16[16,4096]{1,0:T(8,128)(2,1)S(1)}, bf16[16,4096]{1,0:T(8,128)(2,1)}, u32[]{:S(2)}) copy-start(bf16[16,4096]{1,0:T(8,128)(2,1)} %w.1) | copy-start | bytes 393220
  6.3 6.5 %collective-permute-start.1 = (bf16[64,1024]{1,0:T(8,128)(2,1)S(1)}, bf16[64,1024]{1,0:T(8,128)(2,1)S(1)}, u32[]{:S(2)}, u32[]{:S(2)}) collective-permute-start(bf16[64,1024]{1,0:T(8,128)(2,1)S(1)} %get-tuple-element.33), channel_id=1, source_target_pairs={{0,17},{1,5},{2,6},{3,18},{4,21},{5,1},{6,2},{7,22},{8,12},{9,24},... | collective-permute-start | bytes 393224 | tf_op jit(solution)/shard_map/ppermute | solution.py:55
  9.8 4.4 %collective-permute-start.2 = (bf16[64,1024]{1,0:T(8,128)(2,1)S(1)}, bf16[64,1024]{1,0:T(8,128)(2,1)S(1)}, u32[]{:S(2)}, u32[]{:S(2)}) collective-permute-start(bf16[64,1024]{1,0:T(8,128)(2,1)S(1)} %get-tuple-element.34), channel_id=1, source_target_pairs={{0,9},{1,15},{2,12},{3,10},{4,13},{5,11},{6,8},{7,14},{8,6},{9,0},... | collective-permute-start | bytes 393224 | tf_op jit(solution)/shard_map/ppermute | solution.py:55
  10.1 4.4 %collective-permute-start.3 = (bf16[64,1024]{1,0:T(8,128)(2,1)S(1)}, bf16[64,1024]{1,0:T(8,128)(2,1)S(1)}, u32[]{:S(2)}, u32[]{:S(2)}) collective-permute-start(bf16[64,1024]{1,0:T(8,128)(2,1)S(1)} %get-tuple-element.35), channel_id=1, source_target_pairs={{0,24},{1,11},{2,8},{3,27},{4,28},{5,15},{6,12},{7,31},{8,2},{9,17... | collective-permute-start | bytes 393224 | tf_op jit(solution)/shard_map/ppermute | solution.py:55
  14.6 4.9 %collective-permute-start.4 = (bf16[16,1024]{1,0:T(8,128)(2,1)S(1)}, bf16[16,1024]{1,0:T(8,128)(2,1)S(1)}, u32[]{:S(2)}, u32[]{:S(2)}) collective-permute-start(bf16[16,1024]{1,0:T(8,128)(2,1)S(1)} %get-tuple-element.37), channel_id=1, source_target_pairs={{0,4},{1,16},{2,19},{3,7},{4,0},{5,20},{6,23},{7,3},{8,25},{9,13},... | collective-permute-start | bytes 98312 | tf_op jit(solution)/shard_map/ppermute | solution.py:55
  17.4 5.1 %collective-permute-start.5 = (bf16[16,1024]{1,0:T(8,128)(2,1)S(1)}, bf16[16,1024]{1,0:T(8,128)(2,1)S(1)}, u32[]{:S(2)}, u32[]{:S(2)}) collective-permute-start(bf16[16,1024]{1,0:T(8,128)(2,1)S(1)} %get-tuple-element.38), channel_id=1, source_target_pairs={{0,14},{1,8},{2,11},{3,13},{4,10},{5,12},{6,15},{7,9},{8,1},{9,7},... | collective-permute-start | bytes 98312 | tf_op jit(solution)/shard_map/ppermute | solution.py:55
  18.5 4.0 %collective-permute-start.6 = (bf16[16,1024]{1,0:T(8,128)(2,1)S(1)}, bf16[16,1024]{1,0:T(8,128)(2,1)S(1)}, u32[]{:S(2)}, u32[]{:S(2)}) collective-permute-start(bf16[16,1024]{1,0:T(8,128)(2,1)S(1)} %get-tuple-element.39), channel_id=1, source_target_pairs={{0,10},{1,25},{2,26},{3,9},{4,14},{5,29},{6,30},{7,13},{8,16},{9,3... | collective-permute-start | bytes 98312 | tf_op jit(solution)/shard_map/ppermute | solution.py:55
  22.6 5.0 %collective-permute-start.7 = (bf16[16,1024]{1,0:T(8,128)(2,1)S(1)}, bf16[16,1024]{1,0:T(8,128)(2,1)S(1)}, u32[]{:S(2)}, u32[]{:S(2)}) collective-permute-start(bf16[16,1024]{1,0:T(8,128)(2,1)S(1)} %get-tuple-element.42), channel_id=1, source_target_pairs={{0,17},{1,5},{2,6},{3,18},{4,21},{5,1},{6,2},{7,22},{8,12},{9,24},... | collective-permute-start | bytes 98312 | tf_op jit(solution)/shard_map/ppermute | solution.py:55
  24.2 3.7 %collective-permute-start.8 = (bf16[16,1024]{1,0:T(8,128)(2,1)S(1)}, bf16[16,1024]{1,0:T(8,128)(2,1)S(1)}, u32[]{:S(2)}, u32[]{:S(2)}) collective-permute-start(bf16[16,1024]{1,0:T(8,128)(2,1)S(1)} %get-tuple-element.43), channel_id=1, source_target_pairs={{0,9},{1,15},{2,12},{3,10},{4,13},{5,11},{6,8},{7,14},{8,6},{9,0},... | collective-permute-start | bytes 98312 | tf_op jit(solution)/shard_map/ppermute | solution.py:55
  25.0 3.3 %collective-permute-start.9 = (bf16[16,1024]{1,0:T(8,128)(2,1)S(1)}, bf16[16,1024]{1,0:T(8,128)(2,1)S(1)}, u32[]{:S(2)}, u32[]{:S(2)}) collective-permute-start(bf16[16,1024]{1,0:T(8,128)(2,1)S(1)} %get-tuple-element.41.own), channel_id=1, source_target_pairs={{0,24},{1,11},{2,8},{3,27},{4,28},{5,15},{6,12},{7,31},{8,2},{9,17... | collective-permute-start | bytes 98312 | tf_op jit(solution)/shard_map/ppermute | solution.py:55
  28.4 9.7 %collective-permute-start.11 = (bf16[64,1024]{1,0:T(8,128)(2,1)S(1)}, bf16[64,1024]{1,0:T(8,128)(2,1)S(1)}, u32[]{:S(2)}, u32[]{:S(2)}) collective-permute-start(bf16[64,1024]{1,0:T(8,128)(2,1)S(1)} %get-tuple-element.45), channel_id=1, source_target_pairs={{0,4},{1,16},{2,19},{3,7},{4,0},{5,20},{6,23},{7,3},{8,25},{9,13},... | collective-permute-start | bytes 393224 | tf_op jit(solution)/shard_map/ppermute | solution.py:55
  29.8 8.3 %collective-permute-start.13 = (bf16[64,1024]{1,0:T(8,128)(2,1)S(1)}, bf16[64,1024]{1,0:T(8,128)(2,1)S(1)}, u32[]{:S(2)}, u32[]{:S(2)}) collective-permute-start(bf16[64,1024]{1,0:T(8,128)(2,1)S(1)} %get-tuple-element.48), channel_id=1, source_target_pairs={{0,14},{1,8},{2,11},{3,13},{4,10},{5,12},{6,15},{7,9},{8,1},{9,7},... | collective-permute-start | bytes 393224 | tf_op jit(solution)/shard_map/ppermute | solution.py:55
  30.9 7.2 %collective-permute-start.14 = (bf16[64,1024]{1,0:T(8,128)(2,1)S(1)}, bf16[64,1024]{1,0:T(8,128)(2,1)S(1)}, u32[]{:S(2)}, u32[]{:S(2)}) collective-permute-start(bf16[64,1024]{1,0:T(8,128)(2,1)S(1)} %get-tuple-element.44.refs_0_), channel_id=1, source_target_pairs={{0,10},{1,25},{2,26},{3,9},{4,14},{5,29},{6,30},{7,13},{8,16},{9,3... | collective-permute-start | bytes 393224 | tf_op jit(solution)/shard_map/ppermute | solution.py:55
  31.7 6.4 %collective-permute-start.10 = (bf16[64,1024]{1,0:T(8,128)(2,1)S(1)}, bf16[64,1024]{1,0:T(8,128)(2,1)S(1)}, u32[]{:S(2)}, u32[]{:S(2)}) collective-permute-start(bf16[64,1024]{1,0:T(8,128)(2,1)S(1)} %get-tuple-element.44.refs_0_), channel_id=1, source_target_pairs={{0,8},{1,9},{2,10},{3,11},{4,12},{5,13},{6,14},{7,15},{8,0},{9,1},... | collective-permute-start | bytes 393224 | tf_op jit(solution)/shard_map/ppermute | solution.py:55
  34.3 3.8 %collective-permute-start.12 = (bf16[16,1024]{1,0:T(8,128)(2,1)S(1)}, bf16[16,1024]{1,0:T(8,128)(2,1)S(1)}, u32[]{:S(2)}, u32[]{:S(2)}) collective-permute-start(bf16[16,1024]{1,0:T(8,128)(2,1)S(1)} %get-tuple-element.46.refs_3_.grad), channel_id=1, source_target_pairs={{0,24},{1,25},{2,26},{3,27},{4,28},{5,29},{6,30},{7,31},{8,16},{9,... | collective-permute-start | bytes 98312 | tf_op jit(solution)/shard_map/ppermute | solution.py:55
  38.1 2.0 %collective-permute-start.15 = (bf16[224,1024]{1,0:T(8,128)(2,1)S(1)}, bf16[224,1024]{1,0:T(8,128)(2,1)S(1)}, u32[]{:S(2)}, u32[]{:S(2)}) collective-permute-start(bf16[224,1024]{1,0:T(8,128)(2,1)S(1)} %shard_map.84), channel_id=1, source_target_pairs={{0,8},{1,9},{2,10},{3,11},{4,12},{5,13},{6,14},{7,15},{8,0},{9,1},... | collective-permute-start | bytes 1376264 | tf_op jit(solution)/shard_map/ppermute | solution.py:55

commit v4 on v3

--- a/solution.py
+++ b/solution.py
@@ -10,6 +10,7 @@
 F32 = jnp.float32
 BF16 = jnp.bfloat16
 CHUNK = 512
+PARTS = 4
 LOAD_LIMIT = 48 * 1024 * 1024
 KEPT_LIMIT = 50 * 1024 * 1024
 
@@ -114,13 +115,20 @@
     return pl.ds(pl.multiple_of(index * size, size), size)
 
 
+def in_parts(source, out, sems, copies):
+    rows = out.shape[0] // PARTS
+    for i in range(PARTS):
+        at = pl.ds(i * rows, rows)
+        copies.append(pltpu.make_async_copy(source.at[at, :], out.at[at, :], sems.at[len(copies)]))
+        copies[-1].start()
+
+
 def load_kernel(cots_ref, away, first, sems):
     role = place()[0]
     copies = []
     for out, side in ((away, 1 - role), (first, role)):
         at = pl.ds(pl.multiple_of(side * away.shape[1], CHUNK), out.shape[1])
-        copies.append(pltpu.make_async_copy(cots_ref.at[:, at], out, sems.at[len(copies)]))
-        copies[-1].start()
+        in_parts(cots_ref.at[:, at], out, sems, copies)
     for copy in copies:
         copy.wait()
 
@@ -134,18 +142,19 @@
 
 def kept_kernel(turned, first, cots_ref, out, cots, sems):
     role = place()[0]
-    ready, count = first.shape[1] // CHUNK, out.shape[1] // CHUNK
+    skip, later = first.shape[1], cots.shape[1]
     copies = []
-    for i in range(ready, count):
-        source = cots_ref.at[:, block(role * count + i, CHUNK)]
-        copies.append(pltpu.make_async_copy(source, cots.at[i - ready], sems.at[i - ready]))
-        copies[-1].start()
-    for i in range(count):
+    at = pl.ds(pl.multiple_of(role * out.shape[1] + skip, CHUNK), later)
+    in_parts(cots_ref.at[:, at], cots, sems, copies)
+    for i in range(skip // CHUNK):
         at = slice(i * CHUNK, (i + 1) * CHUNK)
-        if i >= ready:
-            copies[i - ready].wait()
-        chunk = cots[i - ready] if i >= ready else first[:, at]
-        out[:, at] = jnp.dot(turned[...], chunk, preferred_element_type=F32)
+        out[:, at] = jnp.dot(turned[...], first[:, at], preferred_element_type=F32)
+    for copy in copies:
+        copy.wait()
+    for i in range(later // CHUNK):
+        at = slice(i * CHUNK, (i + 1) * CHUNK)
+        out[:, skip + i * CHUNK:skip + (i + 1) * CHUNK] = jnp.dot(
+            turned[...], cots[:, at], preferred_element_type=F32)
 
 
 def wide_kernel(rows, kept, came, own, *pieces):
@@ -239,8 +248,8 @@
     role, x, _, _, _ = place()
     side = role ^ sibling
     half_blocks(sibling, parts, half)
-    copies = [pltpu.make_async_copy(half, w_out.at[:, block(side, half.shape[1])], sems.at[0])]
-    copies[0].start()
+    copies = []
+    in_parts(half, w_out.at[:, block(side, half.shape[1])], sems, copies)
     for far, grad in enumerate(grads):
         at = block(2 * side + (x ^ far), grad.shape[1])
         new_m[far], new_v[far] = adamw_moments(m[:, at], v[:, at], grad[...].astype(F32))
@@ -281,19 +290,19 @@
     rest = lax.axis_size("shard") // 8
     wide_rows, narrow_rows = all_rows // 2, all_rows // 8
 
+    later = CHUNK
     away_cots, first = call(
-        load_kernel, [shape((tokens, half), BF16), shape((tokens, quarter), BF16)], out_cotangent,
-        far_in=(0,), scratch=[pltpu.SemaphoreType.DMA((2,))], limit=LOAD_LIMIT,
+        load_kernel, [shape((tokens, half), BF16), shape((tokens, half - later), BF16)], out_cotangent,
+        far_in=(0,), scratch=[pltpu.SemaphoreType.DMA((2 * PARTS,))], limit=LOAD_LIMIT,
     )
     away, turned = call(
         away_kernel, [shape((all_rows, half), BF16), shape((all_rows, tokens), BF16)], hidden_acts, away_cots,
     )
     came = to_sibling(away)
-    later = (half - quarter) // CHUNK
     kept = call(
         kept_kernel, [shape((all_rows, half), F32)], turned, first, out_cotangent,
         far_in=(2,), limit=KEPT_LIMIT,
-        scratch=[pltpu.VMEM((later, tokens, CHUNK), BF16), pltpu.SemaphoreType.DMA((later,))],
+        scratch=[pltpu.VMEM((tokens, later), BF16), pltpu.SemaphoreType.DMA((PARTS,))],
     )[0]
 
     def split(kernel, size, parts, *args):
@@ -324,7 +333,7 @@
     )[0])
     outs = [shape((all_rows, width), BF16), shape((rows, width), F32), shape((rows, width), F32)]
     scratch = [pltpu.VMEM((all_rows, half), BF16)] + [pltpu.VMEM((2, rows, quarter), F32)] * 2
-    scratch += [pltpu.SemaphoreType.DMA((5,))]
+    scratch += [pltpu.SemaphoreType.DMA((PARTS + 4,))]
     written = call(
         write_own_kernel, outs, first_moment, second_moment, grad, far_grad, parts[-1], *came,
         far_out=3, scratch=scratch,

time: 41.3 us -> 41.5 us (level)
  no operation moved by 1% of the time
where the time goes in v4:
time: 41.5 us; the launch traced here: 41.4 us
  starting transfers between devices  19.5 us (47%)
  waiting for transfers between devices  13.6 us (33%)
  Pallas kernels  7.49 us (18%)
  between operations  0.76 us (2%)
    ppermute x16, starting transfers between devices, exchange(): return lax.ppermute(value, ('rep', 'shard'), pairs)  19.5 us
    ppermute x16, waiting for transfers between devices, exchange(): return lax.ppermute(value, ('rep', 'shard'), pairs)  13.6 us
    pallas_call x11, Pallas kernels, call(): pl.pallas_call(kernel, out_shape=outs, in_specs=[far if i in tuple(far_in...  7.49 us
  transfers between devices with their start and end apart: 16, of which 10 were waited for; matrix products, arithmetic and copies ran while one was open for 0% of the time, Pallas kernels for 7%

profile of v4, /device:TPU:0, one launch (start us, length us, event | category | flops | bytes accessed | tf_op | source)
XLA Modules:
  0.0 41.4 jit_solution(4881102639932258224)
XLA Ops:
  0.6 2.7 %shard_map.76 = (bf16[768,2048]{1,0:T(8,128)(2,1)S(1)}, bf16[768,1536]{1,0:T(8,128)(2,1)S(1)}) custom-call(bf16[768,4096]{1,0:T(8,128)(2,1)} %cots_ref.3), custom_call_target="tpu_custom_call" | custom-call | tf_op jit(solution)/shard_map/pallas_call | solution.py:38
  3.3 0.6 %shard_map.77 = (bf16[128,2048]{1,0:T(8,128)(2,1)S(1)}, bf16[128,768]{1,0:T(8,128)(2,1)S(1)}) custom-call(bf16[768,128]{1,0:T(8,128)(2,1)S(1)} %copy-done.2, bf16[768,2048]{1,0:T(8,128)(2,1)S(1)} %get-tuple-element.28.cots), custom_call_target="tpu_custom_call" | custom-call | tf_op jit(solution)/shard_map/pallas_call | solution.py:38
  3.9 0.5 %collective-permute-start = (bf16[128,2048]{1,0:T(8,128)(2,1)S(1)}, bf16[128,2048]{1,0:T(8,128)(2,1)S(1)}, u32[]{:S(2)}, u32[]{:S(2)}) collective-permute-start(bf16[128,2048]{1,0:T(8,128)(2,1)S(1)} %get-tuple-element.31), channel_id=1, source_target_pairs={{0,8},{1,9},{2,10},{3,11},{4,12},{5,13},{6,14},{7,15},{8,0},{9,1},... | collective-permute-start | bytes 1572872 | tf_op jit(solution)/shard_map/ppermute | solution.py:56
  4.5 1.8 %shard_map.78.kept = f32[128,2048]{1,0:T(8,128)S(1)} custom-call(bf16[128,768]{1,0:T(8,128)(2,1)S(1)} %get-tuple-element.29.turned, bf16[768,1536]{1,0:T(8,128)(2,1)S(1)} %get-tuple-element.30.first, bf16[768,4096]{1,0:T(8,128)(2,1)} %cots_ref.3), custom_call_target="tpu_custom_call" | custom-call | tf_op jit(solution)/shard_map/pallas_call | solution.py:38
  6.4 3.5 %collective-permute-start.1 = (bf16[64,1024]{1,0:T(8,128)(2,1)S(1)}, bf16[64,1024]{1,0:T(8,128)(2,1)S(1)}, u32[]{:S(2)}, u32[]{:S(2)}) collective-permute-start(bf16[64,1024]{1,0:T(8,128)(2,1)S(1)} %get-tuple-element.33), channel_id=1, source_target_pairs={{0,17},{1,5},{2,6},{3,18},{4,21},{5,1},{6,2},{7,22},{8,12},{9,24},... | collective-permute-start | bytes 393224 | tf_op jit(solution)/shard_map/ppermute | solution.py:56
  10.3 2.6 %collective-permute-done.1.refs_0_ = bf16[64,1024]{1,0:T(8,128)(2,1)S(1)} collective-permute-done((bf16[64,1024]{1,0:T(8,128)(2,1)S(1)}, bf16[64,1024]{1,0:T(8,128)(2,1)S(1)}, u32[]{:S(2)}, u32[]{:S(2)}) %collective-permute-start.1) | collective-permute-done | bytes 131104 | tf_op jit(solution)/shard_map/ppermute | solution.py:56
  12.9 1.4 %collective-permute-done.2.refs_1_ = bf16[64,1024]{1,0:T(8,128)(2,1)S(1)} collective-permute-done((bf16[64,1024]{1,0:T(8,128)(2,1)S(1)}, bf16[64,1024]{1,0:T(8,128)(2,1)S(1)}, u32[]{:S(2)}, u32[]{:S(2)}) %collective-permute-start.2) | collective-permute-done | bytes 131104 | tf_op jit(solution)/shard_map/ppermute | solution.py:56
  14.7 2.8 %collective-permute-start.4 = (bf16[16,1024]{1,0:T(8,128)(2,1)S(1)}, bf16[16,1024]{1,0:T(8,128)(2,1)S(1)}, u32[]{:S(2)}, u32[]{:S(2)}) collective-permute-start(bf16[16,1024]{1,0:T(8,128)(2,1)S(1)} %get-tuple-element.37), channel_id=1, source_target_pairs={{0,4},{1,16},{2,19},{3,7},{4,0},{5,20},{6,23},{7,3},{8,25},{9,13},... | collective-permute-start | bytes 98312 | tf_op jit(solution)/shard_map/ppermute | solution.py:56
  17.5 1.2 %collective-permute-start.5 = (bf16[16,1024]{1,0:T(8,128)(2,1)S(1)}, bf16[16,1024]{1,0:T(8,128)(2,1)S(1)}, u32[]{:S(2)}, u32[]{:S(2)}) collective-permute-start(bf16[16,1024]{1,0:T(8,128)(2,1)S(1)} %get-tuple-element.38), channel_id=1, source_target_pairs={{0,14},{1,8},{2,11},{3,13},{4,10},{5,12},{6,15},{7,9},{8,1},{9,7},... | collective-permute-start | bytes 98312 | tf_op jit(solution)/shard_map/ppermute | solution.py:56
  18.9 0.7 %collective-permute-done.4.refs_0_ = bf16[16,1024]{1,0:T(8,128)(2,1)S(1)} collective-permute-done((bf16[16,1024]{1,0:T(8,128)(2,1)S(1)}, bf16[16,1024]{1,0:T(8,128)(2,1)S(1)}, u32[]{:S(2)}, u32[]{:S(2)}) %collective-permute-start.4) | collective-permute-done | bytes 32800 | tf_op jit(solution)/shard_map/ppermute | solution.py:56
  19.6 3.1 %collective-permute-done.5.refs_1_ = bf16[16,1024]{1,0:T(8,128)(2,1)S(1)} collective-permute-done((bf16[16,1024]{1,0:T(8,128)(2,1)S(1)}, bf16[16,1024]{1,0:T(8,128)(2,1)S(1)}, u32[]{:S(2)}, u32[]{:S(2)}) %collective-permute-start.5) | collective-permute-done | bytes 32800 | tf_op jit(solution)/shard_map/ppermute | solution.py:56
  22.8 1.5 %collective-permute-start.7 = (bf16[16,1024]{1,0:T(8,128)(2,1)S(1)}, bf16[16,1024]{1,0:T(8,128)(2,1)S(1)}, u32[]{:S(2)}, u32[]{:S(2)}) collective-permute-start(bf16[16,1024]{1,0:T(8,128)(2,1)S(1)} %get-tuple-element.42), channel_id=1, source_target_pairs={{0,17},{1,5},{2,6},{3,18},{4,21},{5,1},{6,2},{7,22},{8,12},{9,24},... | collective-permute-start | bytes 98312 | tf_op jit(solution)/shard_map/ppermute | solution.py:56
  24.3 0.8 %collective-permute-start.8 = (bf16[16,1024]{1,0:T(8,128)(2,1)S(1)}, bf16[16,1024]{1,0:T(8,128)(2,1)S(1)}, u32[]{:S(2)}, u32[]{:S(2)}) collective-permute-start(bf16[16,1024]{1,0:T(8,128)(2,1)S(1)} %get-tuple-element.43), channel_id=1, source_target_pairs={{0,9},{1,15},{2,12},{3,10},{4,13},{5,11},{6,8},{7,14},{8,6},{9,0},... | collective-permute-start | bytes 98312 | tf_op jit(solution)/shard_map/ppermute | solution.py:56
  25.2 0.9 %collective-permute-start.9 = (bf16[16,1024]{1,0:T(8,128)(2,1)S(1)}, bf16[16,1024]{1,0:T(8,128)(2,1)S(1)}, u32[]{:S(2)}, u32[]{:S(2)}) collective-permute-start(bf16[16,1024]{1,0:T(8,128)(2,1)S(1)} %get-tuple-element.41.own), channel_id=1, source_target_pairs={{0,24},{1,11},{2,8},{3,27},{4,28},{5,15},{6,12},{7,31},{8,2},{9,17... | collective-permute-start | bytes 98312 | tf_op jit(solution)/shard_map/ppermute | solution.py:56
  26.1 1.7 %collective-permute-done.7.refs_0_ = bf16[16,1024]{1,0:T(8,128)(2,1)S(1)} collective-permute-done((bf16[16,1024]{1,0:T(8,128)(2,1)S(1)}, bf16[16,1024]{1,0:T(8,128)(2,1)S(1)}, u32[]{:S(2)}, u32[]{:S(2)}) %collective-permute-start.7) | collective-permute-done | bytes 32800 | tf_op jit(solution)/shard_map/ppermute | solution.py:56
  28.5 1.4 %collective-permute-start.11 = (bf16[64,1024]{1,0:T(8,128)(2,1)S(1)}, bf16[64,1024]{1,0:T(8,128)(2,1)S(1)}, u32[]{:S(2)}, u32[]{:S(2)}) collective-permute-start(bf16[64,1024]{1,0:T(8,128)(2,1)S(1)} %get-tuple-element.45), channel_id=1, source_target_pairs={{0,4},{1,16},{2,19},{3,7},{4,0},{5,20},{6,23},{7,3},{8,25},{9,13},... | collective-permute-start | bytes 393224 | tf_op jit(solution)/shard_map/ppermute | solution.py:56
  29.9 1.2 %collective-permute-start.13 = (bf16[64,1024]{1,0:T(8,128)(2,1)S(1)}, bf16[64,1024]{1,0:T(8,128)(2,1)S(1)}, u32[]{:S(2)}, u32[]{:S(2)}) collective-permute-start(bf16[64,1024]{1,0:T(8,128)(2,1)S(1)} %get-tuple-element.48), channel_id=1, source_target_pairs={{0,14},{1,8},{2,11},{3,13},{4,10},{5,12},{6,15},{7,9},{8,1},{9,7},... | collective-permute-start | bytes 393224 | tf_op jit(solution)/shard_map/ppermute | solution.py:56
  31.1 0.7 %collective-permute-start.14 = (bf16[64,1024]{1,0:T(8,128)(2,1)S(1)}, bf16[64,1024]{1,0:T(8,128)(2,1)S(1)}, u32[]{:S(2)}, u32[]{:S(2)}) collective-permute-start(bf16[64,1024]{1,0:T(8,128)(2,1)S(1)} %get-tuple-element.44.refs_0_), channel_id=1, source_target_pairs={{0,10},{1,25},{2,26},{3,9},{4,14},{5,29},{6,30},{7,13},{8,16},{9,3... | collective-permute-start | bytes 393224 | tf_op jit(solution)/shard_map/ppermute | solution.py:56
  31.8 2.7 %collective-permute-start.10 = (bf16[64,1024]{1,0:T(8,128)(2,1)S(1)}, bf16[64,1024]{1,0:T(8,128)(2,1)S(1)}, u32[]{:S(2)}, u32[]{:S(2)}) collective-permute-start(bf16[64,1024]{1,0:T(8,128)(2,1)S(1)} %get-tuple-element.44.refs_0_), channel_id=1, source_target_pairs={{0,8},{1,9},{2,10},{3,11},{4,12},{5,13},{6,14},{7,15},{8,0},{9,1},... | collective-permute-start | bytes 393224 | tf_op jit(solution)/shard_map/ppermute | solution.py:56
  34.5 0.9 %collective-permute-start.12 = (bf16[16,1024]{1,0:T(8,128)(2,1)S(1)}, bf16[16,1024]{1,0:T(8,128)(2,1)S(1)}, u32[]{:S(2)}, u32[]{:S(2)}) collective-permute-start(bf16[16,1024]{1,0:T(8,128)(2,1)S(1)} %get-tuple-element.46.refs_3_.grad), channel_id=1, source_target_pairs={{0,24},{1,25},{2,26},{3,27},{4,28},{5,29},{6,30},{7,31},{8,16},{9,... | collective-permute-start | bytes 98312 | tf_op jit(solution)/shard_map/ppermute | solution.py:56
  35.4 2.7 %collective-permute-done.12.refs_4_.far_grad = bf16[16,1024]{1,0:T(8,128)(2,1)S(1)} collective-permute-done((bf16[16,1024]{1,0:T(8,128)(2,1)S(1)}, bf16[16,1024]{1,0:T(8,128)(2,1)S(1)}, u32[]{:S(2)}, u32[]{:S(2)}) %collective-permute-start.12) | collective-permute-done | bytes 32800 | tf_op jit(solution)/shard_map/ppermute | solution.py:56
  38.2 0.7 %collective-permute-start.15 = (bf16[224,1024]{1,0:T(8,128)(2,1)S(1)}, bf16[224,1024]{1,0:T(8,128)(2,1)S(1)}, u32[]{:S(2)}, u32[]{:S(2)}) collective-permute-start(bf16[224,1024]{1,0:T(8,128)(2,1)S(1)} %shard_map.84), channel_id=1, source_target_pairs={{0,8},{1,9},{2,10},{3,11},{4,12},{5,13},{6,14},{7,15},{8,0},{9,1},... | collective-permute-start | bytes 1376264 | tf_op jit(solution)/shard_map/ppermute | solution.py:56
  38.9 1.0 %shard_map.85 = (bf16[128,4096]{1,0:T(8,128)(2,1)}, f32[16,4096]{1,0:T(8,128)}, f32[16,4096]{1,0:T(8,128)}) custom-call(f32[16,4096]{1,0:T(8,128)S(1)} %copy-done, f32[16,4096]{1,0:T(8,128)S(1)} %copy-done.1, bf16[16,1024]{1,0:T(8,128)(2,1)S(1)} %get-tuple-element.46.refs_3_.grad, bf16[16,1024]{1,0:T(8,128)(2,1)S(1)} %collective-permute-done.12.refs_4_.far_grad, ...), custom_call_target="tpu_custom_call" | custom-call | tf_op jit(solution)/shard_map/pallas_call | solution.py:38
  40.4 1.0 %shard_map.86 = (bf16[128,4096]{1,0:T(8,128)(2,1)}, f32[16,4096]{1,0:T(8,128)}, f32[16,4096]{1,0:T(8,128)}) custom-call(f32[16,4096]{1,0:T(8,128)S(1)} %copy-done, f32[16,4096]{1,0:T(8,128)S(1)} %copy-done.1, bf16[64,1024]{1,0:T(8,128)(2,1)S(1)} %collective-permute-done.10.refs_5_.own, ...), custom_call_target="tpu_custom_call", output_to_operand_aliasing={{0}: (4, {}), {1}: (5, {}), {2}: (6, {})} | custom-call | tf_op jit(solution)/shard_map/pallas_call | solution.py:38
  (27 shorter events, 2.4 us)
Async XLA Ops:
  0.6 2.7 %copy-start.2 = (bf16[768,128]{1,0:T(8,128)(2,1)S(1)}, bf16[768,128]{1,0:T(8,128)(2,1)}, u32[]{:S(2)}) copy-start(bf16[768,128]{1,0:T(8,128)(2,1)} %acts.1) | copy-start | bytes 589828
  3.9 2.4 %collective-permute-start = (bf16[128,2048]{1,0:T(8,128)(2,1)S(1)}, bf16[128,2048]{1,0:T(8,128)(2,1)S(1)}, u32[]{:S(2)}, u32[]{:S(2)}) collective-permute-start(bf16[128,2048]{1,0:T(8,128)(2,1)S(1)} %get-tuple-element.31), channel_id=1, source_target_pairs={{0,8},{1,9},{2,10},{3,11},{4,12},{5,13},{6,14},{7,15},{8,0},{9,1},... | collective-permute-start | bytes 1572872 | tf_op jit(solution)/shard_map/ppermute | solution.py:56
  4.5 18.2 %copy-start = (f32[16,4096]{1,0:T(8,128)S(1)}, f32[16,4096]{1,0:T(8,128)}, u32[]{:S(2)}) copy-start(f32[16,4096]{1,0:T(8,128)} %m.5) | copy-start | bytes 786436
  4.5 18.2 %copy-start.1 = (f32[16,4096]{1,0:T(8,128)S(1)}, f32[16,4096]{1,0:T(8,128)}, u32[]{:S(2)}) copy-start(f32[16,4096]{1,0:T(8,128)} %v.5) | copy-start | bytes 786436
  4.5 18.2 %copy-start.3 = (bf16[16,4096]{1,0:T(8,128)(2,1)S(1)}, bf16[16,4096]{1,0:T(8,128)(2,1)}, u32[]{:S(2)}) copy-start(bf16[16,4096]{1,0:T(8,128)(2,1)} %w.1) | copy-start | bytes 393220
  6.4 6.5 %collective-permute-start.1 = (bf16[64,1024]{1,0:T(8,128)(2,1)S(1)}, bf16[64,1024]{1,0:T(8,128)(2,1)S(1)}, u32[]{:S(2)}, u32[]{:S(2)}) collective-permute-start(bf16[64,1024]{1,0:T(8,128)(2,1)S(1)} %get-tuple-element.33), channel_id=1, source_target_pairs={{0,17},{1,5},{2,6},{3,18},{4,21},{5,1},{6,2},{7,22},{8,12},{9,24},... | collective-permute-start | bytes 393224 | tf_op jit(solution)/shard_map/ppermute | solution.py:56
  10.0 4.4 %collective-permute-start.2 = (bf16[64,1024]{1,0:T(8,128)(2,1)S(1)}, bf16[64,1024]{1,0:T(8,128)(2,1)S(1)}, u32[]{:S(2)}, u32[]{:S(2)}) collective-permute-start(bf16[64,1024]{1,0:T(8,128)(2,1)S(1)} %get-tuple-element.34), channel_id=1, source_target_pairs={{0,9},{1,15},{2,12},{3,10},{4,13},{5,11},{6,8},{7,14},{8,6},{9,0},... | collective-permute-start | bytes 393224 | tf_op jit(solution)/shard_map/ppermute | solution.py:56
  10.3 4.4 %collective-permute-start.3 = (bf16[64,1024]{1,0:T(8,128)(2,1)S(1)}, bf16[64,1024]{1,0:T(8,128)(2,1)S(1)}, u32[]{:S(2)}, u32[]{:S(2)}) collective-permute-start(bf16[64,1024]{1,0:T(8,128)(2,1)S(1)} %get-tuple-element.35), channel_id=1, source_target_pairs={{0,24},{1,11},{2,8},{3,27},{4,28},{5,15},{6,12},{7,31},{8,2},{9,17... | collective-permute-start | bytes 393224 | tf_op jit(solution)/shard_map/ppermute | solution.py:56
  14.7 4.9 %collective-permute-start.4 = (bf16[16,1024]{1,0:T(8,128)(2,1)S(1)}, bf16[16,1024]{1,0:T(8,128)(2,1)S(1)}, u32[]{:S(2)}, u32[]{:S(2)}) collective-permute-start(bf16[16,1024]{1,0:T(8,128)(2,1)S(1)} %get-tuple-element.37), channel_id=1, source_target_pairs={{0,4},{1,16},{2,19},{3,7},{4,0},{5,20},{6,23},{7,3},{8,25},{9,13},... | collective-permute-start | bytes 98312 | tf_op jit(solution)/shard_map/ppermute | solution.py:56
  17.5 5.1 %collective-permute-start.5 = (bf16[16,1024]{1,0:T(8,128)(2,1)S(1)}, bf16[16,1024]{1,0:T(8,128)(2,1)S(1)}, u32[]{:S(2)}, u32[]{:S(2)}) collective-permute-start(bf16[16,1024]{1,0:T(8,128)(2,1)S(1)} %get-tuple-element.38), channel_id=1, source_target_pairs={{0,14},{1,8},{2,11},{3,13},{4,10},{5,12},{6,15},{7,9},{8,1},{9,7},... | collective-permute-start | bytes 98312 | tf_op jit(solution)/shard_map/ppermute | solution.py:56
  18.7 4.0 %collective-permute-start.6 = (bf16[16,1024]{1,0:T(8,128)(2,1)S(1)}, bf16[16,1024]{1,0:T(8,128)(2,1)S(1)}, u32[]{:S(2)}, u32[]{:S(2)}) collective-permute-start(bf16[16,1024]{1,0:T(8,128)(2,1)S(1)} %get-tuple-element.39), channel_id=1, source_target_pairs={{0,10},{1,25},{2,26},{3,9},{4,14},{5,29},{6,30},{7,13},{8,16},{9,3... | collective-permute-start | bytes 98312 | tf_op jit(solution)/shard_map/ppermute | solution.py:56
  22.8 5.0 %collective-permute-start.7 = (bf16[16,1024]{1,0:T(8,128)(2,1)S(1)}, bf16[16,1024]{1,0:T(8,128)(2,1)S(1)}, u32[]{:S(2)}, u32[]{:S(2)}) collective-permute-start(bf16[16,1024]{1,0:T(8,128)(2,1)S(1)} %get-tuple-element.42), channel_id=1, source_target_pairs={{0,17},{1,5},{2,6},{3,18},{4,21},{5,1},{6,2},{7,22},{8,12},{9,24},... | collective-permute-start | bytes 98312 | tf_op jit(solution)/shard_map/ppermute | solution.py:56
  24.3 3.7 %collective-permute-start.8 = (bf16[16,1024]{1,0:T(8,128)(2,1)S(1)}, bf16[16,1024]{1,0:T(8,128)(2,1)S(1)}, u32[]{:S(2)}, u32[]{:S(2)}) collective-permute-start(bf16[16,1024]{1,0:T(8,128)(2,1)S(1)} %get-tuple-element.43), channel_id=1, source_target_pairs={{0,9},{1,15},{2,12},{3,10},{4,13},{5,11},{6,8},{7,14},{8,6},{9,0},... | collective-permute-start | bytes 98312 | tf_op jit(solution)/shard_map/ppermute | solution.py:56
  25.2 3.3 %collective-permute-start.9 = (bf16[16,1024]{1,0:T(8,128)(2,1)S(1)}, bf16[16,1024]{1,0:T(8,128)(2,1)S(1)}, u32[]{:S(2)}, u32[]{:S(2)}) collective-permute-start(bf16[16,1024]{1,0:T(8,128)(2,1)S(1)} %get-tuple-element.41.own), channel_id=1, source_target_pairs={{0,24},{1,11},{2,8},{3,27},{4,28},{5,15},{6,12},{7,31},{8,2},{9,17... | collective-permute-start | bytes 98312 | tf_op jit(solution)/shard_map/ppermute | solution.py:56
  28.5 9.6 %collective-permute-start.11 = (bf16[64,1024]{1,0:T(8,128)(2,1)S(1)}, bf16[64,1024]{1,0:T(8,128)(2,1)S(1)}, u32[]{:S(2)}, u32[]{:S(2)}) collective-permute-start(bf16[64,1024]{1,0:T(8,128)(2,1)S(1)} %get-tuple-element.45), channel_id=1, source_target_pairs={{0,4},{1,16},{2,19},{3,7},{4,0},{5,20},{6,23},{7,3},{8,25},{9,13},... | collective-permute-start | bytes 393224 | tf_op jit(solution)/shard_map/ppermute | solution.py:56
  29.9 8.2 %collective-permute-start.13 = (bf16[64,1024]{1,0:T(8,128)(2,1)S(1)}, bf16[64,1024]{1,0:T(8,128)(2,1)S(1)}, u32[]{:S(2)}, u32[]{:S(2)}) collective-permute-start(bf16[64,1024]{1,0:T(8,128)(2,1)S(1)} %get-tuple-element.48), channel_id=1, source_target_pairs={{0,14},{1,8},{2,11},{3,13},{4,10},{5,12},{6,15},{7,9},{8,1},{9,7},... | collective-permute-start | bytes 393224 | tf_op jit(solution)/shard_map/ppermute | solution.py:56
  31.1 7.0 %collective-permute-start.14 = (bf16[64,1024]{1,0:T(8,128)(2,1)S(1)}, bf16[64,1024]{1,0:T(8,128)(2,1)S(1)}, u32[]{:S(2)}, u32[]{:S(2)}) collective-permute-start(bf16[64,1024]{1,0:T(8,128)(2,1)S(1)} %get-tuple-element.44.refs_0_), channel_id=1, source_target_pairs={{0,10},{1,25},{2,26},{3,9},{4,14},{5,29},{6,30},{7,13},{8,16},{9,3... | collective-permute-start | bytes 393224 | tf_op jit(solution)/shard_map/ppermute | solution.py:56
  31.8 6.3 %collective-permute-start.10 = (bf16[64,1024]{1,0:T(8,128)(2,1)S(1)}, bf16[64,1024]{1,0:T(8,128)(2,1)S(1)}, u32[]{:S(2)}, u32[]{:S(2)}) collective-permute-start(bf16[64,1024]{1,0:T(8,128)(2,1)S(1)} %get-tuple-element.44.refs_0_), channel_id=1, source_target_pairs={{0,8},{1,9},{2,10},{3,11},{4,12},{5,13},{6,14},{7,15},{8,0},{9,1},... | collective-permute-start | bytes 393224 | tf_op jit(solution)/shard_map/ppermute | solution.py:56
  34.5 3.6 %collective-permute-start.12 = (bf16[16,1024]{1,0:T(8,128)(2,1)S(1)}, bf16[16,1024]{1,0:T(8,128)(2,1)S(1)}, u32[]{:S(2)}, u32[]{:S(2)}) collective-permute-start(bf16[16,1024]{1,0:T(8,128)(2,1)S(1)} %get-tuple-element.46.refs_3_.grad), channel_id=1, source_target_pairs={{0,24},{1,25},{2,26},{3,27},{4,28},{5,29},{6,30},{7,31},{8,16},{9,... | collective-permute-start | bytes 98312 | tf_op jit(solution)/shard_map/ppermute | solution.py:56
  38.2 2.2 %collective-permute-start.15 = (bf16[224,1024]{1,0:T(8,128)(2,1)S(1)}, bf16[224,1024]{1,0:T(8,128)(2,1)S(1)}, u32[]{:S(2)}, u32[]{:S(2)}) collective-permute-start(bf16[224,1024]{1,0:T(8,128)(2,1)S(1)} %shard_map.84), channel_id=1, source_target_pairs={{0,8},{1,9},{2,10},{3,11},{4,12},{5,13},{6,14},{7,15},{8,0},{9,1},... | collective-permute-start | bytes 1376264 | tf_op jit(solution)/shard_map/ppermute | solution.py:56

commit v5 on v3

--- a/solution.py
+++ b/solution.py
@@ -60,8 +60,8 @@
 
 
 SQUARE = ((1, 1), (1, 0), (0, 1))
-LINE = (2, 3, 1)
-STEPS = tuple(zip(SQUARE, LINE))
+STEPS = tuple(zip(SQUARE, (2, 3, 1)))
+BACK_STEPS = tuple(zip(SQUARE, (3, 2, 1)))
 STAY = ((0, 0), 0)
 
 
@@ -215,7 +215,7 @@
 
 def narrow_back_kernel(own, *refs):
     parts, outs = (own,) + refs[:-len(STEPS)], refs[-len(STEPS):]
-    for step, ref in zip((STAY,) + STEPS, parts):
+    for step, ref in zip((STAY,) + BACK_STEPS, parts):
         put(outs, block(group_of(step, 1), own.shape[0]), ref[...])
 
 
@@ -225,7 +225,7 @@
     size, quarter = parts[0].shape
     rows = out.shape[0] // lax.axis_size("shard")
     count = size // (4 * rows)
-    for ((dy, dx), k), ref in zip((STAY,) + STEPS, parts):
+    for ((dy, dx), k), ref in zip((STAY,) + BACK_STEPS, parts):
         for group in range(4):
             to_y = jnp.where(square, y ^ dy, group >> 1)
             to_x = jnp.where(square, x ^ dx, group & 1)
@@ -282,14 +282,14 @@
     wide_rows, narrow_rows = all_rows // 2, all_rows // 8
 
     away_cots, first = call(
-        load_kernel, [shape((tokens, half), BF16), shape((tokens, quarter), BF16)], out_cotangent,
+        load_kernel, [shape((tokens, half), BF16), shape((tokens, CHUNK), BF16)], out_cotangent,
         far_in=(0,), scratch=[pltpu.SemaphoreType.DMA((2,))], limit=LOAD_LIMIT,
     )
     away, turned = call(
         away_kernel, [shape((all_rows, half), BF16), shape((all_rows, tokens), BF16)], hidden_acts, away_cots,
     )
     came = to_sibling(away)
-    later = (half - quarter) // CHUNK
+    later = half // CHUNK - 1
     kept = call(
         kept_kernel, [shape((all_rows, half), F32)], turned, first, out_cotangent,
         far_in=(2,), limit=KEPT_LIMIT,
@@ -313,9 +313,9 @@
 
     pieces = [along_rest(new_w, k) for k in range(1, rest)]
     parts = call(rest_back_kernel, [shape((narrow_rows, quarter), BF16)] * len(STEPS), new_w, *pieces)
-    came = [stage(part, step, 0) for step, part in zip(STEPS, parts)]
+    came = [stage(part, step, 0) for step, part in zip(BACK_STEPS, parts)]
     parts = call(narrow_back_kernel, [shape((wide_rows, quarter), BF16)] * len(STEPS), parts[-1], *came)
-    came = [stage(part, step, 1) for step, part in zip(STEPS, parts)]
+    came = [stage(part, step, 1) for step, part in zip(BACK_STEPS, parts)]
     far_grad, own = along_x(grad), to_sibling(parts[-1])
     came[0], far_grad = lax.optimization_barrier((came[0], far_grad))
 

time: 41.3 us -> 42.6 us (1.031)
  starting transfers between devices: 19.3 us -> 20.5 us
    ppermute x16, starting transfers between devices: 19.3 us -> 20.5 us  [exchange(): return lax.ppermute(value, ('rep', 'shard'), pairs)]
where the time goes in v5:
time: 42.6 us; the launch traced here: 42.4 us
  starting transfers between devices  20.5 us (48%)
  waiting for transfers between devices  14 us (33%)
  Pallas kernels  7.16 us (17%)
  between operations  0.78 us (2%)
    ppermute x16, starting transfers between devices, exchange(): return lax.ppermute(value, ('rep', 'shard'), pairs)  20.5 us
    ppermute x16, waiting for transfers between devices, exchange(): return lax.ppermute(value, ('rep', 'shard'), pairs)  14 us
    pallas_call x11, Pallas kernels, call(): pl.pallas_call(kernel, out_shape=outs, in_specs=[far if i in tuple(far_in...  7.16 us
  transfers between devices with their start and end apart: 16, of which 10 were waited for; matrix products, arithmetic and copies ran while one was open for 0% of the time, Pallas kernels for 7%

profile of v5, /device:TPU:0, one launch (start us, length us, event | category | flops | bytes accessed | tf_op | source)
XLA Modules:
  0.0 42.4 jit_solution(14407932864003190862)
XLA Ops:
  0.6 2.1 %shard_map.76 = (bf16[768,2048]{1,0:T(8,128)(2,1)S(1)}, bf16[768,512]{1,0:T(8,128)(2,1)S(1)}) custom-call(bf16[768,4096]{1,0:T(8,128)(2,1)} %cots_ref.3), custom_call_target="tpu_custom_call" | custom-call | tf_op jit(solution)/shard_map/pallas_call | solution.py:37
  2.8 0.6 %shard_map.77 = (bf16[128,2048]{1,0:T(8,128)(2,1)S(1)}, bf16[128,768]{1,0:T(8,128)(2,1)S(1)}) custom-call(bf16[768,128]{1,0:T(8,128)(2,1)S(1)} %copy-done.2, bf16[768,2048]{1,0:T(8,128)(2,1)S(1)} %get-tuple-element.28.cots), custom_call_target="tpu_custom_call" | custom-call | tf_op jit(solution)/shard_map/pallas_call | solution.py:37
  3.5 0.5 %collective-permute-start = (bf16[128,2048]{1,0:T(8,128)(2,1)S(1)}, bf16[128,2048]{1,0:T(8,128)(2,1)S(1)}, u32[]{:S(2)}, u32[]{:S(2)}) collective-permute-start(bf16[128,2048]{1,0:T(8,128)(2,1)S(1)} %get-tuple-element.31), channel_id=1, source_target_pairs={{0,8},{1,9},{2,10},{3,11},{4,12},{5,13},{6,14},{7,15},{8,0},{9,1},... | collective-permute-start | bytes 1572872 | tf_op jit(solution)/shard_map/ppermute | solution.py:55
  4.0 2.1 %shard_map.78.kept = f32[128,2048]{1,0:T(8,128)S(1)} custom-call(bf16[128,768]{1,0:T(8,128)(2,1)S(1)} %get-tuple-element.29.turned, bf16[768,512]{1,0:T(8,128)(2,1)S(1)} %get-tuple-element.30.first, bf16[768,4096]{1,0:T(8,128)(2,1)} %cots_ref.3), custom_call_target="tpu_custom_call" | custom-call | tf_op jit(solution)/shard_map/pallas_call | solution.py:37
  6.2 3.5 %collective-permute-start.1 = (bf16[64,1024]{1,0:T(8,128)(2,1)S(1)}, bf16[64,1024]{1,0:T(8,128)(2,1)S(1)}, u32[]{:S(2)}, u32[]{:S(2)}) collective-permute-start(bf16[64,1024]{1,0:T(8,128)(2,1)S(1)} %get-tuple-element.33), channel_id=1, source_target_pairs={{0,17},{1,5},{2,6},{3,18},{4,21},{5,1},{6,2},{7,22},{8,12},{9,24},... | collective-permute-start | bytes 393224 | tf_op jit(solution)/shard_map/ppermute | solution.py:55
  10.1 2.6 %collective-permute-done.1.refs_0_ = bf16[64,1024]{1,0:T(8,128)(2,1)S(1)} collective-permute-done((bf16[64,1024]{1,0:T(8,128)(2,1)S(1)}, bf16[64,1024]{1,0:T(8,128)(2,1)S(1)}, u32[]{:S(2)}, u32[]{:S(2)}) %collective-permute-start.1) | collective-permute-done | bytes 131104 | tf_op jit(solution)/shard_map/ppermute | solution.py:55
  12.7 1.4 %collective-permute-done.2.refs_1_ = bf16[64,1024]{1,0:T(8,128)(2,1)S(1)} collective-permute-done((bf16[64,1024]{1,0:T(8,128)(2,1)S(1)}, bf16[64,1024]{1,0:T(8,128)(2,1)S(1)}, u32[]{:S(2)}, u32[]{:S(2)}) %collective-permute-start.2) | collective-permute-done | bytes 131104 | tf_op jit(solution)/shard_map/ppermute | solution.py:55
  14.5 2.8 %collective-permute-start.4 = (bf16[16,1024]{1,0:T(8,128)(2,1)S(1)}, bf16[16,1024]{1,0:T(8,128)(2,1)S(1)}, u32[]{:S(2)}, u32[]{:S(2)}) collective-permute-start(bf16[16,1024]{1,0:T(8,128)(2,1)S(1)} %get-tuple-element.37), channel_id=1, source_target_pairs={{0,4},{1,16},{2,19},{3,7},{4,0},{5,20},{6,23},{7,3},{8,25},{9,13},... | collective-permute-start | bytes 98312 | tf_op jit(solution)/shard_map/ppermute | solution.py:55
  17.3 1.2 %collective-permute-start.5 = (bf16[16,1024]{1,0:T(8,128)(2,1)S(1)}, bf16[16,1024]{1,0:T(8,128)(2,1)S(1)}, u32[]{:S(2)}, u32[]{:S(2)}) collective-permute-start(bf16[16,1024]{1,0:T(8,128)(2,1)S(1)} %get-tuple-element.38), channel_id=1, source_target_pairs={{0,14},{1,8},{2,11},{3,13},{4,10},{5,12},{6,15},{7,9},{8,1},{9,7},... | collective-permute-start | bytes 98312 | tf_op jit(solution)/shard_map/ppermute | solution.py:55
  18.6 0.7 %collective-permute-done.4.refs_0_ = bf16[16,1024]{1,0:T(8,128)(2,1)S(1)} collective-permute-done((bf16[16,1024]{1,0:T(8,128)(2,1)S(1)}, bf16[16,1024]{1,0:T(8,128)(2,1)S(1)}, u32[]{:S(2)}, u32[]{:S(2)}) %collective-permute-start.4) | collective-permute-done | bytes 32800 | tf_op jit(solution)/shard_map/ppermute | solution.py:55
  19.4 3.0 %collective-permute-done.5.refs_1_ = bf16[16,1024]{1,0:T(8,128)(2,1)S(1)} collective-permute-done((bf16[16,1024]{1,0:T(8,128)(2,1)S(1)}, bf16[16,1024]{1,0:T(8,128)(2,1)S(1)}, u32[]{:S(2)}, u32[]{:S(2)}) %collective-permute-start.5) | collective-permute-done | bytes 32800 | tf_op jit(solution)/shard_map/ppermute | solution.py:55
  22.5 1.5 %collective-permute-start.7 = (bf16[16,1024]{1,0:T(8,128)(2,1)S(1)}, bf16[16,1024]{1,0:T(8,128)(2,1)S(1)}, u32[]{:S(2)}, u32[]{:S(2)}) collective-permute-start(bf16[16,1024]{1,0:T(8,128)(2,1)S(1)} %get-tuple-element.42), channel_id=1, source_target_pairs={{0,17},{1,15},{2,12},{3,18},{4,21},{5,11},{6,8},{7,22},{8,6},{9,24... | collective-permute-start | bytes 98312 | tf_op jit(solution)/shard_map/ppermute | solution.py:55
  24.0 0.8 %collective-permute-start.8 = (bf16[16,1024]{1,0:T(8,128)(2,1)S(1)}, bf16[16,1024]{1,0:T(8,128)(2,1)S(1)}, u32[]{:S(2)}, u32[]{:S(2)}) collective-permute-start(bf16[16,1024]{1,0:T(8,128)(2,1)S(1)} %get-tuple-element.43), channel_id=1, source_target_pairs={{0,9},{1,5},{2,6},{3,10},{4,13},{5,1},{6,2},{7,14},{8,12},{9,0},{1... | collective-permute-start | bytes 98312 | tf_op jit(solution)/shard_map/ppermute | solution.py:55
  24.9 0.9 %collective-permute-start.9 = (bf16[16,1024]{1,0:T(8,128)(2,1)S(1)}, bf16[16,1024]{1,0:T(8,128)(2,1)S(1)}, u32[]{:S(2)}, u32[]{:S(2)}) collective-permute-start(bf16[16,1024]{1,0:T(8,128)(2,1)S(1)} %get-tuple-element.41.own), channel_id=1, source_target_pairs={{0,24},{1,11},{2,8},{3,27},{4,28},{5,15},{6,12},{7,31},{8,2},{9,17... | collective-permute-start | bytes 98312 | tf_op jit(solution)/shard_map/ppermute | solution.py:55
  25.8 1.7 %collective-permute-done.7.refs_0_ = bf16[16,1024]{1,0:T(8,128)(2,1)S(1)} collective-permute-done((bf16[16,1024]{1,0:T(8,128)(2,1)S(1)}, bf16[16,1024]{1,0:T(8,128)(2,1)S(1)}, u32[]{:S(2)}, u32[]{:S(2)}) %collective-permute-start.7) | collective-permute-done | bytes 32800 | tf_op jit(solution)/shard_map/ppermute | solution.py:55
  27.7 0.5 %collective-permute-done.9.refs_2_ = bf16[16,1024]{1,0:T(8,128)(2,1)S(1)} collective-permute-done((bf16[16,1024]{1,0:T(8,128)(2,1)S(1)}, bf16[16,1024]{1,0:T(8,128)(2,1)S(1)}, u32[]{:S(2)}, u32[]{:S(2)}) %collective-permute-start.9) | collective-permute-done | bytes 32800 | tf_op jit(solution)/shard_map/ppermute | solution.py:55
  28.3 2.5 %collective-permute-start.11 = (bf16[64,1024]{1,0:T(8,128)(2,1)S(1)}, bf16[64,1024]{1,0:T(8,128)(2,1)S(1)}, u32[]{:S(2)}, u32[]{:S(2)}) collective-permute-start(bf16[64,1024]{1,0:T(8,128)(2,1)S(1)} %get-tuple-element.45), channel_id=1, source_target_pairs={{0,14},{1,16},{2,19},{3,13},{4,10},{5,20},{6,23},{7,9},{8,25},{9,7... | collective-permute-start | bytes 393224 | tf_op jit(solution)/shard_map/ppermute | solution.py:55
  30.7 1.4 %collective-permute-start.14 = (bf16[64,1024]{1,0:T(8,128)(2,1)S(1)}, bf16[64,1024]{1,0:T(8,128)(2,1)S(1)}, u32[]{:S(2)}, u32[]{:S(2)}) collective-permute-start(bf16[64,1024]{1,0:T(8,128)(2,1)S(1)} %get-tuple-element.44.refs_0_), channel_id=1, source_target_pairs={{0,10},{1,25},{2,26},{3,9},{4,14},{5,29},{6,30},{7,13},{8,16},{9,3... | collective-permute-start | bytes 393224 | tf_op jit(solution)/shard_map/ppermute | solution.py:55
  32.2 2.9 %collective-permute-start.10 = (bf16[64,1024]{1,0:T(8,128)(2,1)S(1)}, bf16[64,1024]{1,0:T(8,128)(2,1)S(1)}, u32[]{:S(2)}, u32[]{:S(2)}) collective-permute-start(bf16[64,1024]{1,0:T(8,128)(2,1)S(1)} %get-tuple-element.44.refs_0_), channel_id=1, source_target_pairs={{0,8},{1,9},{2,10},{3,11},{4,12},{5,13},{6,14},{7,15},{8,0},{9,1},... | collective-permute-start | bytes 393224 | tf_op jit(solution)/shard_map/ppermute | solution.py:55
  35.1 0.7 %collective-permute-start.12 = (bf16[16,1024]{1,0:T(8,128)(2,1)S(1)}, bf16[16,1024]{1,0:T(8,128)(2,1)S(1)}, u32[]{:S(2)}, u32[]{:S(2)}) collective-permute-start(bf16[16,1024]{1,0:T(8,128)(2,1)S(1)} %get-tuple-element.46.refs_3_.grad), channel_id=1, source_target_pairs={{0,24},{1,25},{2,26},{3,27},{4,28},{5,29},{6,30},{7,31},{8,16},{9,... | collective-permute-start | bytes 98312 | tf_op jit(solution)/shard_map/ppermute | solution.py:55
  35.8 3.0 %collective-permute-done.12.refs_4_.far_grad = bf16[16,1024]{1,0:T(8,128)(2,1)S(1)} collective-permute-done((bf16[16,1024]{1,0:T(8,128)(2,1)S(1)}, bf16[16,1024]{1,0:T(8,128)(2,1)S(1)}, u32[]{:S(2)}, u32[]{:S(2)}) %collective-permute-start.12) | collective-permute-done | bytes 32800 | tf_op jit(solution)/shard_map/ppermute | solution.py:55
  38.9 1.1 %collective-permute-start.15 = (bf16[224,1024]{1,0:T(8,128)(2,1)S(1)}, bf16[224,1024]{1,0:T(8,128)(2,1)S(1)}, u32[]{:S(2)}, u32[]{:S(2)}) collective-permute-start(bf16[224,1024]{1,0:T(8,128)(2,1)S(1)} %shard_map.84), channel_id=1, source_target_pairs={{0,8},{1,9},{2,10},{3,11},{4,12},{5,13},{6,14},{7,15},{8,0},{9,1},... | collective-permute-start | bytes 1376264 | tf_op jit(solution)/shard_map/ppermute | solution.py:55
  40.0 1.0 %shard_map.85 = (bf16[128,4096]{1,0:T(8,128)(2,1)}, f32[16,4096]{1,0:T(8,128)}, f32[16,4096]{1,0:T(8,128)}) custom-call(f32[16,4096]{1,0:T(8,128)S(1)} %copy-done, f32[16,4096]{1,0:T(8,128)S(1)} %copy-done.1, bf16[16,1024]{1,0:T(8,128)(2,1)S(1)} %get-tuple-element.46.refs_3_.grad, bf16[16,1024]{1,0:T(8,128)(2,1)S(1)} %collective-permute-done.12.refs_4_.far_grad, ...), custom_call_target="tpu_custom_call" | custom-call | tf_op jit(solution)/shard_map/pallas_call | solution.py:37
  41.4 1.0 %shard_map.86 = (bf16[128,4096]{1,0:T(8,128)(2,1)}, f32[16,4096]{1,0:T(8,128)}, f32[16,4096]{1,0:T(8,128)}) custom-call(f32[16,4096]{1,0:T(8,128)S(1)} %copy-done, f32[16,4096]{1,0:T(8,128)S(1)} %copy-done.1, bf16[64,1024]{1,0:T(8,128)(2,1)S(1)} %collective-permute-done.10.refs_5_.own, ...), custom_call_target="tpu_custom_call", output_to_operand_aliasing={{0}: (4, {}), {1}: (5, {}), {2}: (6, {})} | custom-call | tf_op jit(solution)/shard_map/pallas_call | solution.py:37
  (27 shorter events, 1.9 us)
Async XLA Ops:
  0.6 2.2 %copy-start.2 = (bf16[768,128]{1,0:T(8,128)(2,1)S(1)}, bf16[768,128]{1,0:T(8,128)(2,1)}, u32[]{:S(2)}) copy-start(bf16[768,128]{1,0:T(8,128)(2,1)} %acts.1) | copy-start | bytes 589828
  2.8 19.6 %copy-start = (f32[16,4096]{1,0:T(8,128)S(1)}, f32[16,4096]{1,0:T(8,128)}, u32[]{:S(2)}) copy-start(f32[16,4096]{1,0:T(8,128)} %m.5) | copy-start | bytes 786436
  2.8 19.6 %copy-start.1 = (f32[16,4096]{1,0:T(8,128)S(1)}, f32[16,4096]{1,0:T(8,128)}, u32[]{:S(2)}) copy-start(f32[16,4096]{1,0:T(8,128)} %v.5) | copy-start | bytes 786436
  2.8 19.6 %copy-start.3 = (bf16[16,4096]{1,0:T(8,128)(2,1)S(1)}, bf16[16,4096]{1,0:T(8,128)(2,1)}, u32[]{:S(2)}) copy-start(bf16[16,4096]{1,0:T(8,128)(2,1)} %w.1) | copy-start | bytes 393220
  3.5 2.6 %collective-permute-start = (bf16[128,2048]{1,0:T(8,128)(2,1)S(1)}, bf16[128,2048]{1,0:T(8,128)(2,1)S(1)}, u32[]{:S(2)}, u32[]{:S(2)}) collective-permute-start(bf16[128,2048]{1,0:T(8,128)(2,1)S(1)} %get-tuple-element.31), channel_id=1, source_target_pairs={{0,8},{1,9},{2,10},{3,11},{4,12},{5,13},{6,14},{7,15},{8,0},{9,1},... | collective-permute-start | bytes 1572872 | tf_op jit(solution)/shard_map/ppermute | solution.py:55
  6.2 6.5 %collective-permute-start.1 = (bf16[64,1024]{1,0:T(8,128)(2,1)S(1)}, bf16[64,1024]{1,0:T(8,128)(2,1)S(1)}, u32[]{:S(2)}, u32[]{:S(2)}) collective-permute-start(bf16[64,1024]{1,0:T(8,128)(2,1)S(1)} %get-tuple-element.33), channel_id=1, source_target_pairs={{0,17},{1,5},{2,6},{3,18},{4,21},{5,1},{6,2},{7,22},{8,12},{9,24},... | collective-permute-start | bytes 393224 | tf_op jit(solution)/shard_map/ppermute | solution.py:55
  9.7 4.4 %collective-permute-start.2 = (bf16[64,1024]{1,0:T(8,128)(2,1)S(1)}, bf16[64,1024]{1,0:T(8,128)(2,1)S(1)}, u32[]{:S(2)}, u32[]{:S(2)}) collective-permute-start(bf16[64,1024]{1,0:T(8,128)(2,1)S(1)} %get-tuple-element.34), channel_id=1, source_target_pairs={{0,9},{1,15},{2,12},{3,10},{4,13},{5,11},{6,8},{7,14},{8,6},{9,0},... | collective-permute-start | bytes 393224 | tf_op jit(solution)/shard_map/ppermute | solution.py:55
  10.0 4.4 %collective-permute-start.3 = (bf16[64,1024]{1,0:T(8,128)(2,1)S(1)}, bf16[64,1024]{1,0:T(8,128)(2,1)S(1)}, u32[]{:S(2)}, u32[]{:S(2)}) collective-permute-start(bf16[64,1024]{1,0:T(8,128)(2,1)S(1)} %get-tuple-element.35), channel_id=1, source_target_pairs={{0,24},{1,11},{2,8},{3,27},{4,28},{5,15},{6,12},{7,31},{8,2},{9,17... | collective-permute-start | bytes 393224 | tf_op jit(solution)/shard_map/ppermute | solution.py:55
  14.5 4.9 %collective-permute-start.4 = (bf16[16,1024]{1,0:T(8,128)(2,1)S(1)}, bf16[16,1024]{1,0:T(8,128)(2,1)S(1)}, u32[]{:S(2)}, u32[]{:S(2)}) collective-permute-start(bf16[16,1024]{1,0:T(8,128)(2,1)S(1)} %get-tuple-element.37), channel_id=1, source_target_pairs={{0,4},{1,16},{2,19},{3,7},{4,0},{5,20},{6,23},{7,3},{8,25},{9,13},... | collective-permute-start | bytes 98312 | tf_op jit(solution)/shard_map/ppermute | solution.py:55
  17.3 5.1 %collective-permute-start.5 = (bf16[16,1024]{1,0:T(8,128)(2,1)S(1)}, bf16[16,1024]{1,0:T(8,128)(2,1)S(1)}, u32[]{:S(2)}, u32[]{:S(2)}) collective-permute-start(bf16[16,1024]{1,0:T(8,128)(2,1)S(1)} %get-tuple-element.38), channel_id=1, source_target_pairs={{0,14},{1,8},{2,11},{3,13},{4,10},{5,12},{6,15},{7,9},{8,1},{9,7},... | collective-permute-start | bytes 98312 | tf_op jit(solution)/shard_map/ppermute | solution.py:55
  18.4 4.0 %collective-permute-start.6 = (bf16[16,1024]{1,0:T(8,128)(2,1)S(1)}, bf16[16,1024]{1,0:T(8,128)(2,1)S(1)}, u32[]{:S(2)}, u32[]{:S(2)}) collective-permute-start(bf16[16,1024]{1,0:T(8,128)(2,1)S(1)} %get-tuple-element.39), channel_id=1, source_target_pairs={{0,10},{1,25},{2,26},{3,9},{4,14},{5,29},{6,30},{7,13},{8,16},{9,3... | collective-permute-start | bytes 98312 | tf_op jit(solution)/shard_map/ppermute | solution.py:55
  22.5 5.0 %collective-permute-start.7 = (bf16[16,1024]{1,0:T(8,128)(2,1)S(1)}, bf16[16,1024]{1,0:T(8,128)(2,1)S(1)}, u32[]{:S(2)}, u32[]{:S(2)}) collective-permute-start(bf16[16,1024]{1,0:T(8,128)(2,1)S(1)} %get-tuple-element.42), channel_id=1, source_target_pairs={{0,17},{1,15},{2,12},{3,18},{4,21},{5,11},{6,8},{7,22},{8,6},{9,24... | collective-permute-start | bytes 98312 | tf_op jit(solution)/shard_map/ppermute | solution.py:55
  24.0 3.7 %collective-permute-start.8 = (bf16[16,1024]{1,0:T(8,128)(2,1)S(1)}, bf16[16,1024]{1,0:T(8,128)(2,1)S(1)}, u32[]{:S(2)}, u32[]{:S(2)}) collective-permute-start(bf16[16,1024]{1,0:T(8,128)(2,1)S(1)} %get-tuple-element.43), channel_id=1, source_target_pairs={{0,9},{1,5},{2,6},{3,10},{4,13},{5,1},{6,2},{7,14},{8,12},{9,0},{1... | collective-permute-start | bytes 98312 | tf_op jit(solution)/shard_map/ppermute | solution.py:55
  24.9 3.3 %collective-permute-start.9 = (bf16[16,1024]{1,0:T(8,128)(2,1)S(1)}, bf16[16,1024]{1,0:T(8,128)(2,1)S(1)}, u32[]{:S(2)}, u32[]{:S(2)}) collective-permute-start(bf16[16,1024]{1,0:T(8,128)(2,1)S(1)} %get-tuple-element.41.own), channel_id=1, source_target_pairs={{0,24},{1,11},{2,8},{3,27},{4,28},{5,15},{6,12},{7,31},{8,2},{9,17... | collective-permute-start | bytes 98312 | tf_op jit(solution)/shard_map/ppermute | solution.py:55
  28.3 10.6 %collective-permute-start.11 = (bf16[64,1024]{1,0:T(8,128)(2,1)S(1)}, bf16[64,1024]{1,0:T(8,128)(2,1)S(1)}, u32[]{:S(2)}, u32[]{:S(2)}) collective-permute-start(bf16[64,1024]{1,0:T(8,128)(2,1)S(1)} %get-tuple-element.45), channel_id=1, source_target_pairs={{0,14},{1,16},{2,19},{3,13},{4,10},{5,20},{6,23},{7,9},{8,25},{9,7... | collective-permute-start | bytes 393224 | tf_op jit(solution)/shard_map/ppermute | solution.py:55
  30.7 8.1 %collective-permute-start.13 = (bf16[64,1024]{1,0:T(8,128)(2,1)S(1)}, bf16[64,1024]{1,0:T(8,128)(2,1)S(1)}, u32[]{:S(2)}, u32[]{:S(2)}) collective-permute-start(bf16[64,1024]{1,0:T(8,128)(2,1)S(1)} %get-tuple-element.48), channel_id=1, source_target_pairs={{0,4},{1,8},{2,11},{3,7},{4,0},{5,12},{6,15},{7,3},{8,1},{9,13},{1... | collective-permute-start | bytes 393224 | tf_op jit(solution)/shard_map/ppermute | solution.py:55
  30.7 8.1 %collective-permute-start.14 = (bf16[64,1024]{1,0:T(8,128)(2,1)S(1)}, bf16[64,1024]{1,0:T(8,128)(2,1)S(1)}, u32[]{:S(2)}, u32[]{:S(2)}) collective-permute-start(bf16[64,1024]{1,0:T(8,128)(2,1)S(1)} %get-tuple-element.44.refs_0_), channel_id=1, source_target_pairs={{0,10},{1,25},{2,26},{3,9},{4,14},{5,29},{6,30},{7,13},{8,16},{9,3... | collective-permute-start | bytes 393224 | tf_op jit(solution)/shard_map/ppermute | solution.py:55
  32.2 6.7 %collective-permute-start.10 = (bf16[64,1024]{1,0:T(8,128)(2,1)S(1)}, bf16[64,1024]{1,0:T(8,128)(2,1)S(1)}, u32[]{:S(2)}, u32[]{:S(2)}) collective-permute-start(bf16[64,1024]{1,0:T(8,128)(2,1)S(1)} %get-tuple-element.44.refs_0_), channel_id=1, source_target_pairs={{0,8},{1,9},{2,10},{3,11},{4,12},{5,13},{6,14},{7,15},{8,0},{9,1},... | collective-permute-start | bytes 393224 | tf_op jit(solution)/shard_map/ppermute | solution.py:55
  35.1 3.8 %collective-permute-start.12 = (bf16[16,1024]{1,0:T(8,128)(2,1)S(1)}, bf16[16,1024]{1,0:T(8,128)(2,1)S(1)}, u32[]{:S(2)}, u32[]{:S(2)}) collective-permute-start(bf16[16,1024]{1,0:T(8,128)(2,1)S(1)} %get-tuple-element.46.refs_3_.grad), channel_id=1, source_target_pairs={{0,24},{1,25},{2,26},{3,27},{4,28},{5,29},{6,30},{7,31},{8,16},{9,... | collective-permute-start | bytes 98312 | tf_op jit(solution)/shard_map/ppermute | solution.py:55
  38.9 2.5 %collective-permute-start.15 = (bf16[224,1024]{1,0:T(8,128)(2,1)S(1)}, bf16[224,1024]{1,0:T(8,128)(2,1)S(1)}, u32[]{:S(2)}, u32[]{:S(2)}) collective-permute-start(bf16[224,1024]{1,0:T(8,128)(2,1)S(1)} %shard_map.84), channel_id=1, source_target_pairs={{0,8},{1,9},{2,10},{3,11},{4,12},{5,13},{6,14},{7,15},{8,0},{9,1},... | collective-permute-start | bytes 1376264 | tf_op jit(solution)/shard_map/ppermute | solution.py:55

commit v6 on v3

--- a/solution.py
+++ b/solution.py
@@ -282,14 +282,14 @@
     wide_rows, narrow_rows = all_rows // 2, all_rows // 8
 
     away_cots, first = call(
-        load_kernel, [shape((tokens, half), BF16), shape((tokens, quarter), BF16)], out_cotangent,
+        load_kernel, [shape((tokens, half), BF16), shape((tokens, CHUNK), BF16)], out_cotangent,
         far_in=(0,), scratch=[pltpu.SemaphoreType.DMA((2,))], limit=LOAD_LIMIT,
     )
     away, turned = call(
         away_kernel, [shape((all_rows, half), BF16), shape((all_rows, tokens), BF16)], hidden_acts, away_cots,
     )
     came = to_sibling(away)
-    later = (half - quarter) // CHUNK
+    later = half // CHUNK - 1
     kept = call(
         kept_kernel, [shape((all_rows, half), F32)], turned, first, out_cotangent,
         far_in=(2,), limit=KEPT_LIMIT,

time: 41.3 us -> 41.2 us (level)
  no operation moved by 1% of the time
where the time goes in v6:
time: 41.2 us; the launch traced here: 41.1 us
  starting transfers between devices  19.4 us (47%)
  waiting for transfers between devices  13.7 us (33%)
  Pallas kernels  7.16 us (17%)
  between operations  0.78 us (2%)
    ppermute x16, starting transfers between devices, exchange(): return lax.ppermute(value, ('rep', 'shard'), pairs)  19.4 us
    ppermute x16, waiting for transfers between devices, exchange(): return lax.ppermute(value, ('rep', 'shard'), pairs)  13.7 us
    pallas_call x11, Pallas kernels, call(): pl.pallas_call(kernel, out_shape=outs, in_specs=[far if i in tuple(far_in...  7.16 us
  transfers between devices with their start and end apart: 16, of which 10 were waited for; matrix products, arithmetic and copies ran while one was open for 0% of the time, Pallas kernels for 7%

profile of v6, /device:TPU:0, one launch (start us, length us, event | category | flops | bytes accessed | tf_op | source)
XLA Modules:
  0.0 41.1 jit_solution(12719804162817536478)
XLA Ops:
  0.6 2.1 %shard_map.76 = (bf16[768,2048]{1,0:T(8,128)(2,1)S(1)}, bf16[768,512]{1,0:T(8,128)(2,1)S(1)}) custom-call(bf16[768,4096]{1,0:T(8,128)(2,1)} %cots_ref.3), custom_call_target="tpu_custom_call" | custom-call | tf_op jit(solution)/shard_map/pallas_call | solution.py:37
  2.8 0.6 %shard_map.77 = (bf16[128,2048]{1,0:T(8,128)(2,1)S(1)}, bf16[128,768]{1,0:T(8,128)(2,1)S(1)}) custom-call(bf16[768,128]{1,0:T(8,128)(2,1)S(1)} %copy-done.2, bf16[768,2048]{1,0:T(8,128)(2,1)S(1)} %get-tuple-element.28.cots), custom_call_target="tpu_custom_call" | custom-call | tf_op jit(solution)/shard_map/pallas_call | solution.py:37
  3.5 0.5 %collective-permute-start = (bf16[128,2048]{1,0:T(8,128)(2,1)S(1)}, bf16[128,2048]{1,0:T(8,128)(2,1)S(1)}, u32[]{:S(2)}, u32[]{:S(2)}) collective-permute-start(bf16[128,2048]{1,0:T(8,128)(2,1)S(1)} %get-tuple-element.31), channel_id=1, source_target_pairs={{0,8},{1,9},{2,10},{3,11},{4,12},{5,13},{6,14},{7,15},{8,0},{9,1},... | collective-permute-start | bytes 1572872 | tf_op jit(solution)/shard_map/ppermute | solution.py:55
  4.0 2.1 %shard_map.78.kept = f32[128,2048]{1,0:T(8,128)S(1)} custom-call(bf16[128,768]{1,0:T(8,128)(2,1)S(1)} %get-tuple-element.29.turned, bf16[768,512]{1,0:T(8,128)(2,1)S(1)} %get-tuple-element.30.first, bf16[768,4096]{1,0:T(8,128)(2,1)} %cots_ref.3), custom_call_target="tpu_custom_call" | custom-call | tf_op jit(solution)/shard_map/pallas_call | solution.py:37
  6.2 3.5 %collective-permute-start.1 = (bf16[64,1024]{1,0:T(8,128)(2,1)S(1)}, bf16[64,1024]{1,0:T(8,128)(2,1)S(1)}, u32[]{:S(2)}, u32[]{:S(2)}) collective-permute-start(bf16[64,1024]{1,0:T(8,128)(2,1)S(1)} %get-tuple-element.33), channel_id=1, source_target_pairs={{0,17},{1,5},{2,6},{3,18},{4,21},{5,1},{6,2},{7,22},{8,12},{9,24},... | collective-permute-start | bytes 393224 | tf_op jit(solution)/shard_map/ppermute | solution.py:55
  10.1 2.6 %collective-permute-done.1.refs_0_ = bf16[64,1024]{1,0:T(8,128)(2,1)S(1)} collective-permute-done((bf16[64,1024]{1,0:T(8,128)(2,1)S(1)}, bf16[64,1024]{1,0:T(8,128)(2,1)S(1)}, u32[]{:S(2)}, u32[]{:S(2)}) %collective-permute-start.1) | collective-permute-done | bytes 131104 | tf_op jit(solution)/shard_map/ppermute | solution.py:55
  12.7 1.4 %collective-permute-done.2.refs_1_ = bf16[64,1024]{1,0:T(8,128)(2,1)S(1)} collective-permute-done((bf16[64,1024]{1,0:T(8,128)(2,1)S(1)}, bf16[64,1024]{1,0:T(8,128)(2,1)S(1)}, u32[]{:S(2)}, u32[]{:S(2)}) %collective-permute-start.2) | collective-permute-done | bytes 131104 | tf_op jit(solution)/shard_map/ppermute | solution.py:55
  14.5 2.8 %collective-permute-start.4 = (bf16[16,1024]{1,0:T(8,128)(2,1)S(1)}, bf16[16,1024]{1,0:T(8,128)(2,1)S(1)}, u32[]{:S(2)}, u32[]{:S(2)}) collective-permute-start(bf16[16,1024]{1,0:T(8,128)(2,1)S(1)} %get-tuple-element.37), channel_id=1, source_target_pairs={{0,4},{1,16},{2,19},{3,7},{4,0},{5,20},{6,23},{7,3},{8,25},{9,13},... | collective-permute-start | bytes 98312 | tf_op jit(solution)/shard_map/ppermute | solution.py:55
  17.3 1.2 %collective-permute-start.5 = (bf16[16,1024]{1,0:T(8,128)(2,1)S(1)}, bf16[16,1024]{1,0:T(8,128)(2,1)S(1)}, u32[]{:S(2)}, u32[]{:S(2)}) collective-permute-start(bf16[16,1024]{1,0:T(8,128)(2,1)S(1)} %get-tuple-element.38), channel_id=1, source_target_pairs={{0,14},{1,8},{2,11},{3,13},{4,10},{5,12},{6,15},{7,9},{8,1},{9,7},... | collective-permute-start | bytes 98312 | tf_op jit(solution)/shard_map/ppermute | solution.py:55
  18.6 0.7 %collective-permute-done.4.refs_0_ = bf16[16,1024]{1,0:T(8,128)(2,1)S(1)} collective-permute-done((bf16[16,1024]{1,0:T(8,128)(2,1)S(1)}, bf16[16,1024]{1,0:T(8,128)(2,1)S(1)}, u32[]{:S(2)}, u32[]{:S(2)}) %collective-permute-start.4) | collective-permute-done | bytes 32800 | tf_op jit(solution)/shard_map/ppermute | solution.py:55
  19.4 3.0 %collective-permute-done.5.refs_1_ = bf16[16,1024]{1,0:T(8,128)(2,1)S(1)} collective-permute-done((bf16[16,1024]{1,0:T(8,128)(2,1)S(1)}, bf16[16,1024]{1,0:T(8,128)(2,1)S(1)}, u32[]{:S(2)}, u32[]{:S(2)}) %collective-permute-start.5) | collective-permute-done | bytes 32800 | tf_op jit(solution)/shard_map/ppermute | solution.py:55
  22.5 1.5 %collective-permute-start.7 = (bf16[16,1024]{1,0:T(8,128)(2,1)S(1)}, bf16[16,1024]{1,0:T(8,128)(2,1)S(1)}, u32[]{:S(2)}, u32[]{:S(2)}) collective-permute-start(bf16[16,1024]{1,0:T(8,128)(2,1)S(1)} %get-tuple-element.42), channel_id=1, source_target_pairs={{0,17},{1,5},{2,6},{3,18},{4,21},{5,1},{6,2},{7,22},{8,12},{9,24},... | collective-permute-start | bytes 98312 | tf_op jit(solution)/shard_map/ppermute | solution.py:55
  24.0 0.8 %collective-permute-start.8 = (bf16[16,1024]{1,0:T(8,128)(2,1)S(1)}, bf16[16,1024]{1,0:T(8,128)(2,1)S(1)}, u32[]{:S(2)}, u32[]{:S(2)}) collective-permute-start(bf16[16,1024]{1,0:T(8,128)(2,1)S(1)} %get-tuple-element.43), channel_id=1, source_target_pairs={{0,9},{1,15},{2,12},{3,10},{4,13},{5,11},{6,8},{7,14},{8,6},{9,0},... | collective-permute-start | bytes 98312 | tf_op jit(solution)/shard_map/ppermute | solution.py:55
  24.9 0.9 %collective-permute-start.9 = (bf16[16,1024]{1,0:T(8,128)(2,1)S(1)}, bf16[16,1024]{1,0:T(8,128)(2,1)S(1)}, u32[]{:S(2)}, u32[]{:S(2)}) collective-permute-start(bf16[16,1024]{1,0:T(8,128)(2,1)S(1)} %get-tuple-element.41.own), channel_id=1, source_target_pairs={{0,24},{1,11},{2,8},{3,27},{4,28},{5,15},{6,12},{7,31},{8,2},{9,17... | collective-permute-start | bytes 98312 | tf_op jit(solution)/shard_map/ppermute | solution.py:55
  25.8 1.7 %collective-permute-done.7.refs_0_ = bf16[16,1024]{1,0:T(8,128)(2,1)S(1)} collective-permute-done((bf16[16,1024]{1,0:T(8,128)(2,1)S(1)}, bf16[16,1024]{1,0:T(8,128)(2,1)S(1)}, u32[]{:S(2)}, u32[]{:S(2)}) %collective-permute-start.7) | collective-permute-done | bytes 32800 | tf_op jit(solution)/shard_map/ppermute | solution.py:55
  28.3 1.4 %collective-permute-start.11 = (bf16[64,1024]{1,0:T(8,128)(2,1)S(1)}, bf16[64,1024]{1,0:T(8,128)(2,1)S(1)}, u32[]{:S(2)}, u32[]{:S(2)}) collective-permute-start(bf16[64,1024]{1,0:T(8,128)(2,1)S(1)} %get-tuple-element.45), channel_id=1, source_target_pairs={{0,4},{1,16},{2,19},{3,7},{4,0},{5,20},{6,23},{7,3},{8,25},{9,13},... | collective-permute-start | bytes 393224 | tf_op jit(solution)/shard_map/ppermute | solution.py:55
  29.7 1.2 %collective-permute-start.13 = (bf16[64,1024]{1,0:T(8,128)(2,1)S(1)}, bf16[64,1024]{1,0:T(8,128)(2,1)S(1)}, u32[]{:S(2)}, u32[]{:S(2)}) collective-permute-start(bf16[64,1024]{1,0:T(8,128)(2,1)S(1)} %get-tuple-element.48), channel_id=1, source_target_pairs={{0,14},{1,8},{2,11},{3,13},{4,10},{5,12},{6,15},{7,9},{8,1},{9,7},... | collective-permute-start | bytes 393224 | tf_op jit(solution)/shard_map/ppermute | solution.py:55
  30.8 0.7 %collective-permute-start.14 = (bf16[64,1024]{1,0:T(8,128)(2,1)S(1)}, bf16[64,1024]{1,0:T(8,128)(2,1)S(1)}, u32[]{:S(2)}, u32[]{:S(2)}) collective-permute-start(bf16[64,1024]{1,0:T(8,128)(2,1)S(1)} %get-tuple-element.44.refs_0_), channel_id=1, source_target_pairs={{0,10},{1,25},{2,26},{3,9},{4,14},{5,29},{6,30},{7,13},{8,16},{9,3... | collective-permute-start | bytes 393224 | tf_op jit(solution)/shard_map/ppermute | solution.py:55
  31.5 2.7 %collective-permute-start.10 = (bf16[64,1024]{1,0:T(8,128)(2,1)S(1)}, bf16[64,1024]{1,0:T(8,128)(2,1)S(1)}, u32[]{:S(2)}, u32[]{:S(2)}) collective-permute-start(bf16[64,1024]{1,0:T(8,128)(2,1)S(1)} %get-tuple-element.44.refs_0_), channel_id=1, source_target_pairs={{0,8},{1,9},{2,10},{3,11},{4,12},{5,13},{6,14},{7,15},{8,0},{9,1},... | collective-permute-start | bytes 393224 | tf_op jit(solution)/shard_map/ppermute | solution.py:55
  34.2 0.9 %collective-permute-start.12 = (bf16[16,1024]{1,0:T(8,128)(2,1)S(1)}, bf16[16,1024]{1,0:T(8,128)(2,1)S(1)}, u32[]{:S(2)}, u32[]{:S(2)}) collective-permute-start(bf16[16,1024]{1,0:T(8,128)(2,1)S(1)} %get-tuple-element.46.refs_3_.grad), channel_id=1, source_target_pairs={{0,24},{1,25},{2,26},{3,27},{4,28},{5,29},{6,30},{7,31},{8,16},{9,... | collective-permute-start | bytes 98312 | tf_op jit(solution)/shard_map/ppermute | solution.py:55
  35.2 2.7 %collective-permute-done.12.refs_4_.far_grad = bf16[16,1024]{1,0:T(8,128)(2,1)S(1)} collective-permute-done((bf16[16,1024]{1,0:T(8,128)(2,1)S(1)}, bf16[16,1024]{1,0:T(8,128)(2,1)S(1)}, u32[]{:S(2)}, u32[]{:S(2)}) %collective-permute-start.12) | collective-permute-done | bytes 32800 | tf_op jit(solution)/shard_map/ppermute | solution.py:55
  37.9 0.7 %collective-permute-start.15 = (bf16[224,1024]{1,0:T(8,128)(2,1)S(1)}, bf16[224,1024]{1,0:T(8,128)(2,1)S(1)}, u32[]{:S(2)}, u32[]{:S(2)}) collective-permute-start(bf16[224,1024]{1,0:T(8,128)(2,1)S(1)} %shard_map.84), channel_id=1, source_target_pairs={{0,8},{1,9},{2,10},{3,11},{4,12},{5,13},{6,14},{7,15},{8,0},{9,1},... | collective-permute-start | bytes 1376264 | tf_op jit(solution)/shard_map/ppermute | solution.py:55
  38.7 1.0 %shard_map.85 = (bf16[128,4096]{1,0:T(8,128)(2,1)}, f32[16,4096]{1,0:T(8,128)}, f32[16,4096]{1,0:T(8,128)}) custom-call(f32[16,4096]{1,0:T(8,128)S(1)} %copy-done, f32[16,4096]{1,0:T(8,128)S(1)} %copy-done.1, bf16[16,1024]{1,0:T(8,128)(2,1)S(1)} %get-tuple-element.46.refs_3_.grad, bf16[16,1024]{1,0:T(8,128)(2,1)S(1)} %collective-permute-done.12.refs_4_.far_grad, ...), custom_call_target="tpu_custom_call" | custom-call | tf_op jit(solution)/shard_map/pallas_call | solution.py:37
  40.1 1.0 %shard_map.86 = (bf16[128,4096]{1,0:T(8,128)(2,1)}, f32[16,4096]{1,0:T(8,128)}, f32[16,4096]{1,0:T(8,128)}) custom-call(f32[16,4096]{1,0:T(8,128)S(1)} %copy-done, f32[16,4096]{1,0:T(8,128)S(1)} %copy-done.1, bf16[64,1024]{1,0:T(8,128)(2,1)S(1)} %collective-permute-done.10.refs_5_.own, ...), custom_call_target="tpu_custom_call", output_to_operand_aliasing={{0}: (4, {}), {1}: (5, {}), {2}: (6, {})} | custom-call | tf_op jit(solution)/shard_map/pallas_call | solution.py:37
  (27 shorter events, 2.4 us)
Async XLA Ops:
  0.6 2.2 %copy-start.2 = (bf16[768,128]{1,0:T(8,128)(2,1)S(1)}, bf16[768,128]{1,0:T(8,128)(2,1)}, u32[]{:S(2)}) copy-start(bf16[768,128]{1,0:T(8,128)(2,1)} %acts.1) | copy-start | bytes 589828
  2.8 19.6 %copy-start = (f32[16,4096]{1,0:T(8,128)S(1)}, f32[16,4096]{1,0:T(8,128)}, u32[]{:S(2)}) copy-start(f32[16,4096]{1,0:T(8,128)} %m.5) | copy-start | bytes 786436
  2.8 19.6 %copy-start.1 = (f32[16,4096]{1,0:T(8,128)S(1)}, f32[16,4096]{1,0:T(8,128)}, u32[]{:S(2)}) copy-start(f32[16,4096]{1,0:T(8,128)} %v.5) | copy-start | bytes 786436
  2.8 19.6 %copy-start.3 = (bf16[16,4096]{1,0:T(8,128)(2,1)S(1)}, bf16[16,4096]{1,0:T(8,128)(2,1)}, u32[]{:S(2)}) copy-start(bf16[16,4096]{1,0:T(8,128)(2,1)} %w.1) | copy-start | bytes 393220
  3.5 2.6 %collective-permute-start = (bf16[128,2048]{1,0:T(8,128)(2,1)S(1)}, bf16[128,2048]{1,0:T(8,128)(2,1)S(1)}, u32[]{:S(2)}, u32[]{:S(2)}) collective-permute-start(bf16[128,2048]{1,0:T(8,128)(2,1)S(1)} %get-tuple-element.31), channel_id=1, source_target_pairs={{0,8},{1,9},{2,10},{3,11},{4,12},{5,13},{6,14},{7,15},{8,0},{9,1},... | collective-permute-start | bytes 1572872 | tf_op jit(solution)/shard_map/ppermute | solution.py:55
  6.2 6.5 %collective-permute-start.1 = (bf16[64,1024]{1,0:T(8,128)(2,1)S(1)}, bf16[64,1024]{1,0:T(8,128)(2,1)S(1)}, u32[]{:S(2)}, u32[]{:S(2)}) collective-permute-start(bf16[64,1024]{1,0:T(8,128)(2,1)S(1)} %get-tuple-element.33), channel_id=1, source_target_pairs={{0,17},{1,5},{2,6},{3,18},{4,21},{5,1},{6,2},{7,22},{8,12},{9,24},... | collective-permute-start | bytes 393224 | tf_op jit(solution)/shard_map/ppermute | solution.py:55
  9.7 4.4 %collective-permute-start.2 = (bf16[64,1024]{1,0:T(8,128)(2,1)S(1)}, bf16[64,1024]{1,0:T(8,128)(2,1)S(1)}, u32[]{:S(2)}, u32[]{:S(2)}) collective-permute-start(bf16[64,1024]{1,0:T(8,128)(2,1)S(1)} %get-tuple-element.34), channel_id=1, source_target_pairs={{0,9},{1,15},{2,12},{3,10},{4,13},{5,11},{6,8},{7,14},{8,6},{9,0},... | collective-permute-start | bytes 393224 | tf_op jit(solution)/shard_map/ppermute | solution.py:55
  10.0 4.4 %collective-permute-start.3 = (bf16[64,1024]{1,0:T(8,128)(2,1)S(1)}, bf16[64,1024]{1,0:T(8,128)(2,1)S(1)}, u32[]{:S(2)}, u32[]{:S(2)}) collective-permute-start(bf16[64,1024]{1,0:T(8,128)(2,1)S(1)} %get-tuple-element.35), channel_id=1, source_target_pairs={{0,24},{1,11},{2,8},{3,27},{4,28},{5,15},{6,12},{7,31},{8,2},{9,17... | collective-permute-start | bytes 393224 | tf_op jit(solution)/shard_map/ppermute | solution.py:55
  14.5 4.9 %collective-permute-start.4 = (bf16[16,1024]{1,0:T(8,128)(2,1)S(1)}, bf16[16,1024]{1,0:T(8,128)(2,1)S(1)}, u32[]{:S(2)}, u32[]{:S(2)}) collective-permute-start(bf16[16,1024]{1,0:T(8,128)(2,1)S(1)} %get-tuple-element.37), channel_id=1, source_target_pairs={{0,4},{1,16},{2,19},{3,7},{4,0},{5,20},{6,23},{7,3},{8,25},{9,13},... | collective-permute-start | bytes 98312 | tf_op jit(solution)/shard_map/ppermute | solution.py:55
  17.3 5.1 %collective-permute-start.5 = (bf16[16,1024]{1,0:T(8,128)(2,1)S(1)}, bf16[16,1024]{1,0:T(8,128)(2,1)S(1)}, u32[]{:S(2)}, u32[]{:S(2)}) collective-permute-start(bf16[16,1024]{1,0:T(8,128)(2,1)S(1)} %get-tuple-element.38), channel_id=1, source_target_pairs={{0,14},{1,8},{2,11},{3,13},{4,10},{5,12},{6,15},{7,9},{8,1},{9,7},... | collective-permute-start | bytes 98312 | tf_op jit(solution)/shard_map/ppermute | solution.py:55
  18.4 4.0 %collective-permute-start.6 = (bf16[16,1024]{1,0:T(8,128)(2,1)S(1)}, bf16[16,1024]{1,0:T(8,128)(2,1)S(1)}, u32[]{:S(2)}, u32[]{:S(2)}) collective-permute-start(bf16[16,1024]{1,0:T(8,128)(2,1)S(1)} %get-tuple-element.39), channel_id=1, source_target_pairs={{0,10},{1,25},{2,26},{3,9},{4,14},{5,29},{6,30},{7,13},{8,16},{9,3... | collective-permute-start | bytes 98312 | tf_op jit(solution)/shard_map/ppermute | solution.py:55
  22.5 5.0 %collective-permute-start.7 = (bf16[16,1024]{1,0:T(8,128)(2,1)S(1)}, bf16[16,1024]{1,0:T(8,128)(2,1)S(1)}, u32[]{:S(2)}, u32[]{:S(2)}) collective-permute-start(bf16[16,1024]{1,0:T(8,128)(2,1)S(1)} %get-tuple-element.42), channel_id=1, source_target_pairs={{0,17},{1,5},{2,6},{3,18},{4,21},{5,1},{6,2},{7,22},{8,12},{9,24},... | collective-permute-start | bytes 98312 | tf_op jit(solution)/shard_map/ppermute | solution.py:55
  24.0 3.7 %collective-permute-start.8 = (bf16[16,1024]{1,0:T(8,128)(2,1)S(1)}, bf16[16,1024]{1,0:T(8,128)(2,1)S(1)}, u32[]{:S(2)}, u32[]{:S(2)}) collective-permute-start(bf16[16,1024]{1,0:T(8,128)(2,1)S(1)} %get-tuple-element.43), channel_id=1, source_target_pairs={{0,9},{1,15},{2,12},{3,10},{4,13},{5,11},{6,8},{7,14},{8,6},{9,0},... | collective-permute-start | bytes 98312 | tf_op jit(solution)/shard_map/ppermute | solution.py:55
  24.9 3.3 %collective-permute-start.9 = (bf16[16,1024]{1,0:T(8,128)(2,1)S(1)}, bf16[16,1024]{1,0:T(8,128)(2,1)S(1)}, u32[]{:S(2)}, u32[]{:S(2)}) collective-permute-start(bf16[16,1024]{1,0:T(8,128)(2,1)S(1)} %get-tuple-element.41.own), channel_id=1, source_target_pairs={{0,24},{1,11},{2,8},{3,27},{4,28},{5,15},{6,12},{7,31},{8,2},{9,17... | collective-permute-start | bytes 98312 | tf_op jit(solution)/shard_map/ppermute | solution.py:55
  28.3 9.6 %collective-permute-start.11 = (bf16[64,1024]{1,0:T(8,128)(2,1)S(1)}, bf16[64,1024]{1,0:T(8,128)(2,1)S(1)}, u32[]{:S(2)}, u32[]{:S(2)}) collective-permute-start(bf16[64,1024]{1,0:T(8,128)(2,1)S(1)} %get-tuple-element.45), channel_id=1, source_target_pairs={{0,4},{1,16},{2,19},{3,7},{4,0},{5,20},{6,23},{7,3},{8,25},{9,13},... | collective-permute-start | bytes 393224 | tf_op jit(solution)/shard_map/ppermute | solution.py:55
  29.7 8.2 %collective-permute-start.13 = (bf16[64,1024]{1,0:T(8,128)(2,1)S(1)}, bf16[64,1024]{1,0:T(8,128)(2,1)S(1)}, u32[]{:S(2)}, u32[]{:S(2)}) collective-permute-start(bf16[64,1024]{1,0:T(8,128)(2,1)S(1)} %get-tuple-element.48), channel_id=1, source_target_pairs={{0,14},{1,8},{2,11},{3,13},{4,10},{5,12},{6,15},{7,9},{8,1},{9,7},... | collective-permute-start | bytes 393224 | tf_op jit(solution)/shard_map/ppermute | solution.py:55
  30.8 7.1 %collective-permute-start.14 = (bf16[64,1024]{1,0:T(8,128)(2,1)S(1)}, bf16[64,1024]{1,0:T(8,128)(2,1)S(1)}, u32[]{:S(2)}, u32[]{:S(2)}) collective-permute-start(bf16[64,1024]{1,0:T(8,128)(2,1)S(1)} %get-tuple-element.44.refs_0_), channel_id=1, source_target_pairs={{0,10},{1,25},{2,26},{3,9},{4,14},{5,29},{6,30},{7,13},{8,16},{9,3... | collective-permute-start | bytes 393224 | tf_op jit(solution)/shard_map/ppermute | solution.py:55
  31.5 6.4 %collective-permute-start.10 = (bf16[64,1024]{1,0:T(8,128)(2,1)S(1)}, bf16[64,1024]{1,0:T(8,128)(2,1)S(1)}, u32[]{:S(2)}, u32[]{:S(2)}) collective-permute-start(bf16[64,1024]{1,0:T(8,128)(2,1)S(1)} %get-tuple-element.44.refs_0_), channel_id=1, source_target_pairs={{0,8},{1,9},{2,10},{3,11},{4,12},{5,13},{6,14},{7,15},{8,0},{9,1},... | collective-permute-start | bytes 393224 | tf_op jit(solution)/shard_map/ppermute | solution.py:55
  34.2 3.6 %collective-permute-start.12 = (bf16[16,1024]{1,0:T(8,128)(2,1)S(1)}, bf16[16,1024]{1,0:T(8,128)(2,1)S(1)}, u32[]{:S(2)}, u32[]{:S(2)}) collective-permute-start(bf16[16,1024]{1,0:T(8,128)(2,1)S(1)} %get-tuple-element.46.refs_3_.grad), channel_id=1, source_target_pairs={{0,24},{1,25},{2,26},{3,27},{4,28},{5,29},{6,30},{7,31},{8,16},{9,... | collective-permute-start | bytes 98312 | tf_op jit(solution)/shard_map/ppermute | solution.py:55
  37.9 2.2 %collective-permute-start.15 = (bf16[224,1024]{1,0:T(8,128)(2,1)S(1)}, bf16[224,1024]{1,0:T(8,128)(2,1)S(1)}, u32[]{:S(2)}, u32[]{:S(2)}) collective-permute-start(bf16[224,1024]{1,0:T(8,128)(2,1)S(1)} %shard_map.84), channel_id=1, source_target_pairs={{0,8},{1,9},{2,10},{3,11},{4,12},{5,13},{6,14},{7,15},{8,0},{9,1},... | collective-permute-start | bytes 1376264 | tf_op jit(solution)/shard_map/ppermute | solution.py:55

commit v7 on v6

--- a/solution.py
+++ b/solution.py
@@ -205,16 +205,17 @@
         out[at, :] = value
 
 
-def rest_back_kernel(*refs):
-    pieces, outs = refs[:-len(STEPS)], refs[-len(STEPS):]
+def rest_back_kernel(grad, *refs):
+    pieces, (*outs, last) = refs[:-1 - len(STEPS)], refs[-1 - len(STEPS):]
     w = place()[4]
-    rows = pieces[0].shape[0]
+    rows = grad.shape[0]
     for k, ref in enumerate(pieces):
         put(outs, block(w ^ k, rows), ref[...])
+    last[...] = grad[...]
 
 
 def narrow_back_kernel(own, *refs):
-    parts, outs = (own,) + refs[:-len(STEPS)], refs[-len(STEPS):]
+    parts, outs = (own,) + refs[:len(STEPS)], refs[-len(STEPS):]
     for step, ref in zip((STAY,) + STEPS, parts):
         put(outs, block(group_of(step, 1), own.shape[0]), ref[...])
 
@@ -312,12 +313,17 @@
     )
 
     pieces = [along_rest(new_w, k) for k in range(1, rest)]
-    parts = call(rest_back_kernel, [shape((narrow_rows, quarter), BF16)] * len(STEPS), new_w, *pieces)
+    *parts, far_grad = call(
+        rest_back_kernel,
+        [shape((narrow_rows, quarter), BF16)] * len(STEPS) + [shape((rows, quarter), BF16)], grad, new_w, *pieces,
+    )
     came = [stage(part, step, 0) for step, part in zip(STEPS, parts)]
-    parts = call(narrow_back_kernel, [shape((wide_rows, quarter), BF16)] * len(STEPS), parts[-1], *came)
+    far_grad = along_x(far_grad)
+    parts = call(
+        narrow_back_kernel, [shape((wide_rows, quarter), BF16)] * len(STEPS), parts[-1], *came, far_grad,
+    )
     came = [stage(part, step, 1) for step, part in zip(STEPS, parts)]
-    far_grad, own = along_x(grad), to_sibling(parts[-1])
-    came[0], far_grad = lax.optimization_barrier((came[0], far_grad))
+    own = to_sibling(parts[-1])
 
     landed = to_sibling(call(
         pack_kernel, [shape((len(STEPS) * wide_rows + 2 * rows, quarter), BF16)], *came, grad, far_grad, own,

time: 41.2 us -> 41 us (level)
  starting transfers between devices: 19.4 us -> 17.9 us
  waiting for transfers between devices: 13.7 us -> 15 us
    ppermute x16, starting transfers between devices: 19.4 us -> 17.9 us  [exchange(): return lax.ppermute(value, ('rep', 'shard'), pairs)]
    ppermute x16, waiting for transfers between devices: 13.7 us -> 15 us  [exchange(): return lax.ppermute(value, ('rep', 'shard'), pairs)]
  transfers between devices with their start and end apart: 16 -> 16, of which waited for: 10 -> 13; matrix products, arithmetic and copies ran while one was open for 0% -> 0% of each run, Pallas kernels for 7% -> 8%
where the time goes in v7:
time: 41 us; the launch traced here: 40.9 us
  starting transfers between devices  17.9 us (44%)
  waiting for transfers between devices  15 us (37%)
  Pallas kernels  7.16 us (17%)
  between operations  0.77 us (2%)
    ppermute x16, starting transfers between devices, exchange(): return lax.ppermute(value, ('rep', 'shard'), pairs)  17.9 us
    ppermute x16, waiting for transfers between devices, exchange(): return lax.ppermute(value, ('rep', 'shard'), pairs)  15 us
    pallas_call x11, Pallas kernels, call(): pl.pallas_call(kernel, out_shape=outs, in_specs=[far if i in tuple(far_in...  7.16 us
  transfers between devices with their start and end apart: 16, of which 13 were waited for; matrix products, arithmetic and copies ran while one was open for 0% of the time, Pallas kernels for 8%

profile of v7, /device:TPU:0, one launch (start us, length us, event | category | flops | bytes accessed | tf_op | source)
XLA Modules:
  0.0 40.9 jit_solution(8997491924531092688)
XLA Ops:
  0.6 2.1 %shard_map.76 = (bf16[768,2048]{1,0:T(8,128)(2,1)S(1)}, bf16[768,512]{1,0:T(8,128)(2,1)S(1)}) custom-call(bf16[768,4096]{1,0:T(8,128)(2,1)} %cots_ref.3), custom_call_target="tpu_custom_call" | custom-call | tf_op jit(solution)/shard_map/pallas_call | solution.py:37
  4.0 2.1 %shard_map.78.kept = f32[128,2048]{1,0:T(8,128)S(1)} custom-call(bf16[128,768]{1,0:T(8,128)(2,1)S(1)} %get-tuple-element.28.turned, bf16[768,512]{1,0:T(8,128)(2,1)S(1)} %get-tuple-element.29.first, bf16[768,4096]{1,0:T(8,128)(2,1)} %cots_ref.3), custom_call_target="tpu_custom_call" | custom-call | tf_op jit(solution)/shard_map/pallas_call | solution.py:37
  6.2 3.5 %collective-permute-start.1 = (bf16[64,1024]{1,0:T(8,128)(2,1)S(1)}, bf16[64,1024]{1,0:T(8,128)(2,1)S(1)}, u32[]{:S(2)}, u32[]{:S(2)}) collective-permute-start(bf16[64,1024]{1,0:T(8,128)(2,1)S(1)} %get-tuple-element.32), channel_id=1, source_target_pairs={{0,17},{1,5},{2,6},{3,18},{4,21},{5,1},{6,2},{7,22},{8,12},{9,24},... | collective-permute-start | bytes 393224 | tf_op jit(solution)/shard_map/ppermute | solution.py:55
  10.1 2.6 %collective-permute-done.1.refs_0_ = bf16[64,1024]{1,0:T(8,128)(2,1)S(1)} collective-permute-done((bf16[64,1024]{1,0:T(8,128)(2,1)S(1)}, bf16[64,1024]{1,0:T(8,128)(2,1)S(1)}, u32[]{:S(2)}, u32[]{:S(2)}) %collective-permute-start.1) | collective-permute-done | bytes 131104 | tf_op jit(solution)/shard_map/ppermute | solution.py:55
  12.7 1.4 %collective-permute-done.2.refs_1_ = bf16[64,1024]{1,0:T(8,128)(2,1)S(1)} collective-permute-done((bf16[64,1024]{1,0:T(8,128)(2,1)S(1)}, bf16[64,1024]{1,0:T(8,128)(2,1)S(1)}, u32[]{:S(2)}, u32[]{:S(2)}) %collective-permute-start.2) | collective-permute-done | bytes 131104 | tf_op jit(solution)/shard_map/ppermute | solution.py:55
  14.5 2.8 %collective-permute-start.4 = (bf16[16,1024]{1,0:T(8,128)(2,1)S(1)}, bf16[16,1024]{1,0:T(8,128)(2,1)S(1)}, u32[]{:S(2)}, u32[]{:S(2)}) collective-permute-start(bf16[16,1024]{1,0:T(8,128)(2,1)S(1)} %get-tuple-element.36), channel_id=1, source_target_pairs={{0,4},{1,16},{2,19},{3,7},{4,0},{5,20},{6,23},{7,3},{8,25},{9,13},... | collective-permute-start | bytes 98312 | tf_op jit(solution)/shard_map/ppermute | solution.py:55
  17.3 1.2 %collective-permute-start.5 = (bf16[16,1024]{1,0:T(8,128)(2,1)S(1)}, bf16[16,1024]{1,0:T(8,128)(2,1)S(1)}, u32[]{:S(2)}, u32[]{:S(2)}) collective-permute-start(bf16[16,1024]{1,0:T(8,128)(2,1)S(1)} %get-tuple-element.37), channel_id=1, source_target_pairs={{0,14},{1,8},{2,11},{3,13},{4,10},{5,12},{6,15},{7,9},{8,1},{9,7},... | collective-permute-start | bytes 98312 | tf_op jit(solution)/shard_map/ppermute | solution.py:55
  18.6 0.7 %collective-permute-done.4.refs_0_ = bf16[16,1024]{1,0:T(8,128)(2,1)S(1)} collective-permute-done((bf16[16,1024]{1,0:T(8,128)(2,1)S(1)}, bf16[16,1024]{1,0:T(8,128)(2,1)S(1)}, u32[]{:S(2)}, u32[]{:S(2)}) %collective-permute-start.4) | collective-permute-done | bytes 32800 | tf_op jit(solution)/shard_map/ppermute | solution.py:55
  19.4 3.0 %collective-permute-done.5.refs_1_ = bf16[16,1024]{1,0:T(8,128)(2,1)S(1)} collective-permute-done((bf16[16,1024]{1,0:T(8,128)(2,1)S(1)}, bf16[16,1024]{1,0:T(8,128)(2,1)S(1)}, u32[]{:S(2)}, u32[]{:S(2)}) %collective-permute-start.5) | collective-permute-done | bytes 32800 | tf_op jit(solution)/shard_map/ppermute | solution.py:55
  22.5 1.5 %collective-permute-start.7 = (bf16[16,1024]{1,0:T(8,128)(2,1)S(1)}, bf16[16,1024]{1,0:T(8,128)(2,1)S(1)}, u32[]{:S(2)}, u32[]{:S(2)}) collective-permute-start(bf16[16,1024]{1,0:T(8,128)(2,1)S(1)} %get-tuple-element.42), channel_id=1, source_target_pairs={{0,17},{1,5},{2,6},{3,18},{4,21},{5,1},{6,2},{7,22},{8,12},{9,24},... | collective-permute-start | bytes 98312 | tf_op jit(solution)/shard_map/ppermute | solution.py:55
  24.0 0.8 %collective-permute-start.8 = (bf16[16,1024]{1,0:T(8,128)(2,1)S(1)}, bf16[16,1024]{1,0:T(8,128)(2,1)S(1)}, u32[]{:S(2)}, u32[]{:S(2)}) collective-permute-start(bf16[16,1024]{1,0:T(8,128)(2,1)S(1)} %get-tuple-element.43), channel_id=1, source_target_pairs={{0,9},{1,15},{2,12},{3,10},{4,13},{5,11},{6,8},{7,14},{8,6},{9,0},... | collective-permute-start | bytes 98312 | tf_op jit(solution)/shard_map/ppermute | solution.py:55
  24.9 0.9 %collective-permute-start.10 = (bf16[16,1024]{1,0:T(8,128)(2,1)S(1)}, bf16[16,1024]{1,0:T(8,128)(2,1)S(1)}, u32[]{:S(2)}, u32[]{:S(2)}) collective-permute-start(bf16[16,1024]{1,0:T(8,128)(2,1)S(1)} %get-tuple-element.44), channel_id=1, source_target_pairs={{0,24},{1,25},{2,26},{3,27},{4,28},{5,29},{6,30},{7,31},{8,16},{9,... | collective-permute-start | bytes 98312 | tf_op jit(solution)/shard_map/ppermute | solution.py:55
  25.8 0.8 %collective-permute-start.9 = (bf16[16,1024]{1,0:T(8,128)(2,1)S(1)}, bf16[16,1024]{1,0:T(8,128)(2,1)S(1)}, u32[]{:S(2)}, u32[]{:S(2)}) collective-permute-start(bf16[16,1024]{1,0:T(8,128)(2,1)S(1)} %get-tuple-element.41.own), channel_id=1, source_target_pairs={{0,24},{1,11},{2,8},{3,27},{4,28},{5,15},{6,12},{7,31},{8,2},{9,17... | collective-permute-start | bytes 98312 | tf_op jit(solution)/shard_map/ppermute | solution.py:55
  26.6 0.9 %collective-permute-done.7.refs_0_ = bf16[16,1024]{1,0:T(8,128)(2,1)S(1)} collective-permute-done((bf16[16,1024]{1,0:T(8,128)(2,1)S(1)}, bf16[16,1024]{1,0:T(8,128)(2,1)S(1)}, u32[]{:S(2)}, u32[]{:S(2)}) %collective-permute-start.7) | collective-permute-done | bytes 32800 | tf_op jit(solution)/shard_map/ppermute | solution.py:55
  28.2 0.9 %collective-permute-done.9.refs_2_ = bf16[16,1024]{1,0:T(8,128)(2,1)S(1)} collective-permute-done((bf16[16,1024]{1,0:T(8,128)(2,1)S(1)}, bf16[16,1024]{1,0:T(8,128)(2,1)S(1)}, u32[]{:S(2)}, u32[]{:S(2)}) %collective-permute-start.9) | collective-permute-done | bytes 32800 | tf_op jit(solution)/shard_map/ppermute | solution.py:55
  29.2 1.1 %collective-permute-start.12 = (bf16[64,1024]{1,0:T(8,128)(2,1)S(1)}, bf16[64,1024]{1,0:T(8,128)(2,1)S(1)}, u32[]{:S(2)}, u32[]{:S(2)}) collective-permute-start(bf16[64,1024]{1,0:T(8,128)(2,1)S(1)} %get-tuple-element.46), channel_id=1, source_target_pairs={{0,4},{1,16},{2,19},{3,7},{4,0},{5,20},{6,23},{7,3},{8,25},{9,13},... | collective-permute-start | bytes 393224 | tf_op jit(solution)/shard_map/ppermute | solution.py:55
  30.3 0.9 %collective-permute-start.13 = (bf16[64,1024]{1,0:T(8,128)(2,1)S(1)}, bf16[64,1024]{1,0:T(8,128)(2,1)S(1)}, u32[]{:S(2)}, u32[]{:S(2)}) collective-permute-start(bf16[64,1024]{1,0:T(8,128)(2,1)S(1)} %get-tuple-element.47), channel_id=1, source_target_pairs={{0,14},{1,8},{2,11},{3,13},{4,10},{5,12},{6,15},{7,9},{8,1},{9,7},... | collective-permute-start | bytes 393224 | tf_op jit(solution)/shard_map/ppermute | solution.py:55
  31.2 1.3 %collective-permute-start.14 = (bf16[64,1024]{1,0:T(8,128)(2,1)S(1)}, bf16[64,1024]{1,0:T(8,128)(2,1)S(1)}, u32[]{:S(2)}, u32[]{:S(2)}) collective-permute-start(bf16[64,1024]{1,0:T(8,128)(2,1)S(1)} %get-tuple-element.45.refs_0_), channel_id=1, source_target_pairs={{0,10},{1,25},{2,26},{3,9},{4,14},{5,29},{6,30},{7,13},{8,16},{9,3... | collective-permute-start | bytes 393224 | tf_op jit(solution)/shard_map/ppermute | solution.py:55
  32.5 1.8 %collective-permute-start.11 = (bf16[64,1024]{1,0:T(8,128)(2,1)S(1)}, bf16[64,1024]{1,0:T(8,128)(2,1)S(1)}, u32[]{:S(2)}, u32[]{:S(2)}) collective-permute-start(bf16[64,1024]{1,0:T(8,128)(2,1)S(1)} %get-tuple-element.45.refs_0_), channel_id=1, source_target_pairs={{0,8},{1,9},{2,10},{3,11},{4,12},{5,13},{6,14},{7,15},{8,0},{9,1},... | collective-permute-start | bytes 393224 | tf_op jit(solution)/shard_map/ppermute | solution.py:55
  34.3 1.0 %collective-permute-done.12.refs_0_.refs_1_ = bf16[64,1024]{1,0:T(8,128)(2,1)S(1)} collective-permute-done((bf16[64,1024]{1,0:T(8,128)(2,1)S(1)}, bf16[64,1024]{1,0:T(8,128)(2,1)S(1)}, u32[]{:S(2)}, u32[]{:S(2)}) %collective-permute-start.12) | collective-permute-done | bytes 131104 | tf_op jit(solution)/shard_map/ppermute | solution.py:55
  35.2 1.4 %collective-permute-done.13.refs_1_.refs_2_ = bf16[64,1024]{1,0:T(8,128)(2,1)S(1)} collective-permute-done((bf16[64,1024]{1,0:T(8,128)(2,1)S(1)}, bf16[64,1024]{1,0:T(8,128)(2,1)S(1)}, u32[]{:S(2)}, u32[]{:S(2)}) %collective-permute-start.13) | collective-permute-done | bytes 131104 | tf_op jit(solution)/shard_map/ppermute | solution.py:55
  36.6 1.3 %collective-permute-done.14.refs_2_.refs_3_ = bf16[64,1024]{1,0:T(8,128)(2,1)S(1)} collective-permute-done((bf16[64,1024]{1,0:T(8,128)(2,1)S(1)}, bf16[64,1024]{1,0:T(8,128)(2,1)S(1)}, u32[]{:S(2)}, u32[]{:S(2)}) %collective-permute-start.14) | collective-permute-done | bytes 131104 | tf_op jit(solution)/shard_map/ppermute | solution.py:55
  38.2 1.0 %shard_map.85 = (bf16[128,4096]{1,0:T(8,128)(2,1)}, f32[16,4096]{1,0:T(8,128)}, f32[16,4096]{1,0:T(8,128)}) custom-call(f32[16,4096]{1,0:T(8,128)S(1)} %copy-done, f32[16,4096]{1,0:T(8,128)S(1)} %copy-done.1, bf16[16,1024]{1,0:T(8,128)(2,1)S(1)} %get-tuple-element.39.grad.refs_3_, bf16[16,1024]{1,0:T(8,128)(2,1)S(1)} %collective-permute-done.10.refs_3_.refs_4_.far_grad, ...), custom_call_target="tpu_custom_call" | custom-call | tf_op jit(solution)/shard_map/pallas_call | solution.py:37
  39.9 1.0 %shard_map.86 = (bf16[128,4096]{1,0:T(8,128)(2,1)}, f32[16,4096]{1,0:T(8,128)}, f32[16,4096]{1,0:T(8,128)}) custom-call(f32[16,4096]{1,0:T(8,128)S(1)} %copy-done, f32[16,4096]{1,0:T(8,128)S(1)} %copy-done.1, bf16[64,1024]{1,0:T(8,128)(2,1)S(1)} %collective-permute-done.11.refs_5_.own, ...), custom_call_target="tpu_custom_call", output_to_operand_aliasing={{0}: (4, {}), {1}: (5, {}), {2}: (6, {})} | custom-call | tf_op jit(solution)/shard_map/pallas_call | solution.py:37
  (27 shorter events, 4.0 us)
Async XLA Ops:
  0.6 2.2 %copy-start.2 = (bf16[768,128]{1,0:T(8,128)(2,1)S(1)}, bf16[768,128]{1,0:T(8,128)(2,1)}, u32[]{:S(2)}) copy-start(bf16[768,128]{1,0:T(8,128)(2,1)} %acts.1) | copy-start | bytes 589828
  2.8 19.6 %copy-start = (f32[16,4096]{1,0:T(8,128)S(1)}, f32[16,4096]{1,0:T(8,128)}, u32[]{:S(2)}) copy-start(f32[16,4096]{1,0:T(8,128)} %m.5) | copy-start | bytes 786436
  2.8 19.6 %copy-start.1 = (f32[16,4096]{1,0:T(8,128)S(1)}, f32[16,4096]{1,0:T(8,128)}, u32[]{:S(2)}) copy-start(f32[16,4096]{1,0:T(8,128)} %v.5) | copy-start | bytes 786436
  2.8 19.6 %copy-start.3 = (bf16[16,4096]{1,0:T(8,128)(2,1)S(1)}, bf16[16,4096]{1,0:T(8,128)(2,1)}, u32[]{:S(2)}) copy-start(bf16[16,4096]{1,0:T(8,128)(2,1)} %w.1) | copy-start | bytes 393220
  3.5 2.6 %collective-permute-start = (bf16[128,2048]{1,0:T(8,128)(2,1)S(1)}, bf16[128,2048]{1,0:T(8,128)(2,1)S(1)}, u32[]{:S(2)}, u32[]{:S(2)}) collective-permute-start(bf16[128,2048]{1,0:T(8,128)(2,1)S(1)} %get-tuple-element.30), channel_id=1, source_target_pairs={{0,8},{1,9},{2,10},{3,11},{4,12},{5,13},{6,14},{7,15},{8,0},{9,1},... | collective-permute-start | bytes 1572872 | tf_op jit(solution)/shard_map/ppermute | solution.py:55
  6.2 6.5 %collective-permute-start.1 = (bf16[64,1024]{1,0:T(8,128)(2,1)S(1)}, bf16[64,1024]{1,0:T(8,128)(2,1)S(1)}, u32[]{:S(2)}, u32[]{:S(2)}) collective-permute-start(bf16[64,1024]{1,0:T(8,128)(2,1)S(1)} %get-tuple-element.32), channel_id=1, source_target_pairs={{0,17},{1,5},{2,6},{3,18},{4,21},{5,1},{6,2},{7,22},{8,12},{9,24},... | collective-permute-start | bytes 393224 | tf_op jit(solution)/shard_map/ppermute | solution.py:55
  9.7 4.4 %collective-permute-start.2 = (bf16[64,1024]{1,0:T(8,128)(2,1)S(1)}, bf16[64,1024]{1,0:T(8,128)(2,1)S(1)}, u32[]{:S(2)}, u32[]{:S(2)}) collective-permute-start(bf16[64,1024]{1,0:T(8,128)(2,1)S(1)} %get-tuple-element.33), channel_id=1, source_target_pairs={{0,9},{1,15},{2,12},{3,10},{4,13},{5,11},{6,8},{7,14},{8,6},{9,0},... | collective-permute-start | bytes 393224 | tf_op jit(solution)/shard_map/ppermute | solution.py:55
  10.0 4.4 %collective-permute-start.3 = (bf16[64,1024]{1,0:T(8,128)(2,1)S(1)}, bf16[64,1024]{1,0:T(8,128)(2,1)S(1)}, u32[]{:S(2)}, u32[]{:S(2)}) collective-permute-start(bf16[64,1024]{1,0:T(8,128)(2,1)S(1)} %get-tuple-element.34), channel_id=1, source_target_pairs={{0,24},{1,11},{2,8},{3,27},{4,28},{5,15},{6,12},{7,31},{8,2},{9,17... | collective-permute-start | bytes 393224 | tf_op jit(solution)/shard_map/ppermute | solution.py:55
  14.5 4.9 %collective-permute-start.4 = (bf16[16,1024]{1,0:T(8,128)(2,1)S(1)}, bf16[16,1024]{1,0:T(8,128)(2,1)S(1)}, u32[]{:S(2)}, u32[]{:S(2)}) collective-permute-start(bf16[16,1024]{1,0:T(8,128)(2,1)S(1)} %get-tuple-element.36), channel_id=1, source_target_pairs={{0,4},{1,16},{2,19},{3,7},{4,0},{5,20},{6,23},{7,3},{8,25},{9,13},... | collective-permute-start | bytes 98312 | tf_op jit(solution)/shard_map/ppermute | solution.py:55
  17.3 5.1 %collective-permute-start.5 = (bf16[16,1024]{1,0:T(8,128)(2,1)S(1)}, bf16[16,1024]{1,0:T(8,128)(2,1)S(1)}, u32[]{:S(2)}, u32[]{:S(2)}) collective-permute-start(bf16[16,1024]{1,0:T(8,128)(2,1)S(1)} %get-tuple-element.37), channel_id=1, source_target_pairs={{0,14},{1,8},{2,11},{3,13},{4,10},{5,12},{6,15},{7,9},{8,1},{9,7},... | collective-permute-start | bytes 98312 | tf_op jit(solution)/shard_map/ppermute | solution.py:55
  18.4 4.0 %collective-permute-start.6 = (bf16[16,1024]{1,0:T(8,128)(2,1)S(1)}, bf16[16,1024]{1,0:T(8,128)(2,1)S(1)}, u32[]{:S(2)}, u32[]{:S(2)}) collective-permute-start(bf16[16,1024]{1,0:T(8,128)(2,1)S(1)} %get-tuple-element.38), channel_id=1, source_target_pairs={{0,10},{1,25},{2,26},{3,9},{4,14},{5,29},{6,30},{7,13},{8,16},{9,3... | collective-permute-start | bytes 98312 | tf_op jit(solution)/shard_map/ppermute | solution.py:55
  22.5 5.0 %collective-permute-start.7 = (bf16[16,1024]{1,0:T(8,128)(2,1)S(1)}, bf16[16,1024]{1,0:T(8,128)(2,1)S(1)}, u32[]{:S(2)}, u32[]{:S(2)}) collective-permute-start(bf16[16,1024]{1,0:T(8,128)(2,1)S(1)} %get-tuple-element.42), channel_id=1, source_target_pairs={{0,17},{1,5},{2,6},{3,18},{4,21},{5,1},{6,2},{7,22},{8,12},{9,24},... | collective-permute-start | bytes 98312 | tf_op jit(solution)/shard_map/ppermute | solution.py:55
  24.0 3.7 %collective-permute-start.8 = (bf16[16,1024]{1,0:T(8,128)(2,1)S(1)}, bf16[16,1024]{1,0:T(8,128)(2,1)S(1)}, u32[]{:S(2)}, u32[]{:S(2)}) collective-permute-start(bf16[16,1024]{1,0:T(8,128)(2,1)S(1)} %get-tuple-element.43), channel_id=1, source_target_pairs={{0,9},{1,15},{2,12},{3,10},{4,13},{5,11},{6,8},{7,14},{8,6},{9,0},... | collective-permute-start | bytes 98312 | tf_op jit(solution)/shard_map/ppermute | solution.py:55
  24.9 3.3 %collective-permute-start.10 = (bf16[16,1024]{1,0:T(8,128)(2,1)S(1)}, bf16[16,1024]{1,0:T(8,128)(2,1)S(1)}, u32[]{:S(2)}, u32[]{:S(2)}) collective-permute-start(bf16[16,1024]{1,0:T(8,128)(2,1)S(1)} %get-tuple-element.44), channel_id=1, source_target_pairs={{0,24},{1,25},{2,26},{3,27},{4,28},{5,29},{6,30},{7,31},{8,16},{9,... | collective-permute-start | bytes 98312 | tf_op jit(solution)/shard_map/ppermute | solution.py:55
  25.8 3.3 %collective-permute-start.9 = (bf16[16,1024]{1,0:T(8,128)(2,1)S(1)}, bf16[16,1024]{1,0:T(8,128)(2,1)S(1)}, u32[]{:S(2)}, u32[]{:S(2)}) collective-permute-start(bf16[16,1024]{1,0:T(8,128)(2,1)S(1)} %get-tuple-element.41.own), channel_id=1, source_target_pairs={{0,24},{1,11},{2,8},{3,27},{4,28},{5,15},{6,12},{7,31},{8,2},{9,17... | collective-permute-start | bytes 98312 | tf_op jit(solution)/shard_map/ppermute | solution.py:55
  29.2 6.1 %collective-permute-start.12 = (bf16[64,1024]{1,0:T(8,128)(2,1)S(1)}, bf16[64,1024]{1,0:T(8,128)(2,1)S(1)}, u32[]{:S(2)}, u32[]{:S(2)}) collective-permute-start(bf16[64,1024]{1,0:T(8,128)(2,1)S(1)} %get-tuple-element.46), channel_id=1, source_target_pairs={{0,4},{1,16},{2,19},{3,7},{4,0},{5,20},{6,23},{7,3},{8,25},{9,13},... | collective-permute-start | bytes 393224 | tf_op jit(solution)/shard_map/ppermute | solution.py:55
  30.3 6.4 %collective-permute-start.13 = (bf16[64,1024]{1,0:T(8,128)(2,1)S(1)}, bf16[64,1024]{1,0:T(8,128)(2,1)S(1)}, u32[]{:S(2)}, u32[]{:S(2)}) collective-permute-start(bf16[64,1024]{1,0:T(8,128)(2,1)S(1)} %get-tuple-element.47), channel_id=1, source_target_pairs={{0,14},{1,8},{2,11},{3,13},{4,10},{5,12},{6,15},{7,9},{8,1},{9,7},... | collective-permute-start | bytes 393224 | tf_op jit(solution)/shard_map/ppermute | solution.py:55
  31.2 6.8 %collective-permute-start.14 = (bf16[64,1024]{1,0:T(8,128)(2,1)S(1)}, bf16[64,1024]{1,0:T(8,128)(2,1)S(1)}, u32[]{:S(2)}, u32[]{:S(2)}) collective-permute-start(bf16[64,1024]{1,0:T(8,128)(2,1)S(1)} %get-tuple-element.45.refs_0_), channel_id=1, source_target_pairs={{0,10},{1,25},{2,26},{3,9},{4,14},{5,29},{6,30},{7,13},{8,16},{9,3... | collective-permute-start | bytes 393224 | tf_op jit(solution)/shard_map/ppermute | solution.py:55
  32.5 5.5 %collective-permute-start.11 = (bf16[64,1024]{1,0:T(8,128)(2,1)S(1)}, bf16[64,1024]{1,0:T(8,128)(2,1)S(1)}, u32[]{:S(2)}, u32[]{:S(2)}) collective-permute-start(bf16[64,1024]{1,0:T(8,128)(2,1)S(1)} %get-tuple-element.45.refs_0_), channel_id=1, source_target_pairs={{0,8},{1,9},{2,10},{3,11},{4,12},{5,13},{6,14},{7,15},{8,0},{9,1},... | collective-permute-start | bytes 393224 | tf_op jit(solution)/shard_map/ppermute | solution.py:55
  38.0 1.9 %collective-permute-start.15 = (bf16[224,1024]{1,0:T(8,128)(2,1)S(1)}, bf16[224,1024]{1,0:T(8,128)(2,1)S(1)}, u32[]{:S(2)}, u32[]{:S(2)}) collective-permute-start(bf16[224,1024]{1,0:T(8,128)(2,1)S(1)} %shard_map.84), channel_id=1, source_target_pairs={{0,8},{1,9},{2,10},{3,11},{4,12},{5,13},{6,14},{7,15},{8,0},{9,1},... | collective-permute-start | bytes 1376264 | tf_op jit(solution)/shard_map/ppermute | solution.py:55

commit v8 on v7

--- a/solution.py
+++ b/solution.py
@@ -236,43 +236,42 @@
                 out[block(8 * w + 2 * to_z + to_y, rows), block(to_x, quarter)] = ref[at:at + rows, :]
 
 
-def write(sibling, parts, grads, m, v, w_out, m_out, v_out, half, new_m, new_v, sems):
-    role, x, _, _, _ = place()
-    side = role ^ sibling
-    half_blocks(sibling, parts, half)
-    copies = [pltpu.make_async_copy(half, w_out.at[:, block(side, half.shape[1])], sems.at[0])]
-    copies[0].start()
-    for far, grad in enumerate(grads):
-        at = block(2 * side + (x ^ far), grad.shape[1])
-        new_m[far], new_v[far] = adamw_moments(m[:, at], v[:, at], grad[...].astype(F32))
-        for source, out in ((new_m, m_out), (new_v, v_out)):
-            copies.append(pltpu.make_async_copy(source.at[far], out.at[:, at], sems.at[len(copies)]))
-            copies[-1].start()
-    for copy in copies:
-        copy.wait()
-
-
 def pack_kernel(*refs):
-    *parts, _, out = refs
+    *parts, out = refs
     at = 0
     for ref in parts:
         out[at:at + ref.shape[0], :] = ref[...]
         at += ref.shape[0]
 
 
-def write_own_kernel(m, v, grad, far_grad, *refs):
-    parts, refs = refs[:1 + len(STEPS)], refs[1 + len(STEPS):]
-    write(0, parts, (grad, far_grad), m, v, *refs)
-
-
-def write_other_kernel(m, v, own, landed, _w, _m, _v, *refs):
-    size, rows = own.shape[0], m.shape[0]
-    sizes = [size] * len(STEPS) + [rows] * 2
-    parts, at = [], 0
-    for count in sizes:
-        parts.append(landed.at[pl.ds(at, count), :])
-        at += count
-    write(1, [own] + parts[:len(STEPS)], parts[len(STEPS):], m, v, *refs)
+def write_half(sibling, parts, out, half, sem):
+    half_blocks(sibling, parts, half)
+    copy = pltpu.make_async_copy(half, out.at[:, block(place()[0] ^ sibling, half.shape[1])], sem)
+    copy.start()
+    return copy
+
+
+def write_own_kernel(m, v, grad, far_grad, early, *refs):
+    parts, (w_out, m_out, v_out, half, sem, new_m, new_v, sems) = refs[:1 + len(STEPS)], refs[1 + len(STEPS):]
+    copies = [write_half(0, parts, w_out, half, sem)]
+    role, x, _, _, _ = place()
+    rows = grad.shape[0]
+    tail = early.shape[0] - 2 * rows
+    grads = [grad, far_grad] + [early.at[pl.ds(tail + i * rows, rows), :] for i in range(2)]
+    for i, ref in enumerate(grads):
+        cols = block(2 * (role ^ (i >> 1)) + (x ^ (i & 1)), grad.shape[1])
+        new_m[:, cols], new_v[:, cols] = adamw_moments(m[:, cols], v[:, cols], ref[...].astype(F32))
+    for i, (source, out) in enumerate(((new_m, m_out), (new_v, v_out))):
+        copies.append(pltpu.make_async_copy(source, out, sems.at[i]))
+        copies[-1].start()
+    for copy in copies:
+        copy.wait()
+
+
+def write_other_kernel(early, late, _, out, half, sem):
+    size = late.shape[0] // 2
+    parts = [ref.at[pl.ds(i * size, size), :] for ref in (early, late) for i in range(2)]
+    write_half(1, parts, out, half, sem).wait()
 
 
 def body(hidden_acts, out_cotangent, weight, first_moment, second_moment):
@@ -323,22 +322,23 @@
         narrow_back_kernel, [shape((wide_rows, quarter), BF16)] * len(STEPS), parts[-1], *came, far_grad,
     )
     came = [stage(part, step, 1) for step, part in zip(STEPS, parts)]
-    own = to_sibling(parts[-1])
-
-    landed = to_sibling(call(
-        pack_kernel, [shape((len(STEPS) * wide_rows + 2 * rows, quarter), BF16)], *came, grad, far_grad, own,
-    )[0])
-    outs = [shape((all_rows, width), BF16), shape((rows, width), F32), shape((rows, width), F32)]
-    scratch = [pltpu.VMEM((all_rows, half), BF16)] + [pltpu.VMEM((2, rows, quarter), F32)] * 2
-    scratch += [pltpu.SemaphoreType.DMA((5,))]
+
+    def swapped(size, *args):
+        return to_sibling(call(pack_kernel, [shape((size, quarter), BF16)], *args)[0])
+
+    early = swapped(2 * wide_rows + 2 * rows, parts[-1], came[0], grad, far_grad)
+    late = swapped(2 * wide_rows, came[1], came[2])
+    new_w = [shape((all_rows, width), BF16)]
+    moments = [shape((rows, width), F32)] * 2
+    scratch = [pltpu.VMEM((all_rows, half), BF16), pltpu.SemaphoreType.DMA]
+    written, new_m, new_v = call(
+        write_own_kernel, new_w + moments, first_moment, second_moment, grad, far_grad, early, parts[-1], *came,
+        far_out=3, scratch=scratch + [pltpu.VMEM((rows, width), F32)] * 2 + [pltpu.SemaphoreType.DMA((2,))],
+    )
     written = call(
-        write_own_kernel, outs, first_moment, second_moment, grad, far_grad, parts[-1], *came,
-        far_out=3, scratch=scratch,
-    )
-    return tuple(call(
-        write_other_kernel, outs, first_moment, second_moment, own, landed, *written,
-        far_in=(4, 5, 6), far_out=3, scratch=scratch, aliases={4: 0, 5: 1, 6: 2},
-    ))
+        write_other_kernel, new_w, early, late, written, far_in=(2,), far_out=1, scratch=scratch, aliases={2: 0},
+    )[0]
+    return written, new_m, new_v
 
 
 def solution(mesh):

time: 41 us -> 40.6 us (level)
  starting transfers between devices: 17.9 us -> 17.3 us
    ppermute x16, starting transfers between devices: 17.9 us -> 17.3 us  [exchange(): return lax.ppermute(value, ('rep', 'shard'), pairs)]
    pallas_call x11 -> x12, Pallas kernels: 7.16 us -> 7.15 us  [call(): pl.pallas_call(kernel, out_shape=outs, in_specs=[far if i in tuple(far_in...]
where the time goes in v8:
time: 40.6 us; the launch traced here: 40.4 us
  starting transfers between devices  17.3 us (43%)
  waiting for transfers between devices  15.2 us (37%)
  Pallas kernels  7.15 us (18%)
  between operations  0.77 us (2%)
    ppermute x16, starting transfers between devices, exchange(): return lax.ppermute(value, ('rep', 'shard'), pairs)  17.3 us
    ppermute x16, waiting for transfers between devices, exchange(): return lax.ppermute(value, ('rep', 'shard'), pairs)  15.2 us
    pallas_call x12, Pallas kernels, call(): pl.pallas_call(kernel, out_shape=outs, in_specs=[far if i in tuple(far_in...  7.15 us
  transfers between devices with their start and end apart: 16, of which 13 were waited for; matrix products, arithmetic and copies ran while one was open for 0% of the time, Pallas kernels for 8%

profile of v8, /device:TPU:0, one launch (start us, length us, event | category | flops | bytes accessed | tf_op | source)
XLA Modules:
  0.0 40.4 jit_solution(9936270134559488613)
XLA Ops:
  0.6 2.1 %shard_map.76 = (bf16[768,2048]{1,0:T(8,128)(2,1)S(1)}, bf16[768,512]{1,0:T(8,128)(2,1)S(1)}) custom-call(bf16[768,4096]{1,0:T(8,128)(2,1)} %cots_ref.3), custom_call_target="tpu_custom_call" | custom-call | tf_op jit(solution)/shard_map/pallas_call | solution.py:37
  2.8 0.6 %shard_map.77 = (bf16[128,2048]{1,0:T(8,128)(2,1)S(1)}, bf16[128,768]{1,0:T(8,128)(2,1)S(1)}) custom-call(bf16[768,128]{1,0:T(8,128)(2,1)S(1)} %copy-done.2, bf16[768,2048]{1,0:T(8,128)(2,1)S(1)} %get-tuple-element.27.cots), custom_call_target="tpu_custom_call" | custom-call | tf_op jit(solution)/shard_map/pallas_call | solution.py:37
  4.0 2.1 %shard_map.78.kept = f32[128,2048]{1,0:T(8,128)S(1)} custom-call(bf16[128,768]{1,0:T(8,128)(2,1)S(1)} %get-tuple-element.28.turned, bf16[768,512]{1,0:T(8,128)(2,1)S(1)} %get-tuple-element.29.first, bf16[768,4096]{1,0:T(8,128)(2,1)} %cots_ref.3), custom_call_target="tpu_custom_call" | custom-call | tf_op jit(solution)/shard_map/pallas_call | solution.py:37
  6.2 3.5 %collective-permute-start.1 = (bf16[64,1024]{1,0:T(8,128)(2,1)S(1)}, bf16[64,1024]{1,0:T(8,128)(2,1)S(1)}, u32[]{:S(2)}, u32[]{:S(2)}) collective-permute-start(bf16[64,1024]{1,0:T(8,128)(2,1)S(1)} %get-tuple-element.32), channel_id=1, source_target_pairs={{0,17},{1,5},{2,6},{3,18},{4,21},{5,1},{6,2},{7,22},{8,12},{9,24},... | collective-permute-start | bytes 393224 | tf_op jit(solution)/shard_map/ppermute | solution.py:55
  10.1 2.6 %collective-permute-done.1.refs_0_ = bf16[64,1024]{1,0:T(8,128)(2,1)S(1)} collective-permute-done((bf16[64,1024]{1,0:T(8,128)(2,1)S(1)}, bf16[64,1024]{1,0:T(8,128)(2,1)S(1)}, u32[]{:S(2)}, u32[]{:S(2)}) %collective-permute-start.1) | collective-permute-done | bytes 131104 | tf_op jit(solution)/shard_map/ppermute | solution.py:55
  12.7 1.4 %collective-permute-done.2.refs_1_ = bf16[64,1024]{1,0:T(8,128)(2,1)S(1)} collective-permute-done((bf16[64,1024]{1,0:T(8,128)(2,1)S(1)}, bf16[64,1024]{1,0:T(8,128)(2,1)S(1)}, u32[]{:S(2)}, u32[]{:S(2)}) %collective-permute-start.2) | collective-permute-done | bytes 131104 | tf_op jit(solution)/shard_map/ppermute | solution.py:55
  14.5 2.8 %collective-permute-start.4 = (bf16[16,1024]{1,0:T(8,128)(2,1)S(1)}, bf16[16,1024]{1,0:T(8,128)(2,1)S(1)}, u32[]{:S(2)}, u32[]{:S(2)}) collective-permute-start(bf16[16,1024]{1,0:T(8,128)(2,1)S(1)} %get-tuple-element.36), channel_id=1, source_target_pairs={{0,4},{1,16},{2,19},{3,7},{4,0},{5,20},{6,23},{7,3},{8,25},{9,13},... | collective-permute-start | bytes 98312 | tf_op jit(solution)/shard_map/ppermute | solution.py:55
  17.3 1.2 %collective-permute-start.5 = (bf16[16,1024]{1,0:T(8,128)(2,1)S(1)}, bf16[16,1024]{1,0:T(8,128)(2,1)S(1)}, u32[]{:S(2)}, u32[]{:S(2)}) collective-permute-start(bf16[16,1024]{1,0:T(8,128)(2,1)S(1)} %get-tuple-element.37), channel_id=1, source_target_pairs={{0,14},{1,8},{2,11},{3,13},{4,10},{5,12},{6,15},{7,9},{8,1},{9,7},... | collective-permute-start | bytes 98312 | tf_op jit(solution)/shard_map/ppermute | solution.py:55
  18.6 0.7 %collective-permute-done.4.refs_0_ = bf16[16,1024]{1,0:T(8,128)(2,1)S(1)} collective-permute-done((bf16[16,1024]{1,0:T(8,128)(2,1)S(1)}, bf16[16,1024]{1,0:T(8,128)(2,1)S(1)}, u32[]{:S(2)}, u32[]{:S(2)}) %collective-permute-start.4) | collective-permute-done | bytes 32800 | tf_op jit(solution)/shard_map/ppermute | solution.py:55
  19.4 3.0 %collective-permute-done.5.refs_1_ = bf16[16,1024]{1,0:T(8,128)(2,1)S(1)} collective-permute-done((bf16[16,1024]{1,0:T(8,128)(2,1)S(1)}, bf16[16,1024]{1,0:T(8,128)(2,1)S(1)}, u32[]{:S(2)}, u32[]{:S(2)}) %collective-permute-start.5) | collective-permute-done | bytes 32800 | tf_op jit(solution)/shard_map/ppermute | solution.py:55
  22.5 1.5 %collective-permute-start.7 = (bf16[16,1024]{1,0:T(8,128)(2,1)S(1)}, bf16[16,1024]{1,0:T(8,128)(2,1)S(1)}, u32[]{:S(2)}, u32[]{:S(2)}) collective-permute-start(bf16[16,1024]{1,0:T(8,128)(2,1)S(1)} %get-tuple-element.42), channel_id=1, source_target_pairs={{0,17},{1,5},{2,6},{3,18},{4,21},{5,1},{6,2},{7,22},{8,12},{9,24},... | collective-permute-start | bytes 98312 | tf_op jit(solution)/shard_map/ppermute | solution.py:55
  24.0 0.8 %collective-permute-start.8 = (bf16[16,1024]{1,0:T(8,128)(2,1)S(1)}, bf16[16,1024]{1,0:T(8,128)(2,1)S(1)}, u32[]{:S(2)}, u32[]{:S(2)}) collective-permute-start(bf16[16,1024]{1,0:T(8,128)(2,1)S(1)} %get-tuple-element.43), channel_id=1, source_target_pairs={{0,9},{1,15},{2,12},{3,10},{4,13},{5,11},{6,8},{7,14},{8,6},{9,0},... | collective-permute-start | bytes 98312 | tf_op jit(solution)/shard_map/ppermute | solution.py:55
  24.9 0.9 %collective-permute-start.10 = (bf16[16,1024]{1,0:T(8,128)(2,1)S(1)}, bf16[16,1024]{1,0:T(8,128)(2,1)S(1)}, u32[]{:S(2)}, u32[]{:S(2)}) collective-permute-start(bf16[16,1024]{1,0:T(8,128)(2,1)S(1)} %get-tuple-element.44), channel_id=1, source_target_pairs={{0,24},{1,25},{2,26},{3,27},{4,28},{5,29},{6,30},{7,31},{8,16},{9,... | collective-permute-start | bytes 98312 | tf_op jit(solution)/shard_map/ppermute | solution.py:55
  25.8 0.8 %collective-permute-start.9 = (bf16[16,1024]{1,0:T(8,128)(2,1)S(1)}, bf16[16,1024]{1,0:T(8,128)(2,1)S(1)}, u32[]{:S(2)}, u32[]{:S(2)}) collective-permute-start(bf16[16,1024]{1,0:T(8,128)(2,1)S(1)} %get-tuple-element.41.own), channel_id=1, source_target_pairs={{0,24},{1,11},{2,8},{3,27},{4,28},{5,15},{6,12},{7,31},{8,2},{9,17... | collective-permute-start | bytes 98312 | tf_op jit(solution)/shard_map/ppermute | solution.py:55
  26.6 0.9 %collective-permute-done.7.refs_0_ = bf16[16,1024]{1,0:T(8,128)(2,1)S(1)} collective-permute-done((bf16[16,1024]{1,0:T(8,128)(2,1)S(1)}, bf16[16,1024]{1,0:T(8,128)(2,1)S(1)}, u32[]{:S(2)}, u32[]{:S(2)}) %collective-permute-start.7) | collective-permute-done | bytes 32800 | tf_op jit(solution)/shard_map/ppermute | solution.py:55
  28.2 0.9 %collective-permute-done.9.refs_2_ = bf16[16,1024]{1,0:T(8,128)(2,1)S(1)} collective-permute-done((bf16[16,1024]{1,0:T(8,128)(2,1)S(1)}, bf16[16,1024]{1,0:T(8,128)(2,1)S(1)}, u32[]{:S(2)}, u32[]{:S(2)}) %collective-permute-start.9) | collective-permute-done | bytes 32800 | tf_op jit(solution)/shard_map/ppermute | solution.py:55
  29.2 1.1 %collective-permute-start.11 = (bf16[64,1024]{1,0:T(8,128)(2,1)S(1)}, bf16[64,1024]{1,0:T(8,128)(2,1)S(1)}, u32[]{:S(2)}, u32[]{:S(2)}) collective-permute-start(bf16[64,1024]{1,0:T(8,128)(2,1)S(1)} %get-tuple-element.46), channel_id=1, source_target_pairs={{0,4},{1,16},{2,19},{3,7},{4,0},{5,20},{6,23},{7,3},{8,25},{9,13},... | collective-permute-start | bytes 393224 | tf_op jit(solution)/shard_map/ppermute | solution.py:55
  30.3 0.9 %collective-permute-start.13 = (bf16[64,1024]{1,0:T(8,128)(2,1)S(1)}, bf16[64,1024]{1,0:T(8,128)(2,1)S(1)}, u32[]{:S(2)}, u32[]{:S(2)}) collective-permute-start(bf16[64,1024]{1,0:T(8,128)(2,1)S(1)} %get-tuple-element.47), channel_id=1, source_target_pairs={{0,14},{1,8},{2,11},{3,13},{4,10},{5,12},{6,15},{7,9},{8,1},{9,7},... | collective-permute-start | bytes 393224 | tf_op jit(solution)/shard_map/ppermute | solution.py:55
  31.2 1.3 %collective-permute-start.14 = (bf16[64,1024]{1,0:T(8,128)(2,1)S(1)}, bf16[64,1024]{1,0:T(8,128)(2,1)S(1)}, u32[]{:S(2)}, u32[]{:S(2)}) collective-permute-start(bf16[64,1024]{1,0:T(8,128)(2,1)S(1)} %get-tuple-element.45.refs_0_), channel_id=1, source_target_pairs={{0,10},{1,25},{2,26},{3,9},{4,14},{5,29},{6,30},{7,13},{8,16},{9,3... | collective-permute-start | bytes 393224 | tf_op jit(solution)/shard_map/ppermute | solution.py:55
  32.5 2.8 %collective-permute-done.11.refs_1_ = bf16[64,1024]{1,0:T(8,128)(2,1)S(1)} collective-permute-done((bf16[64,1024]{1,0:T(8,128)(2,1)S(1)}, bf16[64,1024]{1,0:T(8,128)(2,1)S(1)}, u32[]{:S(2)}, u32[]{:S(2)}) %collective-permute-start.11) | collective-permute-done | bytes 131104 | tf_op jit(solution)/shard_map/ppermute | solution.py:55
  35.3 1.2 %collective-permute-start.12 = (bf16[160,1024]{1,0:T(8,128)(2,1)S(1)}, bf16[160,1024]{1,0:T(8,128)(2,1)S(1)}, u32[]{:S(2)}, u32[]{:S(2)}) collective-permute-start(bf16[160,1024]{1,0:T(8,128)(2,1)S(1)} %shard_map.84), channel_id=1, source_target_pairs={{0,8},{1,9},{2,10},{3,11},{4,12},{5,13},{6,14},{7,15},{8,0},{9,1},... | collective-permute-start | bytes 983048 | tf_op jit(solution)/shard_map/ppermute | solution.py:55
  36.6 1.3 %collective-permute-done.14.refs_1_.refs_3_ = bf16[64,1024]{1,0:T(8,128)(2,1)S(1)} collective-permute-done((bf16[64,1024]{1,0:T(8,128)(2,1)S(1)}, bf16[64,1024]{1,0:T(8,128)(2,1)S(1)}, u32[]{:S(2)}, u32[]{:S(2)}) %collective-permute-start.14) | collective-permute-done | bytes 131104 | tf_op jit(solution)/shard_map/ppermute | solution.py:55
  38.2 1.1 %shard_map.86 = (bf16[128,4096]{1,0:T(8,128)(2,1)}, f32[16,4096]{1,0:T(8,128)}, f32[16,4096]{1,0:T(8,128)}) custom-call(f32[16,4096]{1,0:T(8,128)S(1)} %copy-done, f32[16,4096]{1,0:T(8,128)S(1)} %copy-done.1, bf16[16,1024]{1,0:T(8,128)(2,1)S(1)} %get-tuple-element.39.grad.refs_2_, bf16[16,1024]{1,0:T(8,128)(2,1)S(1)} %collective-permute-done.10.refs_3_.far_grad, ...), custom_call_target="tpu_custom_call" | custom-call | tf_op jit(solution)/shard_map/pallas_call | solution.py:37
  39.6 0.8 %shard_map.87 = bf16[128,4096]{1,0:T(8,128)(2,1)} custom-call(bf16[160,1024]{1,0:T(8,128)(2,1)S(1)} %collective-permute-done.12.early, bf16[128,1024]{1,0:T(8,128)(2,1)S(1)} %collective-permute-done.15.late, bf16[128,4096]{1,0:T(8,128)(2,1)} %get-tuple-element.48._), custom_call_target="tpu_custom_call", output_to_operand_aliasing={{}: (2, {})} | custom-call | tf_op jit(solution)/shard_map/pallas_call | solution.py:37
  (28 shorter events, 3.2 us)
Async XLA Ops:
  0.6 2.2 %copy-start.2 = (bf16[768,128]{1,0:T(8,128)(2,1)S(1)}, bf16[768,128]{1,0:T(8,128)(2,1)}, u32[]{:S(2)}) copy-start(bf16[768,128]{1,0:T(8,128)(2,1)} %acts.1) | copy-start | bytes 589828
  2.8 19.6 %copy-start = (f32[16,4096]{1,0:T(8,128)S(1)}, f32[16,4096]{1,0:T(8,128)}, u32[]{:S(2)}) copy-start(f32[16,4096]{1,0:T(8,128)} %m.3) | copy-start | bytes 786436
  2.8 19.6 %copy-start.1 = (f32[16,4096]{1,0:T(8,128)S(1)}, f32[16,4096]{1,0:T(8,128)}, u32[]{:S(2)}) copy-start(f32[16,4096]{1,0:T(8,128)} %v.3) | copy-start | bytes 786436
  2.8 19.6 %copy-start.3 = (bf16[16,4096]{1,0:T(8,128)(2,1)S(1)}, bf16[16,4096]{1,0:T(8,128)(2,1)}, u32[]{:S(2)}) copy-start(bf16[16,4096]{1,0:T(8,128)(2,1)} %w.1) | copy-start | bytes 393220
  3.5 2.6 %collective-permute-start = (bf16[128,2048]{1,0:T(8,128)(2,1)S(1)}, bf16[128,2048]{1,0:T(8,128)(2,1)S(1)}, u32[]{:S(2)}, u32[]{:S(2)}) collective-permute-start(bf16[128,2048]{1,0:T(8,128)(2,1)S(1)} %get-tuple-element.30), channel_id=1, source_target_pairs={{0,8},{1,9},{2,10},{3,11},{4,12},{5,13},{6,14},{7,15},{8,0},{9,1},... | collective-permute-start | bytes 1572872 | tf_op jit(solution)/shard_map/ppermute | solution.py:55
  6.2 6.5 %collective-permute-start.1 = (bf16[64,1024]{1,0:T(8,128)(2,1)S(1)}, bf16[64,1024]{1,0:T(8,128)(2,1)S(1)}, u32[]{:S(2)}, u32[]{:S(2)}) collective-permute-start(bf16[64,1024]{1,0:T(8,128)(2,1)S(1)} %get-tuple-element.32), channel_id=1, source_target_pairs={{0,17},{1,5},{2,6},{3,18},{4,21},{5,1},{6,2},{7,22},{8,12},{9,24},... | collective-permute-start | bytes 393224 | tf_op jit(solution)/shard_map/ppermute | solution.py:55
  9.7 4.4 %collective-permute-start.2 = (bf16[64,1024]{1,0:T(8,128)(2,1)S(1)}, bf16[64,1024]{1,0:T(8,128)(2,1)S(1)}, u32[]{:S(2)}, u32[]{:S(2)}) collective-permute-start(bf16[64,1024]{1,0:T(8,128)(2,1)S(1)} %get-tuple-element.33), channel_id=1, source_target_pairs={{0,9},{1,15},{2,12},{3,10},{4,13},{5,11},{6,8},{7,14},{8,6},{9,0},... | collective-permute-start | bytes 393224 | tf_op jit(solution)/shard_map/ppermute | solution.py:55
  10.0 4.4 %collective-permute-start.3 = (bf16[64,1024]{1,0:T(8,128)(2,1)S(1)}, bf16[64,1024]{1,0:T(8,128)(2,1)S(1)}, u32[]{:S(2)}, u32[]{:S(2)}) collective-permute-start(bf16[64,1024]{1,0:T(8,128)(2,1)S(1)} %get-tuple-element.34), channel_id=1, source_target_pairs={{0,24},{1,11},{2,8},{3,27},{4,28},{5,15},{6,12},{7,31},{8,2},{9,17... | collective-permute-start | bytes 393224 | tf_op jit(solution)/shard_map/ppermute | solution.py:55
  14.5 4.9 %collective-permute-start.4 = (bf16[16,1024]{1,0:T(8,128)(2,1)S(1)}, bf16[16,1024]{1,0:T(8,128)(2,1)S(1)}, u32[]{:S(2)}, u32[]{:S(2)}) collective-permute-start(bf16[16,1024]{1,0:T(8,128)(2,1)S(1)} %get-tuple-element.36), channel_id=1, source_target_pairs={{0,4},{1,16},{2,19},{3,7},{4,0},{5,20},{6,23},{7,3},{8,25},{9,13},... | collective-permute-start | bytes 98312 | tf_op jit(solution)/shard_map/ppermute | solution.py:55
  17.3 5.1 %collective-permute-start.5 = (bf16[16,1024]{1,0:T(8,128)(2,1)S(1)}, bf16[16,1024]{1,0:T(8,128)(2,1)S(1)}, u32[]{:S(2)}, u32[]{:S(2)}) collective-permute-start(bf16[16,1024]{1,0:T(8,128)(2,1)S(1)} %get-tuple-element.37), channel_id=1, source_target_pairs={{0,14},{1,8},{2,11},{3,13},{4,10},{5,12},{6,15},{7,9},{8,1},{9,7},... | collective-permute-start | bytes 98312 | tf_op jit(solution)/shard_map/ppermute | solution.py:55
  18.4 4.0 %collective-permute-start.6 = (bf16[16,1024]{1,0:T(8,128)(2,1)S(1)}, bf16[16,1024]{1,0:T(8,128)(2,1)S(1)}, u32[]{:S(2)}, u32[]{:S(2)}) collective-permute-start(bf16[16,1024]{1,0:T(8,128)(2,1)S(1)} %get-tuple-element.38), channel_id=1, source_target_pairs={{0,10},{1,25},{2,26},{3,9},{4,14},{5,29},{6,30},{7,13},{8,16},{9,3... | collective-permute-start | bytes 98312 | tf_op jit(solution)/shard_map/ppermute | solution.py:55
  22.5 5.0 %collective-permute-start.7 = (bf16[16,1024]{1,0:T(8,128)(2,1)S(1)}, bf16[16,1024]{1,0:T(8,128)(2,1)S(1)}, u32[]{:S(2)}, u32[]{:S(2)}) collective-permute-start(bf16[16,1024]{1,0:T(8,128)(2,1)S(1)} %get-tuple-element.42), channel_id=1, source_target_pairs={{0,17},{1,5},{2,6},{3,18},{4,21},{5,1},{6,2},{7,22},{8,12},{9,24},... | collective-permute-start | bytes 98312 | tf_op jit(solution)/shard_map/ppermute | solution.py:55
  24.0 3.7 %collective-permute-start.8 = (bf16[16,1024]{1,0:T(8,128)(2,1)S(1)}, bf16[16,1024]{1,0:T(8,128)(2,1)S(1)}, u32[]{:S(2)}, u32[]{:S(2)}) collective-permute-start(bf16[16,1024]{1,0:T(8,128)(2,1)S(1)} %get-tuple-element.43), channel_id=1, source_target_pairs={{0,9},{1,15},{2,12},{3,10},{4,13},{5,11},{6,8},{7,14},{8,6},{9,0},... | collective-permute-start | bytes 98312 | tf_op jit(solution)/shard_map/ppermute | solution.py:55
  24.9 3.3 %collective-permute-start.10 = (bf16[16,1024]{1,0:T(8,128)(2,1)S(1)}, bf16[16,1024]{1,0:T(8,128)(2,1)S(1)}, u32[]{:S(2)}, u32[]{:S(2)}) collective-permute-start(bf16[16,1024]{1,0:T(8,128)(2,1)S(1)} %get-tuple-element.44), channel_id=1, source_target_pairs={{0,24},{1,25},{2,26},{3,27},{4,28},{5,29},{6,30},{7,31},{8,16},{9,... | collective-permute-start | bytes 98312 | tf_op jit(solution)/shard_map/ppermute | solution.py:55
  25.8 3.3 %collective-permute-start.9 = (bf16[16,1024]{1,0:T(8,128)(2,1)S(1)}, bf16[16,1024]{1,0:T(8,128)(2,1)S(1)}, u32[]{:S(2)}, u32[]{:S(2)}) collective-permute-start(bf16[16,1024]{1,0:T(8,128)(2,1)S(1)} %get-tuple-element.41.own), channel_id=1, source_target_pairs={{0,24},{1,11},{2,8},{3,27},{4,28},{5,15},{6,12},{7,31},{8,2},{9,17... | collective-permute-start | bytes 98312 | tf_op jit(solution)/shard_map/ppermute | solution.py:55
  29.2 6.1 %collective-permute-start.11 = (bf16[64,1024]{1,0:T(8,128)(2,1)S(1)}, bf16[64,1024]{1,0:T(8,128)(2,1)S(1)}, u32[]{:S(2)}, u32[]{:S(2)}) collective-permute-start(bf16[64,1024]{1,0:T(8,128)(2,1)S(1)} %get-tuple-element.46), channel_id=1, source_target_pairs={{0,4},{1,16},{2,19},{3,7},{4,0},{5,20},{6,23},{7,3},{8,25},{9,13},... | collective-permute-start | bytes 393224 | tf_op jit(solution)/shard_map/ppermute | solution.py:55
  30.3 6.4 %collective-permute-start.13 = (bf16[64,1024]{1,0:T(8,128)(2,1)S(1)}, bf16[64,1024]{1,0:T(8,128)(2,1)S(1)}, u32[]{:S(2)}, u32[]{:S(2)}) collective-permute-start(bf16[64,1024]{1,0:T(8,128)(2,1)S(1)} %get-tuple-element.47), channel_id=1, source_target_pairs={{0,14},{1,8},{2,11},{3,13},{4,10},{5,12},{6,15},{7,9},{8,1},{9,7},... | collective-permute-start | bytes 393224 | tf_op jit(solution)/shard_map/ppermute | solution.py:55
  31.2 6.8 %collective-permute-start.14 = (bf16[64,1024]{1,0:T(8,128)(2,1)S(1)}, bf16[64,1024]{1,0:T(8,128)(2,1)S(1)}, u32[]{:S(2)}, u32[]{:S(2)}) collective-permute-start(bf16[64,1024]{1,0:T(8,128)(2,1)S(1)} %get-tuple-element.45.refs_0_), channel_id=1, source_target_pairs={{0,10},{1,25},{2,26},{3,9},{4,14},{5,29},{6,30},{7,13},{8,16},{9,3... | collective-permute-start | bytes 393224 | tf_op jit(solution)/shard_map/ppermute | solution.py:55
  35.3 2.9 %collective-permute-start.12 = (bf16[160,1024]{1,0:T(8,128)(2,1)S(1)}, bf16[160,1024]{1,0:T(8,128)(2,1)S(1)}, u32[]{:S(2)}, u32[]{:S(2)}) collective-permute-start(bf16[160,1024]{1,0:T(8,128)(2,1)S(1)} %shard_map.84), channel_id=1, source_target_pairs={{0,8},{1,9},{2,10},{3,11},{4,12},{5,13},{6,14},{7,15},{8,0},{9,1},... | collective-permute-start | bytes 983048 | tf_op jit(solution)/shard_map/ppermute | solution.py:55
  38.0 1.6 %collective-permute-start.15 = (bf16[128,1024]{1,0:T(8,128)(2,1)S(1)}, bf16[128,1024]{1,0:T(8,128)(2,1)S(1)}, u32[]{:S(2)}, u32[]{:S(2)}) collective-permute-start(bf16[128,1024]{1,0:T(8,128)(2,1)S(1)} %shard_map.85), channel_id=1, source_target_pairs={{0,8},{1,9},{2,10},{3,11},{4,12},{5,13},{6,14},{7,15},{8,0},{9,1},... | collective-permute-start | bytes 786440 | tf_op jit(solution)/shard_map/ppermute | solution.py:55

commit v9 on v8

--- a/solution.py
+++ b/solution.py
@@ -114,15 +114,10 @@
     return pl.ds(pl.multiple_of(index * size, size), size)
 
 
-def load_kernel(cots_ref, away, first, sems):
-    role = place()[0]
-    copies = []
-    for out, side in ((away, 1 - role), (first, role)):
-        at = pl.ds(pl.multiple_of(side * away.shape[1], CHUNK), out.shape[1])
-        copies.append(pltpu.make_async_copy(cots_ref.at[:, at], out, sems.at[len(copies)]))
-        copies[-1].start()
-    for copy in copies:
-        copy.wait()
+def load_kernel(cots_ref, away, sem):
+    copy = pltpu.make_async_copy(cots_ref.at[:, block(1 - place()[0], away.shape[1])], away, sem)
+    copy.start()
+    copy.wait()
 
 
 def away_kernel(acts, cots, out, turned):
@@ -132,20 +127,18 @@
         out[:, at] = jnp.dot(turned[...], cots[:, at], preferred_element_type=F32).astype(BF16)
 
 
-def kept_kernel(turned, first, cots_ref, out, cots, sems):
+def kept_kernel(turned, cots_ref, out, cots, sems):
     role = place()[0]
-    ready, count = first.shape[1] // CHUNK, out.shape[1] // CHUNK
+    count = cots.shape[0]
     copies = []
-    for i in range(ready, count):
+    for i in range(count):
         source = cots_ref.at[:, block(role * count + i, CHUNK)]
-        copies.append(pltpu.make_async_copy(source, cots.at[i - ready], sems.at[i - ready]))
+        copies.append(pltpu.make_async_copy(source, cots.at[i], sems.at[i]))
         copies[-1].start()
     for i in range(count):
+        copies[i].wait()
         at = slice(i * CHUNK, (i + 1) * CHUNK)
-        if i >= ready:
-            copies[i - ready].wait()
-        chunk = cots[i - ready] if i >= ready else first[:, at]
-        out[:, at] = jnp.dot(turned[...], chunk, preferred_element_type=F32)
+        out[:, at] = jnp.dot(turned[...], cots[i], preferred_element_type=F32)
 
 
 def wide_kernel(rows, kept, came, own, *pieces):
@@ -281,19 +274,18 @@
     rest = lax.axis_size("shard") // 8
     wide_rows, narrow_rows = all_rows // 2, all_rows // 8
 
-    away_cots, first = call(
-        load_kernel, [shape((tokens, half), BF16), shape((tokens, CHUNK), BF16)], out_cotangent,
-        far_in=(0,), scratch=[pltpu.SemaphoreType.DMA((2,))], limit=LOAD_LIMIT,
-    )
+    away_cots = call(
+        load_kernel, [shape((tokens, half), BF16)], out_cotangent,
+        far_in=(0,), scratch=[pltpu.SemaphoreType.DMA], limit=LOAD_LIMIT,
+    )[0]
     away, turned = call(
         away_kernel, [shape((all_rows, half), BF16), shape((all_rows, tokens), BF16)], hidden_acts, away_cots,
     )
     came = to_sibling(away)
-    later = half // CHUNK - 1
+    count = half // CHUNK
     kept = call(
-        kept_kernel, [shape((all_rows, half), F32)], turned, first, out_cotangent,
-        far_in=(2,), limit=KEPT_LIMIT,
-        scratch=[pltpu.VMEM((later, tokens, CHUNK), BF16), pltpu.SemaphoreType.DMA((later,))],
+        kept_kernel, [shape((all_rows, half), F32)], turned, out_cotangent, far_in=(1,), limit=KEPT_LIMIT,
+        scratch=[pltpu.VMEM((count, tokens, CHUNK), BF16), pltpu.SemaphoreType.DMA((count,))],
     )[0]
 
     def split(kernel, size, parts, *args):

time: 40.6 us -> 40.6 us (level)
  transfers between devices with their start and end apart: 16 -> 16, of which waited for: 13 -> 13; matrix products, arithmetic and copies ran while one was open for 0% -> 0% of each run, Pallas kernels for 8% -> 9%
where the time goes in v9:
time: 40.6 us; the launch traced here: 40.4 us
  starting transfers between devices  17.3 us (43%)
  waiting for transfers between devices  15.2 us (37%)
  Pallas kernels  7.14 us (18%)
  between operations  0.77 us (2%)
    ppermute x16, starting transfers between devices, exchange(): return lax.ppermute(value, ('rep', 'shard'), pairs)  17.3 us
    ppermute x16, waiting for transfers between devices, exchange(): return lax.ppermute(value, ('rep', 'shard'), pairs)  15.2 us
    pallas_call x12, Pallas kernels, call(): pl.pallas_call(kernel, out_shape=outs, in_specs=[far if i in tuple(far_in...  7.14 us
  transfers between devices with their start and end apart: 16, of which 13 were waited for; matrix products, arithmetic and copies ran while one was open for 0% of the time, Pallas kernels for 9%

profile of v9, /device:TPU:0, one launch (start us, length us, event | category | flops | bytes accessed | tf_op | source)
XLA Modules:
  0.0 40.4 jit_solution(10511503794123674207)
XLA Ops:
  0.6 1.9 %shard_map.76.cots = bf16[768,2048]{1,0:T(8,128)(2,1)S(1)} custom-call(bf16[768,4096]{1,0:T(8,128)(2,1)} %cots_ref.3), custom_call_target="tpu_custom_call" | custom-call | tf_op jit(solution)/shard_map/pallas_call | solution.py:37
  2.6 0.6 %shard_map.77 = (bf16[128,2048]{1,0:T(8,128)(2,1)S(1)}, bf16[128,768]{1,0:T(8,128)(2,1)S(1)}) custom-call(bf16[768,128]{1,0:T(8,128)(2,1)S(1)} %copy-done.2, bf16[768,2048]{1,0:T(8,128)(2,1)S(1)} %shard_map.76.cots), custom_call_target="tpu_custom_call" | custom-call | tf_op jit(solution)/shard_map/pallas_call | solution.py:37
  3.8 2.3 %shard_map.78.kept = f32[128,2048]{1,0:T(8,128)S(1)} custom-call(bf16[128,768]{1,0:T(8,128)(2,1)S(1)} %get-tuple-element.25.turned, bf16[768,4096]{1,0:T(8,128)(2,1)} %cots_ref.3), custom_call_target="tpu_custom_call" | custom-call | tf_op jit(solution)/shard_map/pallas_call | solution.py:37
  6.2 3.5 %collective-permute-start.1 = (bf16[64,1024]{1,0:T(8,128)(2,1)S(1)}, bf16[64,1024]{1,0:T(8,128)(2,1)S(1)}, u32[]{:S(2)}, u32[]{:S(2)}) collective-permute-start(bf16[64,1024]{1,0:T(8,128)(2,1)S(1)} %get-tuple-element.28), channel_id=1, source_target_pairs={{0,17},{1,5},{2,6},{3,18},{4,21},{5,1},{6,2},{7,22},{8,12},{9,24},... | collective-permute-start | bytes 393224 | tf_op jit(solution)/shard_map/ppermute | solution.py:55
  10.1 2.6 %collective-permute-done.1.refs_0_ = bf16[64,1024]{1,0:T(8,128)(2,1)S(1)} collective-permute-done((bf16[64,1024]{1,0:T(8,128)(2,1)S(1)}, bf16[64,1024]{1,0:T(8,128)(2,1)S(1)}, u32[]{:S(2)}, u32[]{:S(2)}) %collective-permute-start.1) | collective-permute-done | bytes 131104 | tf_op jit(solution)/shard_map/ppermute | solution.py:55
  12.6 1.4 %collective-permute-done.2.refs_1_ = bf16[64,1024]{1,0:T(8,128)(2,1)S(1)} collective-permute-done((bf16[64,1024]{1,0:T(8,128)(2,1)S(1)}, bf16[64,1024]{1,0:T(8,128)(2,1)S(1)}, u32[]{:S(2)}, u32[]{:S(2)}) %collective-permute-start.2) | collective-permute-done | bytes 131104 | tf_op jit(solution)/shard_map/ppermute | solution.py:55
  14.5 2.8 %collective-permute-start.4 = (bf16[16,1024]{1,0:T(8,128)(2,1)S(1)}, bf16[16,1024]{1,0:T(8,128)(2,1)S(1)}, u32[]{:S(2)}, u32[]{:S(2)}) collective-permute-start(bf16[16,1024]{1,0:T(8,128)(2,1)S(1)} %get-tuple-element.32), channel_id=1, source_target_pairs={{0,4},{1,16},{2,19},{3,7},{4,0},{5,20},{6,23},{7,3},{8,25},{9,13},... | collective-permute-start | bytes 98312 | tf_op jit(solution)/shard_map/ppermute | solution.py:55
  17.3 1.2 %collective-permute-start.5 = (bf16[16,1024]{1,0:T(8,128)(2,1)S(1)}, bf16[16,1024]{1,0:T(8,128)(2,1)S(1)}, u32[]{:S(2)}, u32[]{:S(2)}) collective-permute-start(bf16[16,1024]{1,0:T(8,128)(2,1)S(1)} %get-tuple-element.33), channel_id=1, source_target_pairs={{0,14},{1,8},{2,11},{3,13},{4,10},{5,12},{6,15},{7,9},{8,1},{9,7},... | collective-permute-start | bytes 98312 | tf_op jit(solution)/shard_map/ppermute | solution.py:55
  18.6 0.7 %collective-permute-done.4.refs_0_ = bf16[16,1024]{1,0:T(8,128)(2,1)S(1)} collective-permute-done((bf16[16,1024]{1,0:T(8,128)(2,1)S(1)}, bf16[16,1024]{1,0:T(8,128)(2,1)S(1)}, u32[]{:S(2)}, u32[]{:S(2)}) %collective-permute-start.4) | collective-permute-done | bytes 32800 | tf_op jit(solution)/shard_map/ppermute | solution.py:55
  19.4 3.0 %collective-permute-done.5.refs_1_ = bf16[16,1024]{1,0:T(8,128)(2,1)S(1)} collective-permute-done((bf16[16,1024]{1,0:T(8,128)(2,1)S(1)}, bf16[16,1024]{1,0:T(8,128)(2,1)S(1)}, u32[]{:S(2)}, u32[]{:S(2)}) %collective-permute-start.5) | collective-permute-done | bytes 32800 | tf_op jit(solution)/shard_map/ppermute | solution.py:55
  22.5 1.5 %collective-permute-start.7 = (bf16[16,1024]{1,0:T(8,128)(2,1)S(1)}, bf16[16,1024]{1,0:T(8,128)(2,1)S(1)}, u32[]{:S(2)}, u32[]{:S(2)}) collective-permute-start(bf16[16,1024]{1,0:T(8,128)(2,1)S(1)} %get-tuple-element.38), channel_id=1, source_target_pairs={{0,17},{1,5},{2,6},{3,18},{4,21},{5,1},{6,2},{7,22},{8,12},{9,24},... | collective-permute-start | bytes 98312 | tf_op jit(solution)/shard_map/ppermute | solution.py:55
  24.0 0.8 %collective-permute-start.8 = (bf16[16,1024]{1,0:T(8,128)(2,1)S(1)}, bf16[16,1024]{1,0:T(8,128)(2,1)S(1)}, u32[]{:S(2)}, u32[]{:S(2)}) collective-permute-start(bf16[16,1024]{1,0:T(8,128)(2,1)S(1)} %get-tuple-element.39), channel_id=1, source_target_pairs={{0,9},{1,15},{2,12},{3,10},{4,13},{5,11},{6,8},{7,14},{8,6},{9,0},... | collective-permute-start | bytes 98312 | tf_op jit(solution)/shard_map/ppermute | solution.py:55
  24.9 0.9 %collective-permute-start.10 = (bf16[16,1024]{1,0:T(8,128)(2,1)S(1)}, bf16[16,1024]{1,0:T(8,128)(2,1)S(1)}, u32[]{:S(2)}, u32[]{:S(2)}) collective-permute-start(bf16[16,1024]{1,0:T(8,128)(2,1)S(1)} %get-tuple-element.40), channel_id=1, source_target_pairs={{0,24},{1,25},{2,26},{3,27},{4,28},{5,29},{6,30},{7,31},{8,16},{9,... | collective-permute-start | bytes 98312 | tf_op jit(solution)/shard_map/ppermute | solution.py:55
  25.8 0.8 %collective-permute-start.9 = (bf16[16,1024]{1,0:T(8,128)(2,1)S(1)}, bf16[16,1024]{1,0:T(8,128)(2,1)S(1)}, u32[]{:S(2)}, u32[]{:S(2)}) collective-permute-start(bf16[16,1024]{1,0:T(8,128)(2,1)S(1)} %get-tuple-element.37.own), channel_id=1, source_target_pairs={{0,24},{1,11},{2,8},{3,27},{4,28},{5,15},{6,12},{7,31},{8,2},{9,17... | collective-permute-start | bytes 98312 | tf_op jit(solution)/shard_map/ppermute | solution.py:55
  26.6 0.9 %collective-permute-done.7.refs_0_ = bf16[16,1024]{1,0:T(8,128)(2,1)S(1)} collective-permute-done((bf16[16,1024]{1,0:T(8,128)(2,1)S(1)}, bf16[16,1024]{1,0:T(8,128)(2,1)S(1)}, u32[]{:S(2)}, u32[]{:S(2)}) %collective-permute-start.7) | collective-permute-done | bytes 32800 | tf_op jit(solution)/shard_map/ppermute | solution.py:55
  28.2 0.9 %collective-permute-done.9.refs_2_ = bf16[16,1024]{1,0:T(8,128)(2,1)S(1)} collective-permute-done((bf16[16,1024]{1,0:T(8,128)(2,1)S(1)}, bf16[16,1024]{1,0:T(8,128)(2,1)S(1)}, u32[]{:S(2)}, u32[]{:S(2)}) %collective-permute-start.9) | collective-permute-done | bytes 32800 | tf_op jit(solution)/shard_map/ppermute | solution.py:55
  29.2 1.1 %collective-permute-start.11 = (bf16[64,1024]{1,0:T(8,128)(2,1)S(1)}, bf16[64,1024]{1,0:T(8,128)(2,1)S(1)}, u32[]{:S(2)}, u32[]{:S(2)}) collective-permute-start(bf16[64,1024]{1,0:T(8,128)(2,1)S(1)} %get-tuple-element.42), channel_id=1, source_target_pairs={{0,4},{1,16},{2,19},{3,7},{4,0},{5,20},{6,23},{7,3},{8,25},{9,13},... | collective-permute-start | bytes 393224 | tf_op jit(solution)/shard_map/ppermute | solution.py:55
  30.3 0.9 %collective-permute-start.13 = (bf16[64,1024]{1,0:T(8,128)(2,1)S(1)}, bf16[64,1024]{1,0:T(8,128)(2,1)S(1)}, u32[]{:S(2)}, u32[]{:S(2)}) collective-permute-start(bf16[64,1024]{1,0:T(8,128)(2,1)S(1)} %get-tuple-element.43), channel_id=1, source_target_pairs={{0,14},{1,8},{2,11},{3,13},{4,10},{5,12},{6,15},{7,9},{8,1},{9,7},... | collective-permute-start | bytes 393224 | tf_op jit(solution)/shard_map/ppermute | solution.py:55
  31.2 1.3 %collective-permute-start.14 = (bf16[64,1024]{1,0:T(8,128)(2,1)S(1)}, bf16[64,1024]{1,0:T(8,128)(2,1)S(1)}, u32[]{:S(2)}, u32[]{:S(2)}) collective-permute-start(bf16[64,1024]{1,0:T(8,128)(2,1)S(1)} %get-tuple-element.41.refs_0_), channel_id=1, source_target_pairs={{0,10},{1,25},{2,26},{3,9},{4,14},{5,29},{6,30},{7,13},{8,16},{9,3... | collective-permute-start | bytes 393224 | tf_op jit(solution)/shard_map/ppermute | solution.py:55
  32.5 2.8 %collective-permute-done.11.refs_1_ = bf16[64,1024]{1,0:T(8,128)(2,1)S(1)} collective-permute-done((bf16[64,1024]{1,0:T(8,128)(2,1)S(1)}, bf16[64,1024]{1,0:T(8,128)(2,1)S(1)}, u32[]{:S(2)}, u32[]{:S(2)}) %collective-permute-start.11) | collective-permute-done | bytes 131104 | tf_op jit(solution)/shard_map/ppermute | solution.py:55
  35.3 1.1 %collective-permute-start.12 = (bf16[160,1024]{1,0:T(8,128)(2,1)S(1)}, bf16[160,1024]{1,0:T(8,128)(2,1)S(1)}, u32[]{:S(2)}, u32[]{:S(2)}) collective-permute-start(bf16[160,1024]{1,0:T(8,128)(2,1)S(1)} %shard_map.84), channel_id=1, source_target_pairs={{0,8},{1,9},{2,10},{3,11},{4,12},{5,13},{6,14},{7,15},{8,0},{9,1},... | collective-permute-start | bytes 983048 | tf_op jit(solution)/shard_map/ppermute | solution.py:55
  36.7 1.3 %collective-permute-done.14.refs_1_.refs_3_ = bf16[64,1024]{1,0:T(8,128)(2,1)S(1)} collective-permute-done((bf16[64,1024]{1,0:T(8,128)(2,1)S(1)}, bf16[64,1024]{1,0:T(8,128)(2,1)S(1)}, u32[]{:S(2)}, u32[]{:S(2)}) %collective-permute-start.14) | collective-permute-done | bytes 131104 | tf_op jit(solution)/shard_map/ppermute | solution.py:55
  38.2 1.1 %shard_map.86 = (bf16[128,4096]{1,0:T(8,128)(2,1)}, f32[16,4096]{1,0:T(8,128)}, f32[16,4096]{1,0:T(8,128)}) custom-call(f32[16,4096]{1,0:T(8,128)S(1)} %copy-done, f32[16,4096]{1,0:T(8,128)S(1)} %copy-done.1, bf16[16,1024]{1,0:T(8,128)(2,1)S(1)} %get-tuple-element.35.grad.refs_2_, bf16[16,1024]{1,0:T(8,128)(2,1)S(1)} %collective-permute-done.10.refs_3_.far_grad, ...), custom_call_target="tpu_custom_call" | custom-call | tf_op jit(solution)/shard_map/pallas_call | solution.py:37
  39.6 0.8 %shard_map.87 = bf16[128,4096]{1,0:T(8,128)(2,1)} custom-call(bf16[160,1024]{1,0:T(8,128)(2,1)S(1)} %collective-permute-done.12.early, bf16[128,1024]{1,0:T(8,128)(2,1)S(1)} %collective-permute-done.15.late, bf16[128,4096]{1,0:T(8,128)(2,1)} %get-tuple-element.44._), custom_call_target="tpu_custom_call", output_to_operand_aliasing={{}: (2, {})} | custom-call | tf_op jit(solution)/shard_map/pallas_call | solution.py:37
  (28 shorter events, 3.2 us)
Async XLA Ops:
  0.6 2.0 %copy-start.2 = (bf16[768,128]{1,0:T(8,128)(2,1)S(1)}, bf16[768,128]{1,0:T(8,128)(2,1)}, u32[]{:S(2)}) copy-start(bf16[768,128]{1,0:T(8,128)(2,1)} %acts.1) | copy-start | bytes 589828
  2.6 19.8 %copy-start = (f32[16,4096]{1,0:T(8,128)S(1)}, f32[16,4096]{1,0:T(8,128)}, u32[]{:S(2)}) copy-start(f32[16,4096]{1,0:T(8,128)} %m.3) | copy-start | bytes 786436
  2.6 19.8 %copy-start.1 = (f32[16,4096]{1,0:T(8,128)S(1)}, f32[16,4096]{1,0:T(8,128)}, u32[]{:S(2)}) copy-start(f32[16,4096]{1,0:T(8,128)} %v.3) | copy-start | bytes 786436
  2.6 19.8 %copy-start.3 = (bf16[16,4096]{1,0:T(8,128)(2,1)S(1)}, bf16[16,4096]{1,0:T(8,128)(2,1)}, u32[]{:S(2)}) copy-start(bf16[16,4096]{1,0:T(8,128)(2,1)} %w.1) | copy-start | bytes 393220
  3.3 2.8 %collective-permute-start = (bf16[128,2048]{1,0:T(8,128)(2,1)S(1)}, bf16[128,2048]{1,0:T(8,128)(2,1)S(1)}, u32[]{:S(2)}, u32[]{:S(2)}) collective-permute-start(bf16[128,2048]{1,0:T(8,128)(2,1)S(1)} %get-tuple-element.26), channel_id=1, source_target_pairs={{0,8},{1,9},{2,10},{3,11},{4,12},{5,13},{6,14},{7,15},{8,0},{9,1},... | collective-permute-start | bytes 1572872 | tf_op jit(solution)/shard_map/ppermute | solution.py:55
  6.2 6.5 %collective-permute-start.1 = (bf16[64,1024]{1,0:T(8,128)(2,1)S(1)}, bf16[64,1024]{1,0:T(8,128)(2,1)S(1)}, u32[]{:S(2)}, u32[]{:S(2)}) collective-permute-start(bf16[64,1024]{1,0:T(8,128)(2,1)S(1)} %get-tuple-element.28), channel_id=1, source_target_pairs={{0,17},{1,5},{2,6},{3,18},{4,21},{5,1},{6,2},{7,22},{8,12},{9,24},... | collective-permute-start | bytes 393224 | tf_op jit(solution)/shard_map/ppermute | solution.py:55
  9.7 4.4 %collective-permute-start.2 = (bf16[64,1024]{1,0:T(8,128)(2,1)S(1)}, bf16[64,1024]{1,0:T(8,128)(2,1)S(1)}, u32[]{:S(2)}, u32[]{:S(2)}) collective-permute-start(bf16[64,1024]{1,0:T(8,128)(2,1)S(1)} %get-tuple-element.29), channel_id=1, source_target_pairs={{0,9},{1,15},{2,12},{3,10},{4,13},{5,11},{6,8},{7,14},{8,6},{9,0},... | collective-permute-start | bytes 393224 | tf_op jit(solution)/shard_map/ppermute | solution.py:55
  10.0 4.4 %collective-permute-start.3 = (bf16[64,1024]{1,0:T(8,128)(2,1)S(1)}, bf16[64,1024]{1,0:T(8,128)(2,1)S(1)}, u32[]{:S(2)}, u32[]{:S(2)}) collective-permute-start(bf16[64,1024]{1,0:T(8,128)(2,1)S(1)} %get-tuple-element.30), channel_id=1, source_target_pairs={{0,24},{1,11},{2,8},{3,27},{4,28},{5,15},{6,12},{7,31},{8,2},{9,17... | collective-permute-start | bytes 393224 | tf_op jit(solution)/shard_map/ppermute | solution.py:55
  14.5 4.9 %collective-permute-start.4 = (bf16[16,1024]{1,0:T(8,128)(2,1)S(1)}, bf16[16,1024]{1,0:T(8,128)(2,1)S(1)}, u32[]{:S(2)}, u32[]{:S(2)}) collective-permute-start(bf16[16,1024]{1,0:T(8,128)(2,1)S(1)} %get-tuple-element.32), channel_id=1, source_target_pairs={{0,4},{1,16},{2,19},{3,7},{4,0},{5,20},{6,23},{7,3},{8,25},{9,13},... | collective-permute-start | bytes 98312 | tf_op jit(solution)/shard_map/ppermute | solution.py:55
  17.3 5.1 %collective-permute-start.5 = (bf16[16,1024]{1,0:T(8,128)(2,1)S(1)}, bf16[16,1024]{1,0:T(8,128)(2,1)S(1)}, u32[]{:S(2)}, u32[]{:S(2)}) collective-permute-start(bf16[16,1024]{1,0:T(8,128)(2,1)S(1)} %get-tuple-element.33), channel_id=1, source_target_pairs={{0,14},{1,8},{2,11},{3,13},{4,10},{5,12},{6,15},{7,9},{8,1},{9,7},... | collective-permute-start | bytes 98312 | tf_op jit(solution)/shard_map/ppermute | solution.py:55
  18.4 4.0 %collective-permute-start.6 = (bf16[16,1024]{1,0:T(8,128)(2,1)S(1)}, bf16[16,1024]{1,0:T(8,128)(2,1)S(1)}, u32[]{:S(2)}, u32[]{:S(2)}) collective-permute-start(bf16[16,1024]{1,0:T(8,128)(2,1)S(1)} %get-tuple-element.34), channel_id=1, source_target_pairs={{0,10},{1,25},{2,26},{3,9},{4,14},{5,29},{6,30},{7,13},{8,16},{9,3... | collective-permute-start | bytes 98312 | tf_op jit(solution)/shard_map/ppermute | solution.py:55
  22.5 5.0 %collective-permute-start.7 = (bf16[16,1024]{1,0:T(8,128)(2,1)S(1)}, bf16[16,1024]{1,0:T(8,128)(2,1)S(1)}, u32[]{:S(2)}, u32[]{:S(2)}) collective-permute-start(bf16[16,1024]{1,0:T(8,128)(2,1)S(1)} %get-tuple-element.38), channel_id=1, source_target_pairs={{0,17},{1,5},{2,6},{3,18},{4,21},{5,1},{6,2},{7,22},{8,12},{9,24},... | collective-permute-start | bytes 98312 | tf_op jit(solution)/shard_map/ppermute | solution.py:55
  24.0 3.7 %collective-permute-start.8 = (bf16[16,1024]{1,0:T(8,128)(2,1)S(1)}, bf16[16,1024]{1,0:T(8,128)(2,1)S(1)}, u32[]{:S(2)}, u32[]{:S(2)}) collective-permute-start(bf16[16,1024]{1,0:T(8,128)(2,1)S(1)} %get-tuple-element.39), channel_id=1, source_target_pairs={{0,9},{1,15},{2,12},{3,10},{4,13},{5,11},{6,8},{7,14},{8,6},{9,0},... | collective-permute-start | bytes 98312 | tf_op jit(solution)/shard_map/ppermute | solution.py:55
  24.9 3.3 %collective-permute-start.10 = (bf16[16,1024]{1,0:T(8,128)(2,1)S(1)}, bf16[16,1024]{1,0:T(8,128)(2,1)S(1)}, u32[]{:S(2)}, u32[]{:S(2)}) collective-permute-start(bf16[16,1024]{1,0:T(8,128)(2,1)S(1)} %get-tuple-element.40), channel_id=1, source_target_pairs={{0,24},{1,25},{2,26},{3,27},{4,28},{5,29},{6,30},{7,31},{8,16},{9,... | collective-permute-start | bytes 98312 | tf_op jit(solution)/shard_map/ppermute | solution.py:55
  25.8 3.3 %collective-permute-start.9 = (bf16[16,1024]{1,0:T(8,128)(2,1)S(1)}, bf16[16,1024]{1,0:T(8,128)(2,1)S(1)}, u32[]{:S(2)}, u32[]{:S(2)}) collective-permute-start(bf16[16,1024]{1,0:T(8,128)(2,1)S(1)} %get-tuple-element.37.own), channel_id=1, source_target_pairs={{0,24},{1,11},{2,8},{3,27},{4,28},{5,15},{6,12},{7,31},{8,2},{9,17... | collective-permute-start | bytes 98312 | tf_op jit(solution)/shard_map/ppermute | solution.py:55
  29.2 6.1 %collective-permute-start.11 = (bf16[64,1024]{1,0:T(8,128)(2,1)S(1)}, bf16[64,1024]{1,0:T(8,128)(2,1)S(1)}, u32[]{:S(2)}, u32[]{:S(2)}) collective-permute-start(bf16[64,1024]{1,0:T(8,128)(2,1)S(1)} %get-tuple-element.42), channel_id=1, source_target_pairs={{0,4},{1,16},{2,19},{3,7},{4,0},{5,20},{6,23},{7,3},{8,25},{9,13},... | collective-permute-start | bytes 393224 | tf_op jit(solution)/shard_map/ppermute | solution.py:55
  30.3 6.4 %collective-permute-start.13 = (bf16[64,1024]{1,0:T(8,128)(2,1)S(1)}, bf16[64,1024]{1,0:T(8,128)(2,1)S(1)}, u32[]{:S(2)}, u32[]{:S(2)}) collective-permute-start(bf16[64,1024]{1,0:T(8,128)(2,1)S(1)} %get-tuple-element.43), channel_id=1, source_target_pairs={{0,14},{1,8},{2,11},{3,13},{4,10},{5,12},{6,15},{7,9},{8,1},{9,7},... | collective-permute-start | bytes 393224 | tf_op jit(solution)/shard_map/ppermute | solution.py:55
  31.2 6.8 %collective-permute-start.14 = (bf16[64,1024]{1,0:T(8,128)(2,1)S(1)}, bf16[64,1024]{1,0:T(8,128)(2,1)S(1)}, u32[]{:S(2)}, u32[]{:S(2)}) collective-permute-start(bf16[64,1024]{1,0:T(8,128)(2,1)S(1)} %get-tuple-element.41.refs_0_), channel_id=1, source_target_pairs={{0,10},{1,25},{2,26},{3,9},{4,14},{5,29},{6,30},{7,13},{8,16},{9,3... | collective-permute-start | bytes 393224 | tf_op jit(solution)/shard_map/ppermute | solution.py:55
  35.3 2.9 %collective-permute-start.12 = (bf16[160,1024]{1,0:T(8,128)(2,1)S(1)}, bf16[160,1024]{1,0:T(8,128)(2,1)S(1)}, u32[]{:S(2)}, u32[]{:S(2)}) collective-permute-start(bf16[160,1024]{1,0:T(8,128)(2,1)S(1)} %shard_map.84), channel_id=1, source_target_pairs={{0,8},{1,9},{2,10},{3,11},{4,12},{5,13},{6,14},{7,15},{8,0},{9,1},... | collective-permute-start | bytes 983048 | tf_op jit(solution)/shard_map/ppermute | solution.py:55
  38.0 1.6 %collective-permute-start.15 = (bf16[128,1024]{1,0:T(8,128)(2,1)S(1)}, bf16[128,1024]{1,0:T(8,128)(2,1)S(1)}, u32[]{:S(2)}, u32[]{:S(2)}) collective-permute-start(bf16[128,1024]{1,0:T(8,128)(2,1)S(1)} %shard_map.85), channel_id=1, source_target_pairs={{0,8},{1,9},{2,10},{3,11},{4,12},{5,13},{6,14},{7,15},{8,0},{9,1},... | collective-permute-start | bytes 786440 | tf_op jit(solution)/shard_map/ppermute | solution.py:55

commit v10 on v9

--- a/solution.py
+++ b/solution.py
@@ -59,7 +59,7 @@
     return exchange(value, lambda rep, shard: (rep ^ 1, shard))
 
 
-SQUARE = ((1, 1), (1, 0), (0, 1))
+SQUARE = ((1, 1), (0, 1), (1, 0))
 LINE = (2, 3, 1)
 STEPS = tuple(zip(SQUARE, LINE))
 STAY = ((0, 0), 0)

time: 40.6 us -> 41.6 us (1.025)
  waiting for transfers between devices: 15.2 us -> 17.1 us
  starting transfers between devices: 17.3 us -> 16.3 us
    ppermute x16, waiting for transfers between devices: 15.2 us -> 17.1 us  [exchange(): return lax.ppermute(value, ('rep', 'shard'), pairs)]
    ppermute x16, starting transfers between devices: 17.3 us -> 16.3 us  [exchange(): return lax.ppermute(value, ('rep', 'shard'), pairs)]
  transfers between devices with their start and end apart: 16 -> 16, of which waited for: 13 -> 13; matrix products, arithmetic and copies ran while one was open for 0% -> 0% of each run, Pallas kernels for 9% -> 8%
where the time goes in v10:
time: 41.6 us; the launch traced here: 41.4 us
  waiting for transfers between devices  17.1 us (41%)
  starting transfers between devices  16.3 us (39%)
  Pallas kernels  7.17 us (17%)
  between operations  0.79 us (2%)
    ppermute x16, waiting for transfers between devices, exchange(): return lax.ppermute(value, ('rep', 'shard'), pairs)  17.1 us
    ppermute x16, starting transfers between devices, exchange(): return lax.ppermute(value, ('rep', 'shard'), pairs)  16.3 us
    pallas_call x12, Pallas kernels, call(): pl.pallas_call(kernel, out_shape=outs, in_specs=[far if i in tuple(far_in...  7.17 us
  transfers between devices with their start and end apart: 16, of which 13 were waited for; matrix products, arithmetic and copies ran while one was open for 0% of the time, Pallas kernels for 8%

profile of v10, /device:TPU:0, one launch (start us, length us, event | category | flops | bytes accessed | tf_op | source)
XLA Modules:
  0.0 41.4 jit_solution(3148484791573245578)
XLA Ops:
  0.6 1.9 %shard_map.76.cots = bf16[768,2048]{1,0:T(8,128)(2,1)S(1)} custom-call(bf16[768,4096]{1,0:T(8,128)(2,1)} %cots_ref.3), custom_call_target="tpu_custom_call" | custom-call | tf_op jit(solution)/shard_map/pallas_call | solution.py:37
  2.6 0.6 %shard_map.77 = (bf16[128,2048]{1,0:T(8,128)(2,1)S(1)}, bf16[128,768]{1,0:T(8,128)(2,1)S(1)}) custom-call(bf16[768,128]{1,0:T(8,128)(2,1)S(1)} %copy-done.2, bf16[768,2048]{1,0:T(8,128)(2,1)S(1)} %shard_map.76.cots), custom_call_target="tpu_custom_call" | custom-call | tf_op jit(solution)/shard_map/pallas_call | solution.py:37
  3.3 0.5 %collective-permute-start = (bf16[128,2048]{1,0:T(8,128)(2,1)S(1)}, bf16[128,2048]{1,0:T(8,128)(2,1)S(1)}, u32[]{:S(2)}, u32[]{:S(2)}) collective-permute-start(bf16[128,2048]{1,0:T(8,128)(2,1)S(1)} %get-tuple-element.26), channel_id=1, source_target_pairs={{0,8},{1,9},{2,10},{3,11},{4,12},{5,13},{6,14},{7,15},{8,0},{9,1},... | collective-permute-start | bytes 1572872 | tf_op jit(solution)/shard_map/ppermute | solution.py:55
  3.8 2.3 %shard_map.78.kept = f32[128,2048]{1,0:T(8,128)S(1)} custom-call(bf16[128,768]{1,0:T(8,128)(2,1)S(1)} %get-tuple-element.25.turned, bf16[768,4096]{1,0:T(8,128)(2,1)} %cots_ref.3), custom_call_target="tpu_custom_call" | custom-call | tf_op jit(solution)/shard_map/pallas_call | solution.py:37
  6.2 3.5 %collective-permute-start.1 = (bf16[64,1024]{1,0:T(8,128)(2,1)S(1)}, bf16[64,1024]{1,0:T(8,128)(2,1)S(1)}, u32[]{:S(2)}, u32[]{:S(2)}) collective-permute-start(bf16[64,1024]{1,0:T(8,128)(2,1)S(1)} %get-tuple-element.28), channel_id=1, source_target_pairs={{0,17},{1,5},{2,6},{3,18},{4,21},{5,1},{6,2},{7,22},{8,12},{9,24},... | collective-permute-start | bytes 393224 | tf_op jit(solution)/shard_map/ppermute | solution.py:55
  10.1 2.6 %collective-permute-done.1.refs_0_ = bf16[64,1024]{1,0:T(8,128)(2,1)S(1)} collective-permute-done((bf16[64,1024]{1,0:T(8,128)(2,1)S(1)}, bf16[64,1024]{1,0:T(8,128)(2,1)S(1)}, u32[]{:S(2)}, u32[]{:S(2)}) %collective-permute-start.1) | collective-permute-done | bytes 131104 | tf_op jit(solution)/shard_map/ppermute | solution.py:55
  12.6 1.4 %collective-permute-done.2.refs_1_ = bf16[64,1024]{1,0:T(8,128)(2,1)S(1)} collective-permute-done((bf16[64,1024]{1,0:T(8,128)(2,1)S(1)}, bf16[64,1024]{1,0:T(8,128)(2,1)S(1)}, u32[]{:S(2)}, u32[]{:S(2)}) %collective-permute-start.2) | collective-permute-done | bytes 131104 | tf_op jit(solution)/shard_map/ppermute | solution.py:55
  14.5 2.7 %collective-permute-start.4 = (bf16[16,1024]{1,0:T(8,128)(2,1)S(1)}, bf16[16,1024]{1,0:T(8,128)(2,1)S(1)}, u32[]{:S(2)}, u32[]{:S(2)}) collective-permute-start(bf16[16,1024]{1,0:T(8,128)(2,1)S(1)} %get-tuple-element.32), channel_id=1, source_target_pairs={{0,4},{1,16},{2,19},{3,7},{4,0},{5,20},{6,23},{7,3},{8,25},{9,13},... | collective-permute-start | bytes 98312 | tf_op jit(solution)/shard_map/ppermute | solution.py:55
  17.2 1.2 %collective-permute-start.5 = (bf16[16,1024]{1,0:T(8,128)(2,1)S(1)}, bf16[16,1024]{1,0:T(8,128)(2,1)S(1)}, u32[]{:S(2)}, u32[]{:S(2)}) collective-permute-start(bf16[16,1024]{1,0:T(8,128)(2,1)S(1)} %get-tuple-element.33), channel_id=1, source_target_pairs={{0,14},{1,25},{2,26},{3,13},{4,10},{5,29},{6,30},{7,9},{8,16},{9,7... | collective-permute-start | bytes 98312 | tf_op jit(solution)/shard_map/ppermute | solution.py:55
  18.7 0.7 %collective-permute-done.4.refs_0_ = bf16[16,1024]{1,0:T(8,128)(2,1)S(1)} collective-permute-done((bf16[16,1024]{1,0:T(8,128)(2,1)S(1)}, bf16[16,1024]{1,0:T(8,128)(2,1)S(1)}, u32[]{:S(2)}, u32[]{:S(2)}) %collective-permute-start.4) | collective-permute-done | bytes 32800 | tf_op jit(solution)/shard_map/ppermute | solution.py:55
  19.4 3.0 %collective-permute-done.5.refs_1_ = bf16[16,1024]{1,0:T(8,128)(2,1)S(1)} collective-permute-done((bf16[16,1024]{1,0:T(8,128)(2,1)S(1)}, bf16[16,1024]{1,0:T(8,128)(2,1)S(1)}, u32[]{:S(2)}, u32[]{:S(2)}) %collective-permute-start.5) | collective-permute-done | bytes 32800 | tf_op jit(solution)/shard_map/ppermute | solution.py:55
  22.5 2.5 %collective-permute-start.7 = (bf16[16,1024]{1,0:T(8,128)(2,1)S(1)}, bf16[16,1024]{1,0:T(8,128)(2,1)S(1)}, u32[]{:S(2)}, u32[]{:S(2)}) collective-permute-start(bf16[16,1024]{1,0:T(8,128)(2,1)S(1)} %get-tuple-element.38), channel_id=1, source_target_pairs={{0,17},{1,5},{2,6},{3,18},{4,21},{5,1},{6,2},{7,22},{8,12},{9,24},... | collective-permute-start | bytes 98312 | tf_op jit(solution)/shard_map/ppermute | solution.py:55
  25.0 1.7 %collective-permute-start.10 = (bf16[16,1024]{1,0:T(8,128)(2,1)S(1)}, bf16[16,1024]{1,0:T(8,128)(2,1)S(1)}, u32[]{:S(2)}, u32[]{:S(2)}) collective-permute-start(bf16[16,1024]{1,0:T(8,128)(2,1)S(1)} %get-tuple-element.40), channel_id=1, source_target_pairs={{0,24},{1,25},{2,26},{3,27},{4,28},{5,29},{6,30},{7,31},{8,16},{9,... | collective-permute-start | bytes 98312 | tf_op jit(solution)/shard_map/ppermute | solution.py:55
  26.8 0.6 %collective-permute-done.7.refs_0_ = bf16[16,1024]{1,0:T(8,128)(2,1)S(1)} collective-permute-done((bf16[16,1024]{1,0:T(8,128)(2,1)S(1)}, bf16[16,1024]{1,0:T(8,128)(2,1)S(1)}, u32[]{:S(2)}, u32[]{:S(2)}) %collective-permute-start.7) | collective-permute-done | bytes 32800 | tf_op jit(solution)/shard_map/ppermute | solution.py:55
  27.4 1.0 %collective-permute-done.8.refs_1_ = bf16[16,1024]{1,0:T(8,128)(2,1)S(1)} collective-permute-done((bf16[16,1024]{1,0:T(8,128)(2,1)S(1)}, bf16[16,1024]{1,0:T(8,128)(2,1)S(1)}, u32[]{:S(2)}, u32[]{:S(2)}) %collective-permute-start.8) | collective-permute-done | bytes 32800 | tf_op jit(solution)/shard_map/ppermute | solution.py:55
  28.4 0.4 collective-permute-done.10.refs_3_.far_grad
  28.7 1.4 %collective-permute-done.9.refs_2_ = bf16[16,1024]{1,0:T(8,128)(2,1)S(1)} collective-permute-done((bf16[16,1024]{1,0:T(8,128)(2,1)S(1)}, bf16[16,1024]{1,0:T(8,128)(2,1)S(1)}, u32[]{:S(2)}, u32[]{:S(2)}) %collective-permute-start.9) | collective-permute-done | bytes 32800 | tf_op jit(solution)/shard_map/ppermute | solution.py:55
  30.2 1.0 %collective-permute-start.11 = (bf16[64,1024]{1,0:T(8,128)(2,1)S(1)}, bf16[64,1024]{1,0:T(8,128)(2,1)S(1)}, u32[]{:S(2)}, u32[]{:S(2)}) collective-permute-start(bf16[64,1024]{1,0:T(8,128)(2,1)S(1)} %get-tuple-element.42), channel_id=1, source_target_pairs={{0,4},{1,16},{2,19},{3,7},{4,0},{5,20},{6,23},{7,3},{8,25},{9,13},... | collective-permute-start | bytes 393224 | tf_op jit(solution)/shard_map/ppermute | solution.py:55
  31.1 0.6 %collective-permute-start.13 = (bf16[64,1024]{1,0:T(8,128)(2,1)S(1)}, bf16[64,1024]{1,0:T(8,128)(2,1)S(1)}, u32[]{:S(2)}, u32[]{:S(2)}) collective-permute-start(bf16[64,1024]{1,0:T(8,128)(2,1)S(1)} %get-tuple-element.43), channel_id=1, source_target_pairs={{0,14},{1,25},{2,26},{3,13},{4,10},{5,29},{6,30},{7,9},{8,16},{9,7... | collective-permute-start | bytes 393224 | tf_op jit(solution)/shard_map/ppermute | solution.py:55
  31.8 1.7 %collective-permute-start.14 = (bf16[64,1024]{1,0:T(8,128)(2,1)S(1)}, bf16[64,1024]{1,0:T(8,128)(2,1)S(1)}, u32[]{:S(2)}, u32[]{:S(2)}) collective-permute-start(bf16[64,1024]{1,0:T(8,128)(2,1)S(1)} %get-tuple-element.41.refs_0_), channel_id=1, source_target_pairs={{0,10},{1,8},{2,11},{3,9},{4,14},{5,12},{6,15},{7,13},{8,1},{9,3},... | collective-permute-start | bytes 393224 | tf_op jit(solution)/shard_map/ppermute | solution.py:55
  33.4 4.2 %collective-permute-done.11.refs_1_ = bf16[64,1024]{1,0:T(8,128)(2,1)S(1)} collective-permute-done((bf16[64,1024]{1,0:T(8,128)(2,1)S(1)}, bf16[64,1024]{1,0:T(8,128)(2,1)S(1)}, u32[]{:S(2)}, u32[]{:S(2)}) %collective-permute-start.11) | collective-permute-done | bytes 131104 | tf_op jit(solution)/shard_map/ppermute | solution.py:55
  37.7 1.2 %collective-permute-done.14.refs_1_.refs_3_ = bf16[64,1024]{1,0:T(8,128)(2,1)S(1)} collective-permute-done((bf16[64,1024]{1,0:T(8,128)(2,1)S(1)}, bf16[64,1024]{1,0:T(8,128)(2,1)S(1)}, u32[]{:S(2)}, u32[]{:S(2)}) %collective-permute-start.14) | collective-permute-done | bytes 131104 | tf_op jit(solution)/shard_map/ppermute | solution.py:55
  39.3 1.1 %shard_map.86 = (bf16[128,4096]{1,0:T(8,128)(2,1)}, f32[16,4096]{1,0:T(8,128)}, f32[16,4096]{1,0:T(8,128)}) custom-call(f32[16,4096]{1,0:T(8,128)S(1)} %copy-done, f32[16,4096]{1,0:T(8,128)S(1)} %copy-done.1, bf16[16,1024]{1,0:T(8,128)(2,1)S(1)} %get-tuple-element.35.grad.refs_2_, bf16[16,1024]{1,0:T(8,128)(2,1)S(1)} %collective-permute-done.10.refs_3_.far_grad, ...), custom_call_target="tpu_custom_call" | custom-call | tf_op jit(solution)/shard_map/pallas_call | solution.py:37
  40.5 0.9 %shard_map.87 = bf16[128,4096]{1,0:T(8,128)(2,1)} custom-call(bf16[160,1024]{1,0:T(8,128)(2,1)S(1)} %collective-permute-done.12.early, bf16[128,1024]{1,0:T(8,128)(2,1)S(1)} %collective-permute-done.15.late, bf16[128,4096]{1,0:T(8,128)(2,1)} %get-tuple-element.44._), custom_call_target="tpu_custom_call", output_to_operand_aliasing={{}: (2, {})} | custom-call | tf_op jit(solution)/shard_map/pallas_call | solution.py:37
  (28 shorter events, 1.9 us)
Async XLA Ops:
  0.6 2.0 %copy-start.2 = (bf16[768,128]{1,0:T(8,128)(2,1)S(1)}, bf16[768,128]{1,0:T(8,128)(2,1)}, u32[]{:S(2)}) copy-start(bf16[768,128]{1,0:T(8,128)(2,1)} %acts.1) | copy-start | bytes 589828
  2.6 19.8 %copy-start = (f32[16,4096]{1,0:T(8,128)S(1)}, f32[16,4096]{1,0:T(8,128)}, u32[]{:S(2)}) copy-start(f32[16,4096]{1,0:T(8,128)} %m.3) | copy-start | bytes 786436
  2.6 19.8 %copy-start.1 = (f32[16,4096]{1,0:T(8,128)S(1)}, f32[16,4096]{1,0:T(8,128)}, u32[]{:S(2)}) copy-start(f32[16,4096]{1,0:T(8,128)} %v.3) | copy-start | bytes 786436
  2.6 19.8 %copy-start.3 = (bf16[16,4096]{1,0:T(8,128)(2,1)S(1)}, bf16[16,4096]{1,0:T(8,128)(2,1)}, u32[]{:S(2)}) copy-start(bf16[16,4096]{1,0:T(8,128)(2,1)} %w.1) | copy-start | bytes 393220
  3.3 2.8 %collective-permute-start = (bf16[128,2048]{1,0:T(8,128)(2,1)S(1)}, bf16[128,2048]{1,0:T(8,128)(2,1)S(1)}, u32[]{:S(2)}, u32[]{:S(2)}) collective-permute-start(bf16[128,2048]{1,0:T(8,128)(2,1)S(1)} %get-tuple-element.26), channel_id=1, source_target_pairs={{0,8},{1,9},{2,10},{3,11},{4,12},{5,13},{6,14},{7,15},{8,0},{9,1},... | collective-permute-start | bytes 1572872 | tf_op jit(solution)/shard_map/ppermute | solution.py:55
  6.2 6.5 %collective-permute-start.1 = (bf16[64,1024]{1,0:T(8,128)(2,1)S(1)}, bf16[64,1024]{1,0:T(8,128)(2,1)S(1)}, u32[]{:S(2)}, u32[]{:S(2)}) collective-permute-start(bf16[64,1024]{1,0:T(8,128)(2,1)S(1)} %get-tuple-element.28), channel_id=1, source_target_pairs={{0,17},{1,5},{2,6},{3,18},{4,21},{5,1},{6,2},{7,22},{8,12},{9,24},... | collective-permute-start | bytes 393224 | tf_op jit(solution)/shard_map/ppermute | solution.py:55
  9.7 4.4 %collective-permute-start.2 = (bf16[64,1024]{1,0:T(8,128)(2,1)S(1)}, bf16[64,1024]{1,0:T(8,128)(2,1)S(1)}, u32[]{:S(2)}, u32[]{:S(2)}) collective-permute-start(bf16[64,1024]{1,0:T(8,128)(2,1)S(1)} %get-tuple-element.29), channel_id=1, source_target_pairs={{0,24},{1,15},{2,12},{3,27},{4,28},{5,11},{6,8},{7,31},{8,6},{9,17... | collective-permute-start | bytes 393224 | tf_op jit(solution)/shard_map/ppermute | solution.py:55
  10.0 4.4 %collective-permute-start.3 = (bf16[64,1024]{1,0:T(8,128)(2,1)S(1)}, bf16[64,1024]{1,0:T(8,128)(2,1)S(1)}, u32[]{:S(2)}, u32[]{:S(2)}) collective-permute-start(bf16[64,1024]{1,0:T(8,128)(2,1)S(1)} %get-tuple-element.30), channel_id=1, source_target_pairs={{0,9},{1,11},{2,8},{3,10},{4,13},{5,15},{6,12},{7,14},{8,2},{9,0},... | collective-permute-start | bytes 393224 | tf_op jit(solution)/shard_map/ppermute | solution.py:55
  14.5 4.9 %collective-permute-start.4 = (bf16[16,1024]{1,0:T(8,128)(2,1)S(1)}, bf16[16,1024]{1,0:T(8,128)(2,1)S(1)}, u32[]{:S(2)}, u32[]{:S(2)}) collective-permute-start(bf16[16,1024]{1,0:T(8,128)(2,1)S(1)} %get-tuple-element.32), channel_id=1, source_target_pairs={{0,4},{1,16},{2,19},{3,7},{4,0},{5,20},{6,23},{7,3},{8,25},{9,13},... | collective-permute-start | bytes 98312 | tf_op jit(solution)/shard_map/ppermute | solution.py:55
  17.2 5.1 %collective-permute-start.5 = (bf16[16,1024]{1,0:T(8,128)(2,1)S(1)}, bf16[16,1024]{1,0:T(8,128)(2,1)S(1)}, u32[]{:S(2)}, u32[]{:S(2)}) collective-permute-start(bf16[16,1024]{1,0:T(8,128)(2,1)S(1)} %get-tuple-element.33), channel_id=1, source_target_pairs={{0,14},{1,25},{2,26},{3,13},{4,10},{5,29},{6,30},{7,9},{8,16},{9,7... | collective-permute-start | bytes 98312 | tf_op jit(solution)/shard_map/ppermute | solution.py:55
  18.5 3.9 %collective-permute-start.6 = (bf16[16,1024]{1,0:T(8,128)(2,1)S(1)}, bf16[16,1024]{1,0:T(8,128)(2,1)S(1)}, u32[]{:S(2)}, u32[]{:S(2)}) collective-permute-start(bf16[16,1024]{1,0:T(8,128)(2,1)S(1)} %get-tuple-element.34), channel_id=1, source_target_pairs={{0,10},{1,8},{2,11},{3,9},{4,14},{5,12},{6,15},{7,13},{8,1},{9,3},... | collective-permute-start | bytes 98312 | tf_op jit(solution)/shard_map/ppermute | solution.py:55
  22.5 4.9 %collective-permute-start.7 = (bf16[16,1024]{1,0:T(8,128)(2,1)S(1)}, bf16[16,1024]{1,0:T(8,128)(2,1)S(1)}, u32[]{:S(2)}, u32[]{:S(2)}) collective-permute-start(bf16[16,1024]{1,0:T(8,128)(2,1)S(1)} %get-tuple-element.38), channel_id=1, source_target_pairs={{0,17},{1,5},{2,6},{3,18},{4,21},{5,1},{6,2},{7,22},{8,12},{9,24},... | collective-permute-start | bytes 98312 | tf_op jit(solution)/shard_map/ppermute | solution.py:55
  25.0 3.3 %collective-permute-start.8 = (bf16[16,1024]{1,0:T(8,128)(2,1)S(1)}, bf16[16,1024]{1,0:T(8,128)(2,1)S(1)}, u32[]{:S(2)}, u32[]{:S(2)}) collective-permute-start(bf16[16,1024]{1,0:T(8,128)(2,1)S(1)} %get-tuple-element.39), channel_id=1, source_target_pairs={{0,24},{1,15},{2,12},{3,27},{4,28},{5,11},{6,8},{7,31},{8,6},{9,17... | collective-permute-start | bytes 98312 | tf_op jit(solution)/shard_map/ppermute | solution.py:55
  25.0 3.7 %collective-permute-start.10 = (bf16[16,1024]{1,0:T(8,128)(2,1)S(1)}, bf16[16,1024]{1,0:T(8,128)(2,1)S(1)}, u32[]{:S(2)}, u32[]{:S(2)}) collective-permute-start(bf16[16,1024]{1,0:T(8,128)(2,1)S(1)} %get-tuple-element.40), channel_id=1, source_target_pairs={{0,24},{1,25},{2,26},{3,27},{4,28},{5,29},{6,30},{7,31},{8,16},{9,... | collective-permute-start | bytes 98312 | tf_op jit(solution)/shard_map/ppermute | solution.py:55
  26.8 3.3 %collective-permute-start.9 = (bf16[16,1024]{1,0:T(8,128)(2,1)S(1)}, bf16[16,1024]{1,0:T(8,128)(2,1)S(1)}, u32[]{:S(2)}, u32[]{:S(2)}) collective-permute-start(bf16[16,1024]{1,0:T(8,128)(2,1)S(1)} %get-tuple-element.37.own), channel_id=1, source_target_pairs={{0,9},{1,11},{2,8},{3,10},{4,13},{5,15},{6,12},{7,14},{8,2},{9,0},... | collective-permute-start | bytes 98312 | tf_op jit(solution)/shard_map/ppermute | solution.py:55
  30.2 7.4 %collective-permute-start.11 = (bf16[64,1024]{1,0:T(8,128)(2,1)S(1)}, bf16[64,1024]{1,0:T(8,128)(2,1)S(1)}, u32[]{:S(2)}, u32[]{:S(2)}) collective-permute-start(bf16[64,1024]{1,0:T(8,128)(2,1)S(1)} %get-tuple-element.42), channel_id=1, source_target_pairs={{0,4},{1,16},{2,19},{3,7},{4,0},{5,20},{6,23},{7,3},{8,25},{9,13},... | collective-permute-start | bytes 393224 | tf_op jit(solution)/shard_map/ppermute | solution.py:55
  31.1 6.6 %collective-permute-start.13 = (bf16[64,1024]{1,0:T(8,128)(2,1)S(1)}, bf16[64,1024]{1,0:T(8,128)(2,1)S(1)}, u32[]{:S(2)}, u32[]{:S(2)}) collective-permute-start(bf16[64,1024]{1,0:T(8,128)(2,1)S(1)} %get-tuple-element.43), channel_id=1, source_target_pairs={{0,14},{1,25},{2,26},{3,13},{4,10},{5,29},{6,30},{7,9},{8,16},{9,7... | collective-permute-start | bytes 393224 | tf_op jit(solution)/shard_map/ppermute | solution.py:55
  31.8 7.1 %collective-permute-start.14 = (bf16[64,1024]{1,0:T(8,128)(2,1)S(1)}, bf16[64,1024]{1,0:T(8,128)(2,1)S(1)}, u32[]{:S(2)}, u32[]{:S(2)}) collective-permute-start(bf16[64,1024]{1,0:T(8,128)(2,1)S(1)} %get-tuple-element.41.refs_0_), channel_id=1, source_target_pairs={{0,10},{1,8},{2,11},{3,9},{4,14},{5,12},{6,15},{7,13},{8,1},{9,3},... | collective-permute-start | bytes 393224 | tf_op jit(solution)/shard_map/ppermute | solution.py:55
  37.6 1.7 %collective-permute-start.12 = (bf16[160,1024]{1,0:T(8,128)(2,1)S(1)}, bf16[160,1024]{1,0:T(8,128)(2,1)S(1)}, u32[]{:S(2)}, u32[]{:S(2)}) collective-permute-start(bf16[160,1024]{1,0:T(8,128)(2,1)S(1)} %shard_map.84), channel_id=1, source_target_pairs={{0,8},{1,9},{2,10},{3,11},{4,12},{5,13},{6,14},{7,15},{8,0},{9,1},... | collective-permute-start | bytes 983048 | tf_op jit(solution)/shard_map/ppermute | solution.py:55
  38.9 1.6 %collective-permute-start.15 = (bf16[128,1024]{1,0:T(8,128)(2,1)S(1)}, bf16[128,1024]{1,0:T(8,128)(2,1)S(1)}, u32[]{:S(2)}, u32[]{:S(2)}) collective-permute-start(bf16[128,1024]{1,0:T(8,128)(2,1)S(1)} %shard_map.85), channel_id=1, source_target_pairs={{0,8},{1,9},{2,10},{3,11},{4,12},{5,13},{6,14},{7,15},{8,0},{9,1},... | collective-permute-start | bytes 786440 | tf_op jit(solution)/shard_map/ppermute | solution.py:55

commit v11 on v9

--- a/solution.py
+++ b/solution.py
@@ -66,7 +66,7 @@
 
 
 def role_of(rep, shard):
-    return (rep ^ (rep >> 1) ^ shard ^ (shard >> 1)) & 1
+    return (rep ^ (rep >> 1) ^ shard ^ (shard >> 1) ^ 1) & 1
 
 
 def partner(rep, shard, dy, dx, k):

time: 40.6 us -> 40.9 us (level)
  waiting for transfers between devices: 15.2 us -> 16 us
  starting transfers between devices: 17.3 us -> 16.8 us
    ppermute x16, waiting for transfers between devices: 15.2 us -> 16 us  [exchange(): return lax.ppermute(value, ('rep', 'shard'), pairs)]
    ppermute x16, starting transfers between devices: 17.3 us -> 16.8 us  [exchange(): return lax.ppermute(value, ('rep', 'shard'), pairs)]
  transfers between devices with their start and end apart: 16 -> 16, of which waited for: 13 -> 11; matrix products, arithmetic and copies ran while one was open for 0% -> 0% of each run, Pallas kernels for 9% -> 8%
where the time goes in v11:
time: 40.9 us; the launch traced here: 40.7 us
  starting transfers between devices  16.8 us (41%)
  waiting for transfers between devices  16 us (39%)
  Pallas kernels  7.14 us (17%)
  between operations  0.78 us (2%)
    ppermute x16, starting transfers between devices, exchange(): return lax.ppermute(value, ('rep', 'shard'), pairs)  16.8 us
    ppermute x16, waiting for transfers between devices, exchange(): return lax.ppermute(value, ('rep', 'shard'), pairs)  16 us
    pallas_call x12, Pallas kernels, call(): pl.pallas_call(kernel, out_shape=outs, in_specs=[far if i in tuple(far_in...  7.14 us
  transfers between devices with their start and end apart: 16, of which 11 were waited for; matrix products, arithmetic and copies ran while one was open for 0% of the time, Pallas kernels for 8%

profile of v11, /device:TPU:0, one launch (start us, length us, event | category | flops | bytes accessed | tf_op | source)
XLA Modules:
  0.0 40.7 jit_solution(15116515759106430778)
XLA Ops:
  0.6 1.9 %shard_map.76.cots = bf16[768,2048]{1,0:T(8,128)(2,1)S(1)} custom-call(bf16[768,4096]{1,0:T(8,128)(2,1)} %cots_ref.3), custom_call_target="tpu_custom_call" | custom-call | tf_op jit(solution)/shard_map/pallas_call | solution.py:37
  2.6 0.6 %shard_map.77 = (bf16[128,2048]{1,0:T(8,128)(2,1)S(1)}, bf16[128,768]{1,0:T(8,128)(2,1)S(1)}) custom-call(bf16[768,128]{1,0:T(8,128)(2,1)S(1)} %copy-done.2, bf16[768,2048]{1,0:T(8,128)(2,1)S(1)} %shard_map.76.cots), custom_call_target="tpu_custom_call" | custom-call | tf_op jit(solution)/shard_map/pallas_call | solution.py:37
  3.3 0.5 %collective-permute-start = (bf16[128,2048]{1,0:T(8,128)(2,1)S(1)}, bf16[128,2048]{1,0:T(8,128)(2,1)S(1)}, u32[]{:S(2)}, u32[]{:S(2)}) collective-permute-start(bf16[128,2048]{1,0:T(8,128)(2,1)S(1)} %get-tuple-element.26), channel_id=1, source_target_pairs={{0,8},{1,9},{2,10},{3,11},{4,12},{5,13},{6,14},{7,15},{8,0},{9,1},... | collective-permute-start | bytes 1572872 | tf_op jit(solution)/shard_map/ppermute | solution.py:55
  3.8 2.3 %shard_map.78.kept = f32[128,2048]{1,0:T(8,128)S(1)} custom-call(bf16[128,768]{1,0:T(8,128)(2,1)S(1)} %get-tuple-element.25.turned, bf16[768,4096]{1,0:T(8,128)(2,1)} %cots_ref.3), custom_call_target="tpu_custom_call" | custom-call | tf_op jit(solution)/shard_map/pallas_call | solution.py:37
  6.2 3.7 %collective-permute-start.1 = (bf16[64,1024]{1,0:T(8,128)(2,1)S(1)}, bf16[64,1024]{1,0:T(8,128)(2,1)S(1)}, u32[]{:S(2)}, u32[]{:S(2)}) collective-permute-start(bf16[64,1024]{1,0:T(8,128)(2,1)S(1)} %get-tuple-element.28), channel_id=1, source_target_pairs={{0,4},{1,16},{2,19},{3,7},{4,0},{5,20},{6,23},{7,3},{8,25},{9,13},... | collective-permute-start | bytes 393224 | tf_op jit(solution)/shard_map/ppermute | solution.py:55
  9.8 1.2 %collective-permute-start.2 = (bf16[64,1024]{1,0:T(8,128)(2,1)S(1)}, bf16[64,1024]{1,0:T(8,128)(2,1)S(1)}, u32[]{:S(2)}, u32[]{:S(2)}) collective-permute-start(bf16[64,1024]{1,0:T(8,128)(2,1)S(1)} %get-tuple-element.29), channel_id=1, source_target_pairs={{0,14},{1,8},{2,11},{3,13},{4,10},{5,12},{6,15},{7,9},{8,1},{9,7},... | collective-permute-start | bytes 393224 | tf_op jit(solution)/shard_map/ppermute | solution.py:55
  11.2 3.0 %collective-permute-done.1.refs_0_ = bf16[64,1024]{1,0:T(8,128)(2,1)S(1)} collective-permute-done((bf16[64,1024]{1,0:T(8,128)(2,1)S(1)}, bf16[64,1024]{1,0:T(8,128)(2,1)S(1)}, u32[]{:S(2)}, u32[]{:S(2)}) %collective-permute-start.1) | collective-permute-done | bytes 131104 | tf_op jit(solution)/shard_map/ppermute | solution.py:55
  14.2 2.0 %collective-permute-done.2.refs_1_ = bf16[64,1024]{1,0:T(8,128)(2,1)S(1)} collective-permute-done((bf16[64,1024]{1,0:T(8,128)(2,1)S(1)}, bf16[64,1024]{1,0:T(8,128)(2,1)S(1)}, u32[]{:S(2)}, u32[]{:S(2)}) %collective-permute-start.2) | collective-permute-done | bytes 131104 | tf_op jit(solution)/shard_map/ppermute | solution.py:55
  16.2 0.8 %collective-permute-done.3.refs_2_ = bf16[64,1024]{1,0:T(8,128)(2,1)S(1)} collective-permute-done((bf16[64,1024]{1,0:T(8,128)(2,1)S(1)}, bf16[64,1024]{1,0:T(8,128)(2,1)S(1)}, u32[]{:S(2)}, u32[]{:S(2)}) %collective-permute-start.3) | collective-permute-done | bytes 131104 | tf_op jit(solution)/shard_map/ppermute | solution.py:55
  17.1 2.8 %collective-permute-start.4 = (bf16[16,1024]{1,0:T(8,128)(2,1)S(1)}, bf16[16,1024]{1,0:T(8,128)(2,1)S(1)}, u32[]{:S(2)}, u32[]{:S(2)}) collective-permute-start(bf16[16,1024]{1,0:T(8,128)(2,1)S(1)} %get-tuple-element.32), channel_id=1, source_target_pairs={{0,17},{1,5},{2,6},{3,18},{4,21},{5,1},{6,2},{7,22},{8,12},{9,24},... | collective-permute-start | bytes 98312 | tf_op jit(solution)/shard_map/ppermute | solution.py:55
  19.9 0.4 %collective-permute-start.6 = (bf16[16,1024]{1,0:T(8,128)(2,1)S(1)}, bf16[16,1024]{1,0:T(8,128)(2,1)S(1)}, u32[]{:S(2)}, u32[]{:S(2)}) collective-permute-start(bf16[16,1024]{1,0:T(8,128)(2,1)S(1)} %get-tuple-element.34), channel_id=1, source_target_pairs={{0,24},{1,11},{2,8},{3,27},{4,28},{5,15},{6,12},{7,31},{8,2},{9,17... | collective-permute-start | bytes 98312 | tf_op jit(solution)/shard_map/ppermute | solution.py:55
  20.3 1.6 %collective-permute-done.4.refs_0_ = bf16[16,1024]{1,0:T(8,128)(2,1)S(1)} collective-permute-done((bf16[16,1024]{1,0:T(8,128)(2,1)S(1)}, bf16[16,1024]{1,0:T(8,128)(2,1)S(1)}, u32[]{:S(2)}, u32[]{:S(2)}) %collective-permute-start.4) | collective-permute-done | bytes 32800 | tf_op jit(solution)/shard_map/ppermute | solution.py:55
  21.9 1.3 %collective-permute-done.5.refs_1_ = bf16[16,1024]{1,0:T(8,128)(2,1)S(1)} collective-permute-done((bf16[16,1024]{1,0:T(8,128)(2,1)S(1)}, bf16[16,1024]{1,0:T(8,128)(2,1)S(1)}, u32[]{:S(2)}, u32[]{:S(2)}) %collective-permute-start.5) | collective-permute-done | bytes 32800 | tf_op jit(solution)/shard_map/ppermute | solution.py:55
  23.4 2.3 %collective-permute-start.7 = (bf16[16,1024]{1,0:T(8,128)(2,1)S(1)}, bf16[16,1024]{1,0:T(8,128)(2,1)S(1)}, u32[]{:S(2)}, u32[]{:S(2)}) collective-permute-start(bf16[16,1024]{1,0:T(8,128)(2,1)S(1)} %get-tuple-element.38), channel_id=1, source_target_pairs={{0,4},{1,16},{2,19},{3,7},{4,0},{5,20},{6,23},{7,3},{8,25},{9,13},... | collective-permute-start | bytes 98312 | tf_op jit(solution)/shard_map/ppermute | solution.py:55
  25.7 1.0 %collective-permute-start.8 = (bf16[16,1024]{1,0:T(8,128)(2,1)S(1)}, bf16[16,1024]{1,0:T(8,128)(2,1)S(1)}, u32[]{:S(2)}, u32[]{:S(2)}) collective-permute-start(bf16[16,1024]{1,0:T(8,128)(2,1)S(1)} %get-tuple-element.39), channel_id=1, source_target_pairs={{0,14},{1,8},{2,11},{3,13},{4,10},{5,12},{6,15},{7,9},{8,1},{9,7},... | collective-permute-start | bytes 98312 | tf_op jit(solution)/shard_map/ppermute | solution.py:55
  27.1 0.5 %collective-permute-start.9 = (bf16[16,1024]{1,0:T(8,128)(2,1)S(1)}, bf16[16,1024]{1,0:T(8,128)(2,1)S(1)}, u32[]{:S(2)}, u32[]{:S(2)}) collective-permute-start(bf16[16,1024]{1,0:T(8,128)(2,1)S(1)} %get-tuple-element.37.own), channel_id=1, source_target_pairs={{0,10},{1,25},{2,26},{3,9},{4,14},{5,29},{6,30},{7,13},{8,16},{9,3... | collective-permute-start | bytes 98312 | tf_op jit(solution)/shard_map/ppermute | solution.py:55
  27.6 1.0 %collective-permute-done.7.refs_0_ = bf16[16,1024]{1,0:T(8,128)(2,1)S(1)} collective-permute-done((bf16[16,1024]{1,0:T(8,128)(2,1)S(1)}, bf16[16,1024]{1,0:T(8,128)(2,1)S(1)}, u32[]{:S(2)}, u32[]{:S(2)}) %collective-permute-start.7) | collective-permute-done | bytes 32800 | tf_op jit(solution)/shard_map/ppermute | solution.py:55
  28.6 2.2 %collective-permute-done.8.refs_1_ = bf16[16,1024]{1,0:T(8,128)(2,1)S(1)} collective-permute-done((bf16[16,1024]{1,0:T(8,128)(2,1)S(1)}, bf16[16,1024]{1,0:T(8,128)(2,1)S(1)}, u32[]{:S(2)}, u32[]{:S(2)}) %collective-permute-start.8) | collective-permute-done | bytes 32800 | tf_op jit(solution)/shard_map/ppermute | solution.py:55
  30.9 1.9 %collective-permute-start.11 = (bf16[64,1024]{1,0:T(8,128)(2,1)S(1)}, bf16[64,1024]{1,0:T(8,128)(2,1)S(1)}, u32[]{:S(2)}, u32[]{:S(2)}) collective-permute-start(bf16[64,1024]{1,0:T(8,128)(2,1)S(1)} %get-tuple-element.42), channel_id=1, source_target_pairs={{0,17},{1,5},{2,6},{3,18},{4,21},{5,1},{6,2},{7,22},{8,12},{9,24},... | collective-permute-start | bytes 393224 | tf_op jit(solution)/shard_map/ppermute | solution.py:55
  33.1 1.1 %collective-permute-start.14 = (bf16[64,1024]{1,0:T(8,128)(2,1)S(1)}, bf16[64,1024]{1,0:T(8,128)(2,1)S(1)}, u32[]{:S(2)}, u32[]{:S(2)}) collective-permute-start(bf16[64,1024]{1,0:T(8,128)(2,1)S(1)} %get-tuple-element.41.refs_0_), channel_id=1, source_target_pairs={{0,24},{1,11},{2,8},{3,27},{4,28},{5,15},{6,12},{7,31},{8,2},{9,17... | collective-permute-start | bytes 393224 | tf_op jit(solution)/shard_map/ppermute | solution.py:55
  34.2 2.8 %collective-permute-done.11.refs_1_ = bf16[64,1024]{1,0:T(8,128)(2,1)S(1)} collective-permute-done((bf16[64,1024]{1,0:T(8,128)(2,1)S(1)}, bf16[64,1024]{1,0:T(8,128)(2,1)S(1)}, u32[]{:S(2)}, u32[]{:S(2)}) %collective-permute-start.11) | collective-permute-done | bytes 131104 | tf_op jit(solution)/shard_map/ppermute | solution.py:55
  37.2 1.1 %collective-permute-done.13.refs_0_.refs_2_ = bf16[64,1024]{1,0:T(8,128)(2,1)S(1)} collective-permute-done((bf16[64,1024]{1,0:T(8,128)(2,1)S(1)}, bf16[64,1024]{1,0:T(8,128)(2,1)S(1)}, u32[]{:S(2)}, u32[]{:S(2)}) %collective-permute-start.13) | collective-permute-done | bytes 131104 | tf_op jit(solution)/shard_map/ppermute | solution.py:55
  38.7 1.1 %shard_map.86 = (bf16[128,4096]{1,0:T(8,128)(2,1)}, f32[16,4096]{1,0:T(8,128)}, f32[16,4096]{1,0:T(8,128)}) custom-call(f32[16,4096]{1,0:T(8,128)S(1)} %copy-done, f32[16,4096]{1,0:T(8,128)S(1)} %copy-done.1, bf16[16,1024]{1,0:T(8,128)(2,1)S(1)} %get-tuple-element.35.grad.refs_2_, bf16[16,1024]{1,0:T(8,128)(2,1)S(1)} %collective-permute-done.10.refs_3_.far_grad, ...), custom_call_target="tpu_custom_call" | custom-call | tf_op jit(solution)/shard_map/pallas_call | solution.py:37
  39.9 0.8 %shard_map.87 = bf16[128,4096]{1,0:T(8,128)(2,1)} custom-call(bf16[160,1024]{1,0:T(8,128)(2,1)S(1)} %collective-permute-done.12.early, bf16[128,1024]{1,0:T(8,128)(2,1)S(1)} %collective-permute-done.15.late, bf16[128,4096]{1,0:T(8,128)(2,1)} %get-tuple-element.44._), custom_call_target="tpu_custom_call", output_to_operand_aliasing={{}: (2, {})} | custom-call | tf_op jit(solution)/shard_map/pallas_call | solution.py:37
  (28 shorter events, 2.0 us)
Async XLA Ops:
  0.6 2.0 %copy-start.2 = (bf16[768,128]{1,0:T(8,128)(2,1)S(1)}, bf16[768,128]{1,0:T(8,128)(2,1)}, u32[]{:S(2)}) copy-start(bf16[768,128]{1,0:T(8,128)(2,1)} %acts.1) | copy-start | bytes 589828
  2.6 20.6 %copy-start = (f32[16,4096]{1,0:T(8,128)S(1)}, f32[16,4096]{1,0:T(8,128)}, u32[]{:S(2)}) copy-start(f32[16,4096]{1,0:T(8,128)} %m.3) | copy-start | bytes 786436
  2.6 20.6 %copy-start.1 = (f32[16,4096]{1,0:T(8,128)S(1)}, f32[16,4096]{1,0:T(8,128)}, u32[]{:S(2)}) copy-start(f32[16,4096]{1,0:T(8,128)} %v.3) | copy-start | bytes 786436
  2.6 20.6 %copy-start.3 = (bf16[16,4096]{1,0:T(8,128)(2,1)S(1)}, bf16[16,4096]{1,0:T(8,128)(2,1)}, u32[]{:S(2)}) copy-start(bf16[16,4096]{1,0:T(8,128)(2,1)} %w.1) | copy-start | bytes 393220
  3.3 2.8 %collective-permute-start = (bf16[128,2048]{1,0:T(8,128)(2,1)S(1)}, bf16[128,2048]{1,0:T(8,128)(2,1)S(1)}, u32[]{:S(2)}, u32[]{:S(2)}) collective-permute-start(bf16[128,2048]{1,0:T(8,128)(2,1)S(1)} %get-tuple-element.26), channel_id=1, source_target_pairs={{0,8},{1,9},{2,10},{3,11},{4,12},{5,13},{6,14},{7,15},{8,0},{9,1},... | collective-permute-start | bytes 1572872 | tf_op jit(solution)/shard_map/ppermute | solution.py:55
  6.2 8.0 %collective-permute-start.1 = (bf16[64,1024]{1,0:T(8,128)(2,1)S(1)}, bf16[64,1024]{1,0:T(8,128)(2,1)S(1)}, u32[]{:S(2)}, u32[]{:S(2)}) collective-permute-start(bf16[64,1024]{1,0:T(8,128)(2,1)S(1)} %get-tuple-element.28), channel_id=1, source_target_pairs={{0,4},{1,16},{2,19},{3,7},{4,0},{5,20},{6,23},{7,3},{8,25},{9,13},... | collective-permute-start | bytes 393224 | tf_op jit(solution)/shard_map/ppermute | solution.py:55
  9.8 6.3 %collective-permute-start.2 = (bf16[64,1024]{1,0:T(8,128)(2,1)S(1)}, bf16[64,1024]{1,0:T(8,128)(2,1)S(1)}, u32[]{:S(2)}, u32[]{:S(2)}) collective-permute-start(bf16[64,1024]{1,0:T(8,128)(2,1)S(1)} %get-tuple-element.29), channel_id=1, source_target_pairs={{0,14},{1,8},{2,11},{3,13},{4,10},{5,12},{6,15},{7,9},{8,1},{9,7},... | collective-permute-start | bytes 393224 | tf_op jit(solution)/shard_map/ppermute | solution.py:55
  11.0 6.0 %collective-permute-start.3 = (bf16[64,1024]{1,0:T(8,128)(2,1)S(1)}, bf16[64,1024]{1,0:T(8,128)(2,1)S(1)}, u32[]{:S(2)}, u32[]{:S(2)}) collective-permute-start(bf16[64,1024]{1,0:T(8,128)(2,1)S(1)} %get-tuple-element.30), channel_id=1, source_target_pairs={{0,10},{1,25},{2,26},{3,9},{4,14},{5,29},{6,30},{7,13},{8,16},{9,3... | collective-permute-start | bytes 393224 | tf_op jit(solution)/shard_map/ppermute | solution.py:55
  17.1 4.9 %collective-permute-start.4 = (bf16[16,1024]{1,0:T(8,128)(2,1)S(1)}, bf16[16,1024]{1,0:T(8,128)(2,1)S(1)}, u32[]{:S(2)}, u32[]{:S(2)}) collective-permute-start(bf16[16,1024]{1,0:T(8,128)(2,1)S(1)} %get-tuple-element.32), channel_id=1, source_target_pairs={{0,17},{1,5},{2,6},{3,18},{4,21},{5,1},{6,2},{7,22},{8,12},{9,24},... | collective-permute-start | bytes 98312 | tf_op jit(solution)/shard_map/ppermute | solution.py:55
  19.9 3.3 %collective-permute-start.5 = (bf16[16,1024]{1,0:T(8,128)(2,1)S(1)}, bf16[16,1024]{1,0:T(8,128)(2,1)S(1)}, u32[]{:S(2)}, u32[]{:S(2)}) collective-permute-start(bf16[16,1024]{1,0:T(8,128)(2,1)S(1)} %get-tuple-element.33), channel_id=1, source_target_pairs={{0,9},{1,15},{2,12},{3,10},{4,13},{5,11},{6,8},{7,14},{8,6},{9,0},... | collective-permute-start | bytes 98312 | tf_op jit(solution)/shard_map/ppermute | solution.py:55
  19.9 3.3 %collective-permute-start.6 = (bf16[16,1024]{1,0:T(8,128)(2,1)S(1)}, bf16[16,1024]{1,0:T(8,128)(2,1)S(1)}, u32[]{:S(2)}, u32[]{:S(2)}) collective-permute-start(bf16[16,1024]{1,0:T(8,128)(2,1)S(1)} %get-tuple-element.34), channel_id=1, source_target_pairs={{0,24},{1,11},{2,8},{3,27},{4,28},{5,15},{6,12},{7,31},{8,2},{9,17... | collective-permute-start | bytes 98312 | tf_op jit(solution)/shard_map/ppermute | solution.py:55
  23.4 5.2 %collective-permute-start.7 = (bf16[16,1024]{1,0:T(8,128)(2,1)S(1)}, bf16[16,1024]{1,0:T(8,128)(2,1)S(1)}, u32[]{:S(2)}, u32[]{:S(2)}) collective-permute-start(bf16[16,1024]{1,0:T(8,128)(2,1)S(1)} %get-tuple-element.38), channel_id=1, source_target_pairs={{0,4},{1,16},{2,19},{3,7},{4,0},{5,20},{6,23},{7,3},{8,25},{9,13},... | collective-permute-start | bytes 98312 | tf_op jit(solution)/shard_map/ppermute | solution.py:55
  25.7 5.1 %collective-permute-start.8 = (bf16[16,1024]{1,0:T(8,128)(2,1)S(1)}, bf16[16,1024]{1,0:T(8,128)(2,1)S(1)}, u32[]{:S(2)}, u32[]{:S(2)}) collective-permute-start(bf16[16,1024]{1,0:T(8,128)(2,1)S(1)} %get-tuple-element.39), channel_id=1, source_target_pairs={{0,14},{1,8},{2,11},{3,13},{4,10},{5,12},{6,15},{7,9},{8,1},{9,7},... | collective-permute-start | bytes 98312 | tf_op jit(solution)/shard_map/ppermute | solution.py:55
  26.8 4.1 %collective-permute-start.10 = (bf16[16,1024]{1,0:T(8,128)(2,1)S(1)}, bf16[16,1024]{1,0:T(8,128)(2,1)S(1)}, u32[]{:S(2)}, u32[]{:S(2)}) collective-permute-start(bf16[16,1024]{1,0:T(8,128)(2,1)S(1)} %get-tuple-element.40), channel_id=1, source_target_pairs={{0,24},{1,25},{2,26},{3,27},{4,28},{5,29},{6,30},{7,31},{8,16},{9,... | collective-permute-start | bytes 98312 | tf_op jit(solution)/shard_map/ppermute | solution.py:55
  27.1 3.7 %collective-permute-start.9 = (bf16[16,1024]{1,0:T(8,128)(2,1)S(1)}, bf16[16,1024]{1,0:T(8,128)(2,1)S(1)}, u32[]{:S(2)}, u32[]{:S(2)}) collective-permute-start(bf16[16,1024]{1,0:T(8,128)(2,1)S(1)} %get-tuple-element.37.own), channel_id=1, source_target_pairs={{0,10},{1,25},{2,26},{3,9},{4,14},{5,29},{6,30},{7,13},{8,16},{9,3... | collective-permute-start | bytes 98312 | tf_op jit(solution)/shard_map/ppermute | solution.py:55
  30.9 6.0 %collective-permute-start.11 = (bf16[64,1024]{1,0:T(8,128)(2,1)S(1)}, bf16[64,1024]{1,0:T(8,128)(2,1)S(1)}, u32[]{:S(2)}, u32[]{:S(2)}) collective-permute-start(bf16[64,1024]{1,0:T(8,128)(2,1)S(1)} %get-tuple-element.42), channel_id=1, source_target_pairs={{0,17},{1,5},{2,6},{3,18},{4,21},{5,1},{6,2},{7,22},{8,12},{9,24},... | collective-permute-start | bytes 393224 | tf_op jit(solution)/shard_map/ppermute | solution.py:55
  32.8 5.5 %collective-permute-start.13 = (bf16[64,1024]{1,0:T(8,128)(2,1)S(1)}, bf16[64,1024]{1,0:T(8,128)(2,1)S(1)}, u32[]{:S(2)}, u32[]{:S(2)}) collective-permute-start(bf16[64,1024]{1,0:T(8,128)(2,1)S(1)} %get-tuple-element.43), channel_id=1, source_target_pairs={{0,9},{1,15},{2,12},{3,10},{4,13},{5,11},{6,8},{7,14},{8,6},{9,0},... | collective-permute-start | bytes 393224 | tf_op jit(solution)/shard_map/ppermute | solution.py:55
  33.1 5.1 %collective-permute-start.14 = (bf16[64,1024]{1,0:T(8,128)(2,1)S(1)}, bf16[64,1024]{1,0:T(8,128)(2,1)S(1)}, u32[]{:S(2)}, u32[]{:S(2)}) collective-permute-start(bf16[64,1024]{1,0:T(8,128)(2,1)S(1)} %get-tuple-element.41.refs_0_), channel_id=1, source_target_pairs={{0,24},{1,11},{2,8},{3,27},{4,28},{5,15},{6,12},{7,31},{8,2},{9,17... | collective-permute-start | bytes 393224 | tf_op jit(solution)/shard_map/ppermute | solution.py:55
  37.0 1.7 %collective-permute-start.12 = (bf16[160,1024]{1,0:T(8,128)(2,1)S(1)}, bf16[160,1024]{1,0:T(8,128)(2,1)S(1)}, u32[]{:S(2)}, u32[]{:S(2)}) collective-permute-start(bf16[160,1024]{1,0:T(8,128)(2,1)S(1)} %shard_map.84), channel_id=1, source_target_pairs={{0,8},{1,9},{2,10},{3,11},{4,12},{5,13},{6,14},{7,15},{8,0},{9,1},... | collective-permute-start | bytes 983048 | tf_op jit(solution)/shard_map/ppermute | solution.py:55
  38.3 1.6 %collective-permute-start.15 = (bf16[128,1024]{1,0:T(8,128)(2,1)S(1)}, bf16[128,1024]{1,0:T(8,128)(2,1)S(1)}, u32[]{:S(2)}, u32[]{:S(2)}) collective-permute-start(bf16[128,1024]{1,0:T(8,128)(2,1)S(1)} %shard_map.85), channel_id=1, source_target_pairs={{0,8},{1,9},{2,10},{3,11},{4,12},{5,13},{6,14},{7,15},{8,0},{9,1},... | collective-permute-start | bytes 786440 | tf_op jit(solution)/shard_map/ppermute | solution.py:55

commit v12 on v9

--- a/solution.py
+++ b/solution.py
@@ -9,7 +9,7 @@
 
 F32 = jnp.float32
 BF16 = jnp.bfloat16
-CHUNK = 512
+CHUNK = 256
 LOAD_LIMIT = 48 * 1024 * 1024
 KEPT_LIMIT = 50 * 1024 * 1024
 

time: 40.6 us -> 41.4 us (1.020)
  Pallas kernels: 7.14 us -> 7.95 us
    pallas_call x12, Pallas kernels: 7.14 us -> 7.95 us  [call(): pl.pallas_call(kernel, out_shape=outs, in_specs=[far if i in tuple(far_in...]
  transfers between devices with their start and end apart: 16 -> 16, of which waited for: 13 -> 13; matrix products, arithmetic and copies ran while one was open for 0% -> 0% of each run, Pallas kernels for 9% -> 10%
where the time goes in v12:
time: 41.4 us; the launch traced here: 41.2 us
  starting transfers between devices  17.3 us (42%)
  waiting for transfers between devices  15.2 us (37%)
  Pallas kernels  7.95 us (19%)
  between operations  0.77 us (2%)
    ppermute x16, starting transfers between devices, exchange(): return lax.ppermute(value, ('rep', 'shard'), pairs)  17.3 us
    ppermute x16, waiting for transfers between devices, exchange(): return lax.ppermute(value, ('rep', 'shard'), pairs)  15.2 us
    pallas_call x12, Pallas kernels, call(): pl.pallas_call(kernel, out_shape=outs, in_specs=[far if i in tuple(far_in...  7.95 us
  transfers between devices with their start and end apart: 16, of which 13 were waited for; matrix products, arithmetic and copies ran while one was open for 0% of the time, Pallas kernels for 10%

profile of v12, /device:TPU:0, one launch (start us, length us, event | category | flops | bytes accessed | tf_op | source)
XLA Modules:
  0.0 41.2 jit_solution(4587459828501210469)
XLA Ops:
  0.6 1.9 %shard_map.76.cots = bf16[768,2048]{1,0:T(8,128)(2,1)S(1)} custom-call(bf16[768,4096]{1,0:T(8,128)(2,1)} %cots_ref.3), custom_call_target="tpu_custom_call" | custom-call | tf_op jit(solution)/shard_map/pallas_call | solution.py:37
  2.6 0.6 %shard_map.77 = (bf16[128,2048]{1,0:T(8,128)(2,1)S(1)}, bf16[128,768]{1,0:T(8,128)(2,1)S(1)}) custom-call(bf16[768,128]{1,0:T(8,128)(2,1)S(1)} %copy-done.2, bf16[768,2048]{1,0:T(8,128)(2,1)S(1)} %shard_map.76.cots), custom_call_target="tpu_custom_call" | custom-call | tf_op jit(solution)/shard_map/pallas_call | solution.py:37
  3.8 3.1 %shard_map.78.kept = f32[128,2048]{1,0:T(8,128)S(1)} custom-call(bf16[128,768]{1,0:T(8,128)(2,1)S(1)} %get-tuple-element.25.turned, bf16[768,4096]{1,0:T(8,128)(2,1)} %cots_ref.3), custom_call_target="tpu_custom_call" | custom-call | tf_op jit(solution)/shard_map/pallas_call | solution.py:37
  7.0 3.5 %collective-permute-start.1 = (bf16[64,1024]{1,0:T(8,128)(2,1)S(1)}, bf16[64,1024]{1,0:T(8,128)(2,1)S(1)}, u32[]{:S(2)}, u32[]{:S(2)}) collective-permute-start(bf16[64,1024]{1,0:T(8,128)(2,1)S(1)} %get-tuple-element.28), channel_id=1, source_target_pairs={{0,17},{1,5},{2,6},{3,18},{4,21},{5,1},{6,2},{7,22},{8,12},{9,24},... | collective-permute-start | bytes 393224 | tf_op jit(solution)/shard_map/ppermute | solution.py:55
  10.9 2.6 %collective-permute-done.1.refs_0_ = bf16[64,1024]{1,0:T(8,128)(2,1)S(1)} collective-permute-done((bf16[64,1024]{1,0:T(8,128)(2,1)S(1)}, bf16[64,1024]{1,0:T(8,128)(2,1)S(1)}, u32[]{:S(2)}, u32[]{:S(2)}) %collective-permute-start.1) | collective-permute-done | bytes 131104 | tf_op jit(solution)/shard_map/ppermute | solution.py:55
  13.5 1.4 %collective-permute-done.2.refs_1_ = bf16[64,1024]{1,0:T(8,128)(2,1)S(1)} collective-permute-done((bf16[64,1024]{1,0:T(8,128)(2,1)S(1)}, bf16[64,1024]{1,0:T(8,128)(2,1)S(1)}, u32[]{:S(2)}, u32[]{:S(2)}) %collective-permute-start.2) | collective-permute-done | bytes 131104 | tf_op jit(solution)/shard_map/ppermute | solution.py:55
  15.3 2.8 %collective-permute-start.4 = (bf16[16,1024]{1,0:T(8,128)(2,1)S(1)}, bf16[16,1024]{1,0:T(8,128)(2,1)S(1)}, u32[]{:S(2)}, u32[]{:S(2)}) collective-permute-start(bf16[16,1024]{1,0:T(8,128)(2,1)S(1)} %get-tuple-element.32), channel_id=1, source_target_pairs={{0,4},{1,16},{2,19},{3,7},{4,0},{5,20},{6,23},{7,3},{8,25},{9,13},... | collective-permute-start | bytes 98312 | tf_op jit(solution)/shard_map/ppermute | solution.py:55
  18.1 1.2 %collective-permute-start.5 = (bf16[16,1024]{1,0:T(8,128)(2,1)S(1)}, bf16[16,1024]{1,0:T(8,128)(2,1)S(1)}, u32[]{:S(2)}, u32[]{:S(2)}) collective-permute-start(bf16[16,1024]{1,0:T(8,128)(2,1)S(1)} %get-tuple-element.33), channel_id=1, source_target_pairs={{0,14},{1,8},{2,11},{3,13},{4,10},{5,12},{6,15},{7,9},{8,1},{9,7},... | collective-permute-start | bytes 98312 | tf_op jit(solution)/shard_map/ppermute | solution.py:55
  19.5 0.7 %collective-permute-done.4.refs_0_ = bf16[16,1024]{1,0:T(8,128)(2,1)S(1)} collective-permute-done((bf16[16,1024]{1,0:T(8,128)(2,1)S(1)}, bf16[16,1024]{1,0:T(8,128)(2,1)S(1)}, u32[]{:S(2)}, u32[]{:S(2)}) %collective-permute-start.4) | collective-permute-done | bytes 32800 | tf_op jit(solution)/shard_map/ppermute | solution.py:55
  20.2 3.0 %collective-permute-done.5.refs_1_ = bf16[16,1024]{1,0:T(8,128)(2,1)S(1)} collective-permute-done((bf16[16,1024]{1,0:T(8,128)(2,1)S(1)}, bf16[16,1024]{1,0:T(8,128)(2,1)S(1)}, u32[]{:S(2)}, u32[]{:S(2)}) %collective-permute-start.5) | collective-permute-done | bytes 32800 | tf_op jit(solution)/shard_map/ppermute | solution.py:55
  23.3 1.5 %collective-permute-start.7 = (bf16[16,1024]{1,0:T(8,128)(2,1)S(1)}, bf16[16,1024]{1,0:T(8,128)(2,1)S(1)}, u32[]{:S(2)}, u32[]{:S(2)}) collective-permute-start(bf16[16,1024]{1,0:T(8,128)(2,1)S(1)} %get-tuple-element.38), channel_id=1, source_target_pairs={{0,17},{1,5},{2,6},{3,18},{4,21},{5,1},{6,2},{7,22},{8,12},{9,24},... | collective-permute-start | bytes 98312 | tf_op jit(solution)/shard_map/ppermute | solution.py:55
  24.9 0.8 %collective-permute-start.8 = (bf16[16,1024]{1,0:T(8,128)(2,1)S(1)}, bf16[16,1024]{1,0:T(8,128)(2,1)S(1)}, u32[]{:S(2)}, u32[]{:S(2)}) collective-permute-start(bf16[16,1024]{1,0:T(8,128)(2,1)S(1)} %get-tuple-element.39), channel_id=1, source_target_pairs={{0,9},{1,15},{2,12},{3,10},{4,13},{5,11},{6,8},{7,14},{8,6},{9,0},... | collective-permute-start | bytes 98312 | tf_op jit(solution)/shard_map/ppermute | solution.py:55
  25.7 0.9 %collective-permute-start.10 = (bf16[16,1024]{1,0:T(8,128)(2,1)S(1)}, bf16[16,1024]{1,0:T(8,128)(2,1)S(1)}, u32[]{:S(2)}, u32[]{:S(2)}) collective-permute-start(bf16[16,1024]{1,0:T(8,128)(2,1)S(1)} %get-tuple-element.40), channel_id=1, source_target_pairs={{0,24},{1,25},{2,26},{3,27},{4,28},{5,29},{6,30},{7,31},{8,16},{9,... | collective-permute-start | bytes 98312 | tf_op jit(solution)/shard_map/ppermute | solution.py:55
  26.6 0.8 %collective-permute-start.9 = (bf16[16,1024]{1,0:T(8,128)(2,1)S(1)}, bf16[16,1024]{1,0:T(8,128)(2,1)S(1)}, u32[]{:S(2)}, u32[]{:S(2)}) collective-permute-start(bf16[16,1024]{1,0:T(8,128)(2,1)S(1)} %get-tuple-element.37.own), channel_id=1, source_target_pairs={{0,24},{1,11},{2,8},{3,27},{4,28},{5,15},{6,12},{7,31},{8,2},{9,17... | collective-permute-start | bytes 98312 | tf_op jit(solution)/shard_map/ppermute | solution.py:55
  27.4 0.9 %collective-permute-done.7.refs_0_ = bf16[16,1024]{1,0:T(8,128)(2,1)S(1)} collective-permute-done((bf16[16,1024]{1,0:T(8,128)(2,1)S(1)}, bf16[16,1024]{1,0:T(8,128)(2,1)S(1)}, u32[]{:S(2)}, u32[]{:S(2)}) %collective-permute-start.7) | collective-permute-done | bytes 32800 | tf_op jit(solution)/shard_map/ppermute | solution.py:55
  29.0 0.9 %collective-permute-done.9.refs_2_ = bf16[16,1024]{1,0:T(8,128)(2,1)S(1)} collective-permute-done((bf16[16,1024]{1,0:T(8,128)(2,1)S(1)}, bf16[16,1024]{1,0:T(8,128)(2,1)S(1)}, u32[]{:S(2)}, u32[]{:S(2)}) %collective-permute-start.9) | collective-permute-done | bytes 32800 | tf_op jit(solution)/shard_map/ppermute | solution.py:55
  30.0 1.1 %collective-permute-start.11 = (bf16[64,1024]{1,0:T(8,128)(2,1)S(1)}, bf16[64,1024]{1,0:T(8,128)(2,1)S(1)}, u32[]{:S(2)}, u32[]{:S(2)}) collective-permute-start(bf16[64,1024]{1,0:T(8,128)(2,1)S(1)} %get-tuple-element.42), channel_id=1, source_target_pairs={{0,4},{1,16},{2,19},{3,7},{4,0},{5,20},{6,23},{7,3},{8,25},{9,13},... | collective-permute-start | bytes 393224 | tf_op jit(solution)/shard_map/ppermute | solution.py:55
  31.1 0.9 %collective-permute-start.13 = (bf16[64,1024]{1,0:T(8,128)(2,1)S(1)}, bf16[64,1024]{1,0:T(8,128)(2,1)S(1)}, u32[]{:S(2)}, u32[]{:S(2)}) collective-permute-start(bf16[64,1024]{1,0:T(8,128)(2,1)S(1)} %get-tuple-element.43), channel_id=1, source_target_pairs={{0,14},{1,8},{2,11},{3,13},{4,10},{5,12},{6,15},{7,9},{8,1},{9,7},... | collective-permute-start | bytes 393224 | tf_op jit(solution)/shard_map/ppermute | solution.py:55
  32.0 1.3 %collective-permute-start.14 = (bf16[64,1024]{1,0:T(8,128)(2,1)S(1)}, bf16[64,1024]{1,0:T(8,128)(2,1)S(1)}, u32[]{:S(2)}, u32[]{:S(2)}) collective-permute-start(bf16[64,1024]{1,0:T(8,128)(2,1)S(1)} %get-tuple-element.41.refs_0_), channel_id=1, source_target_pairs={{0,10},{1,25},{2,26},{3,9},{4,14},{5,29},{6,30},{7,13},{8,16},{9,3... | collective-permute-start | bytes 393224 | tf_op jit(solution)/shard_map/ppermute | solution.py:55
  33.3 2.8 %collective-permute-done.11.refs_1_ = bf16[64,1024]{1,0:T(8,128)(2,1)S(1)} collective-permute-done((bf16[64,1024]{1,0:T(8,128)(2,1)S(1)}, bf16[64,1024]{1,0:T(8,128)(2,1)S(1)}, u32[]{:S(2)}, u32[]{:S(2)}) %collective-permute-start.11) | collective-permute-done | bytes 131104 | tf_op jit(solution)/shard_map/ppermute | solution.py:55
  36.1 1.1 %collective-permute-start.12 = (bf16[160,1024]{1,0:T(8,128)(2,1)S(1)}, bf16[160,1024]{1,0:T(8,128)(2,1)S(1)}, u32[]{:S(2)}, u32[]{:S(2)}) collective-permute-start(bf16[160,1024]{1,0:T(8,128)(2,1)S(1)} %shard_map.84), channel_id=1, source_target_pairs={{0,8},{1,9},{2,10},{3,11},{4,12},{5,13},{6,14},{7,15},{8,0},{9,1},... | collective-permute-start | bytes 983048 | tf_op jit(solution)/shard_map/ppermute | solution.py:55
  37.5 1.3 %collective-permute-done.14.refs_1_.refs_3_ = bf16[64,1024]{1,0:T(8,128)(2,1)S(1)} collective-permute-done((bf16[64,1024]{1,0:T(8,128)(2,1)S(1)}, bf16[64,1024]{1,0:T(8,128)(2,1)S(1)}, u32[]{:S(2)}, u32[]{:S(2)}) %collective-permute-start.14) | collective-permute-done | bytes 131104 | tf_op jit(solution)/shard_map/ppermute | solution.py:55
  39.0 1.1 %shard_map.86 = (bf16[128,4096]{1,0:T(8,128)(2,1)}, f32[16,4096]{1,0:T(8,128)}, f32[16,4096]{1,0:T(8,128)}) custom-call(f32[16,4096]{1,0:T(8,128)S(1)} %copy-done, f32[16,4096]{1,0:T(8,128)S(1)} %copy-done.1, bf16[16,1024]{1,0:T(8,128)(2,1)S(1)} %get-tuple-element.35.grad.refs_2_, bf16[16,1024]{1,0:T(8,128)(2,1)S(1)} %collective-permute-done.10.refs_3_.far_grad, ...), custom_call_target="tpu_custom_call" | custom-call | tf_op jit(solution)/shard_map/pallas_call | solution.py:37
  40.4 0.8 %shard_map.87 = bf16[128,4096]{1,0:T(8,128)(2,1)} custom-call(bf16[160,1024]{1,0:T(8,128)(2,1)S(1)} %collective-permute-done.12.early, bf16[128,1024]{1,0:T(8,128)(2,1)S(1)} %collective-permute-done.15.late, bf16[128,4096]{1,0:T(8,128)(2,1)} %get-tuple-element.44._), custom_call_target="tpu_custom_call", output_to_operand_aliasing={{}: (2, {})} | custom-call | tf_op jit(solution)/shard_map/pallas_call | solution.py:37
  (28 shorter events, 3.2 us)
Async XLA Ops:
  0.6 2.0 %copy-start.2 = (bf16[768,128]{1,0:T(8,128)(2,1)S(1)}, bf16[768,128]{1,0:T(8,128)(2,1)}, u32[]{:S(2)}) copy-start(bf16[768,128]{1,0:T(8,128)(2,1)} %acts.1) | copy-start | bytes 589828
  2.6 20.6 %copy-start = (f32[16,4096]{1,0:T(8,128)S(1)}, f32[16,4096]{1,0:T(8,128)}, u32[]{:S(2)}) copy-start(f32[16,4096]{1,0:T(8,128)} %m.3) | copy-start | bytes 786436
  2.6 20.6 %copy-start.1 = (f32[16,4096]{1,0:T(8,128)S(1)}, f32[16,4096]{1,0:T(8,128)}, u32[]{:S(2)}) copy-start(f32[16,4096]{1,0:T(8,128)} %v.3) | copy-start | bytes 786436
  2.6 20.6 %copy-start.3 = (bf16[16,4096]{1,0:T(8,128)(2,1)S(1)}, bf16[16,4096]{1,0:T(8,128)(2,1)}, u32[]{:S(2)}) copy-start(bf16[16,4096]{1,0:T(8,128)(2,1)} %w.1) | copy-start | bytes 393220
  3.3 3.6 %collective-permute-start = (bf16[128,2048]{1,0:T(8,128)(2,1)S(1)}, bf16[128,2048]{1,0:T(8,128)(2,1)S(1)}, u32[]{:S(2)}, u32[]{:S(2)}) collective-permute-start(bf16[128,2048]{1,0:T(8,128)(2,1)S(1)} %get-tuple-element.26), channel_id=1, source_target_pairs={{0,8},{1,9},{2,10},{3,11},{4,12},{5,13},{6,14},{7,15},{8,0},{9,1},... | collective-permute-start | bytes 1572872 | tf_op jit(solution)/shard_map/ppermute | solution.py:55
  7.0 6.5 %collective-permute-start.1 = (bf16[64,1024]{1,0:T(8,128)(2,1)S(1)}, bf16[64,1024]{1,0:T(8,128)(2,1)S(1)}, u32[]{:S(2)}, u32[]{:S(2)}) collective-permute-start(bf16[64,1024]{1,0:T(8,128)(2,1)S(1)} %get-tuple-element.28), channel_id=1, source_target_pairs={{0,17},{1,5},{2,6},{3,18},{4,21},{5,1},{6,2},{7,22},{8,12},{9,24},... | collective-permute-start | bytes 393224 | tf_op jit(solution)/shard_map/ppermute | solution.py:55
  10.5 4.4 %collective-permute-start.2 = (bf16[64,1024]{1,0:T(8,128)(2,1)S(1)}, bf16[64,1024]{1,0:T(8,128)(2,1)S(1)}, u32[]{:S(2)}, u32[]{:S(2)}) collective-permute-start(bf16[64,1024]{1,0:T(8,128)(2,1)S(1)} %get-tuple-element.29), channel_id=1, source_target_pairs={{0,9},{1,15},{2,12},{3,10},{4,13},{5,11},{6,8},{7,14},{8,6},{9,0},... | collective-permute-start | bytes 393224 | tf_op jit(solution)/shard_map/ppermute | solution.py:55
  10.8 4.4 %collective-permute-start.3 = (bf16[64,1024]{1,0:T(8,128)(2,1)S(1)}, bf16[64,1024]{1,0:T(8,128)(2,1)S(1)}, u32[]{:S(2)}, u32[]{:S(2)}) collective-permute-start(bf16[64,1024]{1,0:T(8,128)(2,1)S(1)} %get-tuple-element.30), channel_id=1, source_target_pairs={{0,24},{1,11},{2,8},{3,27},{4,28},{5,15},{6,12},{7,31},{8,2},{9,17... | collective-permute-start | bytes 393224 | tf_op jit(solution)/shard_map/ppermute | solution.py:55
  15.3 4.9 %collective-permute-start.4 = (bf16[16,1024]{1,0:T(8,128)(2,1)S(1)}, bf16[16,1024]{1,0:T(8,128)(2,1)S(1)}, u32[]{:S(2)}, u32[]{:S(2)}) collective-permute-start(bf16[16,1024]{1,0:T(8,128)(2,1)S(1)} %get-tuple-element.32), channel_id=1, source_target_pairs={{0,4},{1,16},{2,19},{3,7},{4,0},{5,20},{6,23},{7,3},{8,25},{9,13},... | collective-permute-start | bytes 98312 | tf_op jit(solution)/shard_map/ppermute | solution.py:55
  18.1 5.1 %collective-permute-start.5 = (bf16[16,1024]{1,0:T(8,128)(2,1)S(1)}, bf16[16,1024]{1,0:T(8,128)(2,1)S(1)}, u32[]{:S(2)}, u32[]{:S(2)}) collective-permute-start(bf16[16,1024]{1,0:T(8,128)(2,1)S(1)} %get-tuple-element.33), channel_id=1, source_target_pairs={{0,14},{1,8},{2,11},{3,13},{4,10},{5,12},{6,15},{7,9},{8,1},{9,7},... | collective-permute-start | bytes 98312 | tf_op jit(solution)/shard_map/ppermute | solution.py:55
  19.3 4.0 %collective-permute-start.6 = (bf16[16,1024]{1,0:T(8,128)(2,1)S(1)}, bf16[16,1024]{1,0:T(8,128)(2,1)S(1)}, u32[]{:S(2)}, u32[]{:S(2)}) collective-permute-start(bf16[16,1024]{1,0:T(8,128)(2,1)S(1)} %get-tuple-element.34), channel_id=1, source_target_pairs={{0,10},{1,25},{2,26},{3,9},{4,14},{5,29},{6,30},{7,13},{8,16},{9,3... | collective-permute-start | bytes 98312 | tf_op jit(solution)/shard_map/ppermute | solution.py:55
  23.3 5.0 %collective-permute-start.7 = (bf16[16,1024]{1,0:T(8,128)(2,1)S(1)}, bf16[16,1024]{1,0:T(8,128)(2,1)S(1)}, u32[]{:S(2)}, u32[]{:S(2)}) collective-permute-start(bf16[16,1024]{1,0:T(8,128)(2,1)S(1)} %get-tuple-element.38), channel_id=1, source_target_pairs={{0,17},{1,5},{2,6},{3,18},{4,21},{5,1},{6,2},{7,22},{8,12},{9,24},... | collective-permute-start | bytes 98312 | tf_op jit(solution)/shard_map/ppermute | solution.py:55
  24.9 3.7 %collective-permute-start.8 = (bf16[16,1024]{1,0:T(8,128)(2,1)S(1)}, bf16[16,1024]{1,0:T(8,128)(2,1)S(1)}, u32[]{:S(2)}, u32[]{:S(2)}) collective-permute-start(bf16[16,1024]{1,0:T(8,128)(2,1)S(1)} %get-tuple-element.39), channel_id=1, source_target_pairs={{0,9},{1,15},{2,12},{3,10},{4,13},{5,11},{6,8},{7,14},{8,6},{9,0},... | collective-permute-start | bytes 98312 | tf_op jit(solution)/shard_map/ppermute | solution.py:55
  25.7 3.3 %collective-permute-start.10 = (bf16[16,1024]{1,0:T(8,128)(2,1)S(1)}, bf16[16,1024]{1,0:T(8,128)(2,1)S(1)}, u32[]{:S(2)}, u32[]{:S(2)}) collective-permute-start(bf16[16,1024]{1,0:T(8,128)(2,1)S(1)} %get-tuple-element.40), channel_id=1, source_target_pairs={{0,24},{1,25},{2,26},{3,27},{4,28},{5,29},{6,30},{7,31},{8,16},{9,... | collective-permute-start | bytes 98312 | tf_op jit(solution)/shard_map/ppermute | solution.py:55
  26.6 3.3 %collective-permute-start.9 = (bf16[16,1024]{1,0:T(8,128)(2,1)S(1)}, bf16[16,1024]{1,0:T(8,128)(2,1)S(1)}, u32[]{:S(2)}, u32[]{:S(2)}) collective-permute-start(bf16[16,1024]{1,0:T(8,128)(2,1)S(1)} %get-tuple-element.37.own), channel_id=1, source_target_pairs={{0,24},{1,11},{2,8},{3,27},{4,28},{5,15},{6,12},{7,31},{8,2},{9,17... | collective-permute-start | bytes 98312 | tf_op jit(solution)/shard_map/ppermute | solution.py:55
  30.0 6.1 %collective-permute-start.11 = (bf16[64,1024]{1,0:T(8,128)(2,1)S(1)}, bf16[64,1024]{1,0:T(8,128)(2,1)S(1)}, u32[]{:S(2)}, u32[]{:S(2)}) collective-permute-start(bf16[64,1024]{1,0:T(8,128)(2,1)S(1)} %get-tuple-element.42), channel_id=1, source_target_pairs={{0,4},{1,16},{2,19},{3,7},{4,0},{5,20},{6,23},{7,3},{8,25},{9,13},... | collective-permute-start | bytes 393224 | tf_op jit(solution)/shard_map/ppermute | solution.py:55
  31.1 6.4 %collective-permute-start.13 = (bf16[64,1024]{1,0:T(8,128)(2,1)S(1)}, bf16[64,1024]{1,0:T(8,128)(2,1)S(1)}, u32[]{:S(2)}, u32[]{:S(2)}) collective-permute-start(bf16[64,1024]{1,0:T(8,128)(2,1)S(1)} %get-tuple-element.43), channel_id=1, source_target_pairs={{0,14},{1,8},{2,11},{3,13},{4,10},{5,12},{6,15},{7,9},{8,1},{9,7},... | collective-permute-start | bytes 393224 | tf_op jit(solution)/shard_map/ppermute | solution.py:55
  32.0 6.8 %collective-permute-start.14 = (bf16[64,1024]{1,0:T(8,128)(2,1)S(1)}, bf16[64,1024]{1,0:T(8,128)(2,1)S(1)}, u32[]{:S(2)}, u32[]{:S(2)}) collective-permute-start(bf16[64,1024]{1,0:T(8,128)(2,1)S(1)} %get-tuple-element.41.refs_0_), channel_id=1, source_target_pairs={{0,10},{1,25},{2,26},{3,9},{4,14},{5,29},{6,30},{7,13},{8,16},{9,3... | collective-permute-start | bytes 393224 | tf_op jit(solution)/shard_map/ppermute | solution.py:55
  36.1 2.9 %collective-permute-start.12 = (bf16[160,1024]{1,0:T(8,128)(2,1)S(1)}, bf16[160,1024]{1,0:T(8,128)(2,1)S(1)}, u32[]{:S(2)}, u32[]{:S(2)}) collective-permute-start(bf16[160,1024]{1,0:T(8,128)(2,1)S(1)} %shard_map.84), channel_id=1, source_target_pairs={{0,8},{1,9},{2,10},{3,11},{4,12},{5,13},{6,14},{7,15},{8,0},{9,1},... | collective-permute-start | bytes 983048 | tf_op jit(solution)/shard_map/ppermute | solution.py:55
  38.8 1.6 %collective-permute-start.15 = (bf16[128,1024]{1,0:T(8,128)(2,1)S(1)}, bf16[128,1024]{1,0:T(8,128)(2,1)S(1)}, u32[]{:S(2)}, u32[]{:S(2)}) collective-permute-start(bf16[128,1024]{1,0:T(8,128)(2,1)S(1)} %shard_map.85), channel_id=1, source_target_pairs={{0,8},{1,9},{2,10},{3,11},{4,12},{5,13},{6,14},{7,15},{8,0},{9,1},... | collective-permute-start | bytes 786440 | tf_op jit(solution)/shard_map/ppermute | solution.py:55

commit v13 on v12

--- a/solution.py
+++ b/solution.py
@@ -9,7 +9,7 @@
 
 F32 = jnp.float32
 BF16 = jnp.bfloat16
-CHUNK = 256
+CHUNK = 1024
 LOAD_LIMIT = 48 * 1024 * 1024
 KEPT_LIMIT = 50 * 1024 * 1024
 

time: 41.4 us -> 40.6 us (0.981)
  Pallas kernels: 7.95 us -> 7.19 us
    pallas_call x12, Pallas kernels: 7.95 us -> 7.19 us  [call(): pl.pallas_call(kernel, out_shape=outs, in_specs=[far if i in tuple(far_in...]
  transfers between devices with their start and end apart: 16 -> 16, of which waited for: 13 -> 13; matrix products, arithmetic and copies ran while one was open for 0% -> 0% of each run, Pallas kernels for 10% -> 9%
where the time goes in v13:
time: 40.6 us; the launch traced here: 40.5 us
  starting transfers between devices  17.3 us (43%)
  waiting for transfers between devices  15.2 us (37%)
  Pallas kernels  7.19 us (18%)
  between operations  0.77 us (2%)
    ppermute x16, starting transfers between devices, exchange(): return lax.ppermute(value, ('rep', 'shard'), pairs)  17.3 us
    ppermute x16, waiting for transfers between devices, exchange(): return lax.ppermute(value, ('rep', 'shard'), pairs)  15.2 us
    pallas_call x12, Pallas kernels, call(): pl.pallas_call(kernel, out_shape=outs, in_specs=[far if i in tuple(far_in...  7.19 us
  transfers between devices with their start and end apart: 16, of which 13 were waited for; matrix products, arithmetic and copies ran while one was open for 0% of the time, Pallas kernels for 9%

profile of v13, /device:TPU:0, one launch (start us, length us, event | category | flops | bytes accessed | tf_op | source)
XLA Modules:
  0.0 40.5 jit_solution(16366133310169071005)
XLA Ops:
  0.6 1.9 %shard_map.76.cots = bf16[768,2048]{1,0:T(8,128)(2,1)S(1)} custom-call(bf16[768,4096]{1,0:T(8,128)(2,1)} %cots_ref.3), custom_call_target="tpu_custom_call" | custom-call | tf_op jit(solution)/shard_map/pallas_call | solution.py:37
  2.6 0.6 %shard_map.77 = (bf16[128,2048]{1,0:T(8,128)(2,1)S(1)}, bf16[128,768]{1,0:T(8,128)(2,1)S(1)}) custom-call(bf16[768,128]{1,0:T(8,128)(2,1)S(1)} %copy-done.2, bf16[768,2048]{1,0:T(8,128)(2,1)S(1)} %shard_map.76.cots), custom_call_target="tpu_custom_call" | custom-call | tf_op jit(solution)/shard_map/pallas_call | solution.py:37
  3.8 2.3 %shard_map.78.kept = f32[128,2048]{1,0:T(8,128)S(1)} custom-call(bf16[128,768]{1,0:T(8,128)(2,1)S(1)} %get-tuple-element.25.turned, bf16[768,4096]{1,0:T(8,128)(2,1)} %cots_ref.3), custom_call_target="tpu_custom_call" | custom-call | tf_op jit(solution)/shard_map/pallas_call | solution.py:37
  6.2 3.5 %collective-permute-start.1 = (bf16[64,1024]{1,0:T(8,128)(2,1)S(1)}, bf16[64,1024]{1,0:T(8,128)(2,1)S(1)}, u32[]{:S(2)}, u32[]{:S(2)}) collective-permute-start(bf16[64,1024]{1,0:T(8,128)(2,1)S(1)} %get-tuple-element.28), channel_id=1, source_target_pairs={{0,17},{1,5},{2,6},{3,18},{4,21},{5,1},{6,2},{7,22},{8,12},{9,24},... | collective-permute-start | bytes 393224 | tf_op jit(solution)/shard_map/ppermute | solution.py:55
  10.1 2.6 %collective-permute-done.1.refs_0_ = bf16[64,1024]{1,0:T(8,128)(2,1)S(1)} collective-permute-done((bf16[64,1024]{1,0:T(8,128)(2,1)S(1)}, bf16[64,1024]{1,0:T(8,128)(2,1)S(1)}, u32[]{:S(2)}, u32[]{:S(2)}) %collective-permute-start.1) | collective-permute-done | bytes 131104 | tf_op jit(solution)/shard_map/ppermute | solution.py:55
  12.7 1.4 %collective-permute-done.2.refs_1_ = bf16[64,1024]{1,0:T(8,128)(2,1)S(1)} collective-permute-done((bf16[64,1024]{1,0:T(8,128)(2,1)S(1)}, bf16[64,1024]{1,0:T(8,128)(2,1)S(1)}, u32[]{:S(2)}, u32[]{:S(2)}) %collective-permute-start.2) | collective-permute-done | bytes 131104 | tf_op jit(solution)/shard_map/ppermute | solution.py:55
  14.5 2.8 %collective-permute-start.4 = (bf16[16,1024]{1,0:T(8,128)(2,1)S(1)}, bf16[16,1024]{1,0:T(8,128)(2,1)S(1)}, u32[]{:S(2)}, u32[]{:S(2)}) collective-permute-start(bf16[16,1024]{1,0:T(8,128)(2,1)S(1)} %get-tuple-element.32), channel_id=1, source_target_pairs={{0,4},{1,16},{2,19},{3,7},{4,0},{5,20},{6,23},{7,3},{8,25},{9,13},... | collective-permute-start | bytes 98312 | tf_op jit(solution)/shard_map/ppermute | solution.py:55
  17.3 1.2 %collective-permute-start.5 = (bf16[16,1024]{1,0:T(8,128)(2,1)S(1)}, bf16[16,1024]{1,0:T(8,128)(2,1)S(1)}, u32[]{:S(2)}, u32[]{:S(2)}) collective-permute-start(bf16[16,1024]{1,0:T(8,128)(2,1)S(1)} %get-tuple-element.33), channel_id=1, source_target_pairs={{0,14},{1,8},{2,11},{3,13},{4,10},{5,12},{6,15},{7,9},{8,1},{9,7},... | collective-permute-start | bytes 98312 | tf_op jit(solution)/shard_map/ppermute | solution.py:55
  18.7 0.7 %collective-permute-done.4.refs_0_ = bf16[16,1024]{1,0:T(8,128)(2,1)S(1)} collective-permute-done((bf16[16,1024]{1,0:T(8,128)(2,1)S(1)}, bf16[16,1024]{1,0:T(8,128)(2,1)S(1)}, u32[]{:S(2)}, u32[]{:S(2)}) %collective-permute-start.4) | collective-permute-done | bytes 32800 | tf_op jit(solution)/shard_map/ppermute | solution.py:55
  19.4 3.0 %collective-permute-done.5.refs_1_ = bf16[16,1024]{1,0:T(8,128)(2,1)S(1)} collective-permute-done((bf16[16,1024]{1,0:T(8,128)(2,1)S(1)}, bf16[16,1024]{1,0:T(8,128)(2,1)S(1)}, u32[]{:S(2)}, u32[]{:S(2)}) %collective-permute-start.5) | collective-permute-done | bytes 32800 | tf_op jit(solution)/shard_map/ppermute | solution.py:55
  22.6 1.5 %collective-permute-start.7 = (bf16[16,1024]{1,0:T(8,128)(2,1)S(1)}, bf16[16,1024]{1,0:T(8,128)(2,1)S(1)}, u32[]{:S(2)}, u32[]{:S(2)}) collective-permute-start(bf16[16,1024]{1,0:T(8,128)(2,1)S(1)} %get-tuple-element.38), channel_id=1, source_target_pairs={{0,17},{1,5},{2,6},{3,18},{4,21},{5,1},{6,2},{7,22},{8,12},{9,24},... | collective-permute-start | bytes 98312 | tf_op jit(solution)/shard_map/ppermute | solution.py:55
  24.1 0.8 %collective-permute-start.8 = (bf16[16,1024]{1,0:T(8,128)(2,1)S(1)}, bf16[16,1024]{1,0:T(8,128)(2,1)S(1)}, u32[]{:S(2)}, u32[]{:S(2)}) collective-permute-start(bf16[16,1024]{1,0:T(8,128)(2,1)S(1)} %get-tuple-element.39), channel_id=1, source_target_pairs={{0,9},{1,15},{2,12},{3,10},{4,13},{5,11},{6,8},{7,14},{8,6},{9,0},... | collective-permute-start | bytes 98312 | tf_op jit(solution)/shard_map/ppermute | solution.py:55
  24.9 0.9 %collective-permute-start.10 = (bf16[16,1024]{1,0:T(8,128)(2,1)S(1)}, bf16[16,1024]{1,0:T(8,128)(2,1)S(1)}, u32[]{:S(2)}, u32[]{:S(2)}) collective-permute-start(bf16[16,1024]{1,0:T(8,128)(2,1)S(1)} %get-tuple-element.40), channel_id=1, source_target_pairs={{0,24},{1,25},{2,26},{3,27},{4,28},{5,29},{6,30},{7,31},{8,16},{9,... | collective-permute-start | bytes 98312 | tf_op jit(solution)/shard_map/ppermute | solution.py:55
  25.8 0.8 %collective-permute-start.9 = (bf16[16,1024]{1,0:T(8,128)(2,1)S(1)}, bf16[16,1024]{1,0:T(8,128)(2,1)S(1)}, u32[]{:S(2)}, u32[]{:S(2)}) collective-permute-start(bf16[16,1024]{1,0:T(8,128)(2,1)S(1)} %get-tuple-element.37.own), channel_id=1, source_target_pairs={{0,24},{1,11},{2,8},{3,27},{4,28},{5,15},{6,12},{7,31},{8,2},{9,17... | collective-permute-start | bytes 98312 | tf_op jit(solution)/shard_map/ppermute | solution.py:55
  26.7 0.9 %collective-permute-done.7.refs_0_ = bf16[16,1024]{1,0:T(8,128)(2,1)S(1)} collective-permute-done((bf16[16,1024]{1,0:T(8,128)(2,1)S(1)}, bf16[16,1024]{1,0:T(8,128)(2,1)S(1)}, u32[]{:S(2)}, u32[]{:S(2)}) %collective-permute-start.7) | collective-permute-done | bytes 32800 | tf_op jit(solution)/shard_map/ppermute | solution.py:55
  28.3 0.9 %collective-permute-done.9.refs_2_ = bf16[16,1024]{1,0:T(8,128)(2,1)S(1)} collective-permute-done((bf16[16,1024]{1,0:T(8,128)(2,1)S(1)}, bf16[16,1024]{1,0:T(8,128)(2,1)S(1)}, u32[]{:S(2)}, u32[]{:S(2)}) %collective-permute-start.9) | collective-permute-done | bytes 32800 | tf_op jit(solution)/shard_map/ppermute | solution.py:55
  29.2 1.1 %collective-permute-start.11 = (bf16[64,1024]{1,0:T(8,128)(2,1)S(1)}, bf16[64,1024]{1,0:T(8,128)(2,1)S(1)}, u32[]{:S(2)}, u32[]{:S(2)}) collective-permute-start(bf16[64,1024]{1,0:T(8,128)(2,1)S(1)} %get-tuple-element.42), channel_id=1, source_target_pairs={{0,4},{1,16},{2,19},{3,7},{4,0},{5,20},{6,23},{7,3},{8,25},{9,13},... | collective-permute-start | bytes 393224 | tf_op jit(solution)/shard_map/ppermute | solution.py:55
  30.3 0.9 %collective-permute-start.13 = (bf16[64,1024]{1,0:T(8,128)(2,1)S(1)}, bf16[64,1024]{1,0:T(8,128)(2,1)S(1)}, u32[]{:S(2)}, u32[]{:S(2)}) collective-permute-start(bf16[64,1024]{1,0:T(8,128)(2,1)S(1)} %get-tuple-element.43), channel_id=1, source_target_pairs={{0,14},{1,8},{2,11},{3,13},{4,10},{5,12},{6,15},{7,9},{8,1},{9,7},... | collective-permute-start | bytes 393224 | tf_op jit(solution)/shard_map/ppermute | solution.py:55
  31.2 1.3 %collective-permute-start.14 = (bf16[64,1024]{1,0:T(8,128)(2,1)S(1)}, bf16[64,1024]{1,0:T(8,128)(2,1)S(1)}, u32[]{:S(2)}, u32[]{:S(2)}) collective-permute-start(bf16[64,1024]{1,0:T(8,128)(2,1)S(1)} %get-tuple-element.41.refs_0_), channel_id=1, source_target_pairs={{0,10},{1,25},{2,26},{3,9},{4,14},{5,29},{6,30},{7,13},{8,16},{9,3... | collective-permute-start | bytes 393224 | tf_op jit(solution)/shard_map/ppermute | solution.py:55
  32.5 2.8 %collective-permute-done.11.refs_1_ = bf16[64,1024]{1,0:T(8,128)(2,1)S(1)} collective-permute-done((bf16[64,1024]{1,0:T(8,128)(2,1)S(1)}, bf16[64,1024]{1,0:T(8,128)(2,1)S(1)}, u32[]{:S(2)}, u32[]{:S(2)}) %collective-permute-start.11) | collective-permute-done | bytes 131104 | tf_op jit(solution)/shard_map/ppermute | solution.py:55
  35.3 1.1 %collective-permute-start.12 = (bf16[160,1024]{1,0:T(8,128)(2,1)S(1)}, bf16[160,1024]{1,0:T(8,128)(2,1)S(1)}, u32[]{:S(2)}, u32[]{:S(2)}) collective-permute-start(bf16[160,1024]{1,0:T(8,128)(2,1)S(1)} %shard_map.84), channel_id=1, source_target_pairs={{0,8},{1,9},{2,10},{3,11},{4,12},{5,13},{6,14},{7,15},{8,0},{9,1},... | collective-permute-start | bytes 983048 | tf_op jit(solution)/shard_map/ppermute | solution.py:55
  36.7 1.3 %collective-permute-done.14.refs_1_.refs_3_ = bf16[64,1024]{1,0:T(8,128)(2,1)S(1)} collective-permute-done((bf16[64,1024]{1,0:T(8,128)(2,1)S(1)}, bf16[64,1024]{1,0:T(8,128)(2,1)S(1)}, u32[]{:S(2)}, u32[]{:S(2)}) %collective-permute-start.14) | collective-permute-done | bytes 131104 | tf_op jit(solution)/shard_map/ppermute | solution.py:55
  38.2 1.1 %shard_map.86 = (bf16[128,4096]{1,0:T(8,128)(2,1)}, f32[16,4096]{1,0:T(8,128)}, f32[16,4096]{1,0:T(8,128)}) custom-call(f32[16,4096]{1,0:T(8,128)S(1)} %copy-done, f32[16,4096]{1,0:T(8,128)S(1)} %copy-done.1, bf16[16,1024]{1,0:T(8,128)(2,1)S(1)} %get-tuple-element.35.grad.refs_2_, bf16[16,1024]{1,0:T(8,128)(2,1)S(1)} %collective-permute-done.10.refs_3_.far_grad, ...), custom_call_target="tpu_custom_call" | custom-call | tf_op jit(solution)/shard_map/pallas_call | solution.py:37
  39.6 0.8 %shard_map.87 = bf16[128,4096]{1,0:T(8,128)(2,1)} custom-call(bf16[160,1024]{1,0:T(8,128)(2,1)S(1)} %collective-permute-done.12.early, bf16[128,1024]{1,0:T(8,128)(2,1)S(1)} %collective-permute-done.15.late, bf16[128,4096]{1,0:T(8,128)(2,1)} %get-tuple-element.44._), custom_call_target="tpu_custom_call", output_to_operand_aliasing={{}: (2, {})} | custom-call | tf_op jit(solution)/shard_map/pallas_call | solution.py:37
  (28 shorter events, 3.2 us)
Async XLA Ops:
  0.6 2.0 %copy-start.2 = (bf16[768,128]{1,0:T(8,128)(2,1)S(1)}, bf16[768,128]{1,0:T(8,128)(2,1)}, u32[]{:S(2)}) copy-start(bf16[768,128]{1,0:T(8,128)(2,1)} %acts.1) | copy-start | bytes 589828
  2.6 19.8 %copy-start = (f32[16,4096]{1,0:T(8,128)S(1)}, f32[16,4096]{1,0:T(8,128)}, u32[]{:S(2)}) copy-start(f32[16,4096]{1,0:T(8,128)} %m.3) | copy-start | bytes 786436
  2.6 19.8 %copy-start.1 = (f32[16,4096]{1,0:T(8,128)S(1)}, f32[16,4096]{1,0:T(8,128)}, u32[]{:S(2)}) copy-start(f32[16,4096]{1,0:T(8,128)} %v.3) | copy-start | bytes 786436
  2.6 19.8 %copy-start.3 = (bf16[16,4096]{1,0:T(8,128)(2,1)S(1)}, bf16[16,4096]{1,0:T(8,128)(2,1)}, u32[]{:S(2)}) copy-start(bf16[16,4096]{1,0:T(8,128)(2,1)} %w.1) | copy-start | bytes 393220
  3.3 2.8 %collective-permute-start = (bf16[128,2048]{1,0:T(8,128)(2,1)S(1)}, bf16[128,2048]{1,0:T(8,128)(2,1)S(1)}, u32[]{:S(2)}, u32[]{:S(2)}) collective-permute-start(bf16[128,2048]{1,0:T(8,128)(2,1)S(1)} %get-tuple-element.26), channel_id=1, source_target_pairs={{0,8},{1,9},{2,10},{3,11},{4,12},{5,13},{6,14},{7,15},{8,0},{9,1},... | collective-permute-start | bytes 1572872 | tf_op jit(solution)/shard_map/ppermute | solution.py:55
  6.2 6.5 %collective-permute-start.1 = (bf16[64,1024]{1,0:T(8,128)(2,1)S(1)}, bf16[64,1024]{1,0:T(8,128)(2,1)S(1)}, u32[]{:S(2)}, u32[]{:S(2)}) collective-permute-start(bf16[64,1024]{1,0:T(8,128)(2,1)S(1)} %get-tuple-element.28), channel_id=1, source_target_pairs={{0,17},{1,5},{2,6},{3,18},{4,21},{5,1},{6,2},{7,22},{8,12},{9,24},... | collective-permute-start | bytes 393224 | tf_op jit(solution)/shard_map/ppermute | solution.py:55
  9.8 4.4 %collective-permute-start.2 = (bf16[64,1024]{1,0:T(8,128)(2,1)S(1)}, bf16[64,1024]{1,0:T(8,128)(2,1)S(1)}, u32[]{:S(2)}, u32[]{:S(2)}) collective-permute-start(bf16[64,1024]{1,0:T(8,128)(2,1)S(1)} %get-tuple-element.29), channel_id=1, source_target_pairs={{0,9},{1,15},{2,12},{3,10},{4,13},{5,11},{6,8},{7,14},{8,6},{9,0},... | collective-permute-start | bytes 393224 | tf_op jit(solution)/shard_map/ppermute | solution.py:55
  10.1 4.4 %collective-permute-start.3 = (bf16[64,1024]{1,0:T(8,128)(2,1)S(1)}, bf16[64,1024]{1,0:T(8,128)(2,1)S(1)}, u32[]{:S(2)}, u32[]{:S(2)}) collective-permute-start(bf16[64,1024]{1,0:T(8,128)(2,1)S(1)} %get-tuple-element.30), channel_id=1, source_target_pairs={{0,24},{1,11},{2,8},{3,27},{4,28},{5,15},{6,12},{7,31},{8,2},{9,17... | collective-permute-start | bytes 393224 | tf_op jit(solution)/shard_map/ppermute | solution.py:55
  14.5 4.9 %collective-permute-start.4 = (bf16[16,1024]{1,0:T(8,128)(2,1)S(1)}, bf16[16,1024]{1,0:T(8,128)(2,1)S(1)}, u32[]{:S(2)}, u32[]{:S(2)}) collective-permute-start(bf16[16,1024]{1,0:T(8,128)(2,1)S(1)} %get-tuple-element.32), channel_id=1, source_target_pairs={{0,4},{1,16},{2,19},{3,7},{4,0},{5,20},{6,23},{7,3},{8,25},{9,13},... | collective-permute-start | bytes 98312 | tf_op jit(solution)/shard_map/ppermute | solution.py:55
  17.3 5.1 %collective-permute-start.5 = (bf16[16,1024]{1,0:T(8,128)(2,1)S(1)}, bf16[16,1024]{1,0:T(8,128)(2,1)S(1)}, u32[]{:S(2)}, u32[]{:S(2)}) collective-permute-start(bf16[16,1024]{1,0:T(8,128)(2,1)S(1)} %get-tuple-element.33), channel_id=1, source_target_pairs={{0,14},{1,8},{2,11},{3,13},{4,10},{5,12},{6,15},{7,9},{8,1},{9,7},... | collective-permute-start | bytes 98312 | tf_op jit(solution)/shard_map/ppermute | solution.py:55
  18.5 4.0 %collective-permute-start.6 = (bf16[16,1024]{1,0:T(8,128)(2,1)S(1)}, bf16[16,1024]{1,0:T(8,128)(2,1)S(1)}, u32[]{:S(2)}, u32[]{:S(2)}) collective-permute-start(bf16[16,1024]{1,0:T(8,128)(2,1)S(1)} %get-tuple-element.34), channel_id=1, source_target_pairs={{0,10},{1,25},{2,26},{3,9},{4,14},{5,29},{6,30},{7,13},{8,16},{9,3... | collective-permute-start | bytes 98312 | tf_op jit(solution)/shard_map/ppermute | solution.py:55
  22.6 5.0 %collective-permute-start.7 = (bf16[16,1024]{1,0:T(8,128)(2,1)S(1)}, bf16[16,1024]{1,0:T(8,128)(2,1)S(1)}, u32[]{:S(2)}, u32[]{:S(2)}) collective-permute-start(bf16[16,1024]{1,0:T(8,128)(2,1)S(1)} %get-tuple-element.38), channel_id=1, source_target_pairs={{0,17},{1,5},{2,6},{3,18},{4,21},{5,1},{6,2},{7,22},{8,12},{9,24},... | collective-permute-start | bytes 98312 | tf_op jit(solution)/shard_map/ppermute | solution.py:55
  24.1 3.7 %collective-permute-start.8 = (bf16[16,1024]{1,0:T(8,128)(2,1)S(1)}, bf16[16,1024]{1,0:T(8,128)(2,1)S(1)}, u32[]{:S(2)}, u32[]{:S(2)}) collective-permute-start(bf16[16,1024]{1,0:T(8,128)(2,1)S(1)} %get-tuple-element.39), channel_id=1, source_target_pairs={{0,9},{1,15},{2,12},{3,10},{4,13},{5,11},{6,8},{7,14},{8,6},{9,0},... | collective-permute-start | bytes 98312 | tf_op jit(solution)/shard_map/ppermute | solution.py:55
  24.9 3.3 %collective-permute-start.10 = (bf16[16,1024]{1,0:T(8,128)(2,1)S(1)}, bf16[16,1024]{1,0:T(8,128)(2,1)S(1)}, u32[]{:S(2)}, u32[]{:S(2)}) collective-permute-start(bf16[16,1024]{1,0:T(8,128)(2,1)S(1)} %get-tuple-element.40), channel_id=1, source_target_pairs={{0,24},{1,25},{2,26},{3,27},{4,28},{5,29},{6,30},{7,31},{8,16},{9,... | collective-permute-start | bytes 98312 | tf_op jit(solution)/shard_map/ppermute | solution.py:55
  25.8 3.3 %collective-permute-start.9 = (bf16[16,1024]{1,0:T(8,128)(2,1)S(1)}, bf16[16,1024]{1,0:T(8,128)(2,1)S(1)}, u32[]{:S(2)}, u32[]{:S(2)}) collective-permute-start(bf16[16,1024]{1,0:T(8,128)(2,1)S(1)} %get-tuple-element.37.own), channel_id=1, source_target_pairs={{0,24},{1,11},{2,8},{3,27},{4,28},{5,15},{6,12},{7,31},{8,2},{9,17... | collective-permute-start | bytes 98312 | tf_op jit(solution)/shard_map/ppermute | solution.py:55
  29.2 6.1 %collective-permute-start.11 = (bf16[64,1024]{1,0:T(8,128)(2,1)S(1)}, bf16[64,1024]{1,0:T(8,128)(2,1)S(1)}, u32[]{:S(2)}, u32[]{:S(2)}) collective-permute-start(bf16[64,1024]{1,0:T(8,128)(2,1)S(1)} %get-tuple-element.42), channel_id=1, source_target_pairs={{0,4},{1,16},{2,19},{3,7},{4,0},{5,20},{6,23},{7,3},{8,25},{9,13},... | collective-permute-start | bytes 393224 | tf_op jit(solution)/shard_map/ppermute | solution.py:55
  30.3 6.4 %collective-permute-start.13 = (bf16[64,1024]{1,0:T(8,128)(2,1)S(1)}, bf16[64,1024]{1,0:T(8,128)(2,1)S(1)}, u32[]{:S(2)}, u32[]{:S(2)}) collective-permute-start(bf16[64,1024]{1,0:T(8,128)(2,1)S(1)} %get-tuple-element.43), channel_id=1, source_target_pairs={{0,14},{1,8},{2,11},{3,13},{4,10},{5,12},{6,15},{7,9},{8,1},{9,7},... | collective-permute-start | bytes 393224 | tf_op jit(solution)/shard_map/ppermute | solution.py:55
  31.2 6.8 %collective-permute-start.14 = (bf16[64,1024]{1,0:T(8,128)(2,1)S(1)}, bf16[64,1024]{1,0:T(8,128)(2,1)S(1)}, u32[]{:S(2)}, u32[]{:S(2)}) collective-permute-start(bf16[64,1024]{1,0:T(8,128)(2,1)S(1)} %get-tuple-element.41.refs_0_), channel_id=1, source_target_pairs={{0,10},{1,25},{2,26},{3,9},{4,14},{5,29},{6,30},{7,13},{8,16},{9,3... | collective-permute-start | bytes 393224 | tf_op jit(solution)/shard_map/ppermute | solution.py:55
  35.3 2.9 %collective-permute-start.12 = (bf16[160,1024]{1,0:T(8,128)(2,1)S(1)}, bf16[160,1024]{1,0:T(8,128)(2,1)S(1)}, u32[]{:S(2)}, u32[]{:S(2)}) collective-permute-start(bf16[160,1024]{1,0:T(8,128)(2,1)S(1)} %shard_map.84), channel_id=1, source_target_pairs={{0,8},{1,9},{2,10},{3,11},{4,12},{5,13},{6,14},{7,15},{8,0},{9,1},... | collective-permute-start | bytes 983048 | tf_op jit(solution)/shard_map/ppermute | solution.py:55
  38.0 1.6 %collective-permute-start.15 = (bf16[128,1024]{1,0:T(8,128)(2,1)S(1)}, bf16[128,1024]{1,0:T(8,128)(2,1)S(1)}, u32[]{:S(2)}, u32[]{:S(2)}) collective-permute-start(bf16[128,1024]{1,0:T(8,128)(2,1)S(1)} %shard_map.85), channel_id=1, source_target_pairs={{0,8},{1,9},{2,10},{3,11},{4,12},{5,13},{6,14},{7,15},{8,0},{9,1},... | collective-permute-start | bytes 786440 | tf_op jit(solution)/shard_map/ppermute | solution.py:55
